TPU v7x, 128 devices: a whole 4x4x4 slice. The times are simulated.
128 devices in a mesh: tm: 4 (over x_lo, core), height: 32 (over x_hi, y, z).
Axes of the slice: x: 4 (x_hi: 2, x_lo: 2; x = x_hi * 2 + x_lo), y: 4, z: 4, core: 2. Of those that a mesh axis runs over, the one named last changes fastest.
Arguments:
- hidden: bfloat16 [12, 64, 48, 3072], P(None, 'height', 'tm'), may hold values from -6 to 6
- mod_scale: float32 [3072], replicated, may hold values from -2.5 to 2.5
- mod_shift: float32 [3072], replicated, may hold values from -4 to 4
- w_out: bfloat16 [3072, 64], replicated, may hold values from -0.109375 to 0.109375
- w_in: bfloat16 [3, 3, 3, 16, 512], replicated, may hold values from -0.3125 to 0.3125
- w_section: bfloat16 [3, 3, 3, 512, 512], replicated, may hold values from -0.0546875 to 0.0546875
- section_grad: bfloat16 [12, 128, 96, 512], P('tm', 'height'), may hold values from -6 to 6
Outputs:
- grad_hidden: bfloat16 [12, 64, 48, 3072], P(None, 'height', 'tm')
- grad_out_weight: float32 [3072, 64], P(('tm', 'height'))
All inputs are finite; a program needn't handle non-finite values.
Results may differ from a plain program's by a relative error of at most 0.015.
Values may be sent and summed in bfloat16 or wider, within the bound.
No kernel may reach another device: no remote copies, remote signals or barrier semaphores. Data moves between devices by JAX's collectives and lax.ppermute only.
A program may use at most 128 MiB of HBM per device.

v0:
```python
import math

import jax
import jax.numpy as jnp
from jax import lax
from jax.sharding import PartitionSpec as P

epsilon = 1e-05


def padded(block, sides, width):
    for axis, dim in sides:
        count = lax.axis_size(axis)
        forward = [(i, i + 1) for i in range(count - 1)]
        backward = [(target, source) for source, target in forward]
        low = lax.ppermute(
            lax.slice_in_dim(block, block.shape[dim] - width, None, axis=dim), axis, forward
        )
        high = lax.ppermute(lax.slice_in_dim(block, 0, width, axis=dim), axis, backward)
        block = jnp.concatenate([low, block, high], axis=dim)
    return block


def modulate(hidden, mod_scale, mod_shift):
    values = hidden.astype(jnp.float32)
    center = jnp.mean(values, axis=-1, keepdims=True)
    spread = jnp.mean((values - center) * (values - center), axis=-1, keepdims=True)
    inverse = lax.rsqrt(spread + epsilon)
    normed = (values - center) * inverse
    modulated = (normed * (1.0 + mod_scale) + mod_shift).astype(jnp.bfloat16)
    return (normed, inverse, modulated)


def to_grid(tokens):
    frame_count, row_count, col_count, token_width = tokens.shape
    lat_width = token_width // 4
    blocks = tokens.reshape(frame_count, row_count, col_count, 2, 2, lat_width)
    blocks = jnp.transpose(blocks, (0, 1, 3, 2, 4, 5))
    return blocks.reshape(frame_count, 2 * row_count, 2 * col_count, lat_width)


def to_tokens(field):
    frame_count, row_count, col_count, lat_width = field.shape
    blocks = field.reshape(frame_count, row_count // 2, 2, col_count // 2, 2, lat_width)
    blocks = jnp.transpose(blocks, (0, 1, 3, 2, 4, 5))
    return blocks.reshape(frame_count, row_count // 2, col_count // 2, 4 * lat_width)


def input_conv(latent_win, w_in, row_count, col_count):
    pieces = []
    for tap_time in range(3):
        for tap_row in range(3):
            for tap_col in range(3):
                pieces.append(
                    latent_win[
                        tap_time, tap_row : tap_row + row_count, tap_col : tap_col + col_count
                    ]
                )
    stacked = jnp.concatenate(pieces, axis=-1)
    flat_weight = w_in.reshape(-1, w_in.shape[-1])
    preact = jnp.dot(
        stacked.reshape(row_count * col_count, -1), flat_weight, preferred_element_type=jnp.float32
    )
    return preact.reshape(row_count, col_count, -1)


def section_back(grad_win, w_section, row_count, col_count):
    channels = w_section.shape[3]
    running = jnp.zeros((row_count * col_count, channels), jnp.float32)
    for tap_time in range(3):
        for tap_row in range(3):
            pieces = [
                grad_win[
                    2 - tap_time,
                    2 - tap_row : 2 - tap_row + row_count,
                    2 - tap_col : 2 - tap_col + col_count,
                ]
                for tap_col in range(3)
            ]
            window = jnp.concatenate(pieces, axis=-1).reshape(row_count * col_count, -1)
            turned = jnp.transpose(w_section[tap_time, tap_row], (0, 2, 1)).reshape(-1, channels)
            running = running + jnp.dot(window, turned, preferred_element_type=jnp.float32)
    return running.reshape(row_count, col_count, channels)


def silu_slope(preact):
    squash = jax.nn.sigmoid(preact)
    return squash * (1.0 + preact * (1.0 - squash))


def spread_back(act_grad, w_in):
    row_count, col_count, channels = act_grad.shape
    lat_width = w_in.shape[3]
    flat_weight = w_in.reshape(-1, channels)
    tap_terms = lax.dot_general(
        act_grad.reshape(row_count * col_count, channels),
        flat_weight,
        (((1,), (1,)), ((), ())),
        preferred_element_type=jnp.float32,
    )
    tap_terms = tap_terms.reshape(row_count, col_count, 3, 3, 3, lat_width)
    placed_terms = jnp.zeros((3, row_count + 2, col_count + 2, lat_width), jnp.float32)
    for tap_time in range(3):
        for tap_row in range(3):
            for tap_col in range(3):
                placed_terms = placed_terms.at[
                    tap_time, tap_row : tap_row + row_count, tap_col : tap_col + col_count
                ].add(tap_terms[:, :, tap_time, tap_row, tap_col])
    return placed_terms


def norm_back(mod_grad, normed, inverse, mod_scale):
    scaled = mod_grad * (1.0 + mod_scale)
    first_mean = jnp.mean(scaled, axis=-1, keepdims=True)
    second_mean = jnp.mean(scaled * normed, axis=-1, keepdims=True)
    return ((scaled - first_mean - normed * second_mean) * inverse).astype(jnp.bfloat16)


def shards(hidden, mod_scale, mod_shift, w_out, w_in, w_section, section_grad):
    normed, inverse, modulated = modulate(hidden, mod_scale, mod_shift)
    frame_count, token_rows, token_cols, model_width = hidden.shape
    token_width = w_out.shape[1]
    lat_width = w_in.shape[3]
    frame_block = section_grad.shape[0]
    row_count = section_grad.shape[1]
    flat_mod = modulated.reshape(-1, model_width)
    latent_tokens = jnp.dot(flat_mod, w_out, preferred_element_type=jnp.float32).astype(
        jnp.bfloat16
    )
    latent_part = to_grid(latent_tokens.reshape(frame_count, token_rows, token_cols, token_width))
    col_count = section_grad.shape[2]
    first_frame = lax.axis_index("tm") * frame_block
    zero_index = first_frame * 0
    latent_full, grad_full = (
        lax.all_gather(latent_part, "tm", axis=2, tiled=True),
        lax.all_gather(section_grad, "tm", axis=0, tiled=True),
    )
    latent_back = lax.dynamic_slice_in_dim(
        jnp.pad(latent_full, ((2, 0), (0, 0), (0, 0), (0, 0))), first_frame, frame_block + 2, 0
    )
    grad_ahead = lax.dynamic_slice_in_dim(
        jnp.pad(grad_full, ((0, 2), (0, 0), (0, 0), (0, 0))), first_frame, frame_block + 2, 0
    )
    combined = jnp.concatenate([latent_back, grad_ahead], axis=-1)
    rimmed = padded(combined, (("height", 1),), 1)
    widened = jnp.pad(rimmed, ((0, 0), (0, 0), (1, 1), (0, 0)))
    latent_win = widened[..., :lat_width]
    grad_win = widened[..., lat_width:]
    holder = jnp.zeros((frame_block + 2, row_count + 2, col_count, lat_width), jnp.float32)
    for local_frame in range(frame_block):
        preact = input_conv(latent_win[local_frame : local_frame + 3], w_in, row_count, col_count)
        back_grad = section_back(
            grad_win[local_frame : local_frame + 3], w_section, row_count, col_count
        )
        act_grad = (back_grad * silu_slope(preact)).astype(jnp.bfloat16)
        holder = holder.at[local_frame : local_frame + 3].add(
            spread_back(act_grad, w_in)[:, :, 1:-1]
        )
    blank = jnp.zeros((frame_count + 2, row_count + 2, col_count, lat_width), jnp.float32)
    placed = lax.dynamic_update_slice(
        blank, holder, (first_frame, zero_index, zero_index, zero_index)
    )[2:]
    summed = lax.psum_scatter(
        placed.astype(jnp.bfloat16), "tm", scatter_dimension=2, tiled=True
    ).astype(jnp.float32)
    edged = padded(summed.astype(jnp.bfloat16), (("height", 1),), 1).astype(summed.dtype)
    latent_grad = summed[:, 1 : row_count + 1]
    latent_grad = latent_grad.at[:, 0].add(edged[:, 0])
    latent_grad = latent_grad.at[:, row_count - 1].add(edged[:, row_count + 3])
    token_grad = to_tokens(latent_grad).astype(jnp.bfloat16)
    flat_grad = token_grad.reshape(-1, token_width)
    mod_grad = lax.dot_general(
        flat_grad, w_out, (((1,), (1,)), ((), ())), preferred_element_type=jnp.float32
    )
    grad_hidden = norm_back(mod_grad.reshape(hidden.shape), normed, inverse, mod_scale)
    device_count = lax.axis_size("tm") * lax.axis_size("height")
    total_tokens = flat_mod.shape[0] * device_count
    weight_part = lax.psum_scatter(
        lax.dot_general(
            flat_mod, flat_grad, (((0,), (0,)), ((), ())), preferred_element_type=jnp.float32
        ),
        ("tm", "height"),
        scatter_dimension=0,
        tiled=True,
    )
    grad_out_weight = weight_part / math.sqrt(total_tokens)
    return (grad_hidden, grad_out_weight)


def solution(mesh):
    placed = (P(None, "height", "tm", None), P(), P(), P(), P(), P(), P("tm", "height", None, None))
    return jax.shard_map(
        shards,
        mesh=mesh,
        in_specs=placed,
        out_specs=(P(None, "height", "tm", None), P(("tm", "height"), None)),
        check_vma=False,
    )
```

profile of v0, /device:TPU:6, one launch (start us, length us, event | category | flops | bytes accessed | tf_op | source)
XLA Modules:
  0.0 1089.7 jit_solution(11723401868495928244)
XLA Ops:
  12.2 2.8 fusion.7
  18.8 14.9 %all_gather.6 = bf16[12,4,96,16]{3,2,1,0:T(8,128)(2,1)S(1)} all-gather(bf16[12,4,24,16]{3,2,1,0:T(8,128)(2,1)S(1)} %bitcast.673), channel_id=1, replica_groups=mesh['tm'=4,'height'=32] {'tm'}, dimensions={2}, use_global_device_ids=true | all-gather | bytes 184320 | tf_op jit(solution)/shard_map/all_gather | solution.py:135
  34.9 31.3 %all-gather.2.cloned.1.call-done = bf16[12,4,96,512]{3,2,1,0:T(8,128)(2,1)} async-done(((bf16[3,4,96,512]{3,2,1,0:T(8,128)(2,1)}), bf16[12,4,96,512]{3,2,1,0:T(8,128)(2,1)}) %all-gather.2.cloned.1.call-update) | async-done | bytes 4718608 | tf_op jit(solution)/shard_map/all_gather | solution.py:136
  69.7 3.8 collective-permute-start
  73.5 8.0 collective-permute-start.1
  81.5 9.4 fusion.174
  116.9 2.8 pad_dynamic-slice_fusion
  119.7 6.3 select_maximum_fusion
  128.4 3.0 fusion.176
  131.5 5.8 fusion.175
  137.2 4.3 maximum_maximum_fusion
  167.6 3.6 concatenate.658
  179.7 3.4 concatenate.636
  183.1 3.1 fusion.50
  189.9 2.9 convolution_add_fusion.23
  204.3 2.6 concatenate.614
  214.4 2.6 scatter-add.389
  261.3 2.7 scatter-add.341
  281.4 2.6 scatter-add.295
  301.6 46.3 %all-reduce.11.cloned.1.call-done = bf16[12,6,96,16]{3,2,1,0:T(8,128)(2,1)} async-done(((bf16[12,6,96,16]{3,2,1,0:T(8,128)(2,1)}), bf16[12,6,96,16]{3,2,1,0:T(8,128)(2,1)}) %all-reduce.11.cloned.1.call-update) | async-done | bytes 221200
  348.8 3.5 collective-permute-start.2
  352.2 8.1 collective-permute-start.3
  370.1 3.0 copy.286
  373.2 708.2 %reduce-scatter.6.cloned.1.call-done = f32[24,64]{1,0:T(8,128)} async-done(((f32[3072,64]{1,0:T(8,128)}), f32[24,64]{1,0:T(8,128)}) %reduce-scatter.6.cloned.1.call-update) | async-done | bytes 6160
  (421 shorter events, 188.3 us)
Async XLA Ops:
  7.2 164.0 %copy-start = (bf16[3,3,3,16,512]{4,3,2,1,0:T(8,128)(2,1)S(1)}, bf16[3,3,3,16,512]{4,3,2,1,0:T(8,128)(2,1)}, u32[]{:S(2)}) copy-start(bf16[3,3,3,16,512]{4,3,2,1,0:T(8,128)(2,1)} %param.183) | copy-start | bytes 1327108
  7.2 3.5 copy-start.1
  7.2 59.0 %all-gather.2.cloned.1.call-start = ((), (), s32[]{:S(2)}) async-start(), calls=%async_computation.1 | async-start | bytes 5898240 | tf_op jit(solution)/shard_map/all_gather | solution.py:136
  7.9 339.9 %all-reduce.11.cloned.1.call-start = ((), (), s32[]{:S(2)}) async-start(), calls=%async_computation.2 | async-start | bytes 3538944
  8.7 2.9 copy-start.80
  8.7 3.5 copy-start.82
  69.7 50.0 %collective-permute-start = (bf16[5,1,96,528]{3,2,1,0:T(8,128)(2,1)}, bf16[5,1,96,528]{3,2,1,0:T(8,128)(2,1)}, u32[]{:S(2)}, u32[]{:S(2)}) collective-permute-start(bf16[5,1,96,528]{3,2,1,0:T(8,128)(2,1)} %get-tuple-element.1142), channel_id=1, source_target_pairs={{0,1},{1,2},{2,3},{3,4},{4,5},{5,6},{6,7},{7,8},{8,9},{9,10},{10,1... | collective-permute-start | bytes 1520648 | tf_op jit(solution)/shard_map/ppermute | solution.py:16
  73.5 46.2 %collective-permute-start.1 = (bf16[5,1,96,528]{3,2,1,0:T(8,128)(2,1)}, bf16[5,1,96,528]{3,2,1,0:T(8,128)(2,1)S(1)}, u32[]{:S(2)}, u32[]{:S(2)}) collective-permute-start(bf16[5,1,96,528]{3,2,1,0:T(8,128)(2,1)} %get-tuple-element.1143), channel_id=1, source_target_pairs={{1,0},{2,1},{3,2},{4,3},{5,4},{6,5},{7,6},{8,7},{9,8},{10,9},{11,1... | collective-permute-start | bytes 1520648 | tf_op jit(solution)/shard_map/ppermute | solution.py:19
  119.7 40.7 %copy-start.60 = (bf16[1,4,96,512]{3,2,1,0:T(8,128)(2,1)}, bf16[1,4,96,512]{3,2,1,0:T(8,128)(2,1)S(1)}, u32[]{:S(2)}) copy-start(bf16[1,4,96,512]{3,2,1,0:T(8,128)(2,1)S(1)} %get-tuple-element.1054) | copy-start | bytes 1179652
  131.4 29.0 %copy-start.53 = (bf16[1,4,96,512]{3,2,1,0:T(8,128)(2,1)}, bf16[1,4,96,512]{3,2,1,0:T(8,128)(2,1)S(1)}, u32[]{:S(2)}) copy-start(bf16[1,4,96,512]{3,2,1,0:T(8,128)(2,1)S(1)} %get-tuple-element.1114) | copy-start | bytes 1179652
  131.4 29.0 %copy-start.54 = (bf16[1,4,96,512]{3,2,1,0:T(8,128)(2,1)}, bf16[1,4,96,512]{3,2,1,0:T(8,128)(2,1)S(1)}, u32[]{:S(2)}) copy-start(bf16[1,4,96,512]{3,2,1,0:T(8,128)(2,1)S(1)} %get-tuple-element.1115) | copy-start | bytes 1179652
  131.4 32.0 %copy-start.49 = (bf16[1,4,96,512]{3,2,1,0:T(8,128)(2,1)}, bf16[1,4,96,512]{3,2,1,0:T(8,128)(2,1)S(1)}, u32[]{:S(2)}) copy-start(bf16[1,4,96,512]{3,2,1,0:T(8,128)(2,1)S(1)} %get-tuple-element.1112) | copy-start | bytes 1179652
  131.4 32.0 %copy-start.51 = (bf16[1,4,96,512]{3,2,1,0:T(8,128)(2,1)}, bf16[1,4,96,512]{3,2,1,0:T(8,128)(2,1)S(1)}, u32[]{:S(2)}) copy-start(bf16[1,4,96,512]{3,2,1,0:T(8,128)(2,1)S(1)} %get-tuple-element.1113) | copy-start | bytes 1179652
  143.9 19.6 %copy-start.66 = (bf16[1,4,96,512]{3,2,1,0:T(8,128)(2,1)}, bf16[1,4,96,512]{3,2,1,0:T(8,128)(2,1)S(1)}, u32[]{:S(2)}) copy-start(bf16[1,4,96,512]{3,2,1,0:T(8,128)(2,1)S(1)} %get-tuple-element.1134) | copy-start | bytes 1179652
  189.9 2.9 copy-start.28
  189.9 2.9 copy-start.50
  189.9 2.9 copy-start.52
  189.9 2.9 copy-start.67
  206.9 3.6 copy-start.39
  217.0 40.2 %copy-start.37 = (f32[4,96,3,3,3,16]{1,5,0,4,3,2:T(8,128)S(1)}, f32[4,96,3,3,3,16]{1,5,0,4,3,2:T(8,128)}, u32[]{:S(2)}) copy-start(f32[4,96,3,3,3,16]{1,5,0,4,3,2:T(8,128)} %fusion.50) | copy-start | bytes 1990660
  261.3 15.5 %copy-start.76 = (f32[1,4,96,16]{2,3,1,0:T(8,128)S(1)}, f32[1,4,96,16]{2,3,1,0:T(8,128)}, u32[]{:S(2)}) copy-start(f32[1,4,96,16]{2,3,1,0:T(8,128)} %fusion.71) | copy-start | bytes 73732
  299.7 781.7 %reduce-scatter.6.cloned.1.call-start = ((), (), s32[]{:S(2)}) async-start(), calls=%async_computation.3 | async-start | bytes 1585152
  348.8 12.8 %collective-permute-start.2 = (bf16[12,1,24,16]{3,2,1,0:T(8,128)(2,1)S(1)}, bf16[12,1,24,16]{3,2,1,0:T(8,128)(2,1)S(1)}, u32[]{:S(2)}, u32[]{:S(2)}) collective-permute-start(bf16[12,1,24,16]{3,2,1,0:T(8,128)(2,1)S(1)} %get-tuple-element.1144), channel_id=1, source_target_pairs={{0,1},{1,2},{2,3},{3,4},{4,5},{5,6},{6,7},{7,8},{8,9},{9,10},{10,1... | collective-permute-start | bytes 27656 | tf_op jit(solution)/shard_map/ppermute | solution.py:16
  352.2 10.1 collective-permute-start.3
  (68 other events, 113.7 us)
Sparse Core Ops, SparseCore 0:
  9.7 56.5 all-gather.1
  299.8 47.9 all-reduce.10
  366.5 714.8 reduce-scatter.5
where the time goes:
time: 1100 us; the launch traced here: 1090 us
  waiting for transfers between devices  787 us (72%)
  local copies, waits for them, and re-layouts  153 us (14%)
  other arithmetic  53.6 us (5%)
  matrix products  41.5 us (4%)
  starting transfers between devices  23.5 us (2%)
  between operations  16.3 us (1%)
  blocking collectives  14.9 us (1%)
    unnamed x5, waiting for transfers between devices  755 us
    scatter-add x81, local copies, waits for them, and re-layouts, spread_back(): placed_terms = placed_terms.at[tap_time, tap_row:tap_row + row_count, tap...  64.5 us
    unnamed x181, local copies, waits for them, and re-layouts  40.8 us
    all_gather x1, waiting for transfers between devices, shards(): lax.all_gather(section_grad, 'tm', axis=0, tiled=True)  31.3 us
    dot_general x27, matrix products, section_back(): jnp.dot(window, turned, preferred_element_type=jnp.float32)  29.2 us
    add x78, other arithmetic, spread_back(): placed_terms = placed_terms.at[tap_time, tap_row:tap_row + row_count, tap...  26.1 us
  transfers between devices with their start and end apart: 7, of which 4 were waited for; matrix products, arithmetic and copies ran while one was open for 5% of the time, Pallas kernels for 0%

commit v1 on v0

v1 whole, which is shorter than its diff:
```python
import functools
import math

import jax
import jax.numpy as jnp
from jax import lax
from jax.experimental import pallas as pl
from jax.experimental.pallas import tpu as pltpu
from jax.sharding import PartitionSpec as P

epsilon = 1e-05
slots = 16
lanes = 128
f32 = jnp.float32
bf16 = jnp.bfloat16
anywhere = pl.BlockSpec(memory_space=pl.ANY)
whole = pl.BlockSpec(memory_space=pltpu.VMEM)


def params(mib, *semantics):
    return pltpu.CompilerParams(
        vmem_limit_bytes=mib * 2**20, dimension_semantics=semantics or None
    )


def dot(lhs, rhs):
    return jnp.dot(lhs, rhs, preferred_element_type=f32)


def dot_turned(lhs, rhs):
    return lax.dot_general(lhs, rhs, (((1,), (1,)), ((), ())), preferred_element_type=f32)


def cut_kernel(grad, ahead, first, last, corner_first, corner_last, sems):
    rows = grad.shape[1]
    pieces = (
        (grad.at[0:2], ahead),
        (grad.at[:, 0:1], first),
        (grad.at[:, rows - 1 : rows], last),
        (grad.at[0:2, 0:1], corner_first),
        (grad.at[0:2, rows - 1 : rows], corner_last),
    )
    copies = [pltpu.make_async_copy(src, dst, sems.at[n]) for n, (src, dst) in enumerate(pieces)]
    for copy in copies:
        copy.start()
    for copy in copies:
        copy.wait()


def cut_halos(grad):
    frames, rows, cols, channels = grad.shape
    shapes = ((2, rows), (frames, 1), (frames, 1), (2, 1), (2, 1))
    return pl.pallas_call(
        cut_kernel,
        out_shape=[jax.ShapeDtypeStruct(s + (cols, channels), grad.dtype) for s in shapes],
        in_specs=[anywhere],
        out_specs=[anywhere] * 5,
        scratch_shapes=[pltpu.SemaphoreType.DMA((5,))],
        name="cut_halos",
    )(grad)


def normalise(values):
    center = jnp.mean(values, axis=-1, keepdims=True)
    shifted = values - center
    spread = jnp.mean(shifted * shifted, axis=-1, keepdims=True)
    inverse = lax.rsqrt(spread + epsilon)
    return shifted * inverse, inverse


def modulate_kernel(hidden, scale, shift, w_out, modulated, send):
    step = pl.program_id(0)
    frames, token_rows, tokens, width = hidden.shape
    gain = 1.0 + scale[...]
    blank = jnp.zeros((slots - tokens, width), f32)
    for frame in range(frames):
        for row in range(token_rows):
            normed, _ = normalise(hidden[frame, row].astype(f32))
            value = jnp.concatenate([normed * gain + shift[...], blank], axis=0)
            modulated[frame, row] = value.astype(bf16)
    flat = modulated[...].reshape(frames * token_rows * slots, width)
    latent = dot(flat, w_out[...]).astype(bf16)
    latent = latent.reshape(frames, token_rows, slots, latent.shape[-1])
    paired = jnp.concatenate([latent[:, 0], latent[:, 1]], axis=-1)
    for frame in range(frames):
        send[step, frame + 2] = paired[frame]

    @pl.when(step == 0)
    def _():
        send[0, 0:2] = jnp.zeros_like(send[0, 0:2])

    @pl.when(step < pl.num_programs(0) - 1)
    def _():
        for frame in range(1, frames):
            send[step + 1, frame - 1] = paired[frame]


def modulate(hidden, mod_scale, mod_shift, w_out, groups):
    frames, token_rows, tokens, width = hidden.shape
    block = frames // groups
    token_width = w_out.shape[1]
    held = lambda *dims: pl.BlockSpec(dims, lambda g: (0,) * len(dims))
    return pl.pallas_call(
        modulate_kernel,
        grid=(groups,),
        out_shape=[
            jax.ShapeDtypeStruct((frames, token_rows, slots, width), bf16),
            jax.ShapeDtypeStruct((groups, block + 2, slots, 2 * token_width), bf16),
        ],
        in_specs=[
            pl.BlockSpec((block, token_rows, tokens, width), lambda g: (g, 0, 0, 0)),
            held(1, width),
            held(1, width),
            held(width, token_width),
        ],
        out_specs=[
            pl.BlockSpec((block, token_rows, slots, width), lambda g: (g, 0, 0, 0)),
            held(groups, block + 2, slots, 2 * token_width),
        ],
        compiler_params=params(40, "arbitrary"),
        cost_estimate=pl.CostEstimate(
            flops=2 * frames * 2 * slots * width * token_width,
            bytes_accessed=8 * frames * slots * width,
            transcendentals=0,
        ),
        name="modulate",
    )(hidden, mod_scale.reshape(1, -1), mod_shift.reshape(1, -1), w_out)


def column_shifts(value):
    cols, channels = value.shape
    wide = value.astype(f32)
    place = lax.broadcasted_iota(jnp.int32, (cols, channels), 0)
    nxt = jnp.where(place == cols - 1, 0.0, pltpu.roll(wide, cols - 1, 0))
    prv = jnp.where(place == 0, 0.0, pltpu.roll(wide, 1, 0))
    return nxt.astype(bf16), prv.astype(bf16)


def tap_of(step):
    turn = step % 3
    return 2 - step // 3, jnp.where(turn == 0, 1, jnp.where(turn == 1, 0, 2))


taps = [(2 - n // 3, (1, 0, 2)[n % 3]) for n in range(9)]


def weight_matrix(w_section):
    return jnp.concatenate([w_section[0, 0, kx] for kx in range(3)], axis=-1)


def flat(value):
    return value.reshape(-1, value.shape[-1])


def own_kernel(grad, w_section, total, shifts):
    step = pl.program_id(0)
    frames, rows, cols, channels = grad.shape

    @pl.when(step == 0)
    def _():
        for frame in range(frames):
            for row in range(rows):
                shifts[0, frame, row], shifts[1, frame, row] = column_shifts(grad[frame, row])

    for n, (kt, ky) in enumerate(taps):

        @pl.when(step == n)
        def _(n=n, kt=kt, ky=ky):
            lo, hi = max(0, ky - 1), rows + min(0, ky - 1)
            src = slice(2 - kt, frames), slice(lo + 1 - ky, hi + 1 - ky)
            window = jnp.concatenate(
                [flat(shifts[(0,) + src]), flat(grad[src]), flat(shifts[(1,) + src])], axis=-1
            )
            part = dot_turned(window, weight_matrix(w_section))
            for lane in range(channels // lanes):
                value = part[:, lane * lanes : (lane + 1) * lanes]
                value = value.reshape(kt + 1, hi - lo, cols, lanes)
                if n == 0:
                    total[lane] = value
                else:
                    total[lane, 0 : kt + 1, lo:hi] += value


def own_part(grad, w_section):
    frames, rows, cols, channels = grad.shape
    return pl.pallas_call(
        own_kernel,
        grid=(9,),
        out_shape=jax.ShapeDtypeStruct((channels // lanes, frames, rows, cols, lanes), f32),
        in_specs=[
            pl.BlockSpec(grad.shape, lambda n: (0, 0, 0, 0)),
            pl.BlockSpec((1, 1, 3, channels, channels), lambda n: tap_of(n) + (0, 0, 0)),
        ],
        out_specs=pl.BlockSpec(
            (channels // lanes, frames, rows, cols, lanes), lambda n: (0, 0, 0, 0, 0)
        ),
        scratch_shapes=[pltpu.VMEM((2,) + grad.shape, bf16)],
        compiler_params=params(48, "arbitrary"),
        cost_estimate=pl.CostEstimate(
            flops=2 * 15 * grad.size * channels,
            bytes_accessed=2 * w_section.size,
            transcendentals=0,
        ),
        name="own_part",
    )(grad, w_section)


def rest_kernel(
    own,
    grad_ahead,
    above,
    below,
    above_ahead,
    below_ahead,
    w_section,
    latent,
    latent_above,
    latent_below,
    w_in,
    centre_out,
    up_out,
    down_out,
    total,
    far,
    near,
    tokens,
    windows,
    patches,
    spread,
):
    step = pl.program_id(0)
    blocks, frames, rows, cols, _ = own.shape
    groups, depth, _, pair = latent.shape
    width = pair // 2
    block = cols // (2 * groups)
    half = cols // 2

    @pl.when(step == 0)
    def _():
        total[...] = own[...]
        for frame in range(2):
            for row in range(rows + 2):
                if row == 0:
                    value = above_ahead[frame, 0]
                elif row == rows + 1:
                    value = below_ahead[frame, 0]
                else:
                    value = grad_ahead[frame, row - 1]
                far[1, frame, row] = value
                far[0, frame, row], far[2, frame, row] = column_shifts(value)
        for frame in range(frames):
            for side, ref in ((0, above), (1, below)):
                value = ref[frame, 0]
                near[1, side, frame] = value
                near[0, side, frame], near[2, side, frame] = column_shifts(value)

    for n, (kt, ky) in enumerate(taps):
        if (kt, ky) == (2, 1):
            continue

        @pl.when(step == n - 1)
        def _(kt=kt, ky=ky):
            pieces, places = [], []
            if kt < 2:
                src = slice(0, 2 - kt), slice(2 - ky, 2 - ky + rows)
                pieces.append([far[(kx,) + src] for kx in range(3)])
                places.append((slice(kt + 1, frames), slice(0, rows)))
            if ky != 1:
                side = 0 if ky == 2 else 1
                edge = 0 if ky == 2 else rows - 1
                pieces.append([near[kx, side, 2 - kt : frames] for kx in range(3)])
                places.append((slice(0, kt + 1), slice(edge, edge + 1)))
            window = jnp.concatenate(
                [jnp.concatenate([flat(v) for v in piece], axis=-1) for piece in pieces], axis=0
            )
            part = dot_turned(window, weight_matrix(w_section))
            at = 0
            for place in places:
                shape = [cut.stop - cut.start for cut in place] + [cols, lanes]
                count = shape[0] * shape[1] * cols
                for lane in range(blocks):
                    value = part[at : at + count, lane * lanes : (lane + 1) * lanes]
                    total[(lane,) + place] += value.reshape(shape)
                at += count

    @pl.when(step == pl.num_programs(0) - 1)
    def _():
        tokens[...] = jnp.zeros_like(tokens)
        for src in range(groups):
            at = slice(8 + src * block, 8 + (src + 1) * block)
            for frame in range(depth):
                value = latent[src, frame].astype(f32)[:block]
                tokens[frame, 1, at] = value[:, :width]
                tokens[frame, 2, at] = value[:, width:]
                tokens[frame, 0, at] = latent_above[src, frame].astype(f32)[:block, width:]
                tokens[frame, 3, at] = latent_below[src, frame].astype(f32)[:block, :width]
        for q in range(2):
            left = tokens[:, :, 7 + q : 7 + q + half]
            right = tokens[:, :, 8 + q : 8 + q + half]
            windows[q] = jnp.concatenate([left, right], axis=-1).astype(bf16)
        patches[...] = jnp.zeros_like(patches)
        lat = width // 4
        for p in range(2):
            for q in range(2):
                for kt in range(3):
                    for a in range(2):
                        for b in range(2):
                            for pp in range(2):
                                for qq in range(2):
                                    ky, kx = p - 1 + 2 * a + pp, q - 1 + 2 * b + qq
                                    if not (0 <= ky < 3 and 0 <= kx < 3):
                                        continue
                                    at = (kt * 2 + a) * pair + b * width + (2 * pp + qq) * lat
                                    patches[2 * p + q, at : at + lat] = w_in[kt, ky, kx]
        spread[...] = jnp.zeros_like(spread)
        for p in range(2):
            for q in range(2):
                window = jnp.concatenate(
                    [
                        flat(windows[q, kt : kt + frames, p + a : p + a + rows // 2])
                        for kt in range(3)
                        for a in range(2)
                    ],
                    axis=-1,
                )
                weight = patches[2 * p + q]
                pre = dot(window, weight)
                back = jnp.concatenate(
                    [
                        jnp.concatenate(
                            [
                                total[lane, frame, 2 * row + p, pl.ds(q, half, stride=2), :]
                                for lane in range(blocks)
                            ],
                            axis=-1,
                        )
                        for frame in range(frames)
                        for row in range(rows // 2)
                    ],
                    axis=0,
                )
                gate = jax.nn.sigmoid(pre)
                act_grad = (back * (gate * (1.0 + pre * (1.0 - gate)))).astype(bf16)
                terms = dot_turned(act_grad, weight)
                for kt in range(3):
                    for a in range(2):
                        at = (kt * 2 + a) * pair
                        spread[kt : kt + frames, p + a : p + a + rows // 2, q : q + half] += terms[
                            :, at : at + pair
                        ].reshape(frames, rows // 2, half, pair)
        centre_out[...] = jnp.zeros_like(centre_out)
        up_out[...] = jnp.zeros_like(up_out)
        down_out[...] = jnp.zeros_like(down_out)
        grid = spread[:, :, 1 : half + 1, :width] + spread[:, :, 0:half, width:]
        tokens[:, :, 0:half] = grid
        for dst in range(groups):
            for frame in range(depth):
                value = [
                    tokens[frame, row, dst * block : (dst + 1) * block] for row in range(4)
                ]
                none = jnp.zeros_like(value[0])
                centre_out[dst, frame, 0:block] = jnp.concatenate([value[1], value[2]], axis=-1)
                up_out[dst, frame, 0:block] = jnp.concatenate([none, value[0]], axis=-1)
                down_out[dst, frame, 0:block] = jnp.concatenate([value[3], none], axis=-1)


def rest_part(own, halos, w_section, latents, w_in):
    blocks, frames, rows, cols, _ = own.shape
    channels = blocks * lanes
    groups, depth, _, pair = latents[0].shape
    held = lambda value: pl.BlockSpec(value.shape, lambda n: (0,) * value.ndim)
    out = jax.ShapeDtypeStruct(latents[0].shape, f32)
    return pl.pallas_call(
        rest_kernel,
        grid=(8,),
        out_shape=[out] * 3,
        in_specs=[held(own)]
        + [held(value) for value in halos]
        + [pl.BlockSpec((1, 1, 3, channels, channels), lambda n: tap_of(n + 1) + (0, 0, 0))]
        + [held(value) for value in latents]
        + [held(w_in)],
        out_specs=[held(out)] * 3,
        scratch_shapes=[
            pltpu.VMEM(own.shape, f32),
            pltpu.VMEM((3, 2, rows + 2, cols, channels), bf16),
            pltpu.VMEM((3, 2, frames, cols, channels), bf16),
            pltpu.VMEM((depth, rows // 2 + 2, 72, pair // 2), f32),
            pltpu.VMEM((2, depth, rows // 2 + 2, cols // 2, pair), bf16),
            pltpu.VMEM((4, 6 * pair, channels), bf16),
            pltpu.VMEM((depth, rows // 2 + 2, cols // 2 + 8, pair), f32),
        ],
        compiler_params=params(56, "arbitrary"),
        cost_estimate=pl.CostEstimate(
            flops=2 * 16 * own.size * channels,
            bytes_accessed=2 * w_section.size,
            transcendentals=2 * own.size,
        ),
        name="rest_part",
    )(own, *halos, w_section, *latents, w_in)


def weight_kernel(shares, modulated, token_grad, send, field):
    groups, depth, _, pair = shares.shape
    width = pair // 2
    frames, token_rows = modulated.shape[:2]
    model = modulated.shape[-1]
    field[...] = jnp.zeros_like(field)
    for src in range(groups):
        at = src * (frames // groups)
        field[at : at + depth] += shares[src].astype(f32)
    values = field[2 : 2 + frames]
    token_grad[:, 0] = values[:, :, :width].astype(bf16)
    token_grad[:, 1] = values[:, :, width:].astype(bf16)
    turned = jnp.transpose(token_grad[...].reshape(-1, width).astype(f32)).astype(bf16)
    weight = dot(turned, modulated[...].reshape(-1, model))
    half = model // (2 * groups)
    for dst in range(groups):
        at = 2 * half * dst
        stacked = jnp.concatenate(
            [weight[:, at : at + half], weight[:, at + half : at + 2 * half]], axis=0
        )
        send[dst] = jnp.transpose(stacked).astype(bf16)


def weight_terms(shares, modulated):
    groups, depth, _, pair = shares.shape
    frames, token_rows, _, model = modulated.shape
    return pl.pallas_call(
        weight_kernel,
        out_shape=[
            jax.ShapeDtypeStruct((frames, token_rows, slots, pair // 2), bf16),
            jax.ShapeDtypeStruct((groups, model // (2 * groups), pair), bf16),
        ],
        in_specs=[whole] * 2,
        out_specs=[whole] * 2,
        scratch_shapes=[pltpu.VMEM((frames + 2, slots, pair), f32)],
        compiler_params=params(40),
        name="weight_terms",
    )(shares, modulated)


def middle_kernel(got, send):
    total = jnp.sum(got[...].astype(f32), axis=0)
    count, rows, width = send.shape
    total = total.reshape(count // 2, rows, 2 * width).astype(bf16)
    send[0 : count // 2] = total[:, :, :width]
    send[count // 2 :] = total[:, :, width:]


def middle_sum(got, count):
    groups, depth, pair = got.shape
    return pl.pallas_call(
        middle_kernel,
        out_shape=jax.ShapeDtypeStruct((count, 2 * depth // count, pair // 2), bf16),
        in_specs=[whole],
        out_specs=whole,
        compiler_params=params(24),
        name="middle_sum",
    )(got)


def hidden_kernel(hidden, token_grad, scale, w_out, grad_hidden):
    frames, token_rows, tokens, width = hidden.shape
    gain = 1.0 + scale[...]
    flat_grad = token_grad[...].reshape(-1, token_grad.shape[-1])
    mod_grad = dot_turned(flat_grad, w_out[...])
    for frame in range(frames):
        for row in range(token_rows):
            at = (frame * token_rows + row) * slots
            scaled = mod_grad[at : at + tokens] * gain
            normed, inverse = normalise(hidden[frame, row].astype(f32))
            first = jnp.mean(scaled, axis=-1, keepdims=True)
            second = jnp.mean(scaled * normed, axis=-1, keepdims=True)
            value = (scaled - first - normed * second) * inverse
            grad_hidden[frame, row] = value.astype(bf16)


def hidden_grad(hidden, token_grad, mod_scale, w_out):
    frames, token_rows, tokens, width = hidden.shape
    token_width = w_out.shape[1]
    block = 2
    return pl.pallas_call(
        hidden_kernel,
        grid=(frames // block,),
        out_shape=jax.ShapeDtypeStruct(hidden.shape, bf16),
        in_specs=[
            pl.BlockSpec((block, token_rows, tokens, width), lambda g: (g, 0, 0, 0)),
            pl.BlockSpec((block, token_rows, slots, token_width), lambda g: (g, 0, 0, 0)),
            pl.BlockSpec((1, width), lambda g: (0, 0)),
            pl.BlockSpec((width, token_width), lambda g: (0, 0)),
        ],
        out_specs=pl.BlockSpec((block, token_rows, tokens, width), lambda g: (g, 0, 0, 0)),
        compiler_params=params(40, "arbitrary"),
        cost_estimate=pl.CostEstimate(
            flops=2 * frames * 2 * slots * width * token_width,
            bytes_accessed=8 * frames * slots * width,
            transcendentals=0,
        ),
        name="hidden_grad",
    )(hidden, token_grad, mod_scale.reshape(1, -1), w_out)


def shards(hidden, mod_scale, mod_shift, w_out, w_in, w_section, section_grad):
    groups, strips = lax.axis_size("tm"), lax.axis_size("height")
    up = [(i + 1, i) for i in range(strips - 1)]
    down = [(i, i + 1) for i in range(strips - 1)]

    ahead, first, last, corner_first, corner_last = cut_halos(section_grad)
    earlier = [(g + 1, g) for g in range(groups - 1)]
    cross = lambda steps: [
        (g * strips + a, h * strips + b) for g, h in earlier for a, b in steps
    ]
    grad_ahead = lax.ppermute(ahead, "tm", earlier)
    below = lax.ppermute(first, "height", up)
    above = lax.ppermute(last, "height", down)
    below_ahead = lax.ppermute(corner_first, ("tm", "height"), cross(up))
    above_ahead = lax.ppermute(corner_last, ("tm", "height"), cross(down))

    modulated, latent_send = modulate(hidden, mod_scale, mod_shift, w_out, groups)
    latent = lax.all_to_all(latent_send, "tm", 0, 0, tiled=True)
    latent_below = lax.ppermute(latent, "height", up)
    latent_above = lax.ppermute(latent, "height", down)

    own = own_part(section_grad, w_section)
    centre, to_above, to_below = rest_part(
        own,
        (grad_ahead, above, below, above_ahead, below_ahead),
        w_section,
        (latent, latent_above, latent_below),
        w_in,
    )
    from_below = lax.ppermute(to_above.astype(bf16), "height", up)
    from_above = lax.ppermute(to_below.astype(bf16), "height", down)
    centre = centre + from_below.astype(f32) + from_above.astype(f32)
    shares = lax.all_to_all(centre.astype(bf16), "tm", 0, 0, tiled=True)

    token_grad, send = weight_terms(shares, modulated)
    got = lax.all_to_all(send, "tm", 0, 0, tiled=True)
    grad_hidden = hidden_grad(hidden, token_grad, mod_scale, w_out)
    pieces = lax.all_to_all(middle_sum(got, strips), "height", 0, 0, tiled=True)
    total_tokens = math.prod(hidden.shape[:3]) * groups * strips
    grad_out_weight = jnp.sum(pieces.astype(f32), axis=0) / math.sqrt(total_tokens)
    return (grad_hidden, grad_out_weight)


def solution(mesh):
    placed = (P(None, "height", "tm", None), P(), P(), P(), P(), P(), P("tm", "height", None, None))
    return jax.shard_map(
        shards,
        mesh=mesh,
        in_specs=placed,
        out_specs=(P(None, "height", "tm", None), P(("tm", "height"), None)),
        check_vma=False,
    )
```

time: 1100 us -> 197 us (0.18)
  the two profiles are of different devices: /device:TPU:6 before, /device:TPU:1 now
where the time goes in v1:
time: 197 us; the launch traced here: 195 us
  Pallas kernels  94.7 us (48%)
  starting transfers between devices  52.4 us (27%)
  blocking collectives  25.1 us (13%)
  local copies, waits for them, and re-layouts  13.3 us (7%)
  waiting for transfers between devices  5.12 us (3%)
  other arithmetic  3.47 us (2%)
    pallas_call x1, Pallas kernels, cut_halos(): pl.pallas_call(cut_kernel, out_shape=[jax.ShapeDtypeStruct(s + (cols, cha...  54.8 us
    all_to_all x1, starting transfers between devices, shards(): pieces = lax.all_to_all(middle_sum(got, strips), 'height', 0, 0, tiled=True)  26.3 us
    pallas_call x1, Pallas kernels, rest_part(): pl.pallas_call(rest_kernel, grid=(8,), out_shape=[out] * 3, in_specs=[hel...  17.7 us
    pallas_call x1, Pallas kernels, own_part(): pl.pallas_call(own_kernel, grid=(9,), out_shape=jax.ShapeDtypeStruct((cha...  13.9 us
    unnamed x33, local copies, waits for them, and re-layouts  13.3 us
    all_to_all x1, blocking collectives, shards(): got = lax.all_to_all(send, 'tm', 0, 0, tiled=True)  9.7 us
    all_to_all x1, blocking collectives, shards(): shares = lax.all_to_all(centre.astype(bf16), 'tm', 0, 0, tiled=True)  8.1 us
    all_to_all x1, blocking collectives, shards(): latent = lax.all_to_all(latent_send, 'tm', 0, 0, tiled=True)  7.35 us
  transfers between devices with their start and end apart: 10, of which 3 were waited for; matrix products, arithmetic and copies ran while one was open for 2% of the time, Pallas kernels for 37%

profile of v1, /device:TPU:1, one launch (start us, length us, event | category | flops | bytes accessed | tf_op | source)
XLA Modules:
  0.0 195.1 jit_solution(6325689708986976359)
XLA Ops:
  0.6 1.4 copy.10.w_out
  2.1 2.0 %copy.11.hidden = bf16[12,2,12,3072]{3,2,1,0:T(8,128)(2,1)S(1)} copy(bf16[12,2,12,3072]{3,1,2,0:T(2,128)(2,1)} %param.7) | data formatting | bytes 3538944 | tf_op args[0]
  4.0 3.2 %modulate.1 = (bf16[12,2,16,3072]{3,2,1,0:T(8,128)(2,1)S(1)}, bf16[4,5,16,128]{3,2,1,0:T(8,128)(2,1)S(1)}) custom-call(bf16[12,2,12,3072]{3,2,1,0:T(8,128)(2,1)S(1)} %copy.11.hidden, f32[1,3072]{1,0:T(1,128)S(1)} %bitcast.2, f32[1,3072]{1,0:T(1,128)S(1)} %bitcast.4, bf16[3072,64]{1,0:T(8,128)(2,1)S(1)} %copy.10.w_out), custom_call_target="tpu_custom_call" | custom-call | flops 150994944 | bytes 4718592 | tf_op jit(solution)/shard_map/modulate/pallas_call | solution.py:103
  7.2 1.4 copy-done
  8.7 7.3 %all_to_all.20.latent = bf16[4,5,16,128]{3,2,1,0:T(8,128)(2,1)S(1)} all-to-all(bf16[4,5,16,128]{3,2,1,0:T(8,128)(2,1)S(1)} %get-tuple-element.19), channel_id=1, replica_groups=mesh['tm'=4,'height'=32] {'tm'}, dimensions={0} | all-to-all | bytes 163840 | tf_op jit(solution)/shard_map/all_to_all | solution.py:520
  16.0 1.3 collective-permute-start.6
  17.3 4.2 %collective-permute-start.5 = (bf16[4,5,16,128]{3,2,1,0:T(8,128)(2,1)S(1)}, bf16[4,5,16,128]{3,2,1,0:T(8,128)(2,1)S(1)}, u32[]{:S(2)}, u32[]{:S(2)}) collective-permute-start(bf16[4,5,16,128]{3,2,1,0:T(8,128)(2,1)S(1)} %all_to_all.20.latent), channel_id=1, source_target_pairs={{0,1},{1,2},{2,3},{3,4},{4,5},{5,6},{6,7},{7,8},{8,9},{9,10},{10,1... | collective-permute-start | bytes 245768 | tf_op jit(solution)/shard_map/ppermute | solution.py:522
  21.5 54.8 %cut_halos.1 = (bf16[2,4,96,512]{3,2,1,0:T(8,128)(2,1)}, bf16[3,1,96,512]{3,2,1,0:T(8,128)(2,1)}, bf16[3,1,96,512]{3,2,1,0:T(8,128)(2,1)}, bf16[2,1,96,512]{3,2,1,0:T(8,128)(2,1)}, bf16[2,1,96,512]{3,2,1,0:T(8,128)(2,1)}) custom-call(bf16[3,4,96,512]{3,2,1,0:T(8,128)(2,1)} %grad.3), custom_call_target="tpu_custom_call" | custom-call | tf_op jit(solution)/shard_map/cut_halos/pallas_call | solution.py:53
  76.3 4.7 %collective-permute-start.3 = (bf16[2,1,96,512]{3,2,1,0:T(8,128)(2,1)}, bf16[2,1,96,512]{3,2,1,0:T(8,128)(2,1)S(1)}, u32[]{:S(2)}, u32[]{:S(2)}) collective-permute-start(bf16[2,1,96,512]{3,2,1,0:T(8,128)(2,1)} %get-tuple-element.17), channel_id=1, source_target_pairs={{32,1},{33,2},{34,3},{35,4},{36,5},{37,6},{38,7},{39,8},{40,9},{41... | collective-permute-start | bytes 589832 | tf_op jit(solution)/shard_map/ppermute | solution.py:517
  81.0 1.3 collective-permute-start.4
  82.3 4.2 %collective-permute-start.1 = (bf16[3,1,96,512]{3,2,1,0:T(8,128)(2,1)}, bf16[3,1,96,512]{3,2,1,0:T(8,128)(2,1)S(1)}, u32[]{:S(2)}, u32[]{:S(2)}) collective-permute-start(bf16[3,1,96,512]{3,2,1,0:T(8,128)(2,1)} %get-tuple-element.15), channel_id=1, source_target_pairs={{0,1},{1,2},{2,3},{3,4},{4,5},{5,6},{6,7},{7,8},{8,9},{9,10},{10,1... | collective-permute-start | bytes 884744 | tf_op jit(solution)/shard_map/ppermute | solution.py:515
  86.5 1.3 collective-permute-start.2
  87.8 1.9 collective-permute-start
  91.0 13.9 %own_part.1.own = f32[4,3,4,96,128]{4,3,2,1,0:T(8,128)S(1)} custom-call(bf16[3,4,96,512]{3,2,1,0:T(8,128)(2,1)S(1)} %copy-done.2, bf16[3,3,3,512,512]{4,3,2,1,0:T(8,128)(2,1)} %w_section.3), custom_call_target="tpu_custom_call" | custom-call | flops 9059696640 | bytes 14155776 | tf_op jit(solution)/shard_map/own_part/pallas_call | solution.py:186
  105.0 1.4 copy-done.5
  108.3 17.7 %rest_part.1 = (f32[4,5,16,128]{3,2,1,0:T(8,128)}, f32[4,5,16,128]{3,2,1,0:T(8,128)}, f32[4,5,16,128]{3,2,1,0:T(8,128)}) custom-call(f32[4,3,4,96,128]{4,3,2,1,0:T(8,128)} %copy-done.5, bf16[2,4,96,512]{3,2,1,0:T(8,128)(2,1)} %copy-done.7, bf16[3,1,96,512]{3,2,1,0:T(8,128)(2,1)} %copy-done.8, bf16[3,1,96,512]{3,2,1,0:T(8,128)(2,1)} %copy-done.9, ...), custom_call_target="tpu_custom_call" | custom-call | flops 9663676416 | bytes 14155776 | tf_op jit(solution)/shard_map/rest_part/pallas_call | solution.py:373
  127.8 6.0 %collective-permute-start.8 = (bf16[4,5,16,128]{3,2,1,0:T(8,128)(2,1)S(1)}, bf16[4,5,16,128]{3,2,1,0:T(8,128)(2,1)S(1)}, u32[]{:S(2)}, u32[]{:S(2)}) collective-permute-start(bf16[4,5,16,128]{3,2,1,0:T(8,128)(2,1)S(1)} %convert_element_type.20), channel_id=1, source_target_pairs={{0,1},{1,2},{2,3},{3,4},{4,5},{5,6},{6,7},{7,8},{8,9},{9,10},{10,1... | collective-permute-start | bytes 245768 | tf_op jit(solution)/shard_map/ppermute | solution.py:533
  133.8 1.3 collective-permute-start.7
  135.3 3.7 %collective-permute-done.7 = bf16[4,5,16,128]{3,2,1,0:T(8,128)(2,1)S(1)} collective-permute-done((bf16[4,5,16,128]{3,2,1,0:T(8,128)(2,1)S(1)}, bf16[4,5,16,128]{3,2,1,0:T(8,128)(2,1)S(1)}, u32[]{:S(2)}, u32[]{:S(2)}) %collective-permute-start.7) | collective-permute-done | bytes 81952 | tf_op jit(solution)/shard_map/ppermute | solution.py:532
  140.0 8.1 %all_to_all.21.shares = bf16[4,5,16,128]{3,2,1,0:T(8,128)(2,1)S(1)} all-to-all(bf16[4,5,16,128]{3,2,1,0:T(8,128)(2,1)S(1)} %add_convert_fusion), channel_id=1, replica_groups=mesh['tm'=4,'height'=32] {'tm'}, dimensions={0} | all-to-all | bytes 163840 | tf_op jit(solution)/shard_map/all_to_all | solution.py:535
  148.8 9.7 %all_to_all.22.got = bf16[4,384,128]{2,1,0:T(8,128)(2,1)S(1)} all-to-all(bf16[4,384,128]{2,1,0:T(8,128)(2,1)S(1)} %get-tuple-element.25), channel_id=1, replica_groups=mesh['tm'=4,'height'=32] {'tm'}, dimensions={0} | all-to-all | bytes 786432 | tf_op jit(solution)/shard_map/all_to_all | solution.py:538
  159.4 26.3 %all-to-all-start.3 = ((bf16[32,2,768]{2,1,0:T(2,128)(2,1)}), bf16[32,2,768]{2,1,0:T(2,128)(2,1)S(1)}, u32[]{:S(2)}, u32[]{:S(2)}) async-start(bf16[32,2,768]{2,1,0:T(2,128)(2,1)} %reshape.13), calls=%async_computation.3 | async-start | bytes 196608 | tf_op jit(solution)/shard_map/all_to_all | solution.py:540
  185.7 4.3 %hidden_grad.1 = bf16[12,2,12,3072]{3,2,1,0:T(8,128)(2,1)S(1)} custom-call(bf16[12,2,12,3072]{3,2,1,0:T(8,128)(2,1)S(1)} %copy.11.hidden, bf16[12,2,16,64]{3,2,1,0:T(8,128)(2,1)S(1)} %get-tuple-element.24.token_grad, f32[1,3072]{1,0:T(1,128)S(1)} %bitcast.3, bf16[3072,64]{1,0:T(8,128)(2,1)S(1)} %copy.10.w_out), custom_call_target="tpu_custom_call" | custom-call | flops 150994944 | bytes 4718592 | tf_op jit(solution)/shard_map/hidden_grad/pallas_call | solution.py:482
  190.0 3.0 %copy.13 = bf16[12,2,12,3072]{3,1,2,0:T(2,128)(2,1)} copy(bf16[12,2,12,3072]{3,2,1,0:T(8,128)(2,1)S(1)} %hidden_grad.1) | data formatting | bytes 3538944
  (44 shorter events, 9.8 us)
Async XLA Ops:
  2.0 2.0 %copy-start.3 = (f32[3072]{0:T(1024)S(1)}, f32[3072]{0:T(1024)}, u32[]{:S(2)}) copy-start(f32[3072]{0:T(1024)} %param.8) | copy-start | bytes 36868
  2.0 2.0 %copy-start.4 = (f32[3072]{0:T(1024)S(1)}, f32[3072]{0:T(1024)}, u32[]{:S(2)}) copy-start(f32[3072]{0:T(1024)} %param.9) | copy-start | bytes 36868
  7.2 1.4 copy-start
  16.0 89.0 %copy-start.6 = (bf16[4,5,16,128]{3,2,1,0:T(8,128)(2,1)}, bf16[4,5,16,128]{3,2,1,0:T(8,128)(2,1)S(1)}, u32[]{:S(2)}) copy-start(bf16[4,5,16,128]{3,2,1,0:T(8,128)(2,1)S(1)} %all_to_all.20.latent) | copy-start | bytes 245764
  16.0 70.5 %collective-permute-start.6 = (bf16[4,5,16,128]{3,2,1,0:T(8,128)(2,1)S(1)}, bf16[4,5,16,128]{3,2,1,0:T(8,128)(2,1)S(1)}, u32[]{:S(2)}, u32[]{:S(2)}) collective-permute-start(bf16[4,5,16,128]{3,2,1,0:T(8,128)(2,1)S(1)} %all_to_all.20.latent), channel_id=1, source_target_pairs={{1,0},{2,1},{3,2},{4,3},{5,4},{6,5},{7,6},{8,7},{9,8},{10,9},{11,1... | collective-permute-start | bytes 245768 | tf_op jit(solution)/shard_map/ppermute | solution.py:521
  17.3 70.5 %collective-permute-start.5 = (bf16[4,5,16,128]{3,2,1,0:T(8,128)(2,1)S(1)}, bf16[4,5,16,128]{3,2,1,0:T(8,128)(2,1)S(1)}, u32[]{:S(2)}, u32[]{:S(2)}) collective-permute-start(bf16[4,5,16,128]{3,2,1,0:T(8,128)(2,1)S(1)} %all_to_all.20.latent), channel_id=1, source_target_pairs={{0,1},{1,2},{2,3},{3,4},{4,5},{5,6},{6,7},{7,8},{8,9},{9,10},{10,1... | collective-permute-start | bytes 245768 | tf_op jit(solution)/shard_map/ppermute | solution.py:522
  76.3 30.2 %collective-permute-start.3 = (bf16[2,1,96,512]{3,2,1,0:T(8,128)(2,1)}, bf16[2,1,96,512]{3,2,1,0:T(8,128)(2,1)S(1)}, u32[]{:S(2)}, u32[]{:S(2)}) collective-permute-start(bf16[2,1,96,512]{3,2,1,0:T(8,128)(2,1)} %get-tuple-element.17), channel_id=1, source_target_pairs={{32,1},{33,2},{34,3},{35,4},{36,5},{37,6},{38,7},{39,8},{40,9},{41... | collective-permute-start | bytes 589832 | tf_op jit(solution)/shard_map/ppermute | solution.py:517
  81.0 25.5 %collective-permute-start.4 = (bf16[2,1,96,512]{3,2,1,0:T(8,128)(2,1)}, bf16[2,1,96,512]{3,2,1,0:T(8,128)(2,1)S(1)}, u32[]{:S(2)}, u32[]{:S(2)}) collective-permute-start(bf16[2,1,96,512]{3,2,1,0:T(8,128)(2,1)} %get-tuple-element.18), channel_id=1, source_target_pairs={{33,0},{34,1},{35,2},{36,3},{37,4},{38,5},{39,6},{40,7},{41,8},{42... | collective-permute-start | bytes 589832 | tf_op jit(solution)/shard_map/ppermute | solution.py:516
  82.3 24.2 %collective-permute-start.1 = (bf16[3,1,96,512]{3,2,1,0:T(8,128)(2,1)}, bf16[3,1,96,512]{3,2,1,0:T(8,128)(2,1)S(1)}, u32[]{:S(2)}, u32[]{:S(2)}) collective-permute-start(bf16[3,1,96,512]{3,2,1,0:T(8,128)(2,1)} %get-tuple-element.15), channel_id=1, source_target_pairs={{0,1},{1,2},{2,3},{3,4},{4,5},{5,6},{6,7},{7,8},{8,9},{9,10},{10,1... | collective-permute-start | bytes 884744 | tf_op jit(solution)/shard_map/ppermute | solution.py:515
  86.5 18.5 %copy-start.12 = (bf16[4,5,16,128]{3,2,1,0:T(8,128)(2,1)}, bf16[4,5,16,128]{3,2,1,0:T(8,128)(2,1)S(1)}, u32[]{:S(2)}) copy-start(bf16[4,5,16,128]{3,2,1,0:T(8,128)(2,1)S(1)} %collective-permute-done.6.latent_below) | copy-start | bytes 245764
  86.5 20.0 %collective-permute-start.2 = (bf16[3,1,96,512]{3,2,1,0:T(8,128)(2,1)}, bf16[3,1,96,512]{3,2,1,0:T(8,128)(2,1)S(1)}, u32[]{:S(2)}, u32[]{:S(2)}) collective-permute-start(bf16[3,1,96,512]{3,2,1,0:T(8,128)(2,1)} %get-tuple-element.16), channel_id=1, source_target_pairs={{1,0},{2,1},{3,2},{4,3},{5,4},{6,5},{7,6},{8,7},{9,8},{10,9},{11,1... | collective-permute-start | bytes 884744 | tf_op jit(solution)/shard_map/ppermute | solution.py:514
  87.8 17.2 %copy-start.13 = (bf16[4,5,16,128]{3,2,1,0:T(8,128)(2,1)}, bf16[4,5,16,128]{3,2,1,0:T(8,128)(2,1)S(1)}, u32[]{:S(2)}) copy-start(bf16[4,5,16,128]{3,2,1,0:T(8,128)(2,1)S(1)} %collective-permute-done.5.latent_above) | copy-start | bytes 245764
  87.8 18.7 %collective-permute-start = (bf16[2,4,96,512]{3,2,1,0:T(8,128)(2,1)}, bf16[2,4,96,512]{3,2,1,0:T(8,128)(2,1)S(1)}, u32[]{:S(2)}, u32[]{:S(2)}) collective-permute-start(bf16[2,4,96,512]{3,2,1,0:T(8,128)(2,1)} %get-tuple-element.14), channel_id=1, source_target_pairs={{32,0},{64,32},{96,64},{33,1},{65,33},{97,65},{34,2},{66,34},{98,6... | collective-permute-start | bytes 2359304 | tf_op jit(solution)/shard_map/ppermute | solution.py:513
  89.8 1.3 copy-start.2
  105.0 1.4 copy-start.5
  106.5 0.7 copy-start.10
  106.5 0.7 copy-start.11
  106.5 0.8 copy-start.8
  106.5 0.9 copy-start.9
  107.4 0.9 copy-start.7
  108.3 39.8 %copy-start.1 = (bf16[12,2,16,3072]{3,2,1,0:T(8,128)(2,1)S(1)}, bf16[12,2,16,3072]{3,2,1,0:T(8,128)(2,1)}, u32[]{:S(2)}) copy-start(bf16[12,2,16,3072]{3,2,1,0:T(8,128)(2,1)} %copy-done) | copy-start | bytes 7077892
  127.8 7.4 %collective-permute-start.8 = (bf16[4,5,16,128]{3,2,1,0:T(8,128)(2,1)S(1)}, bf16[4,5,16,128]{3,2,1,0:T(8,128)(2,1)S(1)}, u32[]{:S(2)}, u32[]{:S(2)}) collective-permute-start(bf16[4,5,16,128]{3,2,1,0:T(8,128)(2,1)S(1)} %convert_element_type.20), channel_id=1, source_target_pairs={{0,1},{1,2},{2,3},{3,4},{4,5},{5,6},{6,7},{7,8},{8,9},{9,10},{10,1... | collective-permute-start | bytes 245768 | tf_op jit(solution)/shard_map/ppermute | solution.py:533
  133.8 5.2 %collective-permute-start.7 = (bf16[4,5,16,128]{3,2,1,0:T(8,128)(2,1)S(1)}, bf16[4,5,16,128]{3,2,1,0:T(8,128)(2,1)S(1)}, u32[]{:S(2)}, u32[]{:S(2)}) collective-permute-start(bf16[4,5,16,128]{3,2,1,0:T(8,128)(2,1)S(1)} %convert_element_type.18), channel_id=1, source_target_pairs={{1,0},{2,1},{3,2},{4,3},{5,4},{6,5},{7,6},{8,7},{9,8},{10,9},{11,1... | collective-permute-start | bytes 245768 | tf_op jit(solution)/shard_map/ppermute | solution.py:532
  159.4 34.8 %all-to-all-start.3 = ((bf16[32,2,768]{2,1,0:T(2,128)(2,1)}), bf16[32,2,768]{2,1,0:T(2,128)(2,1)S(1)}, u32[]{:S(2)}, u32[]{:S(2)}) async-start(bf16[32,2,768]{2,1,0:T(2,128)(2,1)} %reshape.13), calls=%async_computation.3 | async-start | bytes 196608 | tf_op jit(solution)/shard_map/all_to_all | solution.py:540

commit v2 on v1

--- a/solution.py
+++ b/solution.py
@@ -13,7 +13,6 @@
 lanes = 128
 f32 = jnp.float32
 bf16 = jnp.bfloat16
-anywhere = pl.BlockSpec(memory_space=pl.ANY)
 whole = pl.BlockSpec(memory_space=pltpu.VMEM)
 
 
@@ -29,35 +28,6 @@
 
 def dot_turned(lhs, rhs):
     return lax.dot_general(lhs, rhs, (((1,), (1,)), ((), ())), preferred_element_type=f32)
-
-
-def cut_kernel(grad, ahead, first, last, corner_first, corner_last, sems):
-    rows = grad.shape[1]
-    pieces = (
-        (grad.at[0:2], ahead),
-        (grad.at[:, 0:1], first),
-        (grad.at[:, rows - 1 : rows], last),
-        (grad.at[0:2, 0:1], corner_first),
-        (grad.at[0:2, rows - 1 : rows], corner_last),
-    )
-    copies = [pltpu.make_async_copy(src, dst, sems.at[n]) for n, (src, dst) in enumerate(pieces)]
-    for copy in copies:
-        copy.start()
-    for copy in copies:
-        copy.wait()
-
-
-def cut_halos(grad):
-    frames, rows, cols, channels = grad.shape
-    shapes = ((2, rows), (frames, 1), (frames, 1), (2, 1), (2, 1))
-    return pl.pallas_call(
-        cut_kernel,
-        out_shape=[jax.ShapeDtypeStruct(s + (cols, channels), grad.dtype) for s in shapes],
-        in_specs=[anywhere],
-        out_specs=[anywhere] * 5,
-        scratch_shapes=[pltpu.SemaphoreType.DMA((5,))],
-        name="cut_halos",
-    )(grad)
 
 
 def normalise(values):
@@ -79,7 +49,7 @@
             value = jnp.concatenate([normed * gain + shift[...], blank], axis=0)
             modulated[frame, row] = value.astype(bf16)
     flat = modulated[...].reshape(frames * token_rows * slots, width)
-    latent = dot(flat, w_out[...]).astype(bf16)
+    latent = dot_turned(flat, w_out[...]).astype(bf16)
     latent = latent.reshape(frames, token_rows, slots, latent.shape[-1])
     paired = jnp.concatenate([latent[:, 0], latent[:, 1]], axis=-1)
     for frame in range(frames):
@@ -98,7 +68,7 @@
 def modulate(hidden, mod_scale, mod_shift, w_out, groups):
     frames, token_rows, tokens, width = hidden.shape
     block = frames // groups
-    token_width = w_out.shape[1]
+    token_width = w_out.shape[0]
     held = lambda *dims: pl.BlockSpec(dims, lambda g: (0,) * len(dims))
     return pl.pallas_call(
         modulate_kernel,
@@ -111,13 +81,13 @@
             pl.BlockSpec((block, token_rows, tokens, width), lambda g: (g, 0, 0, 0)),
             held(1, width),
             held(1, width),
-            held(width, token_width),
+            held(token_width, width),
         ],
         out_specs=[
             pl.BlockSpec((block, token_rows, slots, width), lambda g: (g, 0, 0, 0)),
             held(groups, block + 2, slots, 2 * token_width),
         ],
-        compiler_params=params(40, "arbitrary"),
+        compiler_params=params(20, "arbitrary"),
         cost_estimate=pl.CostEstimate(
             flops=2 * frames * 2 * slots * width * token_width,
             bytes_accessed=8 * frames * slots * width,
@@ -144,17 +114,57 @@
 taps = [(2 - n // 3, (1, 0, 2)[n % 3]) for n in range(9)]
 
 
-def weight_matrix(w_section):
-    return jnp.concatenate([w_section[0, 0, kx] for kx in range(3)], axis=-1)
-
-
 def flat(value):
     return value.reshape(-1, value.shape[-1])
 
 
-def own_kernel(grad, w_section, total, shifts):
+def pack_kernel(places, own_near, own_far, ahead_near, ahead_far, latent, near, far):
+    channels = own_near.shape[-1]
+    for own, ahead, out in ((own_near, ahead_near, near), (own_far, ahead_far, far)):
+        front = flat(own[...])
+        back = flat(ahead[...])
+        out[0 : front.shape[0]] = front
+        out[front.shape[0] : front.shape[0] + back.shape[0]] = back
+        at = front.shape[0] + back.shape[0]
+        tail = flat(latent[...])
+        count = tail.shape[0] * lanes // channels
+        for lane in range(channels // lanes):
+            out[at : at + count, lane * lanes : (lane + 1) * lanes] = tail[
+                lane * count : (lane + 1) * count
+            ]
+
+
+def pack_rows(places, grad, grad_ahead, latent):
+    frames, rows, cols, channels = grad.shape
+    total = (frames + 2) * cols + latent.size // channels
+    out = jax.ShapeDtypeStruct((total, channels), bf16)
+    near = lambda n, at: (0, at[0], 0, 0)
+    far = lambda n, at: (0, at[1], 0, 0)
+    return pl.pallas_call(
+        pack_kernel,
+        grid_spec=pltpu.PrefetchScalarGridSpec(
+            num_scalar_prefetch=1,
+            grid=(1,),
+            in_specs=[
+                pl.BlockSpec((frames, 1, cols, channels), near),
+                pl.BlockSpec((frames, 1, cols, channels), far),
+                pl.BlockSpec((2, 1, cols, channels), near),
+                pl.BlockSpec((2, 1, cols, channels), far),
+                pl.BlockSpec(latent.shape, lambda n, at: (0, 0, 0, 0)),
+            ],
+            out_specs=[pl.BlockSpec(out.shape, lambda n, at: (0, 0))] * 2,
+        ),
+        out_shape=[out] * 2,
+        compiler_params=params(16, "arbitrary"),
+        name="pack_rows",
+    )(places, grad, grad, grad_ahead, grad_ahead, latent)
+
+
+def own_kernel(grad, w_section, total, turned, shifts):
     step = pl.program_id(0)
     frames, rows, cols, channels = grad.shape
+    for kx in range(3):
+        turned[0, 0, kx] = jnp.transpose(w_section[0, 0, kx])
 
     @pl.when(step == 0)
     def _():
@@ -171,7 +181,7 @@
             window = jnp.concatenate(
                 [flat(shifts[(0,) + src]), flat(grad[src]), flat(shifts[(1,) + src])], axis=-1
             )
-            part = dot_turned(window, weight_matrix(w_section))
+            part = dot(window, flat(turned[0, 0]))
             for lane in range(channels // lanes):
                 value = part[:, lane * lanes : (lane + 1) * lanes]
                 value = value.reshape(kt + 1, hi - lo, cols, lanes)
@@ -186,16 +196,20 @@
     return pl.pallas_call(
         own_kernel,
         grid=(9,),
-        out_shape=jax.ShapeDtypeStruct((channels // lanes, frames, rows, cols, lanes), f32),
+        out_shape=[
+            jax.ShapeDtypeStruct((channels // lanes, frames, rows, cols, lanes), f32),
+            jax.ShapeDtypeStruct(w_section.shape, bf16),
+        ],
         in_specs=[
             pl.BlockSpec(grad.shape, lambda n: (0, 0, 0, 0)),
             pl.BlockSpec((1, 1, 3, channels, channels), lambda n: tap_of(n) + (0, 0, 0)),
         ],
-        out_specs=pl.BlockSpec(
-            (channels // lanes, frames, rows, cols, lanes), lambda n: (0, 0, 0, 0, 0)
-        ),
+        out_specs=[
+            pl.BlockSpec((channels // lanes, frames, rows, cols, lanes), lambda n: (0,) * 5),
+            pl.BlockSpec((1, 1, 3, channels, channels), lambda n: tap_of(n) + (0, 0, 0)),
+        ],
         scratch_shapes=[pltpu.VMEM((2,) + grad.shape, bf16)],
-        compiler_params=params(48, "arbitrary"),
+        compiler_params=params(52, "arbitrary"),
         cost_estimate=pl.CostEstimate(
             flops=2 * 15 * grad.size * channels,
             bytes_accessed=2 * w_section.size,
@@ -206,20 +220,17 @@
 
 
 def rest_kernel(
+    places,
     own,
     grad_ahead,
-    above,
-    below,
-    above_ahead,
-    below_ahead,
-    w_section,
+    near_rows,
+    far_rows,
+    turned,
     latent,
-    latent_above,
-    latent_below,
     w_in,
     centre_out,
-    up_out,
-    down_out,
+    near_out,
+    far_out,
     total,
     far,
     near,
@@ -228,8 +239,10 @@
     patches,
     spread,
 ):
+    even = places[0] != 0
     step = pl.program_id(0)
     blocks, frames, rows, cols, _ = own.shape
+    channels = blocks * lanes
     groups, depth, _, pair = latent.shape
     width = pair // 2
     block = cols // (2 * groups)
@@ -238,21 +251,24 @@
     @pl.when(step == 0)
     def _():
         total[...] = own[...]
+        for frame in range(frames + 2):
+            at = slice(frame * cols, (frame + 1) * cols)
+            ends = near_rows[at], far_rows[at]
+            for side in range(2):
+                value = jnp.where(even == (side == 1), ends[0], ends[1])
+                shifted = column_shifts(value)
+                if frame < frames:
+                    near[1, side, frame] = value
+                    near[0, side, frame], near[2, side, frame] = shifted
+                else:
+                    row = side * (rows + 1)
+                    far[1, frame - frames, row] = value
+                    far[0, frame - frames, row], far[2, frame - frames, row] = shifted
         for frame in range(2):
-            for row in range(rows + 2):
-                if row == 0:
-                    value = above_ahead[frame, 0]
-                elif row == rows + 1:
-                    value = below_ahead[frame, 0]
-                else:
-                    value = grad_ahead[frame, row - 1]
-                far[1, frame, row] = value
-                far[0, frame, row], far[2, frame, row] = column_shifts(value)
-        for frame in range(frames):
-            for side, ref in ((0, above), (1, below)):
-                value = ref[frame, 0]
-                near[1, side, frame] = value
-                near[0, side, frame], near[2, side, frame] = column_shifts(value)
+            for row in range(rows):
+                value = grad_ahead[frame, row]
+                far[1, frame, row + 1] = value
+                far[0, frame, row + 1], far[2, frame, row + 1] = column_shifts(value)
 
     for n, (kt, ky) in enumerate(taps):
         if (kt, ky) == (2, 1):
@@ -273,7 +289,7 @@
             window = jnp.concatenate(
                 [jnp.concatenate([flat(v) for v in piece], axis=-1) for piece in pieces], axis=0
             )
-            part = dot_turned(window, weight_matrix(w_section))
+            part = dot(window, flat(turned[0, 0]))
             at = 0
             for place in places:
                 shape = [cut.stop - cut.start for cut in place] + [cols, lanes]
@@ -292,8 +308,16 @@
                 value = latent[src, frame].astype(f32)[:block]
                 tokens[frame, 1, at] = value[:, :width]
                 tokens[frame, 2, at] = value[:, width:]
-                tokens[frame, 0, at] = latent_above[src, frame].astype(f32)[:block, width:]
-                tokens[frame, 3, at] = latent_below[src, frame].astype(f32)[:block, :width]
+                row = (src * depth + frame) * slots
+                count = groups * depth * slots * lanes // channels
+                lane = row // count * lanes
+                row = (frames + 2) * cols + row % count
+                ends = [
+                    rows_of[row : row + slots, lane : lane + lanes].astype(f32)[:block]
+                    for rows_of in (near_rows, far_rows)
+                ]
+                tokens[frame, 0, at] = jnp.where(even, ends[1], ends[0])[:, width:]
+                tokens[frame, 3, at] = jnp.where(even, ends[0], ends[1])[:, :width]
         for q in range(2):
             left = tokens[:, :, 7 + q : 7 + q + half]
             right = tokens[:, :, 8 + q : 8 + q + half]
@@ -349,8 +373,8 @@
                             :, at : at + pair
                         ].reshape(frames, rows // 2, half, pair)
         centre_out[...] = jnp.zeros_like(centre_out)
-        up_out[...] = jnp.zeros_like(up_out)
-        down_out[...] = jnp.zeros_like(down_out)
+        near_out[...] = jnp.zeros_like(near_out)
+        far_out[...] = jnp.zeros_like(far_out)
         grid = spread[:, :, 1 : half + 1, :width] + spread[:, :, 0:half, width:]
         tokens[:, :, 0:half] = grid
         for dst in range(groups):
@@ -359,44 +383,60 @@
                     tokens[frame, row, dst * block : (dst + 1) * block] for row in range(4)
                 ]
                 none = jnp.zeros_like(value[0])
-                centre_out[dst, frame, 0:block] = jnp.concatenate([value[1], value[2]], axis=-1)
-                up_out[dst, frame, 0:block] = jnp.concatenate([none, value[0]], axis=-1)
-                down_out[dst, frame, 0:block] = jnp.concatenate([value[3], none], axis=-1)
-
-
-def rest_part(own, halos, w_section, latents, w_in):
+                centre = jnp.concatenate([value[1], value[2]], axis=-1)
+                up = jnp.concatenate([none, value[0]], axis=-1)
+                down = jnp.concatenate([value[3], none], axis=-1)
+                fill = jnp.zeros((slots - block, 2 * width), f32)
+                padded = lambda v: jnp.concatenate([v, fill], axis=0).astype(bf16)
+                centre_out[dst, frame] = padded(centre)
+                near_out[dst, frame] = padded(jnp.where(even, down, up))
+                far_out[dst, frame] = padded(jnp.where(even, up, down))
+
+
+def rest_part(places, own, grad_ahead, near_rows, far_rows, turned, latent, w_in):
     blocks, frames, rows, cols, _ = own.shape
     channels = blocks * lanes
-    groups, depth, _, pair = latents[0].shape
-    held = lambda value: pl.BlockSpec(value.shape, lambda n: (0,) * value.ndim)
-    out = jax.ShapeDtypeStruct(latents[0].shape, f32)
+    groups, depth, _, pair = latent.shape
+    held = lambda value: pl.BlockSpec(
+        value.shape, lambda n, at: (0,) * len(value.shape), pipeline_mode=pl.Buffered(1)
+    )
+    out = jax.ShapeDtypeStruct(latent.shape, bf16)
     return pl.pallas_call(
         rest_kernel,
-        grid=(8,),
         out_shape=[out] * 3,
-        in_specs=[held(own)]
-        + [held(value) for value in halos]
-        + [pl.BlockSpec((1, 1, 3, channels, channels), lambda n: tap_of(n + 1) + (0, 0, 0))]
-        + [held(value) for value in latents]
-        + [held(w_in)],
-        out_specs=[held(out)] * 3,
-        scratch_shapes=[
-            pltpu.VMEM(own.shape, f32),
-            pltpu.VMEM((3, 2, rows + 2, cols, channels), bf16),
-            pltpu.VMEM((3, 2, frames, cols, channels), bf16),
-            pltpu.VMEM((depth, rows // 2 + 2, 72, pair // 2), f32),
-            pltpu.VMEM((2, depth, rows // 2 + 2, cols // 2, pair), bf16),
-            pltpu.VMEM((4, 6 * pair, channels), bf16),
-            pltpu.VMEM((depth, rows // 2 + 2, cols // 2 + 8, pair), f32),
-        ],
-        compiler_params=params(56, "arbitrary"),
+        grid_spec=pltpu.PrefetchScalarGridSpec(
+            num_scalar_prefetch=1,
+            grid=(8,),
+            in_specs=[
+                held(own),
+                pl.BlockSpec((2, rows, cols, channels), lambda n, at: (0, 0, 0, 0)),
+                held(near_rows),
+                held(far_rows),
+                pl.BlockSpec(
+                    (1, 1, 3, channels, channels), lambda n, at: tap_of(n + 1) + (0, 0, 0)
+                ),
+                held(latent),
+                held(w_in),
+            ],
+            out_specs=[held(out)] * 3,
+            scratch_shapes=[
+                pltpu.VMEM(own.shape, f32),
+                pltpu.VMEM((3, 2, rows + 2, cols, channels), bf16),
+                pltpu.VMEM((3, 2, frames, cols, channels), bf16),
+                pltpu.VMEM((depth, rows // 2 + 2, 72, pair // 2), f32),
+                pltpu.VMEM((2, depth, rows // 2 + 2, cols // 2, pair), bf16),
+                pltpu.VMEM((4, 6 * pair, channels), bf16),
+                pltpu.VMEM((depth, rows // 2 + 2, cols // 2 + 8, pair), f32),
+            ],
+        ),
+        compiler_params=params(52, "arbitrary"),
         cost_estimate=pl.CostEstimate(
             flops=2 * 16 * own.size * channels,
-            bytes_accessed=2 * w_section.size,
+            bytes_accessed=2 * turned.size,
             transcendentals=2 * own.size,
         ),
         name="rest_part",
-    )(own, *halos, w_section, *latents, w_in)
+    )(places, own, grad_ahead, near_rows, far_rows, turned, latent, w_in)
 
 
 def weight_kernel(shares, modulated, token_grad, send, field):
@@ -434,7 +474,7 @@
         in_specs=[whole] * 2,
         out_specs=[whole] * 2,
         scratch_shapes=[pltpu.VMEM((frames + 2, slots, pair), f32)],
-        compiler_params=params(40),
+        compiler_params=params(24),
         name="weight_terms",
     )(shares, modulated)
 
@@ -463,7 +503,7 @@
     frames, token_rows, tokens, width = hidden.shape
     gain = 1.0 + scale[...]
     flat_grad = token_grad[...].reshape(-1, token_grad.shape[-1])
-    mod_grad = dot_turned(flat_grad, w_out[...])
+    mod_grad = dot(flat_grad, w_out[...])
     for frame in range(frames):
         for row in range(token_rows):
             at = (frame * token_rows + row) * slots
@@ -477,7 +517,7 @@
 
 def hidden_grad(hidden, token_grad, mod_scale, w_out):
     frames, token_rows, tokens, width = hidden.shape
-    token_width = w_out.shape[1]
+    token_width = w_out.shape[0]
     block = 2
     return pl.pallas_call(
         hidden_kernel,
@@ -487,10 +527,10 @@
             pl.BlockSpec((block, token_rows, tokens, width), lambda g: (g, 0, 0, 0)),
             pl.BlockSpec((block, token_rows, slots, token_width), lambda g: (g, 0, 0, 0)),
             pl.BlockSpec((1, width), lambda g: (0, 0)),
-            pl.BlockSpec((width, token_width), lambda g: (0, 0)),
+            pl.BlockSpec((token_width, width), lambda g: (0, 0)),
         ],
         out_specs=pl.BlockSpec((block, token_rows, tokens, width), lambda g: (g, 0, 0, 0)),
-        compiler_params=params(40, "arbitrary"),
+        compiler_params=params(20, "arbitrary"),
         cost_estimate=pl.CostEstimate(
             flops=2 * frames * 2 * slots * width * token_width,
             bytes_accessed=8 * frames * slots * width,
@@ -502,36 +542,28 @@
 
 def shards(hidden, mod_scale, mod_shift, w_out, w_in, w_section, section_grad):
     groups, strips = lax.axis_size("tm"), lax.axis_size("height")
-    up = [(i + 1, i) for i in range(strips - 1)]
-    down = [(i, i + 1) for i in range(strips - 1)]
-
-    ahead, first, last, corner_first, corner_last = cut_halos(section_grad)
-    earlier = [(g + 1, g) for g in range(groups - 1)]
-    cross = lambda steps: [
-        (g * strips + a, h * strips + b) for g, h in earlier for a, b in steps
-    ]
-    grad_ahead = lax.ppermute(ahead, "tm", earlier)
-    below = lax.ppermute(first, "height", up)
-    above = lax.ppermute(last, "height", down)
-    below_ahead = lax.ppermute(corner_first, ("tm", "height"), cross(up))
-    above_ahead = lax.ppermute(corner_last, ("tm", "height"), cross(down))
-
+    rows = section_grad.shape[1]
+    swap = lambda a, b: [(a, b), (b, a)]
+    near = sum([swap(i, i + 1) for i in range(0, strips - 1, 2)], [])
+    far = sum([swap(i, i + 1) for i in range(1, strips - 1, 2)], [])
+    odd = lax.rem(lax.axis_index("height"), 2)
+    places = jnp.stack([(1 - odd) * (rows - 1), odd * (rows - 1)]).astype(jnp.int32)
+    w_out = jnp.transpose(w_out)
+
+    grad_ahead = lax.ppermute(section_grad, "tm", [(g + 1, g) for g in range(groups - 1)])
     modulated, latent_send = modulate(hidden, mod_scale, mod_shift, w_out, groups)
     latent = lax.all_to_all(latent_send, "tm", 0, 0, tiled=True)
-    latent_below = lax.ppermute(latent, "height", up)
-    latent_above = lax.ppermute(latent, "height", down)
-
-    own = own_part(section_grad, w_section)
-    centre, to_above, to_below = rest_part(
-        own,
-        (grad_ahead, above, below, above_ahead, below_ahead),
-        w_section,
-        (latent, latent_above, latent_below),
-        w_in,
+    near_send, far_send = pack_rows(places, section_grad, grad_ahead, latent)
+    far_rows = lax.ppermute(far_send, "height", far)
+    near_rows = lax.ppermute(near_send, "height", near)
+
+    own, turned = own_part(section_grad, w_section)
+    centre, near_share, far_share = rest_part(
+        places, own, grad_ahead, near_rows, far_rows, turned, latent, w_in
     )
-    from_below = lax.ppermute(to_above.astype(bf16), "height", up)
-    from_above = lax.ppermute(to_below.astype(bf16), "height", down)
-    centre = centre + from_below.astype(f32) + from_above.astype(f32)
+    far_share = lax.ppermute(far_share, "height", far)
+    near_share = lax.ppermute(near_share, "height", near)
+    centre = centre.astype(f32) + near_share.astype(f32) + far_share.astype(f32)
     shares = lax.all_to_all(centre.astype(bf16), "tm", 0, 0, tiled=True)
 
     token_grad, send = weight_terms(shares, modulated)

time: 197 us -> 114 us (0.58)
  Pallas kernels: 94.7 us -> 46.3 us
  starting transfers between devices: 52.4 us -> 30.4 us
  blocking collectives: 25.1 us -> 17.8 us
  local copies, waits for them, and re-layouts: 13.3 us -> 8.01 us
  waiting for transfers between devices: 5.12 us -> 7.98 us
  other arithmetic: 3.47 us -> 0.77 us
    pallas_call x3, Pallas kernels: 86.4 us -> 38.6 us  [the longest x1 20.1 us: own_part(): pl.pallas_call(own_kernel, grid=(9,), out_shape=[jax.ShapeDtypeStruct((ch...]
    ppermute x9 -> x5, starting transfers between devices: 26.1 us -> 10.9 us  [the longest x1 4.28 us: shards(): near_share = lax.ppermute(near_share, 'height', near)]
    all_to_all x1, starting transfers between devices: 26.3 us -> 15.4 us  [shards(): pieces = lax.all_to_all(middle_sum(got, strips), 'height', 0, 0, tiled=True)]
    all_to_all x1 -> x0, blocking collectives: 7.35 us -> none  [shards(): latent = lax.all_to_all(latent_send, 'tm', 0, 0, tiled=True)]
    unnamed x33 -> x22, local copies, waits for them, and re-layouts: 13.3 us -> 8.01 us
    all_to_all x0 -> x1, waiting for transfers between devices: none -> 4.77 us  [shards(): latent = lax.all_to_all(latent_send, 'tm', 0, 0, tiled=True)]
    all_to_all x0 -> x1, starting transfers between devices: none -> 3.99 us  [shards(): latent = lax.all_to_all(latent_send, 'tm', 0, 0, tiled=True)]
    ppermute x9 -> x5, waiting for transfers between devices: 3.91 us -> 1.18 us  [the longest x1 1.17 us: shards(): near_share = lax.ppermute(near_share, 'height', near)]
  transfers between devices with their start and end apart: 10 -> 7, of which waited for: 3 -> 3; matrix products, arithmetic and copies ran while one was open for 2% -> 5% of each run, Pallas kernels for 37% -> 24%
where the time goes in v2:
time: 114 us; the launch traced here: 112 us
  Pallas kernels  46.3 us (41%)
  starting transfers between devices  30.4 us (27%)
  blocking collectives  17.8 us (16%)
  local copies, waits for them, and re-layouts  8.01 us (7%)
  waiting for transfers between devices  7.98 us (7%)
    pallas_call x1, Pallas kernels, own_part(): pl.pallas_call(own_kernel, grid=(9,), out_shape=[jax.ShapeDtypeStruct((ch...  20.1 us
    pallas_call x1, Pallas kernels, rest_part(): pl.pallas_call(rest_kernel, out_shape=[out] * 3, grid_spec=pltpu.Prefetch...  16.7 us
    all_to_all x1, starting transfers between devices, shards(): pieces = lax.all_to_all(middle_sum(got, strips), 'height', 0, 0, tiled=True)  15.4 us
    all_to_all x1, blocking collectives, shards(): got = lax.all_to_all(send, 'tm', 0, 0, tiled=True)  9.7 us
    all_to_all x1, blocking collectives, shards(): shares = lax.all_to_all(centre.astype(bf16), 'tm', 0, 0, tiled=True)  8.12 us
    unnamed x22, local copies, waits for them, and re-layouts  8.01 us
    all_to_all x1, waiting for transfers between devices, shards(): latent = lax.all_to_all(latent_send, 'tm', 0, 0, tiled=True)  4.77 us
    ppermute x1, starting transfers between devices, shards(): near_share = lax.ppermute(near_share, 'height', near)  4.28 us
  transfers between devices with their start and end apart: 7, of which 3 were waited for; matrix products, arithmetic and copies ran while one was open for 5% of the time, Pallas kernels for 24%

profile of v2, /device:TPU:1, one launch (start us, length us, event | category | flops | bytes accessed | tf_op | source)
XLA Modules:
  0.0 112.1 jit_solution(10039819304722032589)
XLA Ops:
  0.7 3.5 %collective-permute-start = (bf16[3,4,96,512]{3,2,1,0:T(8,128)(2,1)}, bf16[3,4,96,512]{3,2,1,0:T(8,128)(2,1)}, u32[]{:S(2)}, u32[]{:S(2)}) collective-permute-start(bf16[3,4,96,512]{3,2,1,0:T(8,128)(2,1)} %own_far.1), channel_id=1, source_target_pairs={{32,0},{64,32},{96,64},{33,1},{65,33},{97,65},{34,2},{66,34},{98,6... | collective-permute-start | bytes 3538952 | tf_op jit(solution)/shard_map/ppermute | solution.py:553
  4.1 2.0 %copy.10.hidden = bf16[12,2,12,3072]{3,2,1,0:T(8,128)(2,1)S(1)} copy(bf16[12,2,12,3072]{3,1,2,0:T(2,128)(2,1)} %param.7) | data formatting | bytes 3538944 | tf_op args[0]
  6.1 3.2 %modulate.1 = (bf16[12,2,16,3072]{3,2,1,0:T(8,128)(2,1)S(1)}, bf16[4,5,16,128]{3,2,1,0:T(8,128)(2,1)S(1)}) custom-call(bf16[12,2,12,3072]{3,2,1,0:T(8,128)(2,1)S(1)} %copy.10.hidden, f32[1,3072]{1,0:T(1,128)S(1)} %bitcast.7, f32[1,3072]{1,0:T(1,128)S(1)} %bitcast.9, bf16[64,3072]{1,0:T(8,128)(2,1)S(1)} %bitcast.5), custom_call_target="tpu_custom_call" | custom-call | flops 150994944 | bytes 4718592 | tf_op jit(solution)/shard_map/modulate/pallas_call | solution.py:73
  9.3 1.4 %copy-done.1 = bf16[12,2,16,3072]{3,2,1,0:T(8,128)(2,1)} copy-done((bf16[12,2,16,3072]{3,2,1,0:T(8,128)(2,1)}, bf16[12,2,16,3072]{3,2,1,0:T(8,128)(2,1)S(1)}, u32[]{:S(2)}) %copy-start.1) | copy-done | bytes 2359320
  10.7 0.6 copy-done.5
  11.3 4.0 %all-to-all-start = ((bf16[4,5,16,128]{3,2,1,0:T(8,128)(2,1)}), bf16[4,5,16,128]{3,2,1,0:T(8,128)(2,1)}, u32[]{:S(2)}, u32[]{:S(2)}) async-start(bf16[4,5,16,128]{3,2,1,0:T(8,128)(2,1)} %copy-done.5), calls=%async_computation | async-start | bytes 163840 | tf_op jit(solution)/shard_map/all_to_all | solution.py:555
  15.4 4.8 %all-to-all-done.latent = bf16[4,5,16,128]{3,2,1,0:T(8,128)(2,1)} async-done(((bf16[4,5,16,128]{3,2,1,0:T(8,128)(2,1)}), bf16[4,5,16,128]{3,2,1,0:T(8,128)(2,1)}, u32[]{:S(2)}, u32[]{:S(2)}) %all-to-all-start) | async-done | bytes 81952 | tf_op jit(solution)/shard_map/all_to_all | solution.py:555
  20.2 1.7 %pack_rows.1 = (bf16[560,512]{1,0:T(8,128)(2,1)S(1)}, bf16[560,512]{1,0:T(8,128)(2,1)S(1)}) custom-call(s32[2]{0:T(128)S(1)} %pad_add_fusion.places, bf16[3,4,96,512]{3,2,1,0:T(8,128)(2,1)S(1)} %copy-done, bf16[3,4,96,512]{3,2,1,0:T(8,128)(2,1)S(1)} %copy-done, bf16[3,4,96,512]{3,2,1,0:T(8,128)(2,1)} %collective-permute-done.ahead_near.ahead_far.grad_ahead, ...), custom_call_target="tpu_custom_call" | custom-call | tf_op jit(solution)/shard_map/pack_rows/pallas_call | solution.py:143
  21.9 1.7 %collective-permute-start.1 = (bf16[560,512]{1,0:T(8,128)(2,1)S(1)}, bf16[560,512]{1,0:T(8,128)(2,1)S(1)}, u32[]{:S(2)}, u32[]{:S(2)}) collective-permute-start(bf16[560,512]{1,0:T(8,128)(2,1)S(1)} %get-tuple-element.15), channel_id=1, source_target_pairs={{0,1},{1,0},{2,3},{3,2},{4,5},{5,4},{6,7},{7,6},{8,9},{9,8},{10,11... | collective-permute-start | bytes 1720328 | tf_op jit(solution)/shard_map/ppermute | solution.py:558
  23.6 0.8 collective-permute-start.2
  24.5 20.1 %own_part.1 = (f32[4,3,4,96,128]{4,3,2,1,0:T(8,128)}, bf16[3,3,3,512,512]{4,3,2,1,0:T(8,128)(2,1)}) custom-call(bf16[3,4,96,512]{3,2,1,0:T(8,128)(2,1)S(1)} %copy-done, bf16[3,3,3,512,512]{4,3,2,1,0:T(8,128)(2,1)} %w_section.1), custom_call_target="tpu_custom_call" | custom-call | flops 9059696640 | bytes 14155776 | tf_op jit(solution)/shard_map/own_part/pallas_call | solution.py:196
  44.6 16.7 %rest_part.1 = (bf16[4,5,16,128]{3,2,1,0:T(8,128)(2,1)S(1)}, bf16[4,5,16,128]{3,2,1,0:T(8,128)(2,1)S(1)}, bf16[4,5,16,128]{3,2,1,0:T(8,128)(2,1)S(1)}) custom-call(s32[2]{0:T(128)S(1)} %pad_add_fusion.places, f32[4,3,4,96,128]{4,3,2,1,0:T(8,128)} %get-tuple-element.13.own, bf16[3,4,96,512]{3,2,1,0:T(8,128)(2,1)} %collective-permute-done.ahead_near.ahead_far.grad_ahead, ...), custom_call_target="tpu_custom_call" | custom-call | flops 9663676416 | bytes 14155776 | tf_op jit(solution)/shard_map/rest_part/pallas_call | solution.py:404
  61.4 4.3 %collective-permute-start.3 = (bf16[4,5,16,128]{3,2,1,0:T(8,128)(2,1)S(1)}, bf16[4,5,16,128]{3,2,1,0:T(8,128)(2,1)S(1)}, u32[]{:S(2)}, u32[]{:S(2)}) collective-permute-start(bf16[4,5,16,128]{3,2,1,0:T(8,128)(2,1)S(1)} %get-tuple-element.19), channel_id=1, source_target_pairs={{0,1},{1,0},{2,3},{3,2},{4,5},{5,4},{6,7},{7,6},{8,9},{9,8},{10,11... | collective-permute-start | bytes 245768 | tf_op jit(solution)/shard_map/ppermute | solution.py:565
  65.7 0.7 collective-permute-start.4
  66.3 1.2 %collective-permute-done.3 = bf16[4,5,16,128]{3,2,1,0:T(8,128)(2,1)S(1)} collective-permute-done((bf16[4,5,16,128]{3,2,1,0:T(8,128)(2,1)S(1)}, bf16[4,5,16,128]{3,2,1,0:T(8,128)(2,1)S(1)}, u32[]{:S(2)}, u32[]{:S(2)}) %collective-permute-start.3) | collective-permute-done | bytes 81952 | tf_op jit(solution)/shard_map/ppermute | solution.py:565
  67.5 8.1 %all_to_all.20.shares = bf16[4,5,16,128]{3,2,1,0:T(8,128)(2,1)S(1)} all-to-all(bf16[4,5,16,128]{3,2,1,0:T(8,128)(2,1)S(1)} %add_convert_fusion), channel_id=1, replica_groups=mesh['tm'=4,'height'=32] {'tm'}, dimensions={0} | all-to-all | bytes 163840 | tf_op jit(solution)/shard_map/all_to_all | solution.py:567
  75.7 0.7 weight_terms.1
  76.4 9.7 %all_to_all.21.got = bf16[4,384,128]{2,1,0:T(8,128)(2,1)S(1)} all-to-all(bf16[4,384,128]{2,1,0:T(8,128)(2,1)S(1)} %get-tuple-element.23), channel_id=1, replica_groups=mesh['tm'=4,'height'=32] {'tm'}, dimensions={0} | all-to-all | bytes 786432 | tf_op jit(solution)/shard_map/all_to_all | solution.py:570
  86.2 0.8 reshape.13
  87.0 15.4 %all-to-all-start.3 = ((bf16[32,2,768]{2,1,0:T(2,128)(2,1)}), bf16[32,2,768]{2,1,0:T(2,128)(2,1)S(1)}, u32[]{:S(2)}, u32[]{:S(2)}) async-start(bf16[32,2,768]{2,1,0:T(2,128)(2,1)} %reshape.13), calls=%async_computation.3 | async-start | bytes 196608 | tf_op jit(solution)/shard_map/all_to_all | solution.py:572
  102.5 3.7 %hidden_grad.1 = bf16[12,2,12,3072]{3,2,1,0:T(8,128)(2,1)S(1)} custom-call(bf16[12,2,12,3072]{3,2,1,0:T(8,128)(2,1)S(1)} %copy.10.hidden, bf16[12,2,16,64]{3,2,1,0:T(8,128)(2,1)S(1)} %get-tuple-element.22.token_grad, f32[1,3072]{1,0:T(1,128)S(1)} %bitcast.8, bf16[64,3072]{1,0:T(8,128)(2,1)S(1)} %bitcast.6), custom_call_target="tpu_custom_call" | custom-call | flops 150994944 | bytes 4718592 | tf_op jit(solution)/shard_map/hidden_grad/pallas_call | solution.py:522
  106.2 3.0 %copy.11 = bf16[12,2,12,3072]{3,1,2,0:T(2,128)(2,1)} copy(bf16[12,2,12,3072]{3,2,1,0:T(8,128)(2,1)S(1)} %hidden_grad.1) | data formatting | bytes 3538944
  109.2 2.0 %all-to-all-done.3 = bf16[32,2,768]{2,1,0:T(2,128)(2,1)S(1)} async-done(((bf16[32,2,768]{2,1,0:T(2,128)(2,1)}), bf16[32,2,768]{2,1,0:T(2,128)(2,1)S(1)}, u32[]{:S(2)}, u32[]{:S(2)}) %all-to-all-start.3) | async-done | bytes 98336 | tf_op jit(solution)/shard_map/all_to_all | solution.py:572
  111.5 0.6 broadcast_multiply_fusion
  (25 shorter events, 0.5 us)
Async XLA Ops:
  0.6 5.5 %copy-start.3 = (bf16[3072,64]{0,1:T(8,128)(2,1)S(1)}, bf16[3072,64]{0,1:T(8,128)(2,1)}, u32[]{:S(2)}) copy-start(bf16[3072,64]{0,1:T(8,128)(2,1)} %param.10) | copy-start | bytes 1179652
  0.6 5.5 %copy-start.7 = (f32[3072]{0:T(1024)S(1)}, f32[3072]{0:T(1024)}, u32[]{:S(2)}) copy-start(f32[3072]{0:T(1024)} %param.9) | copy-start | bytes 36868
  0.7 5.5 %copy-start.6 = (f32[3072]{0:T(1024)S(1)}, f32[3072]{0:T(1024)}, u32[]{:S(2)}) copy-start(f32[3072]{0:T(1024)} %param.8) | copy-start | bytes 36868
  0.7 19.5 %collective-permute-start = (bf16[3,4,96,512]{3,2,1,0:T(8,128)(2,1)}, bf16[3,4,96,512]{3,2,1,0:T(8,128)(2,1)}, u32[]{:S(2)}, u32[]{:S(2)}) collective-permute-start(bf16[3,4,96,512]{3,2,1,0:T(8,128)(2,1)} %own_far.1), channel_id=1, source_target_pairs={{32,0},{64,32},{96,64},{33,1},{65,33},{97,65},{34,2},{66,34},{98,6... | collective-permute-start | bytes 3538952 | tf_op jit(solution)/shard_map/ppermute | solution.py:553
  6.1 14.1 %copy-start = (bf16[3,4,96,512]{3,2,1,0:T(8,128)(2,1)S(1)}, bf16[3,4,96,512]{3,2,1,0:T(8,128)(2,1)}, u32[]{:S(2)}) copy-start(bf16[3,4,96,512]{3,2,1,0:T(8,128)(2,1)} %own_far.1) | copy-start | bytes 3538948
  9.3 1.4 %copy-start.1 = (bf16[12,2,16,3072]{3,2,1,0:T(8,128)(2,1)}, bf16[12,2,16,3072]{3,2,1,0:T(8,128)(2,1)S(1)}, u32[]{:S(2)}) copy-start(bf16[12,2,16,3072]{3,2,1,0:T(8,128)(2,1)S(1)} %get-tuple-element.21.modulated) | copy-start | bytes 7077892
  10.7 0.6 copy-start.5
  11.3 8.8 %all-to-all-start = ((bf16[4,5,16,128]{3,2,1,0:T(8,128)(2,1)}), bf16[4,5,16,128]{3,2,1,0:T(8,128)(2,1)}, u32[]{:S(2)}, u32[]{:S(2)}) async-start(bf16[4,5,16,128]{3,2,1,0:T(8,128)(2,1)} %copy-done.5), calls=%async_computation | async-start | bytes 163840 | tf_op jit(solution)/shard_map/all_to_all | solution.py:555
  21.9 22.7 %collective-permute-start.1 = (bf16[560,512]{1,0:T(8,128)(2,1)S(1)}, bf16[560,512]{1,0:T(8,128)(2,1)S(1)}, u32[]{:S(2)}, u32[]{:S(2)}) collective-permute-start(bf16[560,512]{1,0:T(8,128)(2,1)S(1)} %get-tuple-element.15), channel_id=1, source_target_pairs={{0,1},{1,0},{2,3},{3,2},{4,5},{5,4},{6,7},{7,6},{8,9},{9,8},{10,11... | collective-permute-start | bytes 1720328 | tf_op jit(solution)/shard_map/ppermute | solution.py:558
  23.6 21.0 %copy-start.8 = (bf16[3,3,3,16,512]{4,3,2,1,0:T(8,128)(2,1)S(1)}, bf16[3,3,3,16,512]{4,3,2,1,0:T(8,128)(2,1)}, u32[]{:S(2)}) copy-start(bf16[3,3,3,16,512]{4,3,2,1,0:T(8,128)(2,1)} %w_in.1) | copy-start | bytes 1327108
  23.6 21.0 %collective-permute-start.2 = (bf16[560,512]{1,0:T(8,128)(2,1)S(1)}, bf16[560,512]{1,0:T(8,128)(2,1)S(1)}, u32[]{:S(2)}, u32[]{:S(2)}) collective-permute-start(bf16[560,512]{1,0:T(8,128)(2,1)S(1)} %get-tuple-element.16), channel_id=1, source_target_pairs={{1,2},{2,1},{3,4},{4,3},{5,6},{6,5},{7,8},{8,7},{9,10},{10,9},{11,... | collective-permute-start | bytes 1720328 | tf_op jit(solution)/shard_map/ppermute | solution.py:557
  44.6 31.0 %copy-start.2 = (bf16[12,2,16,3072]{3,2,1,0:T(8,128)(2,1)S(1)}, bf16[12,2,16,3072]{3,2,1,0:T(8,128)(2,1)}, u32[]{:S(2)}) copy-start(bf16[12,2,16,3072]{3,2,1,0:T(8,128)(2,1)} %copy-done.1) | copy-start | bytes 7077892
  61.4 6.1 %collective-permute-start.3 = (bf16[4,5,16,128]{3,2,1,0:T(8,128)(2,1)S(1)}, bf16[4,5,16,128]{3,2,1,0:T(8,128)(2,1)S(1)}, u32[]{:S(2)}, u32[]{:S(2)}) collective-permute-start(bf16[4,5,16,128]{3,2,1,0:T(8,128)(2,1)S(1)} %get-tuple-element.19), channel_id=1, source_target_pairs={{0,1},{1,0},{2,3},{3,2},{4,5},{5,4},{6,7},{7,6},{8,9},{9,8},{10,11... | collective-permute-start | bytes 245768 | tf_op jit(solution)/shard_map/ppermute | solution.py:565
  65.7 1.8 %collective-permute-start.4 = (bf16[4,5,16,128]{3,2,1,0:T(8,128)(2,1)S(1)}, bf16[4,5,16,128]{3,2,1,0:T(8,128)(2,1)S(1)}, u32[]{:S(2)}, u32[]{:S(2)}) collective-permute-start(bf16[4,5,16,128]{3,2,1,0:T(8,128)(2,1)S(1)} %get-tuple-element.20), channel_id=1, source_target_pairs={{1,2},{2,1},{3,4},{4,3},{5,6},{6,5},{7,8},{8,7},{9,10},{10,9},{11,... | collective-permute-start | bytes 245768 | tf_op jit(solution)/shard_map/ppermute | solution.py:564
  67.5 35.0 %copy-start.4 = (bf16[3072,64]{0,1:T(8,128)(2,1)S(1)}, bf16[3072,64]{0,1:T(8,128)(2,1)}, u32[]{:S(2)}) copy-start(bf16[3072,64]{0,1:T(8,128)(2,1)} %param.10) | copy-start | bytes 1179652
  87.0 24.2 %all-to-all-start.3 = ((bf16[32,2,768]{2,1,0:T(2,128)(2,1)}), bf16[32,2,768]{2,1,0:T(2,128)(2,1)S(1)}, u32[]{:S(2)}, u32[]{:S(2)}) async-start(bf16[32,2,768]{2,1,0:T(2,128)(2,1)} %reshape.13), calls=%async_computation.3 | async-start | bytes 196608 | tf_op jit(solution)/shard_map/all_to_all | solution.py:572

commit v3 on v2

v3 whole, which is shorter than its diff:
```python
import functools
import math

import jax
import jax.numpy as jnp
from jax import lax
from jax.experimental import pallas as pl
from jax.experimental.pallas import tpu as pltpu
from jax.sharding import PartitionSpec as P

epsilon = 1e-05
slots = 16
lanes = 128
f32 = jnp.float32
bf16 = jnp.bfloat16
whole = pl.BlockSpec(memory_space=pltpu.VMEM)


def params(mib):
    return pltpu.CompilerParams(vmem_limit_bytes=mib * 2**20)


def dot(lhs, rhs):
    return jnp.dot(lhs, rhs, preferred_element_type=f32)


def dot_turned(lhs, rhs):
    return lax.dot_general(lhs, rhs, (((1,), (1,)), ((), ())), preferred_element_type=f32)


def normalise(values):
    center = jnp.mean(values, axis=-1, keepdims=True)
    shifted = values - center
    spread = jnp.mean(shifted * shifted, axis=-1, keepdims=True)
    inverse = lax.rsqrt(spread + epsilon)
    return shifted * inverse, inverse


def modulate_kernel(hidden, scale, shift, w_out, modulated, send):
    groups, depth = send.shape[:2]
    block = depth - 2
    _, token_rows, tokens, width = hidden.shape
    gain = 1.0 + scale[...]
    blank = jnp.zeros((slots - tokens, width), f32)
    send[0, 0:2] = jnp.zeros_like(send[0, 0:2])

    def share(step, carry):
        for frame in range(block):
            for row in range(token_rows):
                normed, _ = normalise(hidden[step * block + frame, row].astype(f32))
                value = jnp.concatenate([normed * gain + shift[...], blank], axis=0)
                modulated[step * block + frame, row] = value.astype(bf16)
        rows = modulated[pl.ds(step * block, block)].reshape(-1, width)
        latent = dot_turned(rows, w_out[...]).astype(bf16)
        latent = latent.reshape(block, token_rows, slots, latent.shape[-1])
        paired = jnp.concatenate([latent[:, 0], latent[:, 1]], axis=-1)
        for frame in range(block):
            send[step, frame + 2] = paired[frame]

        @pl.when(step < groups - 1)
        def _():
            for frame in range(1, block):
                send[step + 1, frame - 1] = paired[frame]

        return carry

    lax.fori_loop(0, groups, share, 0)


def modulate(hidden, mod_scale, mod_shift, w_out, groups):
    frames, token_rows, tokens, width = hidden.shape
    token_width = w_out.shape[0]
    return pl.pallas_call(
        modulate_kernel,
        out_shape=[
            jax.ShapeDtypeStruct((frames, token_rows, slots, width), bf16),
            jax.ShapeDtypeStruct((groups, frames // groups + 2, slots, 2 * token_width), bf16),
        ],
        in_specs=[whole] * 4,
        out_specs=[whole] * 2,
        compiler_params=params(8),
        cost_estimate=pl.CostEstimate(
            flops=2 * frames * 2 * slots * width * token_width,
            bytes_accessed=8 * frames * slots * width,
            transcendentals=0,
        ),
        name="modulate",
    )(hidden, mod_scale.reshape(1, -1), mod_shift.reshape(1, -1), w_out)


def column_shifts(value):
    cols, channels = value.shape
    wide = value.astype(f32)
    place = lax.broadcasted_iota(jnp.int32, (cols, channels), 0)
    nxt = jnp.where(place == cols - 1, 0.0, pltpu.roll(wide, cols - 1, 0))
    prv = jnp.where(place == 0, 0.0, pltpu.roll(wide, 1, 0))
    return nxt.astype(bf16), prv.astype(bf16)


taps = [(2 - n // 3, (1, 0, 2)[n % 3]) for n in range(9)]


def flat(value):
    return value.reshape(-1, value.shape[-1])


def weight_matrix(w_section, kt, ky):
    return jnp.concatenate([w_section[kt, ky, kx] for kx in range(3)], axis=-1)


def pack_kernel(places, grad, grad_ahead, latent, near, far):
    frames, _, cols, channels = grad.shape
    for side, out in ((0, near), (1, far)):
        row = places[side]
        for frame in range(frames):
            out[frame * cols : (frame + 1) * cols] = grad[frame, row]
        for frame in range(2):
            at = (frames + frame) * cols
            out[at : at + cols] = grad_ahead[frame, row]
        at = (frames + 2) * cols
        tail = flat(latent[...])
        count = tail.shape[0] * lanes // channels
        for lane in range(channels // lanes):
            out[at : at + count, lane * lanes : (lane + 1) * lanes] = tail[
                lane * count : (lane + 1) * count
            ]


def pack_rows(places, grad, grad_ahead, latent):
    frames, rows, cols, channels = grad.shape
    total = (frames + 2) * cols + latent.size // channels
    return pl.pallas_call(
        pack_kernel,
        in_specs=[pl.BlockSpec(memory_space=pltpu.SMEM)] + [whole] * 3,
        out_specs=[whole] * 2,
        out_shape=[jax.ShapeDtypeStruct((total, channels), bf16)] * 2,
        compiler_params=params(4),
        name="pack_rows",
    )(places, grad, grad_ahead, latent)


def own_kernel(grad, w_section, total, held, shifts, sems):
    frames, rows, cols, channels = grad.shape
    copies = [
        pltpu.make_async_copy(w_section.at[kt, ky], held.at[kt, ky], sems.at[n])
        for n, (kt, ky) in enumerate(taps)
    ]
    for copy in copies:
        copy.start()
    for frame in range(frames):
        for row in range(rows):
            shifts[0, frame, row], shifts[1, frame, row] = column_shifts(grad[frame, row])
    for n, (kt, ky) in enumerate(taps):
        lo, hi = max(0, ky - 1), rows + min(0, ky - 1)
        src = slice(2 - kt, frames), slice(lo + 1 - ky, hi + 1 - ky)
        window = jnp.concatenate(
            [flat(shifts[(0,) + src]), flat(grad[src]), flat(shifts[(1,) + src])], axis=-1
        )
        copies[n].wait()
        part = dot_turned(window, weight_matrix(held, kt, ky))
        for lane in range(channels // lanes):
            value = part[:, lane * lanes : (lane + 1) * lanes]
            value = value.reshape(kt + 1, hi - lo, cols, lanes)
            if n == 0:
                total[lane] = value
            else:
                total[lane, 0 : kt + 1, lo:hi] += value


def own_part(grad, w_section):
    frames, rows, cols, channels = grad.shape
    return pl.pallas_call(
        own_kernel,
        out_shape=[
            jax.ShapeDtypeStruct((channels // lanes, frames, rows, cols, lanes), f32),
            jax.ShapeDtypeStruct(w_section.shape, bf16),
        ],
        in_specs=[whole, pl.BlockSpec(memory_space=pltpu.HBM)],
        out_specs=[whole] * 2,
        scratch_shapes=[
            pltpu.VMEM((2,) + grad.shape, bf16),
            pltpu.SemaphoreType.DMA((len(taps),)),
        ],
        compiler_params=params(24),
        cost_estimate=pl.CostEstimate(
            flops=2 * 15 * grad.size * channels,
            bytes_accessed=2 * w_section.size,
            transcendentals=0,
        ),
        name="own_part",
    )(grad, w_section)


def rest_kernel(
    places,
    own,
    grad_ahead,
    near_rows,
    far_rows,
    w_section,
    latent,
    w_in,
    centre_out,
    near_out,
    far_out,
    total,
    far,
    near,
    tokens,
    windows,
    patches,
    spread,
):
    even = places[0] != 0
    blocks, frames, rows, cols, _ = own.shape
    channels = blocks * lanes
    groups, depth, _, pair = latent.shape
    width = pair // 2
    block = cols // (2 * groups)
    half = cols // 2
    total[...] = own[...]
    for frame in range(frames + 2):
        at = slice(frame * cols, (frame + 1) * cols)
        ends = near_rows[at], far_rows[at]
        for side in range(2):
            value = jnp.where(even == (side == 1), ends[0], ends[1])
            shifted = column_shifts(value)
            if frame < frames:
                near[1, side, frame] = value
                near[0, side, frame], near[2, side, frame] = shifted
            else:
                row = side * (rows + 1)
                far[1, frame - frames, row] = value
                far[0, frame - frames, row], far[2, frame - frames, row] = shifted
    for frame in range(2):
        for row in range(rows):
            value = grad_ahead[frame, row]
            far[1, frame, row + 1] = value
            far[0, frame, row + 1], far[2, frame, row + 1] = column_shifts(value)

    for n, (kt, ky) in enumerate(taps):
        if (kt, ky) == (2, 1):
            continue
        pieces, places = [], []
        if kt < 2:
            src = slice(0, 2 - kt), slice(2 - ky, 2 - ky + rows)
            pieces.append([far[(kx,) + src] for kx in range(3)])
            places.append((slice(kt + 1, frames), slice(0, rows)))
        if ky != 1:
            side = 0 if ky == 2 else 1
            edge = 0 if ky == 2 else rows - 1
            pieces.append([near[kx, side, 2 - kt : frames] for kx in range(3)])
            places.append((slice(0, kt + 1), slice(edge, edge + 1)))
        window = jnp.concatenate(
            [jnp.concatenate([flat(v) for v in piece], axis=-1) for piece in pieces], axis=0
        )
        part = dot_turned(window, weight_matrix(w_section, kt, ky))
        at = 0
        for place in places:
            shape = [cut.stop - cut.start for cut in place] + [cols, lanes]
            count = shape[0] * shape[1] * cols
            for lane in range(blocks):
                value = part[at : at + count, lane * lanes : (lane + 1) * lanes]
                total[(lane,) + place] += value.reshape(shape)
            at += count
    tokens[...] = jnp.zeros_like(tokens)
    for src in range(groups):
        at = slice(8 + src * block, 8 + (src + 1) * block)
        for frame in range(depth):
            value = latent[src, frame].astype(f32)[:block]
            tokens[frame, 1, at] = value[:, :width]
            tokens[frame, 2, at] = value[:, width:]
            row = (src * depth + frame) * slots
            count = groups * depth * slots * lanes // channels
            lane = row // count * lanes
            row = (frames + 2) * cols + row % count
            ends = [
                rows_of[row : row + slots, lane : lane + lanes].astype(f32)[:block]
                for rows_of in (near_rows, far_rows)
            ]
            tokens[frame, 0, at] = jnp.where(even, ends[1], ends[0])[:, width:]
            tokens[frame, 3, at] = jnp.where(even, ends[0], ends[1])[:, :width]
    for q in range(2):
        left = tokens[:, :, 7 + q : 7 + q + half]
        right = tokens[:, :, 8 + q : 8 + q + half]
        windows[q] = jnp.concatenate([left, right], axis=-1).astype(bf16)
    patches[...] = jnp.zeros_like(patches)
    lat = width // 4
    for p in range(2):
        for q in range(2):
            for kt in range(3):
                for a in range(2):
                    for b in range(2):
                        for pp in range(2):
                            for qq in range(2):
                                ky, kx = p - 1 + 2 * a + pp, q - 1 + 2 * b + qq
                                if not (0 <= ky < 3 and 0 <= kx < 3):
                                    continue
                                at = (kt * 2 + a) * pair + b * width + (2 * pp + qq) * lat
                                patches[2 * p + q, at : at + lat] = w_in[kt, ky, kx]
    spread[...] = jnp.zeros_like(spread)
    for p in range(2):
        for q in range(2):
            window = jnp.concatenate(
                [
                    flat(windows[q, kt : kt + frames, p + a : p + a + rows // 2])
                    for kt in range(3)
                    for a in range(2)
                ],
                axis=-1,
            )
            weight = patches[2 * p + q]
            pre = dot(window, weight)
            back = jnp.concatenate(
                [
                    jnp.concatenate(
                        [
                            total[lane, frame, 2 * row + p, pl.ds(q, half, stride=2), :]
                            for lane in range(blocks)
                        ],
                        axis=-1,
                    )
                    for frame in range(frames)
                    for row in range(rows // 2)
                ],
                axis=0,
            )
            gate = jax.nn.sigmoid(pre)
            act_grad = (back * (gate * (1.0 + pre * (1.0 - gate)))).astype(bf16)
            terms = dot_turned(act_grad, weight)
            for kt in range(3):
                for a in range(2):
                    at = (kt * 2 + a) * pair
                    spread[kt : kt + frames, p + a : p + a + rows // 2, q : q + half] += terms[
                        :, at : at + pair
                    ].reshape(frames, rows // 2, half, pair)
    centre_out[...] = jnp.zeros_like(centre_out)
    near_out[...] = jnp.zeros_like(near_out)
    far_out[...] = jnp.zeros_like(far_out)
    grid = spread[:, :, 1 : half + 1, :width] + spread[:, :, 0:half, width:]
    tokens[:, :, 0:half] = grid
    for dst in range(groups):
        for frame in range(depth):
            value = [
                tokens[frame, row, dst * block : (dst + 1) * block] for row in range(4)
            ]
            none = jnp.zeros_like(value[0])
            centre = jnp.concatenate([value[1], value[2]], axis=-1)
            up = jnp.concatenate([none, value[0]], axis=-1)
            down = jnp.concatenate([value[3], none], axis=-1)
            fill = jnp.zeros((slots - block, 2 * width), f32)
            padded = lambda v: jnp.concatenate([v, fill], axis=0).astype(bf16)
            centre_out[dst, frame] = padded(centre)
            near_out[dst, frame] = padded(jnp.where(even, down, up))
            far_out[dst, frame] = padded(jnp.where(even, up, down))


def rest_part(places, own, grad_ahead, near_rows, far_rows, w_section, latent, w_in):
    blocks, frames, rows, cols, _ = own.shape
    channels = blocks * lanes
    groups, depth, _, pair = latent.shape
    out = jax.ShapeDtypeStruct(latent.shape, bf16)
    return pl.pallas_call(
        rest_kernel,
        out_shape=[out] * 3,
        in_specs=[pl.BlockSpec(memory_space=pltpu.SMEM)] + [whole] * 7,
        out_specs=[whole] * 3,
        scratch_shapes=[
            pltpu.VMEM(own.shape, f32),
            pltpu.VMEM((3, 2, rows + 2, cols, channels), bf16),
            pltpu.VMEM((3, 2, frames, cols, channels), bf16),
            pltpu.VMEM((depth, rows // 2 + 2, 72, pair // 2), f32),
            pltpu.VMEM((2, depth, rows // 2 + 2, cols // 2, pair), bf16),
            pltpu.VMEM((4, 6 * pair, channels), bf16),
            pltpu.VMEM((depth, rows // 2 + 2, cols // 2 + 8, pair), f32),
        ],
        compiler_params=params(24),
        cost_estimate=pl.CostEstimate(
            flops=2 * 16 * own.size * channels,
            bytes_accessed=2 * w_section.size,
            transcendentals=2 * own.size,
        ),
        name="rest_part",
    )(places, own, grad_ahead, near_rows, far_rows, w_section, latent, w_in)


def weight_kernel(shares, modulated, token_grad, send, field):
    groups, depth, _, pair = shares.shape
    width = pair // 2
    frames, token_rows = modulated.shape[:2]
    model = modulated.shape[-1]
    field[...] = jnp.zeros_like(field)
    for src in range(groups):
        at = src * (frames // groups)
        field[at : at + depth] += shares[src].astype(f32)
    values = field[2 : 2 + frames]
    token_grad[:, 0] = values[:, :, :width].astype(bf16)
    token_grad[:, 1] = values[:, :, width:].astype(bf16)
    turned = jnp.transpose(token_grad[...].reshape(-1, width).astype(f32)).astype(bf16)
    weight = dot(turned, modulated[...].reshape(-1, model))
    half = model // (2 * groups)
    for dst in range(groups):
        at = 2 * half * dst
        stacked = jnp.concatenate(
            [weight[:, at : at + half], weight[:, at + half : at + 2 * half]], axis=0
        )
        send[dst] = jnp.transpose(stacked).astype(bf16)


def weight_terms(shares, modulated):
    groups, depth, _, pair = shares.shape
    frames, token_rows, _, model = modulated.shape
    return pl.pallas_call(
        weight_kernel,
        out_shape=[
            jax.ShapeDtypeStruct((frames, token_rows, slots, pair // 2), bf16),
            jax.ShapeDtypeStruct((groups, model // (2 * groups), pair), bf16),
        ],
        in_specs=[whole] * 2,
        out_specs=[whole] * 2,
        scratch_shapes=[pltpu.VMEM((frames + 2, slots, pair), f32)],
        compiler_params=params(12),
        name="weight_terms",
    )(shares, modulated)


def middle_kernel(got, send):
    total = jnp.sum(got[...].astype(f32), axis=0)
    count, rows, width = send.shape
    total = total.reshape(count // 2, rows, 2 * width).astype(bf16)
    send[0 : count // 2] = total[:, :, :width]
    send[count // 2 :] = total[:, :, width:]


def middle_sum(got, count):
    groups, depth, pair = got.shape
    return pl.pallas_call(
        middle_kernel,
        out_shape=jax.ShapeDtypeStruct((count, 2 * depth // count, pair // 2), bf16),
        in_specs=[whole],
        out_specs=whole,
        compiler_params=params(4),
        name="middle_sum",
    )(got)


def hidden_kernel(hidden, token_grad, scale, w_out, grad_hidden):
    frames, token_rows, tokens, width = hidden.shape
    gain = 1.0 + scale[...]
    block = 3

    def share(step, carry):
        rows = token_grad[pl.ds(step * block, block)].reshape(-1, token_grad.shape[-1])
        mod_grad = dot(rows, w_out[...])
        for frame in range(block):
            for row in range(token_rows):
                at = (frame * token_rows + row) * slots
                scaled = mod_grad[at : at + tokens] * gain
                normed, inverse = normalise(hidden[step * block + frame, row].astype(f32))
                first = jnp.mean(scaled, axis=-1, keepdims=True)
                second = jnp.mean(scaled * normed, axis=-1, keepdims=True)
                value = (scaled - first - normed * second) * inverse
                grad_hidden[step * block + frame, row] = value.astype(bf16)
        return carry

    lax.fori_loop(0, frames // block, share, 0)


def hidden_grad(hidden, token_grad, mod_scale, w_out):
    frames, token_rows, tokens, width = hidden.shape
    return pl.pallas_call(
        hidden_kernel,
        out_shape=jax.ShapeDtypeStruct(hidden.shape, bf16),
        in_specs=[whole] * 4,
        out_specs=whole,
        compiler_params=params(8),
        cost_estimate=pl.CostEstimate(
            flops=2 * frames * 2 * slots * width * w_out.shape[0],
            bytes_accessed=8 * frames * slots * width,
            transcendentals=0,
        ),
        name="hidden_grad",
    )(hidden, token_grad, mod_scale.reshape(1, -1), w_out)


def shards(hidden, mod_scale, mod_shift, w_out, w_in, w_section, section_grad):
    groups, strips = lax.axis_size("tm"), lax.axis_size("height")
    rows = section_grad.shape[1]
    swap = lambda a, b: [(a, b), (b, a)]
    near = sum([swap(i, i + 1) for i in range(0, strips - 1, 2)], [])
    far = sum([swap(i, i + 1) for i in range(1, strips - 1, 2)], [])
    odd = lax.rem(lax.axis_index("height"), 2)
    places = jnp.stack([(1 - odd) * (rows - 1), odd * (rows - 1)]).astype(jnp.int32)
    w_out = jnp.transpose(w_out)

    grad_ahead = lax.ppermute(section_grad, "tm", [(g + 1, g) for g in range(groups - 1)])
    modulated, latent_send = modulate(hidden, mod_scale, mod_shift, w_out, groups)
    latent = lax.all_to_all(latent_send, "tm", 0, 0, tiled=True)
    near_send, far_send = pack_rows(places, section_grad, grad_ahead, latent)
    far_rows = lax.ppermute(far_send, "height", far)
    near_rows = lax.ppermute(near_send, "height", near)

    own, held = own_part(section_grad, w_section)
    centre, near_share, far_share = rest_part(
        places, own, grad_ahead, near_rows, far_rows, held, latent, w_in
    )
    far_share = lax.ppermute(far_share, "height", far)
    near_share = lax.ppermute(near_share, "height", near)
    centre = centre.astype(f32) + near_share.astype(f32) + far_share.astype(f32)
    shares = lax.all_to_all(centre.astype(bf16), "tm", 0, 0, tiled=True)

    token_grad, send = weight_terms(shares, modulated)
    got = lax.all_to_all(send, "tm", 0, 0, tiled=True)
    grad_hidden = hidden_grad(hidden, token_grad, mod_scale, w_out)
    got, grad_hidden = lax.optimization_barrier((got, grad_hidden))
    pieces = lax.all_to_all(middle_sum(got, strips), "height", 0, 0, tiled=True)
    total_tokens = math.prod(hidden.shape[:3]) * groups * strips
    grad_out_weight = jnp.sum(pieces.astype(f32), axis=0) / math.sqrt(total_tokens)
    return (grad_hidden, grad_out_weight)


def solution(mesh):
    placed = (P(None, "height", "tm", None), P(), P(), P(), P(), P(), P("tm", "height", None, None))
    return jax.shard_map(
        shards,
        mesh=mesh,
        in_specs=placed,
        out_specs=(P(None, "height", "tm", None), P(("tm", "height"), None)),
        check_vma=False,
    )
```

time: 114 us -> 108 us (0.947)
  Pallas kernels: 46.3 us -> 34.6 us
  blocking collectives: 17.8 us -> 8.17 us
  starting transfers between devices: 30.4 us -> 39.2 us
  local copies, waits for them, and re-layouts: 8.01 us -> 11.8 us
  waiting for transfers between devices: 7.98 us -> 11.4 us
    pallas_call x5, Pallas kernels: 45.5 us -> 32.9 us  [the longest x1 12.2 us: own_part(): pl.pallas_call(own_kernel, out_shape=[jax.ShapeDtypeStruct((channels // l...]
    all_to_all x1 -> x0, blocking collectives: 9.7 us -> none  [shards(): got = lax.all_to_all(send, 'tm', 0, 0, tiled=True)]
    all_to_all x1, starting transfers between devices: 15.4 us -> 19.9 us  [shards(): pieces = lax.all_to_all(middle_sum(got, strips), 'height', 0, 0, tiled=True)]
    all_to_all x0 -> x1, starting transfers between devices: none -> 4.33 us  [shards(): got = lax.all_to_all(send, 'tm', 0, 0, tiled=True)]
    unnamed x22, local copies, waits for them, and re-layouts: 8.01 us -> 11.8 us
    all_to_all x1, waiting for transfers between devices: 2.03 us -> 4.06 us  [shards(): pieces = lax.all_to_all(middle_sum(got, strips), 'height', 0, 0, tiled=True)]
    all_to_all x0 -> x1, waiting for transfers between devices: none -> 1.52 us  [shards(): got = lax.all_to_all(send, 'tm', 0, 0, tiled=True)]
  transfers between devices with their start and end apart: 7 -> 8, of which waited for: 3 -> 4; matrix products, arithmetic and copies ran while one was open for 5% -> 6% of each run, Pallas kernels for 24% -> 18%
where the time goes in v3:
time: 108 us; the launch traced here: 107 us
  starting transfers between devices  39.2 us (36%)
  Pallas kernels  34.6 us (32%)
  local copies, waits for them, and re-layouts  11.8 us (11%)
  waiting for transfers between devices  11.4 us (11%)
  blocking collectives  8.17 us (8%)
    all_to_all x1, starting transfers between devices, shards(): pieces = lax.all_to_all(middle_sum(got, strips), 'height', 0, 0, tiled=True)  19.9 us
    pallas_call x1, Pallas kernels, own_part(): pl.pallas_call(own_kernel, out_shape=[jax.ShapeDtypeStruct((channels // l...  12.2 us
    pallas_call x1, Pallas kernels, rest_part(): pl.pallas_call(rest_kernel, out_shape=[out] * 3, in_specs=[pl.BlockSpec(m...  11.9 us
    unnamed x22, local copies, waits for them, and re-layouts  11.8 us
    all_to_all x1, blocking collectives, shards(): shares = lax.all_to_all(centre.astype(bf16), 'tm', 0, 0, tiled=True)  8.17 us
    all_to_all x1, waiting for transfers between devices, shards(): latent = lax.all_to_all(latent_send, 'tm', 0, 0, tiled=True)  4.66 us
    all_to_all x1, starting transfers between devices, shards(): got = lax.all_to_all(send, 'tm', 0, 0, tiled=True)  4.33 us
    ppermute x1, starting transfers between devices, shards(): near_share = lax.ppermute(near_share, 'height', near)  4.27 us
  transfers between devices with their start and end apart: 8, of which 4 were waited for; matrix products, arithmetic and copies ran while one was open for 6% of the time, Pallas kernels for 18%

profile of v3, /device:TPU:1, one launch (start us, length us, event | category | flops | bytes accessed | tf_op | source)
XLA Modules:
  0.0 106.7 jit_solution(16609802572322106160)
XLA Ops:
  0.7 3.5 %collective-permute-start = (bf16[3,4,96,512]{3,2,1,0:T(8,128)(2,1)}, bf16[3,4,96,512]{3,2,1,0:T(8,128)(2,1)}, u32[]{:S(2)}, u32[]{:S(2)}) collective-permute-start(bf16[3,4,96,512]{3,2,1,0:T(8,128)(2,1)} %grad.3), channel_id=1, source_target_pairs={{32,0},{64,32},{96,64},{33,1},{65,33},{97,65},{34,2},{66,34},{98,6... | collective-permute-start | bytes 3538952 | tf_op jit(solution)/shard_map/ppermute | solution.py:496
  4.1 1.9 %copy.9.hidden = bf16[12,2,12,3072]{3,2,1,0:T(8,128)(2,1)S(1)} copy(bf16[12,2,12,3072]{3,1,2,0:T(2,128)(2,1)} %param.7) | data formatting | bytes 3538944 | tf_op args[0]
  6.1 3.8 %modulate.1 = (bf16[12,2,16,3072]{3,2,1,0:T(8,128)(2,1)S(1)}, bf16[4,5,16,128]{3,2,1,0:T(8,128)(2,1)}) custom-call(bf16[12,2,12,3072]{3,2,1,0:T(8,128)(2,1)S(1)} %copy.9.hidden, f32[1,3072]{1,0:T(1,128)S(1)} %bitcast.7, f32[1,3072]{1,0:T(1,128)S(1)} %bitcast.9, bf16[64,3072]{1,0:T(8,128)(2,1)S(1)} %bitcast.5), custom_call_target="tpu_custom_call" | custom-call | flops 150994944 | bytes 4718592 | tf_op jit(solution)/shard_map/modulate/pallas_call | solution.py:73
  9.9 1.4 %copy-done.1 = bf16[12,2,16,3072]{3,2,1,0:T(8,128)(2,1)} copy-done((bf16[12,2,16,3072]{3,2,1,0:T(8,128)(2,1)}, bf16[12,2,16,3072]{3,2,1,0:T(8,128)(2,1)S(1)}, u32[]{:S(2)}) %copy-start.1) | copy-done | bytes 2359320
  11.3 4.0 %all-to-all-start = ((bf16[4,5,16,128]{3,2,1,0:T(8,128)(2,1)}), bf16[4,5,16,128]{3,2,1,0:T(8,128)(2,1)S(1)}, u32[]{:S(2)}, u32[]{:S(2)}) async-start(bf16[4,5,16,128]{3,2,1,0:T(8,128)(2,1)} %get-tuple-element.16), calls=%async_computation | async-start | bytes 163840 | tf_op jit(solution)/shard_map/all_to_all | solution.py:498
  15.4 4.7 %all-to-all-done.latent = bf16[4,5,16,128]{3,2,1,0:T(8,128)(2,1)S(1)} async-done(((bf16[4,5,16,128]{3,2,1,0:T(8,128)(2,1)}), bf16[4,5,16,128]{3,2,1,0:T(8,128)(2,1)S(1)}, u32[]{:S(2)}, u32[]{:S(2)}) %all-to-all-start) | async-done | bytes 81952 | tf_op jit(solution)/shard_map/all_to_all | solution.py:498
  20.1 1.3 %copy-done.4 = bf16[3,4,96,512]{3,2,1,0:T(8,128)(2,1)S(1)} copy-done((bf16[3,4,96,512]{3,2,1,0:T(8,128)(2,1)S(1)}, bf16[3,4,96,512]{3,2,1,0:T(8,128)(2,1)}, u32[]{:S(2)}) %copy-start.4) | copy-done | bytes 1179672
  21.3 1.5 %pack_rows.1 = (bf16[560,512]{1,0:T(8,128)(2,1)S(1)}, bf16[560,512]{1,0:T(8,128)(2,1)S(1)}) custom-call(s32[2]{0:T(128)S(1)} %pad_add_fusion.places, bf16[3,4,96,512]{3,2,1,0:T(8,128)(2,1)S(1)} %copy-done.4, bf16[3,4,96,512]{3,2,1,0:T(8,128)(2,1)} %collective-permute-done.grad_ahead, bf16[4,5,16,128]{3,2,1,0:T(8,128)(2,1)S(1)} %all-to-all-done.latent), custom_call_target="tpu_custom_call" | custom-call | tf_op jit(solution)/shard_map/pack_rows/pallas_call | solution.py:132
  22.8 1.7 %collective-permute-start.1 = (bf16[560,512]{1,0:T(8,128)(2,1)S(1)}, bf16[560,512]{1,0:T(8,128)(2,1)S(1)}, u32[]{:S(2)}, u32[]{:S(2)}) collective-permute-start(bf16[560,512]{1,0:T(8,128)(2,1)S(1)} %get-tuple-element.17), channel_id=1, source_target_pairs={{0,1},{1,0},{2,3},{3,2},{4,5},{5,4},{6,7},{7,6},{8,9},{9,8},{10,11... | collective-permute-start | bytes 1720328 | tf_op jit(solution)/shard_map/ppermute | solution.py:501
  24.5 0.8 collective-permute-start.2
  25.4 12.2 %own_part.1 = (f32[4,3,4,96,128]{4,3,2,1,0:T(8,128)S(1)}, bf16[3,3,3,512,512]{4,3,2,1,0:T(8,128)(2,1)S(1)}) custom-call(bf16[3,4,96,512]{3,2,1,0:T(8,128)(2,1)S(1)} %copy-done.5, bf16[3,3,3,512,512]{4,3,2,1,0:T(8,128)(2,1)} %w_section.1), custom_call_target="tpu_custom_call" | custom-call | flops 9059696640 | bytes 14155776 | tf_op jit(solution)/shard_map/own_part/pallas_call | solution.py:172
  37.6 11.9 %rest_part.1 = (bf16[4,5,16,128]{3,2,1,0:T(8,128)(2,1)S(1)}, bf16[4,5,16,128]{3,2,1,0:T(8,128)(2,1)S(1)}, bf16[4,5,16,128]{3,2,1,0:T(8,128)(2,1)S(1)}) custom-call(s32[2]{0:T(128)S(1)} %pad_add_fusion.places, f32[4,3,4,96,128]{4,3,2,1,0:T(8,128)S(1)} %get-tuple-element.15.own, bf16[3,4,96,512]{3,2,1,0:T(8,128)(2,1)} %collective-permute-done.grad_ahead, ...), custom_call_target="tpu_custom_call" | custom-call | flops 9663676416 | bytes 14155776 | tf_op jit(solution)/shard_map/rest_part/pallas_call | solution.py:363
  49.5 4.3 %collective-permute-start.3 = (bf16[4,5,16,128]{3,2,1,0:T(8,128)(2,1)S(1)}, bf16[4,5,16,128]{3,2,1,0:T(8,128)(2,1)S(1)}, u32[]{:S(2)}, u32[]{:S(2)}) collective-permute-start(bf16[4,5,16,128]{3,2,1,0:T(8,128)(2,1)S(1)} %get-tuple-element.21), channel_id=1, source_target_pairs={{0,1},{1,0},{2,3},{3,2},{4,5},{5,4},{6,7},{7,6},{8,9},{9,8},{10,11... | collective-permute-start | bytes 245768 | tf_op jit(solution)/shard_map/ppermute | solution.py:508
  54.4 1.2 %collective-permute-done.3 = bf16[4,5,16,128]{3,2,1,0:T(8,128)(2,1)S(1)} collective-permute-done((bf16[4,5,16,128]{3,2,1,0:T(8,128)(2,1)S(1)}, bf16[4,5,16,128]{3,2,1,0:T(8,128)(2,1)S(1)}, u32[]{:S(2)}, u32[]{:S(2)}) %collective-permute-start.3) | collective-permute-done | bytes 81952 | tf_op jit(solution)/shard_map/ppermute | solution.py:508
  55.7 8.2 %all_to_all.20.shares = bf16[4,5,16,128]{3,2,1,0:T(8,128)(2,1)S(1)} all-to-all(bf16[4,5,16,128]{3,2,1,0:T(8,128)(2,1)S(1)} %add_convert_fusion), channel_id=1, replica_groups=mesh['tm'=4,'height'=32] {'tm'}, dimensions={0} | all-to-all | bytes 163840 | tf_op jit(solution)/shard_map/all_to_all | solution.py:510
  63.8 1.5 %weight_terms.1 = (bf16[12,2,16,64]{3,2,1,0:T(8,128)(2,1)S(1)}, bf16[4,384,128]{2,1,0:T(8,128)(2,1)}) custom-call(bf16[4,5,16,128]{3,2,1,0:T(8,128)(2,1)S(1)} %all_to_all.20.shares, bf16[12,2,16,3072]{3,2,1,0:T(8,128)(2,1)S(1)} %copy-done.2), custom_call_target="tpu_custom_call" | custom-call | tf_op jit(solution)/shard_map/weight_terms/pallas_call | solution.py:413
  65.3 4.3 %all-to-all-start.2 = ((bf16[4,384,128]{2,1,0:T(8,128)(2,1)}), bf16[4,384,128]{2,1,0:T(8,128)(2,1)S(1)}, u32[]{:S(2)}, u32[]{:S(2)}) async-start(bf16[4,384,128]{2,1,0:T(8,128)(2,1)} %get-tuple-element.24), calls=%async_computation.2 | async-start | bytes 786432 | tf_op jit(solution)/shard_map/all_to_all | solution.py:513
  69.7 3.6 %hidden_grad.1 = bf16[12,2,12,3072]{3,2,1,0:T(8,128)(2,1)S(1)} custom-call(bf16[12,2,12,3072]{3,2,1,0:T(8,128)(2,1)S(1)} %copy.9.hidden, bf16[12,2,16,64]{3,2,1,0:T(8,128)(2,1)S(1)} %get-tuple-element.25.token_grad, f32[1,3072]{1,0:T(1,128)S(1)} %bitcast.8, bf16[64,3072]{1,0:T(8,128)(2,1)S(1)} %bitcast.6), custom_call_target="tpu_custom_call" | custom-call | flops 150994944 | bytes 4718592 | tf_op jit(solution)/shard_map/hidden_grad/pallas_call | solution.py:471
  73.3 1.4 %copy-done = bf16[12,2,12,3072]{3,2,1,0:T(8,128)(2,1)} copy-done((bf16[12,2,12,3072]{3,2,1,0:T(8,128)(2,1)}, bf16[12,2,12,3072]{3,2,1,0:T(8,128)(2,1)S(1)}, u32[]{:S(2)}) %copy-start) | copy-done | bytes 1769496
  74.7 1.5 %all-to-all-done.2.got = bf16[4,384,128]{2,1,0:T(8,128)(2,1)S(1)} async-done(((bf16[4,384,128]{2,1,0:T(8,128)(2,1)}), bf16[4,384,128]{2,1,0:T(8,128)(2,1)S(1)}, u32[]{:S(2)}, u32[]{:S(2)}) %all-to-all-start.2) | async-done | bytes 393248 | tf_op jit(solution)/shard_map/all_to_all | solution.py:513
  76.4 0.8 reshape.13
  77.2 19.9 %all-to-all-start.3 = ((bf16[32,2,768]{2,1,0:T(2,128)(2,1)}), bf16[32,2,768]{2,1,0:T(2,128)(2,1)S(1)}, u32[]{:S(2)}, u32[]{:S(2)}) async-start(bf16[32,2,768]{2,1,0:T(2,128)(2,1)} %reshape.13), calls=%async_computation.3 | async-start | bytes 196608 | tf_op jit(solution)/shard_map/all_to_all | solution.py:516
  97.1 4.7 %copy.11 = bf16[12,2,12,3072]{3,1,2,0:T(2,128)(2,1)} copy(bf16[12,2,12,3072]{3,2,1,0:T(8,128)(2,1)} %copy-done) | data formatting | bytes 3538944
  101.8 4.1 %all-to-all-done.3 = bf16[32,2,768]{2,1,0:T(2,128)(2,1)S(1)} async-done(((bf16[32,2,768]{2,1,0:T(2,128)(2,1)}), bf16[32,2,768]{2,1,0:T(2,128)(2,1)S(1)}, u32[]{:S(2)}, u32[]{:S(2)}) %all-to-all-start.3) | async-done | bytes 98336 | tf_op jit(solution)/shard_map/all_to_all | solution.py:516
  (26 shorter events, 1.8 us)
Async XLA Ops:
  0.6 5.5 %copy-start.3 = (bf16[3072,64]{0,1:T(8,128)(2,1)S(1)}, bf16[3072,64]{0,1:T(8,128)(2,1)}, u32[]{:S(2)}) copy-start(bf16[3072,64]{0,1:T(8,128)(2,1)} %param.10) | copy-start | bytes 1179652
  0.6 5.5 %copy-start.7 = (f32[3072]{0:T(1024)S(1)}, f32[3072]{0:T(1024)}, u32[]{:S(2)}) copy-start(f32[3072]{0:T(1024)} %param.9) | copy-start | bytes 36868
  0.7 5.5 %copy-start.6 = (f32[3072]{0:T(1024)S(1)}, f32[3072]{0:T(1024)}, u32[]{:S(2)}) copy-start(f32[3072]{0:T(1024)} %param.8) | copy-start | bytes 36868
  0.7 19.4 %collective-permute-start = (bf16[3,4,96,512]{3,2,1,0:T(8,128)(2,1)}, bf16[3,4,96,512]{3,2,1,0:T(8,128)(2,1)}, u32[]{:S(2)}, u32[]{:S(2)}) collective-permute-start(bf16[3,4,96,512]{3,2,1,0:T(8,128)(2,1)} %grad.3), channel_id=1, source_target_pairs={{32,0},{64,32},{96,64},{33,1},{65,33},{97,65},{34,2},{66,34},{98,6... | collective-permute-start | bytes 3538952 | tf_op jit(solution)/shard_map/ppermute | solution.py:496
  9.9 1.4 %copy-start.1 = (bf16[12,2,16,3072]{3,2,1,0:T(8,128)(2,1)}, bf16[12,2,16,3072]{3,2,1,0:T(8,128)(2,1)S(1)}, u32[]{:S(2)}) copy-start(bf16[12,2,16,3072]{3,2,1,0:T(8,128)(2,1)S(1)} %get-tuple-element.23.modulated) | copy-start | bytes 7077892
  11.3 8.7 %all-to-all-start = ((bf16[4,5,16,128]{3,2,1,0:T(8,128)(2,1)}), bf16[4,5,16,128]{3,2,1,0:T(8,128)(2,1)S(1)}, u32[]{:S(2)}, u32[]{:S(2)}) async-start(bf16[4,5,16,128]{3,2,1,0:T(8,128)(2,1)} %get-tuple-element.16), calls=%async_computation | async-start | bytes 163840 | tf_op jit(solution)/shard_map/all_to_all | solution.py:498
  20.1 1.3 %copy-start.4 = (bf16[3,4,96,512]{3,2,1,0:T(8,128)(2,1)S(1)}, bf16[3,4,96,512]{3,2,1,0:T(8,128)(2,1)}, u32[]{:S(2)}) copy-start(bf16[3,4,96,512]{3,2,1,0:T(8,128)(2,1)} %grad.3) | copy-start | bytes 3538948
  21.3 4.0 %copy-start.5 = (bf16[3,4,96,512]{3,2,1,0:T(8,128)(2,1)S(1)}, bf16[3,4,96,512]{3,2,1,0:T(8,128)(2,1)}, u32[]{:S(2)}) copy-start(bf16[3,4,96,512]{3,2,1,0:T(8,128)(2,1)} %grad.3) | copy-start | bytes 3538948
  22.8 14.8 %collective-permute-start.1 = (bf16[560,512]{1,0:T(8,128)(2,1)S(1)}, bf16[560,512]{1,0:T(8,128)(2,1)S(1)}, u32[]{:S(2)}, u32[]{:S(2)}) collective-permute-start(bf16[560,512]{1,0:T(8,128)(2,1)S(1)} %get-tuple-element.17), channel_id=1, source_target_pairs={{0,1},{1,0},{2,3},{3,2},{4,5},{5,4},{6,7},{7,6},{8,9},{9,8},{10,11... | collective-permute-start | bytes 1720328 | tf_op jit(solution)/shard_map/ppermute | solution.py:501
  24.5 13.1 %copy-start.8 = (bf16[3,3,3,16,512]{4,3,2,1,0:T(8,128)(2,1)S(1)}, bf16[3,3,3,16,512]{4,3,2,1,0:T(8,128)(2,1)}, u32[]{:S(2)}) copy-start(bf16[3,3,3,16,512]{4,3,2,1,0:T(8,128)(2,1)} %w_in.1) | copy-start | bytes 1327108
  24.5 13.1 %collective-permute-start.2 = (bf16[560,512]{1,0:T(8,128)(2,1)S(1)}, bf16[560,512]{1,0:T(8,128)(2,1)S(1)}, u32[]{:S(2)}, u32[]{:S(2)}) collective-permute-start(bf16[560,512]{1,0:T(8,128)(2,1)S(1)} %get-tuple-element.18), channel_id=1, source_target_pairs={{1,2},{2,1},{3,4},{4,3},{5,6},{6,5},{7,8},{8,7},{9,10},{10,9},{11,... | collective-permute-start | bytes 1720328 | tf_op jit(solution)/shard_map/ppermute | solution.py:500
  37.6 26.2 %copy-start.2 = (bf16[12,2,16,3072]{3,2,1,0:T(8,128)(2,1)S(1)}, bf16[12,2,16,3072]{3,2,1,0:T(8,128)(2,1)}, u32[]{:S(2)}) copy-start(bf16[12,2,16,3072]{3,2,1,0:T(8,128)(2,1)} %copy-done.1) | copy-start | bytes 7077892
  49.5 6.1 %collective-permute-start.3 = (bf16[4,5,16,128]{3,2,1,0:T(8,128)(2,1)S(1)}, bf16[4,5,16,128]{3,2,1,0:T(8,128)(2,1)S(1)}, u32[]{:S(2)}, u32[]{:S(2)}) collective-permute-start(bf16[4,5,16,128]{3,2,1,0:T(8,128)(2,1)S(1)} %get-tuple-element.21), channel_id=1, source_target_pairs={{0,1},{1,0},{2,3},{3,2},{4,5},{5,4},{6,7},{7,6},{8,9},{9,8},{10,11... | collective-permute-start | bytes 245768 | tf_op jit(solution)/shard_map/ppermute | solution.py:508
  53.8 1.8 %collective-permute-start.4 = (bf16[4,5,16,128]{3,2,1,0:T(8,128)(2,1)S(1)}, bf16[4,5,16,128]{3,2,1,0:T(8,128)(2,1)S(1)}, u32[]{:S(2)}, u32[]{:S(2)}) collective-permute-start(bf16[4,5,16,128]{3,2,1,0:T(8,128)(2,1)S(1)} %get-tuple-element.22), channel_id=1, source_target_pairs={{1,2},{2,1},{3,4},{4,3},{5,6},{6,5},{7,8},{8,7},{9,10},{10,9},{11,... | collective-permute-start | bytes 245768 | tf_op jit(solution)/shard_map/ppermute | solution.py:507
  65.3 10.9 %all-to-all-start.2 = ((bf16[4,384,128]{2,1,0:T(8,128)(2,1)}), bf16[4,384,128]{2,1,0:T(8,128)(2,1)S(1)}, u32[]{:S(2)}, u32[]{:S(2)}) async-start(bf16[4,384,128]{2,1,0:T(8,128)(2,1)} %get-tuple-element.24), calls=%async_computation.2 | async-start | bytes 786432 | tf_op jit(solution)/shard_map/all_to_all | solution.py:513
  73.3 1.4 %copy-start = (bf16[12,2,12,3072]{3,2,1,0:T(8,128)(2,1)}, bf16[12,2,12,3072]{3,2,1,0:T(8,128)(2,1)S(1)}, u32[]{:S(2)}) copy-start(bf16[12,2,12,3072]{3,2,1,0:T(8,128)(2,1)S(1)} %hidden_grad.1) | copy-start | bytes 5308420
  77.2 28.7 %all-to-all-start.3 = ((bf16[32,2,768]{2,1,0:T(2,128)(2,1)}), bf16[32,2,768]{2,1,0:T(2,128)(2,1)S(1)}, u32[]{:S(2)}, u32[]{:S(2)}) async-start(bf16[32,2,768]{2,1,0:T(2,128)(2,1)} %reshape.13), calls=%async_computation.3 | async-start | bytes 196608 | tf_op jit(solution)/shard_map/all_to_all | solution.py:516

commit v4 on v3

v4 whole, which is shorter than its diff:
```python
import functools
import math

import jax
import jax.numpy as jnp
from jax import lax
from jax.experimental import pallas as pl
from jax.experimental.pallas import tpu as pltpu
from jax.sharding import PartitionSpec as P

epsilon = 1e-05
slots = 16
lanes = 128
f32 = jnp.float32
bf16 = jnp.bfloat16
whole = pl.BlockSpec(memory_space=pltpu.VMEM)
scalars = pl.BlockSpec(memory_space=pltpu.SMEM)
far_off = pl.BlockSpec(memory_space=pltpu.HBM)
early = 2


def params(mib):
    return pltpu.CompilerParams(vmem_limit_bytes=int(mib * 2**20))


def dot(lhs, rhs):
    return jnp.dot(lhs, rhs, preferred_element_type=f32)


def dot_turned(lhs, rhs):
    return lax.dot_general(lhs, rhs, (((1,), (1,)), ((), ())), preferred_element_type=f32)


def normalise(values):
    center = jnp.mean(values, axis=-1, keepdims=True)
    shifted = values - center
    spread = jnp.mean(shifted * shifted, axis=-1, keepdims=True)
    inverse = lax.rsqrt(spread + epsilon)
    return shifted * inverse, inverse


def fetch_kernel(grad, ahead, last, sems):
    copies = [
        pltpu.make_async_copy(grad.at[0:2], ahead, sems.at[0]),
        pltpu.make_async_copy(grad.at[2:3], last, sems.at[1]),
    ]
    for copy in copies:
        copy.start()
    for copy in copies:
        copy.wait()


def fetch(grad):
    return pl.pallas_call(
        fetch_kernel,
        out_shape=[
            jax.ShapeDtypeStruct((2,) + grad.shape[1:], bf16),
            jax.ShapeDtypeStruct((1,) + grad.shape[1:], bf16),
        ],
        in_specs=[far_off],
        out_specs=[whole] * 2,
        scratch_shapes=[pltpu.SemaphoreType.DMA((2,))],
        compiler_params=params(4),
        name="fetch",
    )(grad)


def modulate_kernel(
    hidden, scale, shift, w_out, w_section, modulated, latent, held, rows, sems, out_sems
):
    frames, token_rows, tokens, width = hidden.shape
    block = 3
    gain = 1.0 + scale[...]
    blank = jnp.zeros((slots - tokens, width), f32)
    copies = [
        pltpu.make_async_copy(w_section.at[kt, ky], held.at[n], sems.at[n])
        for n, (kt, ky) in enumerate(taps[:early])
    ]
    for copy in copies:
        copy.start()

    def out_copy(step):
        at = pl.ds(step * block, block)
        return pltpu.make_async_copy(rows.at[at], modulated.at[at], out_sems.at[step])

    def share(step, carry):
        for frame in range(block):
            for row in range(token_rows):
                normed, _ = normalise(hidden[step * block + frame, row].astype(f32))
                value = jnp.concatenate([normed * gain + shift[...], blank], axis=0)
                rows[step * block + frame, row] = value.astype(bf16)
        out_copy(step).start()
        value = rows[pl.ds(step * block, block)].reshape(-1, width)
        value = dot_turned(value, w_out[...]).astype(bf16)
        value = value.reshape(block, token_rows, slots, value.shape[-1])
        latent[pl.ds(step * block, block)] = jnp.concatenate([value[:, 0], value[:, 1]], axis=-1)
        return carry

    lax.fori_loop(0, frames // block, share, 0)
    for copy in copies:
        copy.wait()
    for step in range(frames // block):
        out_copy(step).wait()


def modulate(hidden, mod_scale, mod_shift, w_out, w_section):
    frames, token_rows, tokens, width = hidden.shape
    token_width = w_out.shape[0]
    out = jax.ShapeDtypeStruct((frames, token_rows, slots, width), bf16)
    return pl.pallas_call(
        modulate_kernel,
        out_shape=[
            out,
            jax.ShapeDtypeStruct((frames, slots, 2 * token_width), bf16),
            jax.ShapeDtypeStruct((early,) + w_section.shape[2:], bf16),
        ],
        in_specs=[whole] * 4 + [far_off],
        out_specs=[far_off, whole, whole],
        scratch_shapes=[
            pltpu.VMEM(out.shape, bf16),
            pltpu.SemaphoreType.DMA((early,)),
            pltpu.SemaphoreType.DMA((frames // 3,)),
        ],
        compiler_params=params(44),
        cost_estimate=pl.CostEstimate(
            flops=2 * frames * 2 * slots * width * token_width,
            bytes_accessed=8 * frames * slots * width,
            transcendentals=0,
        ),
        name="modulate",
    )(hidden, mod_scale.reshape(1, -1), mod_shift.reshape(1, -1), w_out, w_section)


def column_shifts(value):
    cols, channels = value.shape
    wide = value.astype(f32)
    place = lax.broadcasted_iota(jnp.int32, (cols, channels), 0)
    nxt = jnp.where(place == cols - 1, 0.0, pltpu.roll(wide, cols - 1, 0))
    prv = jnp.where(place == 0, 0.0, pltpu.roll(wide, 1, 0))
    return nxt.astype(bf16), prv.astype(bf16)


taps = [(2 - n // 3, (1, 0, 2)[n % 3]) for n in range(9)]


def flat(value):
    return value.reshape(-1, value.shape[-1])


def weight_matrix(held_first, held_rest, n):
    block = held_first[n] if n < early else held_rest[n - early]
    return jnp.concatenate([block[kx] for kx in range(3)], axis=-1)


def pack_kernel(places, ahead, last, grad_ahead, latent, near, far):
    cols, channels = ahead.shape[-2:]
    for side, out in ((0, near), (1, far)):
        row = places[side]
        pieces = [ahead[0, row], ahead[1, row], last[0, row]]
        pieces += [grad_ahead[0, row], grad_ahead[1, row]]
        for n, piece in enumerate(pieces):
            out[n * cols : (n + 1) * cols] = piece
        at = len(pieces) * cols
        tail = flat(latent[...])
        count = tail.shape[0] * lanes // channels
        for lane in range(channels // lanes):
            out[at : at + count, lane * lanes : (lane + 1) * lanes] = tail[
                lane * count : (lane + 1) * count
            ]


def pack_rows(places, ahead, last, grad_ahead, latent):
    cols, channels = ahead.shape[-2:]
    total = 5 * cols + latent.size // channels
    return pl.pallas_call(
        pack_kernel,
        in_specs=[scalars] + [whole] * 4,
        out_specs=[whole] * 2,
        out_shape=[jax.ShapeDtypeStruct((total, channels), bf16)] * 2,
        compiler_params=params(4),
        name="pack_rows",
    )(places, ahead, last, grad_ahead, latent)


def latent_kernel(places, near_rows, far_rows, latent, send):
    even = places[0] != 0
    frames, _, pair = latent.shape
    groups, depth = send.shape[:2]
    block = depth - 2
    channels = near_rows.shape[1]
    count = frames * slots * pair // channels
    start = near_rows.shape[0] - count
    send[0, 0:2] = jnp.zeros_like(send[0, 0:2])
    for frame in range(frames):
        row, lane = frame * slots % count, frame * slots // count * lanes
        ends = [
            ref[start + row : start + row + slots, lane : lane + lanes]
            for ref in (near_rows, far_rows)
        ]
        above = jnp.where(even, ends[1], ends[0])[:, pair // 2 :]
        below = jnp.where(even, ends[0], ends[1])[:, : pair // 2]
        value = jnp.concatenate([latent[frame], below, above], axis=-1)
        for dst in range(groups):
            at = frame + 2 - block * dst
            if 0 <= at < depth:
                send[dst, at] = value


def latent_shares(places, near_rows, far_rows, latent, groups):
    frames, _, pair = latent.shape
    return pl.pallas_call(
        latent_kernel,
        in_specs=[scalars] + [whole] * 3,
        out_specs=whole,
        out_shape=jax.ShapeDtypeStruct((groups, frames // groups + 2, slots, 2 * pair), bf16),
        compiler_params=params(4),
        name="latent_shares",
    )(places, near_rows, far_rows, latent)


def own_kernel(ahead, last, w_section, held_first, total, held_rest, shifts, sems):
    _, rows, cols, channels = ahead.shape
    frames = 3
    copies = [
        pltpu.make_async_copy(w_section.at[kt, ky], held_rest.at[n], sems.at[n])
        for n, (kt, ky) in enumerate(taps[early:])
    ]
    for copy in copies:
        copy.start()
    for frame in range(frames):
        for row in range(rows):
            value = ahead[frame, row] if frame < 2 else last[0, row]
            shifts[0, frame, row], shifts[1, frame, row] = column_shifts(value)
    for n, (kt, ky) in enumerate(taps):
        lo, hi = max(0, ky - 1), rows + min(0, ky - 1)
        at = slice(lo + 1 - ky, hi + 1 - ky)
        src = slice(2 - kt, frames), at
        centre = flat(last[:, at])
        if kt > 0:
            centre = jnp.concatenate([flat(ahead[2 - kt : 2, at]), centre], axis=0)
        window = jnp.concatenate(
            [flat(shifts[(0,) + src]), centre, flat(shifts[(1,) + src])], axis=-1
        )
        if n >= early:
            copies[n - early].wait()
        part = dot_turned(window, weight_matrix(held_first, held_rest, n))
        for lane in range(channels // lanes):
            value = part[:, lane * lanes : (lane + 1) * lanes]
            value = value.reshape(kt + 1, hi - lo, cols, lanes)
            if n == 0:
                total[lane] = value
            else:
                total[lane, 0 : kt + 1, lo:hi] += value


def own_part(ahead, last, w_section, held_first):
    _, rows, cols, channels = ahead.shape
    return pl.pallas_call(
        own_kernel,
        out_shape=[
            jax.ShapeDtypeStruct((channels // lanes, 3, rows, cols, lanes), f32),
            jax.ShapeDtypeStruct((9 - early,) + w_section.shape[2:], bf16),
        ],
        in_specs=[whole, whole, far_off, whole],
        out_specs=[whole] * 2,
        scratch_shapes=[
            pltpu.VMEM((2, 3, rows, cols, channels), bf16),
            pltpu.SemaphoreType.DMA((9 - early,)),
        ],
        compiler_params=params(30),
        cost_estimate=pl.CostEstimate(
            flops=2 * 45 * rows * cols * channels * channels,
            bytes_accessed=2 * w_section.size,
            transcendentals=0,
        ),
        name="own_part",
    )(ahead, last, w_section, held_first)


def edge_kernel(
    places, own, grad_ahead, near_rows, far_rows, held_first, held_rest, w_in,
    total, far, patches, near,
):
    even = places[0] != 0
    blocks, frames, rows, cols, _ = own.shape
    for lane in range(blocks):
        total[lane, :, 0] = own[lane, :, 0]
        total[lane, :, 1] = own[lane, :, rows - 1]
    for frame in range(frames + 2):
        at = slice(frame * cols, (frame + 1) * cols)
        ends = near_rows[at], far_rows[at]
        for side in range(2):
            value = jnp.where(even == (side == 1), ends[0], ends[1])
            shifted = column_shifts(value)
            if frame < frames:
                near[1, side, frame] = value
                near[0, side, frame], near[2, side, frame] = shifted
            else:
                row = side * (rows + 1)
                far[1, frame - frames, row] = value
                far[0, frame - frames, row], far[2, frame - frames, row] = shifted
    for frame in range(2):
        for row in range(rows):
            value = grad_ahead[frame, row]
            far[1, frame, row + 1] = value
            far[0, frame, row + 1], far[2, frame, row + 1] = column_shifts(value)

    patches[...] = jnp.zeros_like(patches)
    lat = w_in.shape[3]
    for n in range(4 * 3 * 2 * 2 * 2 * 2):
        p, q, kt, a, b, pp, qq = [
            n // size % top
            for size, top in ((96, 2), (48, 2), (16, 3), (8, 2), (4, 2), (2, 2), (1, 2))
        ]
        ky, kx = p - 1 + 2 * a + pp, q - 1 + 2 * b + qq
        if 0 <= ky < 3 and 0 <= kx < 3:
            at = (((kt * 2 + a) * 2 + b) * 4 + 2 * pp + qq) * lat
            patches[2 * p + q, at : at + lat] = w_in[kt, ky, kx]

    for n, (kt, ky) in enumerate(taps):
        pieces, places_of = [], []
        if kt < 2:
            for side, row in ((0, 0), (1, rows - 1)):
                pieces.append([far[kx, 0 : 2 - kt, row + 2 - ky] for kx in range(3)])
                places_of.append((slice(kt + 1, frames), side))
        if ky != 1:
            side = 0 if ky == 2 else 1
            pieces.append([near[kx, side, 2 - kt : frames] for kx in range(3)])
            places_of.append((slice(0, kt + 1), side))
        if not pieces:
            continue
        window = jnp.concatenate(
            [jnp.concatenate([flat(v) for v in piece], axis=-1) for piece in pieces], axis=0
        )
        part = dot_turned(window, weight_matrix(held_first, held_rest, n))
        at = 0
        for place, side in places_of:
            count = (place.stop - place.start) * cols
            for lane in range(blocks):
                value = part[at : at + count, lane * lanes : (lane + 1) * lanes]
                total[lane, place, side] += value.reshape(-1, cols, lanes)
            at += count


def edge_part(places, own, grad_ahead, near_rows, far_rows, held_first, held_rest, w_in):
    blocks, frames, rows, cols, _ = own.shape
    channels = blocks * lanes
    pair = 8 * w_in.shape[3]
    return pl.pallas_call(
        edge_kernel,
        out_shape=[
            jax.ShapeDtypeStruct((blocks, frames, 2, cols, lanes), f32),
            jax.ShapeDtypeStruct((3, 2, rows + 2, cols, channels), bf16),
            jax.ShapeDtypeStruct((4, 6 * pair, channels), bf16),
        ],
        in_specs=[scalars] + [whole] * 7,
        out_specs=[whole] * 3,
        scratch_shapes=[pltpu.VMEM((3, 2, frames, cols, channels), bf16)],
        compiler_params=params(12),
        cost_estimate=pl.CostEstimate(
            flops=2 * 5 * own.size * channels, bytes_accessed=0, transcendentals=0
        ),
        name="edge_part",
    )(places, own, grad_ahead, near_rows, far_rows, held_first, held_rest, w_in)


def latent_phase(total, slot_of, row_of, spread_row, windows, patches, spread):
    blocks, frames, _, cols, _ = total.shape
    half = cols // 2
    pair = windows.shape[-1]
    for p in range(2):
        for q in range(2):
            top = row_of[p] + p
            window = jnp.concatenate(
                [
                    flat(windows[q, kt : kt + frames, top + a])
                    for kt in range(3)
                    for a in range(2)
                ],
                axis=-1,
            )
            weight = patches[2 * p + q]
            pre = dot(window, weight)
            back = jnp.concatenate(
                [
                    jnp.concatenate(
                        [
                            total[lane, frame, slot_of[p], pl.ds(q, half, stride=2), :]
                            for lane in range(blocks)
                        ],
                        axis=-1,
                    )
                    for frame in range(frames)
                ],
                axis=0,
            )
            gate = jax.nn.sigmoid(pre)
            act_grad = (back * (gate * (1.0 + pre * (1.0 - gate)))).astype(bf16)
            terms = dot_turned(act_grad, weight)
            for kt in range(3):
                for a in range(2):
                    at = (kt * 2 + a) * pair
                    spread[kt : kt + frames, top + a - spread_row, q : q + half] += terms[
                        :, at : at + pair
                    ].reshape(frames, half, pair)


def shares_of(spread, row, half):
    width = spread.shape[-1] // 2
    return spread[:, row, 1 : half + 1, :width] + spread[:, row, 0:half, width:]


def edge_latent_kernel(
    places, total, latent, patches, near_out, far_out, windows, spread, tokens
):
    even = places[0] != 0
    groups, depth = latent.shape[:2]
    width = latent.shape[-1] // 4
    half = windows.shape[3]
    block = half // groups
    tokens[...] = jnp.zeros_like(tokens)
    for src in range(groups):
        at = slice(8 + src * block, 8 + (src + 1) * block)
        for frame in range(depth):
            value = latent[src, frame].astype(f32)[:block]
            for n, row in enumerate((1, 2, 3, 0)):
                tokens[frame, row, at] = value[:, n * width : (n + 1) * width]
    for q in range(2):
        left = tokens[:, :, 7 + q : 7 + q + half]
        right = tokens[:, :, 8 + q : 8 + q + half]
        windows[q] = jnp.concatenate([left, right], axis=-1).astype(bf16)
    spread[...] = jnp.zeros_like(spread)
    latent_phase(total, (0, 1), (0, 1), 0, windows, patches, spread)
    for n, row in enumerate((0, 3)):
        tokens[:, n, 0:half] = shares_of(spread, row, half)
    none = jnp.zeros((block, width), f32)
    fill = jnp.zeros((slots - block, 2 * width), f32)
    for dst in range(groups):
        at = slice(dst * block, (dst + 1) * block)
        for frame in range(depth):
            up = jnp.concatenate([none, tokens[frame, 0, at]], axis=-1)
            down = jnp.concatenate([tokens[frame, 1, at], none], axis=-1)
            padded = lambda v: jnp.concatenate([v, fill], axis=0).astype(bf16)
            near_out[dst, frame] = padded(jnp.where(even, down, up))
            far_out[dst, frame] = padded(jnp.where(even, up, down))


def edge_latent(places, total, latent, patches):
    groups, depth, _, quad = latent.shape
    cols = total.shape[3]
    out = jax.ShapeDtypeStruct((groups, depth, slots, quad // 2), bf16)
    return pl.pallas_call(
        edge_latent_kernel,
        out_shape=[
            out,
            out,
            jax.ShapeDtypeStruct((2, depth, 4, cols // 2, quad // 2), bf16),
            jax.ShapeDtypeStruct((depth, 4, cols // 2 + 8, quad // 2), f32),
        ],
        in_specs=[scalars] + [whole] * 3,
        out_specs=[whole] * 4,
        scratch_shapes=[pltpu.VMEM((depth, 4, 72, quad // 4), f32)],
        compiler_params=params(10),
        name="edge_latent",
    )(places, total, latent, patches)


def inner_kernel(
    own, far, held_first, held_rest, windows, patches, spread_in, out, total, spread, tokens
):
    blocks, frames, rows, cols, _ = own.shape
    half = windows.shape[3]
    groups, depth = out.shape[:2]
    block = half // groups
    total[...] = own[:, :, 1 : rows - 1]
    spread[...] = spread_in[:, 1:3]
    for n, (kt, ky) in enumerate(taps):
        if kt == 2:
            continue
        src = slice(0, 2 - kt), slice(3 - ky, rows + 1 - ky)
        window = jnp.concatenate([flat(far[(kx,) + src]) for kx in range(3)], axis=-1)
        part = dot_turned(window, weight_matrix(held_first, held_rest, n))
        for lane in range(blocks):
            value = part[:, lane * lanes : (lane + 1) * lanes]
            total[lane, kt + 1 : frames] += value.reshape(2 - kt, rows - 2, cols, lanes)
    latent_phase(total, (1, 0), (1, 0), 1, windows, patches, spread)
    for row in range(2):
        tokens[:, row] = shares_of(spread, row, half)
    fill = jnp.zeros((slots - block, out.shape[-1]), f32)
    for dst in range(groups):
        at = slice(dst * block, (dst + 1) * block)
        for frame in range(depth):
            value = jnp.concatenate([tokens[frame, 0, at], tokens[frame, 1, at]], axis=-1)
            out[dst, frame] = jnp.concatenate([value, fill], axis=0)


def inner_part(own, far, held_first, held_rest, windows, patches, spread, groups):
    blocks, frames, rows, cols, _ = own.shape
    channels = blocks * lanes
    depth, _, wide, pair = spread.shape
    return pl.pallas_call(
        inner_kernel,
        out_shape=jax.ShapeDtypeStruct((groups, depth, slots, pair), f32),
        in_specs=[whole] * 7,
        out_specs=whole,
        scratch_shapes=[
            pltpu.VMEM((blocks, frames, rows - 2, cols, lanes), f32),
            pltpu.VMEM((depth, 2, wide, pair), f32),
            pltpu.VMEM((depth, 2, cols // 2, pair // 2), f32),
        ],
        compiler_params=params(12),
        cost_estimate=pl.CostEstimate(
            flops=2 * 4 * own.size * channels, bytes_accessed=0, transcendentals=own.size
        ),
        name="inner_part",
    )(own, far, held_first, held_rest, windows, patches, spread)


def weight_kernel(shares, modulated, token_grad, send, field):
    groups, depth, _, pair = shares.shape
    width = pair // 2
    frames, token_rows = modulated.shape[:2]
    model = modulated.shape[-1]
    field[...] = jnp.zeros_like(field)
    for src in range(groups):
        at = src * (frames // groups)
        field[at : at + depth] += shares[src].astype(f32)
    values = field[2 : 2 + frames]
    token_grad[:, 0] = values[:, :, :width].astype(bf16)
    token_grad[:, 1] = values[:, :, width:].astype(bf16)
    turned = jnp.transpose(token_grad[...].reshape(-1, width).astype(f32)).astype(bf16)
    weight = dot(turned, modulated[...].reshape(-1, model))
    half = model // (2 * groups)
    for dst in range(groups):
        at = 2 * half * dst
        stacked = jnp.concatenate(
            [weight[:, at : at + half], weight[:, at + half : at + 2 * half]], axis=0
        )
        send[dst] = jnp.transpose(stacked).astype(bf16)


def weight_terms(shares, modulated):
    groups, depth, _, pair = shares.shape
    frames, token_rows, _, model = modulated.shape
    return pl.pallas_call(
        weight_kernel,
        out_shape=[
            jax.ShapeDtypeStruct((frames, token_rows, slots, pair // 2), bf16),
            jax.ShapeDtypeStruct((groups, model // (2 * groups), pair), bf16),
        ],
        in_specs=[whole] * 2,
        out_specs=[whole] * 2,
        scratch_shapes=[pltpu.VMEM((frames + 2, slots, pair), f32)],
        compiler_params=params(12),
        name="weight_terms",
    )(shares, modulated)


def middle_kernel(got, send):
    total = jnp.sum(got[...].astype(f32), axis=0)
    count, rows, width = send.shape
    total = total.reshape(count // 2, rows, 2 * width).astype(bf16)
    send[0 : count // 2] = total[:, :, :width]
    send[count // 2 :] = total[:, :, width:]


def middle_sum(got, count):
    groups, depth, pair = got.shape
    return pl.pallas_call(
        middle_kernel,
        out_shape=jax.ShapeDtypeStruct((count, 2 * depth // count, pair // 2), bf16),
        in_specs=[whole],
        out_specs=whole,
        compiler_params=params(4),
        name="middle_sum",
    )(got)


def hidden_kernel(hidden, token_grad, scale, w_out, grad_hidden):
    frames, token_rows, tokens, width = hidden.shape
    gain = 1.0 + scale[...]
    block = 3

    def share(step, carry):
        rows = token_grad[pl.ds(step * block, block)].reshape(-1, token_grad.shape[-1])
        mod_grad = dot(rows, w_out[...])
        for frame in range(block):
            for row in range(token_rows):
                at = (frame * token_rows + row) * slots
                scaled = mod_grad[at : at + tokens] * gain
                normed, inverse = normalise(hidden[step * block + frame, row].astype(f32))
                first = jnp.mean(scaled, axis=-1, keepdims=True)
                second = jnp.mean(scaled * normed, axis=-1, keepdims=True)
                value = (scaled - first - normed * second) * inverse
                grad_hidden[step * block + frame, row] = value.astype(bf16)
        return carry

    lax.fori_loop(0, frames // block, share, 0)


def hidden_grad(hidden, token_grad, mod_scale, w_out):
    frames, token_rows, tokens, width = hidden.shape
    return pl.pallas_call(
        hidden_kernel,
        out_shape=jax.ShapeDtypeStruct(hidden.shape, bf16),
        in_specs=[whole] * 4,
        out_specs=whole,
        compiler_params=params(8),
        cost_estimate=pl.CostEstimate(
            flops=2 * frames * 2 * slots * width * w_out.shape[0],
            bytes_accessed=8 * frames * slots * width,
            transcendentals=0,
        ),
        name="hidden_grad",
    )(hidden, token_grad, mod_scale.reshape(1, -1), w_out)


def shards(hidden, mod_scale, mod_shift, w_out, w_in, w_section, section_grad):
    groups, strips = lax.axis_size("tm"), lax.axis_size("height")
    rows = section_grad.shape[1]
    swap = lambda a, b: [(a, b), (b, a)]
    near = sum([swap(i, i + 1) for i in range(0, strips - 1, 2)], [])
    far = sum([swap(i, i + 1) for i in range(1, strips - 1, 2)], [])
    odd = lax.rem(lax.axis_index("height"), 2)
    places = jnp.stack([(1 - odd) * (rows - 1), odd * (rows - 1)]).astype(jnp.int32)
    w_out = jnp.transpose(w_out)

    ahead, last = fetch(section_grad)
    grad_ahead = lax.ppermute(ahead, "tm", [(g + 1, g) for g in range(groups - 1)])
    modulated, latent, held_first = modulate(hidden, mod_scale, mod_shift, w_out, w_section)
    near_send, far_send = pack_rows(places, ahead, last, grad_ahead, latent)
    far_rows = lax.ppermute(far_send, "height", far)
    near_rows = lax.ppermute(near_send, "height", near)
    own, held_rest = own_part(ahead, last, w_section, held_first)
    latent_send = latent_shares(places, near_rows, far_rows, latent, groups)
    latent_got = lax.all_to_all(latent_send, "tm", 0, 0, tiled=True)
    edge, far_grad, patches = edge_part(
        places, own, grad_ahead, near_rows, far_rows, held_first, held_rest, w_in
    )
    near_share, far_share, windows, spread = edge_latent(places, edge, latent_got, patches)
    far_share = lax.ppermute(far_share, "height", far)
    near_share = lax.ppermute(near_share, "height", near)
    centre = inner_part(own, far_grad, held_first, held_rest, windows, patches, spread, groups)
    centre = centre + near_share.astype(f32) + far_share.astype(f32)
    shares = lax.all_to_all(centre.astype(bf16), "tm", 0, 0, tiled=True)

    token_grad, send = weight_terms(shares, modulated)
    got = lax.all_to_all(send, "tm", 0, 0, tiled=True)
    grad_hidden = hidden_grad(hidden, token_grad, mod_scale, w_out)
    pieces = lax.all_to_all(middle_sum(got, strips), "height", 0, 0, tiled=True)
    total_tokens = math.prod(hidden.shape[:3]) * groups * strips
    grad_out_weight = jnp.sum(pieces.astype(f32), axis=0) / math.sqrt(total_tokens)
    return (grad_hidden, grad_out_weight)


def solution(mesh):
    placed = (P(None, "height", "tm", None), P(), P(), P(), P(), P(), P("tm", "height", None, None))
    return jax.shard_map(
        shards,
        mesh=mesh,
        in_specs=placed,
        out_specs=(P(None, "height", "tm", None), P(("tm", "height"), None)),
        check_vma=False,
    )
```

time: 108 us -> 136 us (1.26)
  local copies, waits for them, and re-layouts: 11.8 us -> 46.2 us
  starting transfers between devices: 39.2 us -> 28.4 us
  blocking collectives: 8.17 us -> 15.2 us
  waiting for transfers between devices: 11.4 us -> 4.58 us
  Pallas kernels: 34.6 us -> 37.9 us
    unnamed x22 -> x64, local copies, waits for them, and re-layouts: 11.8 us -> 46.2 us
    all_to_all x0 -> x1, blocking collectives: none -> 9.7 us  [shards(): got = lax.all_to_all(send, 'tm', 0, 0, tiled=True)]
    all_to_all x1, starting transfers between devices: 19.9 us -> 12.2 us  [shards(): pieces = lax.all_to_all(middle_sum(got, strips), 'height', 0, 0, tiled=True)]
    all_to_all x2 -> x1, waiting for transfers between devices: 6.18 us -> 0.01 us  [shards(): latent_got = lax.all_to_all(latent_send, 'tm', 0, 0, tiled=True)]
    pallas_call x3 -> x7, Pallas kernels: 17.1 us -> 21.7 us  [the longest x1 5.69 us: edge_part(): pl.pallas_call(edge_kernel, out_shape=[jax.ShapeDtypeStruct((blocks, fram...]
    all_to_all x2 -> x1, starting transfers between devices: 8.32 us -> 4.15 us  [shards(): latent_got = lax.all_to_all(latent_send, 'tm', 0, 0, tiled=True)]
    ppermute x1, waiting for transfers between devices: 0.01 us -> 2.67 us  [shards(): lax.ppermute(ahead, 'tm', [(g + 1, g) for g in range(groups - 1)])]
    all_to_all x1, blocking collectives: 8.17 us -> 5.53 us  [shards(): shares = lax.all_to_all(centre.astype(bf16), 'tm', 0, 0, tiled=True)]
  transfers between devices with their start and end apart: 8 -> 7, of which waited for: 4 -> 2; matrix products, arithmetic and copies ran while one was open for 6% -> 4% of each run, Pallas kernels for 18% -> 23%
where the time goes in v4:
time: 136 us; the launch traced here: 134 us
  local copies, waits for them, and re-layouts  46.2 us (34%)
  Pallas kernels  37.9 us (28%)
  starting transfers between devices  28.4 us (21%)
  blocking collectives  15.2 us (11%)
  waiting for transfers between devices  4.58 us (3%)
    unnamed x64, local copies, waits for them, and re-layouts  46.2 us
    all_to_all x1, starting transfers between devices, shards(): pieces = lax.all_to_all(middle_sum(got, strips), 'height', 0, 0, tiled=True)  12.2 us
    pallas_call x1, Pallas kernels, own_part(): pl.pallas_call(own_kernel, out_shape=[jax.ShapeDtypeStruct((channels // l...  11.8 us
    all_to_all x1, blocking collectives, shards(): got = lax.all_to_all(send, 'tm', 0, 0, tiled=True)  9.7 us
    pallas_call x1, Pallas kernels, edge_part(): pl.pallas_call(edge_kernel, out_shape=[jax.ShapeDtypeStruct((blocks, fram...  5.69 us
    pallas_call x1, Pallas kernels, inner_part(): pl.pallas_call(inner_kernel, out_shape=jax.ShapeDtypeStruct((groups, dept...  5.59 us
    all_to_all x1, blocking collectives, shards(): shares = lax.all_to_all(centre.astype(bf16), 'tm', 0, 0, tiled=True)  5.53 us
    ppermute x1, starting transfers between devices, shards(): near_share = lax.ppermute(near_share, 'height', near)  5.53 us
  transfers between devices with their start and end apart: 7, of which 2 were waited for; matrix products, arithmetic and copies ran while one was open for 4% of the time, Pallas kernels for 23%

profile of v4, /device:TPU:1, one launch (start us, length us, event | category | flops | bytes accessed | tf_op | source)
XLA Modules:
  0.0 134.1 jit_solution(15257731039240722396)
XLA Ops:
  3.8 3.4 %collective-permute-start = (bf16[2,4,96,512]{3,2,1,0:T(8,128)(2,1)}, bf16[2,4,96,512]{3,2,1,0:T(8,128)(2,1)S(1)}, u32[]{:S(2)}, u32[]{:S(2)}) collective-permute-start(bf16[2,4,96,512]{3,2,1,0:T(8,128)(2,1)} %get-tuple-element.20.ahead), channel_id=1, source_target_pairs={{32,0},{64,32},{96,64},{33,1},{65,33},{97,65},{34,2},{66,34},{98,6... | collective-permute-start | bytes 2359304 | tf_op jit(solution)/shard_map/ppermute | solution.py:629
  7.3 2.0 %copy.10.hidden = bf16[12,2,12,3072]{3,2,1,0:T(8,128)(2,1)S(1)} copy(bf16[12,2,12,3072]{3,1,2,0:T(2,128)(2,1)} %param.7) | data formatting | bytes 3538944 | tf_op args[0]
  10.0 4.1 %modulate.1 = (bf16[12,2,16,3072]{3,2,1,0:T(8,128)(2,1)S(1)}, bf16[12,16,128]{2,1,0:T(8,128)(2,1)S(1)}, bf16[2,3,512,512]{3,2,1,0:T(8,128)(2,1)S(1)}) custom-call(bf16[12,2,12,3072]{3,2,1,0:T(8,128)(2,1)S(1)} %copy.10.hidden, f32[1,3072]{1,0:T(1,128)S(1)} %bitcast.7, f32[1,3072]{1,0:T(1,128)S(1)} %bitcast.9, bf16[64,3072]{1,0:T(8,128)(2,1)S(1)} %bitcast.5, ...), custom_call_target="tpu_custom_call" | custom-call | flops 150994944 | bytes 4718592 | tf_op jit(solution)/shard_map/modulate/pallas_call | solution.py:110
  15.6 2.7 %collective-permute-done.grad_ahead = bf16[2,4,96,512]{3,2,1,0:T(8,128)(2,1)S(1)} collective-permute-done((bf16[2,4,96,512]{3,2,1,0:T(8,128)(2,1)}, bf16[2,4,96,512]{3,2,1,0:T(8,128)(2,1)S(1)}, u32[]{:S(2)}, u32[]{:S(2)}) %collective-permute-start) | collective-permute-done | bytes 786464 | tf_op jit(solution)/shard_map/ppermute | solution.py:629
  21.9 11.8 %own_part.1 = (f32[4,3,4,96,128]{4,3,2,1,0:T(8,128)S(1)}, bf16[7,3,512,512]{3,2,1,0:T(8,128)(2,1)S(1)}) custom-call(bf16[2,4,96,512]{3,2,1,0:T(8,128)(2,1)} %get-tuple-element.20.ahead, bf16[1,4,96,512]{3,2,1,0:T(8,128)(2,1)S(1)} %copy-done.27, bf16[3,3,3,512,512]{4,3,2,1,0:T(8,128)(2,1)} %w_section.3, bf16[2,3,512,512]{3,2,1,0:T(8,128)(2,1)S(1)} %get-tuple-element.22.held_first), custom_call_target="tpu_custom_call" | custom-call | flops 9059696640 | bytes 14155776 | tf_op jit(solution)/shard_map/own_part/pallas_call | solution.py:258
  33.8 4.2 %copy-done = bf16[7,3,512,512]{3,2,1,0:T(8,128)(2,1)} copy-done((bf16[7,3,512,512]{3,2,1,0:T(8,128)(2,1)}, bf16[7,3,512,512]{3,2,1,0:T(8,128)(2,1)S(1)}, u32[]{:S(2)}) %copy-start) | copy-done | bytes 11010072
  42.2 4.1 %all-to-all-start = ((bf16[4,5,16,256]{3,2,1,0:T(8,128)(2,1)}), bf16[4,5,16,256]{3,2,1,0:T(8,128)(2,1)}, u32[]{:S(2)}, u32[]{:S(2)}) async-start(bf16[4,5,16,256]{3,2,1,0:T(8,128)(2,1)} %copy-done.24), calls=%async_computation | async-start | bytes 327680 | tf_op jit(solution)/shard_map/all_to_all | solution.py:636
  46.4 4.1 %copy-done.1 = bf16[7,3,512,512]{3,2,1,0:T(8,128)(2,1)S(1)} copy-done((bf16[7,3,512,512]{3,2,1,0:T(8,128)(2,1)S(1)}, bf16[7,3,512,512]{3,2,1,0:T(8,128)(2,1)}, u32[]{:S(2)}) %copy-start.1) | copy-done | bytes 11010072
  50.5 1.9 %copy-done.4 = bf16[2,3,512,512]{3,2,1,0:T(8,128)(2,1)S(1)} copy-done((bf16[2,3,512,512]{3,2,1,0:T(8,128)(2,1)S(1)}, bf16[2,3,512,512]{3,2,1,0:T(8,128)(2,1)}, u32[]{:S(2)}) %copy-start.4) | copy-done | bytes 3145752
  57.2 5.7 %edge_part.1 = (f32[4,3,2,96,128]{4,3,2,1,0:T(8,128)S(1)}, bf16[3,2,6,96,512]{4,3,2,1,0:T(8,128)(2,1)S(1)}, bf16[4,768,512]{2,1,0:T(8,128)(2,1)S(1)}) custom-call(s32[2]{0:T(128)S(1)} %pad_add_fusion.places, f32[4,3,4,96,128]{4,3,2,1,0:T(8,128)S(1)} %copy-done.10, bf16[2,4,96,512]{3,2,1,0:T(8,128)(2,1)S(1)} %collective-permute-done.grad_ahead, ...), custom_call_target="tpu_custom_call" | custom-call | flops 3019898880 | tf_op jit(solution)/shard_map/edge_part/pallas_call | solution.py:349
  64.5 1.8 %copy-done.12 = bf16[3,2,6,96,512]{4,3,2,1,0:T(8,128)(2,1)} copy-done((bf16[3,2,6,96,512]{4,3,2,1,0:T(8,128)(2,1)}, bf16[3,2,6,96,512]{4,3,2,1,0:T(8,128)(2,1)S(1)}, u32[]{:S(2)}) %copy-start.12) | copy-done | bytes 3538968
  67.3 2.0 %copy-done.7 = bf16[4,768,512]{2,1,0:T(8,128)(2,1)S(1)} copy-done((bf16[4,768,512]{2,1,0:T(8,128)(2,1)S(1)}, bf16[4,768,512]{2,1,0:T(8,128)(2,1)}, u32[]{:S(2)}) %copy-start.7) | copy-done | bytes 3145752
  70.7 3.3 %edge_latent.1 = (bf16[4,5,16,128]{3,2,1,0:T(8,128)(2,1)S(1)}, bf16[4,5,16,128]{3,2,1,0:T(8,128)(2,1)S(1)}, bf16[2,5,4,48,128]{4,3,2,1,0:T(8,128)(2,1)S(1)}, f32[5,4,56,128]{3,2,1,0:T(8,128)S(1)}) custom-call(s32[2]{0:T(128)S(1)} %pad_add_fusion.places, f32[4,3,2,96,128]{4,3,2,1,0:T(8,128)S(1)} %copy-done.22, bf16[4,5,16,256]{3,2,1,0:T(8,128)(2,1)} %all-to-all-done.latent, ...), custom_call_target="tpu_custom_call" | custom-call | tf_op jit(solution)/shard_map/edge_latent/pallas_call | solution.py:452
  74.7 5.5 %collective-permute-start.3 = (bf16[4,5,16,128]{3,2,1,0:T(8,128)(2,1)S(1)}, bf16[4,5,16,128]{3,2,1,0:T(8,128)(2,1)S(1)}, u32[]{:S(2)}, u32[]{:S(2)}) collective-permute-start(bf16[4,5,16,128]{3,2,1,0:T(8,128)(2,1)S(1)} %get-tuple-element.33), channel_id=1, source_target_pairs={{0,1},{1,0},{2,3},{3,2},{4,5},{5,4},{6,7},{7,6},{8,9},{9,8},{10,11... | collective-permute-start | bytes 245768 | tf_op jit(solution)/shard_map/ppermute | solution.py:642
  80.2 4.1 %copy-done.2 = bf16[7,3,512,512]{3,2,1,0:T(8,128)(2,1)S(1)} copy-done((bf16[7,3,512,512]{3,2,1,0:T(8,128)(2,1)S(1)}, bf16[7,3,512,512]{3,2,1,0:T(8,128)(2,1)}, u32[]{:S(2)}) %copy-start.2) | copy-done | bytes 11010072
  84.3 1.9 %copy-done.8 = bf16[4,768,512]{2,1,0:T(8,128)(2,1)S(1)} copy-done((bf16[4,768,512]{2,1,0:T(8,128)(2,1)S(1)}, bf16[4,768,512]{2,1,0:T(8,128)(2,1)}, u32[]{:S(2)}) %copy-start.8) | copy-done | bytes 3145752
  87.9 2.0 %copy-done.13 = bf16[3,2,6,96,512]{4,3,2,1,0:T(8,128)(2,1)S(1)} copy-done((bf16[3,2,6,96,512]{4,3,2,1,0:T(8,128)(2,1)S(1)}, bf16[3,2,6,96,512]{4,3,2,1,0:T(8,128)(2,1)}, u32[]{:S(2)}) %copy-start.13) | copy-done | bytes 3538968
  89.9 5.6 %inner_part.1 = f32[4,5,16,128]{3,2,1,0:T(8,128)S(1)} custom-call(f32[4,3,4,96,128]{4,3,2,1,0:T(8,128)S(1)} %copy-done.11, bf16[3,2,6,96,512]{4,3,2,1,0:T(8,128)(2,1)S(1)} %copy-done.13, bf16[2,3,512,512]{3,2,1,0:T(8,128)(2,1)S(1)} %copy-done.5, bf16[7,3,512,512]{3,2,1,0:T(8,128)(2,1)S(1)} %copy-done.2, ...), custom_call_target="tpu_custom_call" | custom-call | flops 2415919104 | tf_op jit(solution)/shard_map/inner_part/pallas_call | solution.py:501
  95.5 5.5 %all_to_all.20.shares = bf16[4,5,16,128]{3,2,1,0:T(8,128)(2,1)S(1)} all-to-all(bf16[4,5,16,128]{3,2,1,0:T(8,128)(2,1)S(1)} %add_convert_fusion), channel_id=1, replica_groups=mesh['tm'=4,'height'=32] {'tm'}, dimensions={0} | all-to-all | bytes 163840 | tf_op jit(solution)/shard_map/all_to_all | solution.py:645
  101.8 9.7 %all_to_all.21.got = bf16[4,384,128]{2,1,0:T(8,128)(2,1)S(1)} all-to-all(bf16[4,384,128]{2,1,0:T(8,128)(2,1)S(1)} %get-tuple-element.37), channel_id=1, replica_groups=mesh['tm'=4,'height'=32] {'tm'}, dimensions={0} | all-to-all | bytes 786432 | tf_op jit(solution)/shard_map/all_to_all | solution.py:648
  112.4 12.2 %all-to-all-start.3 = ((bf16[32,2,768]{2,1,0:T(2,128)(2,1)}), bf16[32,2,768]{2,1,0:T(2,128)(2,1)S(1)}, u32[]{:S(2)}, u32[]{:S(2)}) async-start(bf16[32,2,768]{2,1,0:T(2,128)(2,1)} %reshape.13), calls=%async_computation.3 | async-start | bytes 196608 | tf_op jit(solution)/shard_map/all_to_all | solution.py:650
  124.7 3.6 %hidden_grad.1 = bf16[12,2,12,3072]{3,2,1,0:T(8,128)(2,1)S(1)} custom-call(bf16[12,2,12,3072]{3,2,1,0:T(8,128)(2,1)S(1)} %copy.10.hidden, bf16[12,2,16,64]{3,2,1,0:T(8,128)(2,1)S(1)} %get-tuple-element.36.token_grad, f32[1,3072]{1,0:T(1,128)S(1)} %bitcast.8, bf16[64,3072]{1,0:T(8,128)(2,1)S(1)} %bitcast.6), custom_call_target="tpu_custom_call" | custom-call | flops 150994944 | bytes 4718592 | tf_op jit(solution)/shard_map/hidden_grad/pallas_call | solution.py:603
  128.3 3.0 %copy.11 = bf16[12,2,12,3072]{3,1,2,0:T(2,128)(2,1)} copy(bf16[12,2,12,3072]{3,2,1,0:T(8,128)(2,1)S(1)} %hidden_grad.1) | data formatting | bytes 3538944
  131.3 1.9 %all-to-all-done.3 = bf16[32,2,768]{2,1,0:T(2,128)(2,1)S(1)} async-done(((bf16[32,2,768]{2,1,0:T(2,128)(2,1)}), bf16[32,2,768]{2,1,0:T(2,128)(2,1)S(1)}, u32[]{:S(2)}, u32[]{:S(2)}) %all-to-all-start.3) | async-done | bytes 98336 | tf_op jit(solution)/shard_map/all_to_all | solution.py:650
  (71 shorter events, 26.8 us)
Async XLA Ops:
  3.8 5.4 %copy-start.20 = (bf16[3072,64]{0,1:T(8,128)(2,1)S(1)}, bf16[3072,64]{0,1:T(8,128)(2,1)}, u32[]{:S(2)}) copy-start(bf16[3072,64]{0,1:T(8,128)(2,1)} %param.10) | copy-start | bytes 1179652
  3.8 5.4 %copy-start.28 = (f32[3072]{0:T(1024)S(1)}, f32[3072]{0:T(1024)}, u32[]{:S(2)}) copy-start(f32[3072]{0:T(1024)} %param.8) | copy-start | bytes 36868
  3.8 14.5 %collective-permute-start = (bf16[2,4,96,512]{3,2,1,0:T(8,128)(2,1)}, bf16[2,4,96,512]{3,2,1,0:T(8,128)(2,1)S(1)}, u32[]{:S(2)}, u32[]{:S(2)}) collective-permute-start(bf16[2,4,96,512]{3,2,1,0:T(8,128)(2,1)} %get-tuple-element.20.ahead), channel_id=1, source_target_pairs={{32,0},{64,32},{96,64},{33,1},{65,33},{97,65},{34,2},{66,34},{98,6... | collective-permute-start | bytes 2359304 | tf_op jit(solution)/shard_map/ppermute | solution.py:629
  9.9 8.4 %copy-start.27 = (bf16[1,4,96,512]{3,2,1,0:T(8,128)(2,1)S(1)}, bf16[1,4,96,512]{3,2,1,0:T(8,128)(2,1)}, u32[]{:S(2)}) copy-start(bf16[1,4,96,512]{3,2,1,0:T(8,128)(2,1)} %copy-done.26) | copy-start | bytes 1179652
  15.6 18.2 %copy-start.3 = (bf16[2,3,512,512]{3,2,1,0:T(8,128)(2,1)}, bf16[2,3,512,512]{3,2,1,0:T(8,128)(2,1)S(1)}, u32[]{:S(2)}) copy-start(bf16[2,3,512,512]{3,2,1,0:T(8,128)(2,1)S(1)} %get-tuple-element.22.held_first) | copy-start | bytes 9437188
  19.5 19.9 %collective-permute-start.1 = (bf16[528,512]{1,0:T(8,128)(2,1)S(1)}, bf16[528,512]{1,0:T(8,128)(2,1)S(1)}, u32[]{:S(2)}, u32[]{:S(2)}) collective-permute-start(bf16[528,512]{1,0:T(8,128)(2,1)S(1)} %get-tuple-element.25), channel_id=1, source_target_pairs={{0,1},{1,0},{2,3},{3,2},{4,5},{5,4},{6,7},{7,6},{8,9},{9,8},{10,11... | collective-permute-start | bytes 1622024 | tf_op jit(solution)/shard_map/ppermute | solution.py:633
  21.2 18.1 %collective-permute-start.2 = (bf16[528,512]{1,0:T(8,128)(2,1)S(1)}, bf16[528,512]{1,0:T(8,128)(2,1)S(1)}, u32[]{:S(2)}, u32[]{:S(2)}) collective-permute-start(bf16[528,512]{1,0:T(8,128)(2,1)S(1)} %get-tuple-element.26), channel_id=1, source_target_pairs={{1,2},{2,1},{3,4},{4,3},{5,6},{6,5},{7,8},{8,7},{9,10},{10,9},{11,... | collective-permute-start | bytes 1622024 | tf_op jit(solution)/shard_map/ppermute | solution.py:632
  33.7 4.2 %copy-start = (bf16[7,3,512,512]{3,2,1,0:T(8,128)(2,1)}, bf16[7,3,512,512]{3,2,1,0:T(8,128)(2,1)S(1)}, u32[]{:S(2)}) copy-start(bf16[7,3,512,512]{3,2,1,0:T(8,128)(2,1)S(1)} %get-tuple-element.27.held_rest) | copy-start | bytes 33030148
  42.2 25.1 %all-to-all-start = ((bf16[4,5,16,256]{3,2,1,0:T(8,128)(2,1)}), bf16[4,5,16,256]{3,2,1,0:T(8,128)(2,1)}, u32[]{:S(2)}, u32[]{:S(2)}) async-start(bf16[4,5,16,256]{3,2,1,0:T(8,128)(2,1)} %copy-done.24), calls=%async_computation | async-start | bytes 327680 | tf_op jit(solution)/shard_map/all_to_all | solution.py:636
  46.4 4.1 %copy-start.1 = (bf16[7,3,512,512]{3,2,1,0:T(8,128)(2,1)S(1)}, bf16[7,3,512,512]{3,2,1,0:T(8,128)(2,1)}, u32[]{:S(2)}) copy-start(bf16[7,3,512,512]{3,2,1,0:T(8,128)(2,1)} %copy-done) | copy-start | bytes 33030148
  50.5 1.9 %copy-start.4 = (bf16[2,3,512,512]{3,2,1,0:T(8,128)(2,1)S(1)}, bf16[2,3,512,512]{3,2,1,0:T(8,128)(2,1)}, u32[]{:S(2)}) copy-start(bf16[2,3,512,512]{3,2,1,0:T(8,128)(2,1)} %copy-done.3) | copy-start | bytes 9437188
  52.4 1.7 %copy-start.10 = (f32[4,3,4,96,128]{4,3,2,1,0:T(8,128)S(1)}, f32[4,3,4,96,128]{4,3,2,1,0:T(8,128)}, u32[]{:S(2)}) copy-start(f32[4,3,4,96,128]{4,3,2,1,0:T(8,128)} %copy-done.9) | copy-start | bytes 7077892
  62.9 1.6 %copy-start.6 = (bf16[4,768,512]{2,1,0:T(8,128)(2,1)}, bf16[4,768,512]{2,1,0:T(8,128)(2,1)S(1)}, u32[]{:S(2)}) copy-start(bf16[4,768,512]{2,1,0:T(8,128)(2,1)S(1)} %get-tuple-element.30.patches) | copy-start | bytes 9437188
  64.5 1.8 %copy-start.12 = (bf16[3,2,6,96,512]{4,3,2,1,0:T(8,128)(2,1)}, bf16[3,2,6,96,512]{4,3,2,1,0:T(8,128)(2,1)S(1)}, u32[]{:S(2)}) copy-start(bf16[3,2,6,96,512]{4,3,2,1,0:T(8,128)(2,1)S(1)} %get-tuple-element.28.far) | copy-start | bytes 10616836
  67.3 12.9 %copy-start.5 = (bf16[2,3,512,512]{3,2,1,0:T(8,128)(2,1)S(1)}, bf16[2,3,512,512]{3,2,1,0:T(8,128)(2,1)}, u32[]{:S(2)}) copy-start(bf16[2,3,512,512]{3,2,1,0:T(8,128)(2,1)} %copy-done.3) | copy-start | bytes 9437188
  67.3 2.0 %copy-start.7 = (bf16[4,768,512]{2,1,0:T(8,128)(2,1)S(1)}, bf16[4,768,512]{2,1,0:T(8,128)(2,1)}, u32[]{:S(2)}) copy-start(bf16[4,768,512]{2,1,0:T(8,128)(2,1)} %copy-done.6) | copy-start | bytes 9437188
  74.0 21.5 %collective-permute-start.4 = (bf16[4,5,16,128]{3,2,1,0:T(8,128)(2,1)S(1)}, bf16[4,5,16,128]{3,2,1,0:T(8,128)(2,1)S(1)}, u32[]{:S(2)}, u32[]{:S(2)}) collective-permute-start(bf16[4,5,16,128]{3,2,1,0:T(8,128)(2,1)S(1)} %get-tuple-element.34), channel_id=1, source_target_pairs={{1,2},{2,1},{3,4},{4,3},{5,6},{6,5},{7,8},{8,7},{9,10},{10,9},{11,... | collective-permute-start | bytes 245768 | tf_op jit(solution)/shard_map/ppermute | solution.py:641
  74.7 20.8 %collective-permute-start.3 = (bf16[4,5,16,128]{3,2,1,0:T(8,128)(2,1)S(1)}, bf16[4,5,16,128]{3,2,1,0:T(8,128)(2,1)S(1)}, u32[]{:S(2)}, u32[]{:S(2)}) collective-permute-start(bf16[4,5,16,128]{3,2,1,0:T(8,128)(2,1)S(1)} %get-tuple-element.33), channel_id=1, source_target_pairs={{0,1},{1,0},{2,3},{3,2},{4,5},{5,4},{6,7},{7,6},{8,9},{9,8},{10,11... | collective-permute-start | bytes 245768 | tf_op jit(solution)/shard_map/ppermute | solution.py:642
  80.2 4.1 %copy-start.2 = (bf16[7,3,512,512]{3,2,1,0:T(8,128)(2,1)S(1)}, bf16[7,3,512,512]{3,2,1,0:T(8,128)(2,1)}, u32[]{:S(2)}) copy-start(bf16[7,3,512,512]{3,2,1,0:T(8,128)(2,1)} %copy-done) | copy-start | bytes 33030148
  84.3 1.9 %copy-start.8 = (bf16[4,768,512]{2,1,0:T(8,128)(2,1)S(1)}, bf16[4,768,512]{2,1,0:T(8,128)(2,1)}, u32[]{:S(2)}) copy-start(bf16[4,768,512]{2,1,0:T(8,128)(2,1)} %copy-done.6) | copy-start | bytes 9437188
  86.2 1.7 %copy-start.11 = (f32[4,3,4,96,128]{4,3,2,1,0:T(8,128)S(1)}, f32[4,3,4,96,128]{4,3,2,1,0:T(8,128)}, u32[]{:S(2)}) copy-start(f32[4,3,4,96,128]{4,3,2,1,0:T(8,128)} %copy-done.9) | copy-start | bytes 7077892
  87.9 2.0 %copy-start.13 = (bf16[3,2,6,96,512]{4,3,2,1,0:T(8,128)(2,1)S(1)}, bf16[3,2,6,96,512]{4,3,2,1,0:T(8,128)(2,1)}, u32[]{:S(2)}) copy-start(bf16[3,2,6,96,512]{4,3,2,1,0:T(8,128)(2,1)} %copy-done.12) | copy-start | bytes 10616836
  89.9 11.2 %copy-start.15 = (bf16[12,2,16,3072]{3,2,1,0:T(8,128)(2,1)S(1)}, bf16[12,2,16,3072]{3,2,1,0:T(8,128)(2,1)}, u32[]{:S(2)}) copy-start(bf16[12,2,16,3072]{3,2,1,0:T(8,128)(2,1)} %copy-done.14) | copy-start | bytes 7077892
  112.4 20.8 %all-to-all-start.3 = ((bf16[32,2,768]{2,1,0:T(2,128)(2,1)}), bf16[32,2,768]{2,1,0:T(2,128)(2,1)S(1)}, u32[]{:S(2)}, u32[]{:S(2)}) async-start(bf16[32,2,768]{2,1,0:T(2,128)(2,1)} %reshape.13), calls=%async_computation.3 | async-start | bytes 196608 | tf_op jit(solution)/shard_map/all_to_all | solution.py:650
  (13 other events, 13.3 us)

commit v5 on v4

v5 whole, which is shorter than its diff:
```python
import functools
import math

import jax
import jax.numpy as jnp
from jax import lax
from jax.experimental import pallas as pl
from jax.experimental.pallas import tpu as pltpu
from jax.sharding import PartitionSpec as P

epsilon = 1e-05
slots = 16
lanes = 128
f32 = jnp.float32
bf16 = jnp.bfloat16
whole = pl.BlockSpec(memory_space=pltpu.VMEM)
scalars = pl.BlockSpec(memory_space=pltpu.SMEM)
far_off = pl.BlockSpec(memory_space=pltpu.HBM)


def params(mib):
    return pltpu.CompilerParams(vmem_limit_bytes=int(mib * 2**20))


def dot(lhs, rhs):
    return jnp.dot(lhs, rhs, preferred_element_type=f32)


def dot_turned(lhs, rhs):
    return lax.dot_general(lhs, rhs, (((1,), (1,)), ((), ())), preferred_element_type=f32)


def normalise(values):
    center = jnp.mean(values, axis=-1, keepdims=True)
    shifted = values - center
    spread = jnp.mean(shifted * shifted, axis=-1, keepdims=True)
    inverse = lax.rsqrt(spread + epsilon)
    return shifted * inverse, inverse


def modulate_kernel(source, scale, shift, w_out, modulated, send, hidden, rows, in_sems, out_sems):
    frames, token_rows, tokens, width = hidden.shape
    groups = send.shape[0]
    block = frames // groups
    gain = 1.0 + scale[...]
    blank = jnp.zeros((slots - tokens, width), f32)
    send[0, 0:2] = jnp.zeros_like(send[0, 0:2])

    def in_copy(step):
        at = pl.ds(step * block, block)
        return pltpu.make_async_copy(source.at[at], hidden.at[at], in_sems.at[step])

    for step in range(groups):
        in_copy(step).start()

    def out_copy(step):
        at = pl.ds(step * block, block)
        return pltpu.make_async_copy(rows.at[at], modulated.at[at], out_sems.at[step])

    def share(step, carry):
        in_copy(step).wait()
        for frame in range(block):
            for row in range(token_rows):
                normed, _ = normalise(hidden[step * block + frame, row].astype(f32))
                value = jnp.concatenate([normed * gain + shift[...], blank], axis=0)
                rows[step * block + frame, row] = value.astype(bf16)
        out_copy(step).start()
        value = rows[pl.ds(step * block, block)].reshape(-1, width)
        value = dot_turned(value, w_out[...]).astype(bf16)
        value = value.reshape(block, token_rows, slots, value.shape[-1])
        paired = jnp.concatenate([value[:, 0], value[:, 1]], axis=-1)
        for frame in range(block):
            send[step, frame + 2] = paired[frame]

        @pl.when(step < groups - 1)
        def _():
            for frame in range(1, block):
                send[step + 1, frame - 1] = paired[frame]

        return carry

    lax.fori_loop(0, groups, share, 0)
    for step in range(groups):
        out_copy(step).wait()


def modulate(hidden, mod_scale, mod_shift, w_out, groups):
    frames, token_rows, tokens, width = hidden.shape
    token_width = w_out.shape[0]
    out = jax.ShapeDtypeStruct((frames, token_rows, slots, width), bf16)
    return pl.pallas_call(
        modulate_kernel,
        out_shape=[
            out,
            jax.ShapeDtypeStruct((groups, frames // groups + 2, slots, 2 * token_width), bf16),
        ],
        in_specs=[far_off] + [whole] * 3,
        out_specs=[far_off, whole],
        scratch_shapes=[
            pltpu.VMEM(hidden.shape, bf16),
            pltpu.VMEM(out.shape, bf16),
            pltpu.SemaphoreType.DMA((groups,)),
            pltpu.SemaphoreType.DMA((groups,)),
        ],
        compiler_params=params(53),
        cost_estimate=pl.CostEstimate(
            flops=2 * frames * 2 * slots * width * token_width,
            bytes_accessed=8 * frames * slots * width,
            transcendentals=0,
        ),
        name="modulate",
    )(hidden, mod_scale.reshape(1, -1), mod_shift.reshape(1, -1), w_out)


def column_shifts(value):
    cols, channels = value.shape
    wide = value.astype(f32)
    place = lax.broadcasted_iota(jnp.int32, (cols, channels), 0)
    nxt = jnp.where(place == cols - 1, 0.0, pltpu.roll(wide, cols - 1, 0))
    prv = jnp.where(place == 0, 0.0, pltpu.roll(wide, 1, 0))
    return nxt.astype(bf16), prv.astype(bf16)


taps = [(2 - n // 3, (1, 0, 2)[n % 3]) for n in range(9)]


def flat(value):
    return value.reshape(-1, value.shape[-1])


def weight_matrix(held, kt, ky):
    return jnp.concatenate([held[kt, ky, kx] for kx in range(3)], axis=-1)


def pack_kernel(places, grad, grad_ahead, latent, near, far, sems):
    frames, _, cols, channels = grad.shape
    copies = [
        pltpu.make_async_copy(
            grad.at[frame, places[side]],
            out.at[frame * cols : (frame + 1) * cols],
            sems.at[side * frames + frame],
        )
        for side, out in ((0, near), (1, far))
        for frame in range(frames)
    ]
    for copy in copies:
        copy.start()
    for side, out in ((0, near), (1, far)):
        for frame in range(2):
            at = (frames + frame) * cols
            out[at : at + cols] = grad_ahead[frame, places[side]]
        at = (frames + 2) * cols
        tail = flat(latent[...])
        count = tail.shape[0] * lanes // channels
        for lane in range(channels // lanes):
            out[at : at + count, lane * lanes : (lane + 1) * lanes] = tail[
                lane * count : (lane + 1) * count
            ]
    for copy in copies:
        copy.wait()


def pack_rows(places, grad, grad_ahead, latent):
    frames, _, cols, channels = grad.shape
    total = (frames + 2) * cols + latent.size // channels
    return pl.pallas_call(
        pack_kernel,
        in_specs=[scalars, far_off, whole, whole],
        out_specs=[whole] * 2,
        out_shape=[jax.ShapeDtypeStruct((total, channels), bf16)] * 2,
        scratch_shapes=[pltpu.SemaphoreType.DMA((2 * frames,))],
        compiler_params=params(4),
        name="pack_rows",
    )(places, grad, grad_ahead, latent)


def own_kernel(grad, grad_ahead, w_section, total, held, shifts, sems):
    frames, rows, cols, channels = grad.shape
    copies = [
        pltpu.make_async_copy(w_section.at[kt, ky], held.at[kt, ky], sems.at[n])
        for n, (kt, ky) in enumerate(taps)
    ]
    for copy in copies:
        copy.start()
    for frame in range(frames + 2):
        for row in range(rows):
            value = grad[frame, row] if frame < frames else grad_ahead[frame - frames, row]
            shifts[0, frame, row], shifts[1, frame, row] = column_shifts(value)
    for n, (kt, ky) in enumerate(taps):
        lo, hi = max(0, ky - 1), rows + min(0, ky - 1)
        at = slice(lo + 1 - ky, hi + 1 - ky)
        src = slice(2 - kt, frames + 2 - kt), at
        centre = flat(grad[2 - kt :, at])
        if kt < 2:
            centre = jnp.concatenate([centre, flat(grad_ahead[: 2 - kt, at])], axis=0)
        window = jnp.concatenate(
            [flat(shifts[(0,) + src]), centre, flat(shifts[(1,) + src])], axis=-1
        )
        copies[n].wait()
        part = dot_turned(window, weight_matrix(held, kt, ky))
        for lane in range(channels // lanes):
            value = part[:, lane * lanes : (lane + 1) * lanes]
            value = value.reshape(frames, hi - lo, cols, lanes)
            if n == 0:
                total[lane] = value
            else:
                total[lane, :, lo:hi] += value


def own_part(grad, grad_ahead, w_section):
    frames, rows, cols, channels = grad.shape
    return pl.pallas_call(
        own_kernel,
        out_shape=[
            jax.ShapeDtypeStruct((channels // lanes, frames, rows, cols, lanes), f32),
            jax.ShapeDtypeStruct(w_section.shape, bf16),
        ],
        in_specs=[whole, whole, far_off],
        out_specs=[whole] * 2,
        scratch_shapes=[
            pltpu.VMEM((2, frames + 2, rows, cols, channels), bf16),
            pltpu.SemaphoreType.DMA((len(taps),)),
        ],
        compiler_params=params(26),
        cost_estimate=pl.CostEstimate(
            flops=2 * 24 * grad.size * channels,
            bytes_accessed=2 * w_section.size,
            transcendentals=0,
        ),
        name="own_part",
    )(grad, grad_ahead, w_section)


def edge_kernel(places, own, near_rows, far_rows, held, w_in, total, patches, near):
    even = places[0] != 0
    blocks, frames, rows, cols, _ = own.shape
    for lane in range(blocks):
        total[lane, :, 0] = own[lane, :, 0]
        total[lane, :, 1] = own[lane, :, rows - 1]
    for frame in range(frames + 2):
        at = slice(frame * cols, (frame + 1) * cols)
        ends = near_rows[at], far_rows[at]
        for side in range(2):
            value = jnp.where(even == (side == 1), ends[0], ends[1])
            near[1, side, frame] = value
            near[0, side, frame], near[2, side, frame] = column_shifts(value)

    patches[...] = jnp.zeros_like(patches)
    lat = w_in.shape[3]
    for n in range(4 * 3 * 2 * 2 * 2 * 2):
        p, q, kt, a, b, pp, qq = [
            n // size % top
            for size, top in ((96, 2), (48, 2), (16, 3), (8, 2), (4, 2), (2, 2), (1, 2))
        ]
        ky, kx = p - 1 + 2 * a + pp, q - 1 + 2 * b + qq
        if 0 <= ky < 3 and 0 <= kx < 3:
            at = (((kt * 2 + a) * 2 + b) * 4 + 2 * pp + qq) * lat
            patches[2 * p + q, at : at + lat] = w_in[kt, ky, kx]

    for kt, ky in taps:
        if ky == 1:
            continue
        side = 0 if ky == 2 else 1
        window = jnp.concatenate(
            [flat(near[kx, side, 2 - kt : frames + 2 - kt]) for kx in range(3)], axis=-1
        )
        part = dot_turned(window, weight_matrix(held, kt, ky))
        for lane in range(blocks):
            value = part[:, lane * lanes : (lane + 1) * lanes]
            total[lane, :, side] += value.reshape(frames, cols, lanes)


def edge_part(places, own, near_rows, far_rows, held, w_in):
    blocks, frames, _, cols, _ = own.shape
    channels = blocks * lanes
    pair = 8 * w_in.shape[3]
    return pl.pallas_call(
        edge_kernel,
        out_shape=[
            jax.ShapeDtypeStruct((blocks, frames, 2, cols, lanes), f32),
            jax.ShapeDtypeStruct((4, 6 * pair, channels), bf16),
        ],
        in_specs=[scalars] + [whole] * 5,
        out_specs=[whole] * 2,
        scratch_shapes=[pltpu.VMEM((3, 2, frames + 2, cols, channels), bf16)],
        compiler_params=params(10),
        cost_estimate=pl.CostEstimate(
            flops=2 * 4 * own.size * channels, bytes_accessed=0, transcendentals=0
        ),
        name="edge_part",
    )(places, own, near_rows, far_rows, held, w_in)


def latent_phase(total, slot_of, row_of, spread_row, windows, patches, spread):
    blocks, frames, _, cols, _ = total.shape
    half = cols // 2
    pair = windows.shape[-1]
    for p in range(2):
        for q in range(2):
            top = row_of[p] + p
            window = jnp.concatenate(
                [
                    flat(windows[q, kt : kt + frames, top + a])
                    for kt in range(3)
                    for a in range(2)
                ],
                axis=-1,
            )
            weight = patches[2 * p + q]
            pre = dot(window, weight)
            back = jnp.concatenate(
                [
                    jnp.concatenate(
                        [
                            total[lane, frame, slot_of[p], pl.ds(q, half, stride=2), :]
                            for lane in range(blocks)
                        ],
                        axis=-1,
                    )
                    for frame in range(frames)
                ],
                axis=0,
            )
            gate = jax.nn.sigmoid(pre)
            act_grad = (back * (gate * (1.0 + pre * (1.0 - gate)))).astype(bf16)
            terms = dot_turned(act_grad, weight)
            for kt in range(3):
                for a in range(2):
                    at = (kt * 2 + a) * pair
                    spread[kt : kt + frames, top + a - spread_row, q : q + half] += terms[
                        :, at : at + pair
                    ].reshape(frames, half, pair)


def shares_of(spread, row, half):
    width = spread.shape[-1] // 2
    return spread[:, row, 1 : half + 1, :width] + spread[:, row, 0:half, width:]


def edge_latent_kernel(
    places, total, latent, near_rows, far_rows, patches,
    near_out, far_out, windows, spread, tokens,
):
    even = places[0] != 0
    groups, depth, _, pair = latent.shape
    width = pair // 2
    count = groups * depth * slots * lanes // near_rows.shape[1]
    start = near_rows.shape[0] - count
    half = windows.shape[3]
    block = half // groups
    tokens[...] = jnp.zeros_like(tokens)
    for src in range(groups):
        at = slice(8 + src * block, 8 + (src + 1) * block)
        for frame in range(depth):
            value = latent[src, frame].astype(f32)[:block]
            tokens[frame, 1, at] = value[:, :width]
            tokens[frame, 2, at] = value[:, width:]
            row = (src * depth + frame) * slots
            lane = row // count * lanes
            row = start + row % count
            ends = [
                ref[row : row + slots, lane : lane + lanes].astype(f32)[:block]
                for ref in (near_rows, far_rows)
            ]
            tokens[frame, 0, at] = jnp.where(even, ends[1], ends[0])[:, width:]
            tokens[frame, 3, at] = jnp.where(even, ends[0], ends[1])[:, :width]
    for q in range(2):
        left = tokens[:, :, 7 + q : 7 + q + half]
        right = tokens[:, :, 8 + q : 8 + q + half]
        windows[q] = jnp.concatenate([left, right], axis=-1).astype(bf16)
    spread[...] = jnp.zeros_like(spread)
    latent_phase(total, (0, 1), (0, 1), 0, windows, patches, spread)
    for n, row in enumerate((0, 3)):
        tokens[:, n, 0:half] = shares_of(spread, row, half)
    none = jnp.zeros((block, width), f32)
    fill = jnp.zeros((slots - block, 2 * width), f32)
    for dst in range(groups):
        at = slice(dst * block, (dst + 1) * block)
        for frame in range(depth):
            up = jnp.concatenate([none, tokens[frame, 0, at]], axis=-1)
            down = jnp.concatenate([tokens[frame, 1, at], none], axis=-1)
            padded = lambda v: jnp.concatenate([v, fill], axis=0).astype(bf16)
            near_out[dst, frame] = padded(jnp.where(even, down, up))
            far_out[dst, frame] = padded(jnp.where(even, up, down))


def edge_latent(places, total, latent, near_rows, far_rows, patches):
    groups, depth, _, pair = latent.shape
    cols = total.shape[3]
    out = jax.ShapeDtypeStruct(latent.shape, bf16)
    return pl.pallas_call(
        edge_latent_kernel,
        out_shape=[
            out,
            out,
            jax.ShapeDtypeStruct((2, depth, 4, cols // 2, pair), bf16),
            jax.ShapeDtypeStruct((depth, 4, cols // 2 + 8, pair), f32),
        ],
        in_specs=[scalars] + [whole] * 5,
        out_specs=[whole] * 4,
        scratch_shapes=[pltpu.VMEM((depth, 4, 72, pair // 2), f32)],
        compiler_params=params(10),
        name="edge_latent",
    )(places, total, latent, near_rows, far_rows, patches)


def inner_kernel(own, windows, patches, spread_in, out, spread, tokens):
    half = windows.shape[3]
    groups, depth = out.shape[:2]
    block = half // groups
    spread[...] = spread_in[:, 1:3]
    latent_phase(own, (2, 1), (1, 0), 1, windows, patches, spread)
    for row in range(2):
        tokens[:, row] = shares_of(spread, row, half)
    fill = jnp.zeros((slots - block, out.shape[-1]), f32)
    for dst in range(groups):
        at = slice(dst * block, (dst + 1) * block)
        for frame in range(depth):
            value = jnp.concatenate([tokens[frame, 0, at], tokens[frame, 1, at]], axis=-1)
            out[dst, frame] = jnp.concatenate([value, fill], axis=0)


def inner_part(own, windows, patches, spread, groups):
    cols = own.shape[3]
    depth, _, wide, pair = spread.shape
    return pl.pallas_call(
        inner_kernel,
        out_shape=jax.ShapeDtypeStruct((groups, depth, slots, pair), f32),
        in_specs=[whole] * 4,
        out_specs=whole,
        scratch_shapes=[
            pltpu.VMEM((depth, 2, wide, pair), f32),
            pltpu.VMEM((depth, 2, cols // 2, pair // 2), f32),
        ],
        compiler_params=params(10),
        cost_estimate=pl.CostEstimate(
            flops=8 * own.size * 6 * pair, bytes_accessed=0, transcendentals=own.size
        ),
        name="inner_part",
    )(own, windows, patches, spread)


def weight_kernel(shares, modulated, token_grad, send, field):
    groups, depth, _, pair = shares.shape
    width = pair // 2
    frames, token_rows = modulated.shape[:2]
    model = modulated.shape[-1]
    field[...] = jnp.zeros_like(field)
    for src in range(groups):
        at = src * (frames // groups)
        field[at : at + depth] += shares[src].astype(f32)
    values = field[2 : 2 + frames]
    token_grad[:, 0] = values[:, :, :width].astype(bf16)
    token_grad[:, 1] = values[:, :, width:].astype(bf16)
    turned = jnp.transpose(token_grad[...].reshape(-1, width).astype(f32)).astype(bf16)
    weight = dot(turned, modulated[...].reshape(-1, model))
    half = model // (2 * groups)
    for dst in range(groups):
        at = 2 * half * dst
        stacked = jnp.concatenate(
            [weight[:, at : at + half], weight[:, at + half : at + 2 * half]], axis=0
        )
        send[dst] = jnp.transpose(stacked).astype(bf16)


def weight_terms(shares, modulated):
    groups, depth, _, pair = shares.shape
    frames, token_rows, _, model = modulated.shape
    return pl.pallas_call(
        weight_kernel,
        out_shape=[
            jax.ShapeDtypeStruct((frames, token_rows, slots, pair // 2), bf16),
            jax.ShapeDtypeStruct((groups, model // (2 * groups), pair), bf16),
        ],
        in_specs=[whole] * 2,
        out_specs=[whole] * 2,
        scratch_shapes=[pltpu.VMEM((frames + 2, slots, pair), f32)],
        compiler_params=params(12),
        name="weight_terms",
    )(shares, modulated)


def middle_kernel(got, send):
    total = jnp.sum(got[...].astype(f32), axis=0)
    count, rows, width = send.shape
    total = total.reshape(count // 2, rows, 2 * width).astype(bf16)
    send[0 : count // 2] = total[:, :, :width]
    send[count // 2 :] = total[:, :, width:]


def middle_sum(got, count):
    groups, depth, pair = got.shape
    return pl.pallas_call(
        middle_kernel,
        out_shape=jax.ShapeDtypeStruct((count, 2 * depth // count, pair // 2), bf16),
        in_specs=[whole],
        out_specs=whole,
        compiler_params=params(4),
        name="middle_sum",
    )(got)


def hidden_kernel(hidden, token_grad, scale, w_out, grad_hidden):
    frames, token_rows, tokens, width = hidden.shape
    gain = 1.0 + scale[...]
    block = 3

    def share(step, carry):
        rows = token_grad[pl.ds(step * block, block)].reshape(-1, token_grad.shape[-1])
        mod_grad = dot(rows, w_out[...])
        for frame in range(block):
            for row in range(token_rows):
                at = (frame * token_rows + row) * slots
                scaled = mod_grad[at : at + tokens] * gain
                normed, inverse = normalise(hidden[step * block + frame, row].astype(f32))
                first = jnp.mean(scaled, axis=-1, keepdims=True)
                second = jnp.mean(scaled * normed, axis=-1, keepdims=True)
                value = (scaled - first - normed * second) * inverse
                grad_hidden[step * block + frame, row] = value.astype(bf16)
        return carry

    lax.fori_loop(0, frames // block, share, 0)


def hidden_grad(hidden, token_grad, mod_scale, w_out):
    frames, token_rows, tokens, width = hidden.shape
    return pl.pallas_call(
        hidden_kernel,
        out_shape=jax.ShapeDtypeStruct(hidden.shape, bf16),
        in_specs=[whole] * 4,
        out_specs=whole,
        compiler_params=params(8),
        cost_estimate=pl.CostEstimate(
            flops=2 * frames * 2 * slots * width * w_out.shape[0],
            bytes_accessed=8 * frames * slots * width,
            transcendentals=0,
        ),
        name="hidden_grad",
    )(hidden, token_grad, mod_scale.reshape(1, -1), w_out)


def shards(hidden, mod_scale, mod_shift, w_out, w_in, w_section, section_grad):
    groups, strips = lax.axis_size("tm"), lax.axis_size("height")
    rows = section_grad.shape[1]
    swap = lambda a, b: [(a, b), (b, a)]
    near = sum([swap(i, i + 1) for i in range(0, strips - 1, 2)], [])
    far = sum([swap(i, i + 1) for i in range(1, strips - 1, 2)], [])
    odd = lax.rem(lax.axis_index("height"), 2)
    places = jnp.stack([(1 - odd) * (rows - 1), odd * (rows - 1)]).astype(jnp.int32)
    w_out = jnp.transpose(w_out)

    grad_ahead = lax.ppermute(section_grad, "tm", [(g + 1, g) for g in range(groups - 1)])
    modulated, latent_send = modulate(hidden, mod_scale, mod_shift, w_out, groups)
    latent = lax.all_to_all(latent_send, "tm", 0, 0, tiled=True)
    near_send, far_send = pack_rows(places, section_grad, grad_ahead, latent)
    far_rows = lax.ppermute(far_send, "height", far)
    near_rows = lax.ppermute(near_send, "height", near)
    own, held = own_part(section_grad, grad_ahead, w_section)
    edge, patches = edge_part(places, own, near_rows, far_rows, held, w_in)
    near_share, far_share, windows, spread = edge_latent(
        places, edge, latent, near_rows, far_rows, patches
    )
    far_share = lax.ppermute(far_share, "height", far)
    near_share = lax.ppermute(near_share, "height", near)
    centre = inner_part(own, windows, patches, spread, groups)
    centre = centre + near_share.astype(f32) + far_share.astype(f32)
    shares = lax.all_to_all(centre.astype(bf16), "tm", 0, 0, tiled=True)

    token_grad, send = weight_terms(shares, modulated)
    got = lax.all_to_all(send, "tm", 0, 0, tiled=True)
    grad_hidden = hidden_grad(hidden, token_grad, mod_scale, w_out)
    pieces = lax.all_to_all(middle_sum(got, strips), "height", 0, 0, tiled=True)
    total_tokens = math.prod(hidden.shape[:3]) * groups * strips
    grad_out_weight = jnp.sum(pieces.astype(f32), axis=0) / math.sqrt(total_tokens)
    return (grad_hidden, grad_out_weight)


def solution(mesh):
    placed = (P(None, "height", "tm", None), P(), P(), P(), P(), P(), P("tm", "height", None, None))
    return jax.shard_map(
        shards,
        mesh=mesh,
        in_specs=placed,
        out_specs=(P(None, "height", "tm", None), P(("tm", "height"), None)),
        check_vma=False,
    )
```

time: 136 us -> 100 us (0.74)
  local copies, waits for them, and re-layouts: 46.2 us -> 7.41 us
  blocking collectives: 15.2 us -> 17.2 us
    unnamed x64 -> x18, local copies, waits for them, and re-layouts: 46.2 us -> 7.41 us
    pallas_call x1, Pallas kernels: 11.8 us -> 16.9 us  [own_part(): pl.pallas_call(own_kernel, out_shape=[jax.ShapeDtypeStruct((channels // l...]
    all_to_all x1, waiting for transfers between devices: 0.01 us -> 3.7 us  [shards(): latent = lax.all_to_all(latent_send, 'tm', 0, 0, tiled=True)]
    pallas_call x1, Pallas kernels: 5.59 us -> 2.29 us  [inner_part(): pl.pallas_call(inner_kernel, out_shape=jax.ShapeDtypeStruct((groups, dept...]
    ppermute x1, waiting for transfers between devices: 2.67 us -> 0.01 us  [shards(): lax.ppermute(section_grad, 'tm', [(g + 1, g) for g in range(groups - 1)])]
    all_to_all x1, starting transfers between devices: 12.2 us -> 14.7 us  [shards(): pieces = lax.all_to_all(middle_sum(got, strips), 'height', 0, 0, tiled=True)]
    all_to_all x1, blocking collectives: 5.53 us -> 7.54 us  [shards(): shares = lax.all_to_all(centre.astype(bf16), 'tm', 0, 0, tiled=True)]
    pallas_call x1, Pallas kernels: 5.69 us -> 3.88 us  [edge_part(): pl.pallas_call(edge_kernel, out_shape=[jax.ShapeDtypeStruct((blocks, fram...]
  transfers between devices with their start and end apart: 7 -> 7, of which waited for: 2 -> 2; matrix products, arithmetic and copies ran while one was open for 4% -> 7% of each run, Pallas kernels for 23% -> 29%
where the time goes in v5:
time: 100 us; the launch traced here: 98.5 us
  Pallas kernels  37.5 us (38%)
  starting transfers between devices  29 us (29%)
  blocking collectives  17.2 us (17%)
  local copies, waits for them, and re-layouts  7.41 us (7%)
  waiting for transfers between devices  5.82 us (6%)
    pallas_call x1, Pallas kernels, own_part(): pl.pallas_call(own_kernel, out_shape=[jax.ShapeDtypeStruct((channels // l...  16.9 us
    all_to_all x1, starting transfers between devices, shards(): pieces = lax.all_to_all(middle_sum(got, strips), 'height', 0, 0, tiled=True)  14.7 us
    all_to_all x1, blocking collectives, shards(): got = lax.all_to_all(send, 'tm', 0, 0, tiled=True)  9.7 us
    all_to_all x1, blocking collectives, shards(): shares = lax.all_to_all(centre.astype(bf16), 'tm', 0, 0, tiled=True)  7.54 us
    unnamed x18, local copies, waits for them, and re-layouts  7.41 us
    pallas_call x1, Pallas kernels, modulate(): pl.pallas_call(modulate_kernel, out_shape=[out, jax.ShapeDtypeStruct((gro...  5.43 us
    ppermute x1, starting transfers between devices, shards(): near_share = lax.ppermute(near_share, 'height', near)  4.27 us
    pallas_call x1, Pallas kernels, edge_part(): pl.pallas_call(edge_kernel, out_shape=[jax.ShapeDtypeStruct((blocks, fram...  3.88 us
  transfers between devices with their start and end apart: 7, of which 2 were waited for; matrix products, arithmetic and copies ran while one was open for 7% of the time, Pallas kernels for 29%

profile of v5, /device:TPU:1, one launch (start us, length us, event | category | flops | bytes accessed | tf_op | source)
XLA Modules:
  0.0 98.5 jit_solution(10634581785595171281)
XLA Ops:
  0.7 3.5 %collective-permute-start = (bf16[3,4,96,512]{3,2,1,0:T(8,128)(2,1)}, bf16[3,4,96,512]{3,2,1,0:T(8,128)(2,1)S(1)}, u32[]{:S(2)}, u32[]{:S(2)}) collective-permute-start(bf16[3,4,96,512]{3,2,1,0:T(8,128)(2,1)} %grad.3), channel_id=1, source_target_pairs={{32,0},{64,32},{96,64},{33,1},{65,33},{97,65},{34,2},{66,34},{98,6... | collective-permute-start | bytes 3538952 | tf_op jit(solution)/shard_map/ppermute | solution.py:552
  4.1 3.4 %copy.10.source.hidden = bf16[12,2,12,3072]{3,2,1,0:T(8,128)(2,1)} copy(bf16[12,2,12,3072]{3,1,2,0:T(2,128)(2,1)} %param.7) | data formatting | bytes 3538944 | tf_op args[0]
  7.5 5.4 %modulate.1 = (bf16[12,2,16,3072]{3,2,1,0:T(8,128)(2,1)}, bf16[4,5,16,128]{3,2,1,0:T(8,128)(2,1)}) custom-call(bf16[12,2,12,3072]{3,2,1,0:T(8,128)(2,1)} %copy.10.source.hidden, f32[1,3072]{1,0:T(1,128)S(1)} %bitcast.7, f32[1,3072]{1,0:T(1,128)S(1)} %bitcast.9, bf16[64,3072]{1,0:T(8,128)(2,1)S(1)} %bitcast.5), custom_call_target="tpu_custom_call" | custom-call | flops 150994944 | bytes 4718592 | tf_op jit(solution)/shard_map/modulate/pallas_call | solution.py:91
  13.0 3.3 %all-to-all-start = ((bf16[4,5,16,128]{3,2,1,0:T(8,128)(2,1)}), bf16[4,5,16,128]{3,2,1,0:T(8,128)(2,1)S(1)}, u32[]{:S(2)}, u32[]{:S(2)}) async-start(bf16[4,5,16,128]{3,2,1,0:T(8,128)(2,1)} %get-tuple-element.17), calls=%async_computation | async-start | bytes 163840 | tf_op jit(solution)/shard_map/all_to_all | solution.py:554
  16.4 3.7 %all-to-all-done.latent = bf16[4,5,16,128]{3,2,1,0:T(8,128)(2,1)S(1)} async-done(((bf16[4,5,16,128]{3,2,1,0:T(8,128)(2,1)}), bf16[4,5,16,128]{3,2,1,0:T(8,128)(2,1)S(1)}, u32[]{:S(2)}, u32[]{:S(2)}) %all-to-all-start) | async-done | bytes 81952 | tf_op jit(solution)/shard_map/all_to_all | solution.py:554
  20.1 1.4 %pack_rows.1 = (bf16[560,512]{1,0:T(8,128)(2,1)S(1)}, bf16[560,512]{1,0:T(8,128)(2,1)S(1)}) custom-call(s32[2]{0:T(128)S(1)} %pad_add_fusion.places, bf16[3,4,96,512]{3,2,1,0:T(8,128)(2,1)S(1)} %copy-done.3, bf16[3,4,96,512]{3,2,1,0:T(8,128)(2,1)S(1)} %collective-permute-done.grad_ahead, bf16[4,5,16,128]{3,2,1,0:T(8,128)(2,1)S(1)} %all-to-all-done.latent), custom_call_target="tpu_custom_call" | custom-call | tf_op jit(solution)/shard_map/pack_rows/pallas_call | solution.py:166
  21.5 1.7 %collective-permute-start.1 = (bf16[560,512]{1,0:T(8,128)(2,1)S(1)}, bf16[560,512]{1,0:T(8,128)(2,1)S(1)}, u32[]{:S(2)}, u32[]{:S(2)}) collective-permute-start(bf16[560,512]{1,0:T(8,128)(2,1)S(1)} %get-tuple-element.18), channel_id=1, source_target_pairs={{0,1},{1,0},{2,3},{3,2},{4,5},{5,4},{6,7},{7,6},{8,9},{9,8},{10,11... | collective-permute-start | bytes 1720328 | tf_op jit(solution)/shard_map/ppermute | solution.py:557
  23.2 0.8 collective-permute-start.2
  24.0 16.9 %own_part.1 = (f32[4,3,4,96,128]{4,3,2,1,0:T(8,128)S(1)}, bf16[3,3,3,512,512]{4,3,2,1,0:T(8,128)(2,1)S(1)}) custom-call(bf16[3,4,96,512]{3,2,1,0:T(8,128)(2,1)S(1)} %copy-done.3, bf16[3,4,96,512]{3,2,1,0:T(8,128)(2,1)S(1)} %collective-permute-done.grad_ahead, bf16[3,3,3,512,512]{4,3,2,1,0:T(8,128)(2,1)} %w_section.1), custom_call_target="tpu_custom_call" | custom-call | flops 14495514624 | bytes 14155776 | tf_op jit(solution)/shard_map/own_part/pallas_call | solution.py:212
  41.0 3.9 %edge_part.1 = (f32[4,3,2,96,128]{4,3,2,1,0:T(8,128)S(1)}, bf16[4,768,512]{2,1,0:T(8,128)(2,1)S(1)}) custom-call(s32[2]{0:T(128)S(1)} %pad_add_fusion.places, f32[4,3,4,96,128]{4,3,2,1,0:T(8,128)S(1)} %get-tuple-element.16.own, bf16[560,512]{1,0:T(8,128)(2,1)S(1)} %collective-permute-done.1.near_rows, bf16[560,512]{1,0:T(8,128)(2,1)S(1)} %collective-permute-done.2.far_rows, ...), custom_call_target="tpu_custom_call" | custom-call | flops 2415919104 | tf_op jit(solution)/shard_map/edge_part/pallas_call | solution.py:277
  44.9 3.0 %edge_latent.1 = (bf16[4,5,16,128]{3,2,1,0:T(8,128)(2,1)S(1)}, bf16[4,5,16,128]{3,2,1,0:T(8,128)(2,1)S(1)}, bf16[2,5,4,48,128]{4,3,2,1,0:T(8,128)(2,1)S(1)}, f32[5,4,56,128]{3,2,1,0:T(8,128)S(1)}) custom-call(s32[2]{0:T(128)S(1)} %pad_add_fusion.places, f32[4,3,2,96,128]{4,3,2,1,0:T(8,128)S(1)} %get-tuple-element.21.total, ...), custom_call_target="tpu_custom_call" | custom-call | tf_op jit(solution)/shard_map/edge_latent/pallas_call | solution.py:391
  47.9 4.3 %collective-permute-start.3 = (bf16[4,5,16,128]{3,2,1,0:T(8,128)(2,1)S(1)}, bf16[4,5,16,128]{3,2,1,0:T(8,128)(2,1)S(1)}, u32[]{:S(2)}, u32[]{:S(2)}) collective-permute-start(bf16[4,5,16,128]{3,2,1,0:T(8,128)(2,1)S(1)} %get-tuple-element.25), channel_id=1, source_target_pairs={{0,1},{1,0},{2,3},{3,2},{4,5},{5,4},{6,7},{7,6},{8,9},{9,8},{10,11... | collective-permute-start | bytes 245768 | tf_op jit(solution)/shard_map/ppermute | solution.py:564
  52.2 0.7 collective-permute-start.4
  52.9 2.3 %inner_part.1 = f32[4,5,16,128]{3,2,1,0:T(8,128)S(1)} custom-call(f32[4,3,4,96,128]{4,3,2,1,0:T(8,128)S(1)} %get-tuple-element.16.own, bf16[2,5,4,48,128]{4,3,2,1,0:T(8,128)(2,1)S(1)} %get-tuple-element.23.windows, bf16[4,768,512]{2,1,0:T(8,128)(2,1)S(1)} %get-tuple-element.22.patches, f32[5,4,56,128]{3,2,1,0:T(8,128)S(1)} %get-tuple-element.24.spread_in), custom_call_target="tpu_custom_call" | custom-call | flops 3623878656 | tf_op jit(solution)/shard_map/inner_part/pallas_call | solution.py:426
  55.3 7.5 %all_to_all.20.shares = bf16[4,5,16,128]{3,2,1,0:T(8,128)(2,1)S(1)} all-to-all(bf16[4,5,16,128]{3,2,1,0:T(8,128)(2,1)S(1)} %add_convert_fusion), channel_id=1, replica_groups=mesh['tm'=4,'height'=32] {'tm'}, dimensions={0} | all-to-all | bytes 163840 | tf_op jit(solution)/shard_map/all_to_all | solution.py:567
  62.8 0.8 weight_terms.1
  63.6 9.7 %all_to_all.21.got = bf16[4,384,128]{2,1,0:T(8,128)(2,1)S(1)} all-to-all(bf16[4,384,128]{2,1,0:T(8,128)(2,1)S(1)} %get-tuple-element.29), channel_id=1, replica_groups=mesh['tm'=4,'height'=32] {'tm'}, dimensions={0} | all-to-all | bytes 786432 | tf_op jit(solution)/shard_map/all_to_all | solution.py:570
  73.4 0.8 reshape.13
  74.2 14.7 %all-to-all-start.3 = ((bf16[32,2,768]{2,1,0:T(2,128)(2,1)}), bf16[32,2,768]{2,1,0:T(2,128)(2,1)S(1)}, u32[]{:S(2)}, u32[]{:S(2)}) async-start(bf16[32,2,768]{2,1,0:T(2,128)(2,1)} %reshape.13), calls=%async_computation.3 | async-start | bytes 196608 | tf_op jit(solution)/shard_map/all_to_all | solution.py:572
  88.9 3.6 %hidden_grad.1 = bf16[12,2,12,3072]{3,2,1,0:T(8,128)(2,1)S(1)} custom-call(bf16[12,2,12,3072]{3,2,1,0:T(8,128)(2,1)S(1)} %copy-done, bf16[12,2,16,64]{3,2,1,0:T(8,128)(2,1)S(1)} %get-tuple-element.28.token_grad, f32[1,3072]{1,0:T(1,128)S(1)} %bitcast.8, bf16[64,3072]{1,0:T(8,128)(2,1)S(1)} %bitcast.6), custom_call_target="tpu_custom_call" | custom-call | flops 150994944 | bytes 4718592 | tf_op jit(solution)/shard_map/hidden_grad/pallas_call | solution.py:527
  92.5 3.0 %copy.11 = bf16[12,2,12,3072]{3,1,2,0:T(2,128)(2,1)} copy(bf16[12,2,12,3072]{3,2,1,0:T(8,128)(2,1)S(1)} %hidden_grad.1) | data formatting | bytes 3538944
  95.6 2.1 %all-to-all-done.3 = bf16[32,2,768]{2,1,0:T(2,128)(2,1)S(1)} async-done(((bf16[32,2,768]{2,1,0:T(2,128)(2,1)}), bf16[32,2,768]{2,1,0:T(2,128)(2,1)S(1)}, u32[]{:S(2)}, u32[]{:S(2)}) %all-to-all-start.3) | async-done | bytes 98336 | tf_op jit(solution)/shard_map/all_to_all | solution.py:572
  97.7 0.2 reshape.14
  97.9 0.6 broadcast_multiply_fusion
  (23 shorter events, 0.3 us)
Async XLA Ops:
  0.6 6.9 %copy-start.2 = (bf16[3072,64]{0,1:T(8,128)(2,1)S(1)}, bf16[3072,64]{0,1:T(8,128)(2,1)}, u32[]{:S(2)}) copy-start(bf16[3072,64]{0,1:T(8,128)(2,1)} %param.10) | copy-start | bytes 1179652
  0.6 6.9 %copy-start.6 = (f32[3072]{0:T(1024)S(1)}, f32[3072]{0:T(1024)}, u32[]{:S(2)}) copy-start(f32[3072]{0:T(1024)} %param.9) | copy-start | bytes 36868
  0.7 6.9 %copy-start.5 = (f32[3072]{0:T(1024)S(1)}, f32[3072]{0:T(1024)}, u32[]{:S(2)}) copy-start(f32[3072]{0:T(1024)} %param.8) | copy-start | bytes 36868
  0.7 19.4 %collective-permute-start = (bf16[3,4,96,512]{3,2,1,0:T(8,128)(2,1)}, bf16[3,4,96,512]{3,2,1,0:T(8,128)(2,1)S(1)}, u32[]{:S(2)}, u32[]{:S(2)}) collective-permute-start(bf16[3,4,96,512]{3,2,1,0:T(8,128)(2,1)} %grad.3), channel_id=1, source_target_pairs={{32,0},{64,32},{96,64},{33,1},{65,33},{97,65},{34,2},{66,34},{98,6... | collective-permute-start | bytes 3538952 | tf_op jit(solution)/shard_map/ppermute | solution.py:552
  7.5 12.5 %copy-start.3 = (bf16[3,4,96,512]{3,2,1,0:T(8,128)(2,1)S(1)}, bf16[3,4,96,512]{3,2,1,0:T(8,128)(2,1)}, u32[]{:S(2)}) copy-start(bf16[3,4,96,512]{3,2,1,0:T(8,128)(2,1)} %grad.3) | copy-start | bytes 3538948
  13.0 7.1 %all-to-all-start = ((bf16[4,5,16,128]{3,2,1,0:T(8,128)(2,1)}), bf16[4,5,16,128]{3,2,1,0:T(8,128)(2,1)S(1)}, u32[]{:S(2)}, u32[]{:S(2)}) async-start(bf16[4,5,16,128]{3,2,1,0:T(8,128)(2,1)} %get-tuple-element.17), calls=%async_computation | async-start | bytes 163840 | tf_op jit(solution)/shard_map/all_to_all | solution.py:554
  21.5 19.5 %collective-permute-start.1 = (bf16[560,512]{1,0:T(8,128)(2,1)S(1)}, bf16[560,512]{1,0:T(8,128)(2,1)S(1)}, u32[]{:S(2)}, u32[]{:S(2)}) collective-permute-start(bf16[560,512]{1,0:T(8,128)(2,1)S(1)} %get-tuple-element.18), channel_id=1, source_target_pairs={{0,1},{1,0},{2,3},{3,2},{4,5},{5,4},{6,7},{7,6},{8,9},{9,8},{10,11... | collective-permute-start | bytes 1720328 | tf_op jit(solution)/shard_map/ppermute | solution.py:557
  23.2 17.8 %copy-start.4 = (bf16[3,3,3,16,512]{4,3,2,1,0:T(8,128)(2,1)S(1)}, bf16[3,3,3,16,512]{4,3,2,1,0:T(8,128)(2,1)}, u32[]{:S(2)}) copy-start(bf16[3,3,3,16,512]{4,3,2,1,0:T(8,128)(2,1)} %w_in.1) | copy-start | bytes 1327108
  23.2 17.8 %collective-permute-start.2 = (bf16[560,512]{1,0:T(8,128)(2,1)S(1)}, bf16[560,512]{1,0:T(8,128)(2,1)S(1)}, u32[]{:S(2)}, u32[]{:S(2)}) collective-permute-start(bf16[560,512]{1,0:T(8,128)(2,1)S(1)} %get-tuple-element.19), channel_id=1, source_target_pairs={{1,2},{2,1},{3,4},{4,3},{5,6},{6,5},{7,8},{8,7},{9,10},{10,9},{11,... | collective-permute-start | bytes 1720328 | tf_op jit(solution)/shard_map/ppermute | solution.py:556
  47.9 7.3 %collective-permute-start.3 = (bf16[4,5,16,128]{3,2,1,0:T(8,128)(2,1)S(1)}, bf16[4,5,16,128]{3,2,1,0:T(8,128)(2,1)S(1)}, u32[]{:S(2)}, u32[]{:S(2)}) collective-permute-start(bf16[4,5,16,128]{3,2,1,0:T(8,128)(2,1)S(1)} %get-tuple-element.25), channel_id=1, source_target_pairs={{0,1},{1,0},{2,3},{3,2},{4,5},{5,4},{6,7},{7,6},{8,9},{9,8},{10,11... | collective-permute-start | bytes 245768 | tf_op jit(solution)/shard_map/ppermute | solution.py:564
  52.2 3.0 %collective-permute-start.4 = (bf16[4,5,16,128]{3,2,1,0:T(8,128)(2,1)S(1)}, bf16[4,5,16,128]{3,2,1,0:T(8,128)(2,1)S(1)}, u32[]{:S(2)}, u32[]{:S(2)}) collective-permute-start(bf16[4,5,16,128]{3,2,1,0:T(8,128)(2,1)S(1)} %get-tuple-element.26), channel_id=1, source_target_pairs={{1,2},{2,1},{3,4},{4,3},{5,6},{6,5},{7,8},{8,7},{9,10},{10,9},{11,... | collective-permute-start | bytes 245768 | tf_op jit(solution)/shard_map/ppermute | solution.py:563
  52.9 9.9 %copy-start.1 = (bf16[12,2,16,3072]{3,2,1,0:T(8,128)(2,1)S(1)}, bf16[12,2,16,3072]{3,2,1,0:T(8,128)(2,1)}, u32[]{:S(2)}) copy-start(bf16[12,2,16,3072]{3,2,1,0:T(8,128)(2,1)} %get-tuple-element.27.modulated) | copy-start | bytes 7077892
  55.2 33.7 %copy-start = (bf16[12,2,12,3072]{3,2,1,0:T(8,128)(2,1)S(1)}, bf16[12,2,12,3072]{3,2,1,0:T(8,128)(2,1)}, u32[]{:S(2)}) copy-start(bf16[12,2,12,3072]{3,2,1,0:T(8,128)(2,1)} %copy.10.source.hidden) | copy-start | bytes 5308420
  74.2 23.5 %all-to-all-start.3 = ((bf16[32,2,768]{2,1,0:T(2,128)(2,1)}), bf16[32,2,768]{2,1,0:T(2,128)(2,1)S(1)}, u32[]{:S(2)}, u32[]{:S(2)}) async-start(bf16[32,2,768]{2,1,0:T(2,128)(2,1)} %reshape.13), calls=%async_computation.3 | async-start | bytes 196608 | tf_op jit(solution)/shard_map/all_to_all | solution.py:572

commit v6 on v5

--- a/solution.py
+++ b/solution.py
@@ -16,6 +16,7 @@
 whole = pl.BlockSpec(memory_space=pltpu.VMEM)
 scalars = pl.BlockSpec(memory_space=pltpu.SMEM)
 far_off = pl.BlockSpec(memory_space=pltpu.HBM)
+early = 1
 
 
 def params(mib):
@@ -38,78 +39,53 @@
     return shifted * inverse, inverse
 
 
-def modulate_kernel(source, scale, shift, w_out, modulated, send, hidden, rows, in_sems, out_sems):
+def modulate_kernel(places, hidden, scale, shift, w_out, modulated, *rest):
+    pieces, latent = rest[:-1], rest[-1]
     frames, token_rows, tokens, width = hidden.shape
-    groups = send.shape[0]
+    groups = len(pieces)
     block = frames // groups
     gain = 1.0 + scale[...]
     blank = jnp.zeros((slots - tokens, width), f32)
-    send[0, 0:2] = jnp.zeros_like(send[0, 0:2])
-
-    def in_copy(step):
-        at = pl.ds(step * block, block)
-        return pltpu.make_async_copy(source.at[at], hidden.at[at], in_sems.at[step])
-
-    for step in range(groups):
-        in_copy(step).start()
-
-    def out_copy(step):
-        at = pl.ds(step * block, block)
-        return pltpu.make_async_copy(rows.at[at], modulated.at[at], out_sems.at[step])
+    latent[0:2] = jnp.zeros_like(latent[0:2])
 
     def share(step, carry):
-        in_copy(step).wait()
         for frame in range(block):
             for row in range(token_rows):
                 normed, _ = normalise(hidden[step * block + frame, row].astype(f32))
                 value = jnp.concatenate([normed * gain + shift[...], blank], axis=0)
-                rows[step * block + frame, row] = value.astype(bf16)
-        out_copy(step).start()
-        value = rows[pl.ds(step * block, block)].reshape(-1, width)
+                modulated[step * block + frame, row] = value.astype(bf16)
+        value = modulated[pl.ds(step * block, block)].reshape(-1, width)
         value = dot_turned(value, w_out[...]).astype(bf16)
         value = value.reshape(block, token_rows, slots, value.shape[-1])
         paired = jnp.concatenate([value[:, 0], value[:, 1]], axis=-1)
-        for frame in range(block):
-            send[step, frame + 2] = paired[frame]
-
-        @pl.when(step < groups - 1)
-        def _():
-            for frame in range(1, block):
-                send[step + 1, frame - 1] = paired[frame]
-
+        latent[pl.ds(step * block + 2, block)] = paired
         return carry
 
     lax.fori_loop(0, groups, share, 0)
-    for step in range(groups):
-        out_copy(step).wait()
-
-
-def modulate(hidden, mod_scale, mod_shift, w_out, groups):
+    for step, piece in enumerate(pieces):
+        dst = lax.rem(places[2] + step, groups)
+        piece[...] = latent[pl.ds(dst * block, block + 2)]
+
+
+def modulate(places, hidden, mod_scale, mod_shift, w_out, groups):
     frames, token_rows, tokens, width = hidden.shape
-    token_width = w_out.shape[0]
-    out = jax.ShapeDtypeStruct((frames, token_rows, slots, width), bf16)
+    pair = 2 * w_out.shape[0]
+    piece = jax.ShapeDtypeStruct((frames // groups + 2, slots, pair), bf16)
     return pl.pallas_call(
         modulate_kernel,
-        out_shape=[
-            out,
-            jax.ShapeDtypeStruct((groups, frames // groups + 2, slots, 2 * token_width), bf16),
-        ],
-        in_specs=[far_off] + [whole] * 3,
-        out_specs=[far_off, whole],
-        scratch_shapes=[
-            pltpu.VMEM(hidden.shape, bf16),
-            pltpu.VMEM(out.shape, bf16),
-            pltpu.SemaphoreType.DMA((groups,)),
-            pltpu.SemaphoreType.DMA((groups,)),
-        ],
-        compiler_params=params(53),
+        out_shape=[jax.ShapeDtypeStruct((frames, token_rows, slots, width), bf16)]
+        + [piece] * groups,
+        in_specs=[scalars] + [whole] * 4,
+        out_specs=[whole] * (1 + groups),
+        scratch_shapes=[pltpu.VMEM((frames + 2, slots, pair), bf16)],
+        compiler_params=params(8),
         cost_estimate=pl.CostEstimate(
-            flops=2 * frames * 2 * slots * width * token_width,
+            flops=2 * frames * slots * width * pair,
             bytes_accessed=8 * frames * slots * width,
             transcendentals=0,
         ),
         name="modulate",
-    )(hidden, mod_scale.reshape(1, -1), mod_shift.reshape(1, -1), w_out)
+    )(places, hidden, mod_scale.reshape(1, -1), mod_shift.reshape(1, -1), w_out)
 
 
 def column_shifts(value):
@@ -128,27 +104,32 @@
     return value.reshape(-1, value.shape[-1])
 
 
-def weight_matrix(held, kt, ky):
-    return jnp.concatenate([held[kt, ky, kx] for kx in range(3)], axis=-1)
-
-
-def pack_kernel(places, grad, grad_ahead, latent, near, far, sems):
-    frames, _, cols, channels = grad.shape
+def weight_matrix(held_first, held_rest, n):
+    block = held_first[n] if n < early else held_rest[n - early]
+    return jnp.concatenate([block[kx] for kx in range(3)], axis=-1)
+
+
+def pack_kernel(
+    places, grad, grad_ahead, w_section, w_in, *rest
+):
+    pieces = rest[:4]
+    near, far, latent, shifts, patches, held, sems = rest[4:]
+    frames, rows, cols, channels = grad.shape
+    groups = len(pieces)
     copies = [
-        pltpu.make_async_copy(
-            grad.at[frame, places[side]],
-            out.at[frame * cols : (frame + 1) * cols],
-            sems.at[side * frames + frame],
-        )
-        for side, out in ((0, near), (1, far))
-        for frame in range(frames)
+        pltpu.make_async_copy(w_section.at[kt, ky], held.at[n], sems.at[n])
+        for n, (kt, ky) in enumerate(taps[:early])
     ]
     for copy in copies:
         copy.start()
+    for step, piece in enumerate(pieces):
+        latent[lax.rem(places[2] + groups - step, groups)] = piece[...]
     for side, out in ((0, near), (1, far)):
-        for frame in range(2):
-            at = (frames + frame) * cols
-            out[at : at + cols] = grad_ahead[frame, places[side]]
+        row = places[side]
+        for frame in range(frames + 2):
+            at = frame * cols
+            value = grad[frame, row] if frame < frames else grad_ahead[frame - frames, row]
+            out[at : at + cols] = value
         at = (frames + 2) * cols
         tail = flat(latent[...])
         count = tail.shape[0] * lanes // channels
@@ -156,36 +137,57 @@
             out[at : at + count, lane * lanes : (lane + 1) * lanes] = tail[
                 lane * count : (lane + 1) * count
             ]
-    for copy in copies:
-        copy.wait()
-
-
-def pack_rows(places, grad, grad_ahead, latent):
-    frames, _, cols, channels = grad.shape
-    total = (frames + 2) * cols + latent.size // channels
-    return pl.pallas_call(
-        pack_kernel,
-        in_specs=[scalars, far_off, whole, whole],
-        out_specs=[whole] * 2,
-        out_shape=[jax.ShapeDtypeStruct((total, channels), bf16)] * 2,
-        scratch_shapes=[pltpu.SemaphoreType.DMA((2 * frames,))],
-        compiler_params=params(4),
-        name="pack_rows",
-    )(places, grad, grad_ahead, latent)
-
-
-def own_kernel(grad, grad_ahead, w_section, total, held, shifts, sems):
-    frames, rows, cols, channels = grad.shape
-    copies = [
-        pltpu.make_async_copy(w_section.at[kt, ky], held.at[kt, ky], sems.at[n])
-        for n, (kt, ky) in enumerate(taps)
-    ]
-    for copy in copies:
-        copy.start()
     for frame in range(frames + 2):
         for row in range(rows):
             value = grad[frame, row] if frame < frames else grad_ahead[frame - frames, row]
             shifts[0, frame, row], shifts[1, frame, row] = column_shifts(value)
+
+    patches[...] = jnp.zeros_like(patches)
+    lat = w_in.shape[3]
+    for n in range(4 * 3 * 2 * 2 * 2 * 2):
+        p, q, kt, a, b, pp, qq = [
+            n // size % top
+            for size, top in ((96, 2), (48, 2), (16, 3), (8, 2), (4, 2), (2, 2), (1, 2))
+        ]
+        ky, kx = p - 1 + 2 * a + pp, q - 1 + 2 * b + qq
+        if 0 <= ky < 3 and 0 <= kx < 3:
+            at = (((kt * 2 + a) * 2 + b) * 4 + 2 * pp + qq) * lat
+            patches[2 * p + q, at : at + lat] = w_in[kt, ky, kx]
+    for copy in copies:
+        copy.wait()
+
+
+def pack_rows(places, grad, grad_ahead, w_section, w_in, pieces):
+    frames, rows, cols, channels = grad.shape
+    groups = len(pieces)
+    latent = jax.ShapeDtypeStruct((groups,) + pieces[0].shape, bf16)
+    total = (frames + 2) * cols + latent.size // channels
+    return pl.pallas_call(
+        pack_kernel,
+        in_specs=[scalars, whole, whole, far_off, whole] + [whole] * groups,
+        out_specs=[whole] * 6,
+        out_shape=[
+            jax.ShapeDtypeStruct((total, channels), bf16),
+            jax.ShapeDtypeStruct((total, channels), bf16),
+            latent,
+            jax.ShapeDtypeStruct((2, frames + 2, rows, cols, channels), bf16),
+            jax.ShapeDtypeStruct((4, 48 * w_in.shape[3], channels), bf16),
+            jax.ShapeDtypeStruct((early,) + w_section.shape[2:], bf16),
+        ],
+        scratch_shapes=[pltpu.SemaphoreType.DMA((early,))],
+        compiler_params=params(8),
+        name="pack_rows",
+    )(places, grad, grad_ahead, w_section, w_in, *pieces)
+
+
+def own_kernel(grad, grad_ahead, shifts, w_section, held_first, total, held_rest, sems):
+    frames, rows, cols, channels = grad.shape
+    copies = [
+        pltpu.make_async_copy(w_section.at[kt, ky], held_rest.at[n], sems.at[n])
+        for n, (kt, ky) in enumerate(taps[early:])
+    ]
+    for copy in copies:
+        copy.start()
     for n, (kt, ky) in enumerate(taps):
         lo, hi = max(0, ky - 1), rows + min(0, ky - 1)
         at = slice(lo + 1 - ky, hi + 1 - ky)
@@ -196,8 +198,9 @@
         window = jnp.concatenate(
             [flat(shifts[(0,) + src]), centre, flat(shifts[(1,) + src])], axis=-1
         )
-        copies[n].wait()
-        part = dot_turned(window, weight_matrix(held, kt, ky))
+        if n >= early:
+            copies[n - early].wait()
+        part = dot_turned(window, weight_matrix(held_first, held_rest, n))
         for lane in range(channels // lanes):
             value = part[:, lane * lanes : (lane + 1) * lanes]
             value = value.reshape(frames, hi - lo, cols, lanes)
@@ -207,31 +210,28 @@
                 total[lane, :, lo:hi] += value
 
 
-def own_part(grad, grad_ahead, w_section):
+def own_part(grad, grad_ahead, shifts, w_section, held_first):
     frames, rows, cols, channels = grad.shape
     return pl.pallas_call(
         own_kernel,
         out_shape=[
             jax.ShapeDtypeStruct((channels // lanes, frames, rows, cols, lanes), f32),
-            jax.ShapeDtypeStruct(w_section.shape, bf16),
+            jax.ShapeDtypeStruct((len(taps) - early,) + w_section.shape[2:], bf16),
         ],
-        in_specs=[whole, whole, far_off],
+        in_specs=[whole, whole, whole, far_off, whole],
         out_specs=[whole] * 2,
-        scratch_shapes=[
-            pltpu.VMEM((2, frames + 2, rows, cols, channels), bf16),
-            pltpu.SemaphoreType.DMA((len(taps),)),
-        ],
-        compiler_params=params(26),
+        scratch_shapes=[pltpu.SemaphoreType.DMA((len(taps) - early,))],
+        compiler_params=params(12),
         cost_estimate=pl.CostEstimate(
             flops=2 * 24 * grad.size * channels,
             bytes_accessed=2 * w_section.size,
             transcendentals=0,
         ),
         name="own_part",
-    )(grad, grad_ahead, w_section)
-
-
-def edge_kernel(places, own, near_rows, far_rows, held, w_in, total, patches, near):
+    )(grad, grad_ahead, shifts, w_section, held_first)
+
+
+def edge_kernel(places, own, near_rows, far_rows, held_first, held_rest, total, near):
     even = places[0] != 0
     blocks, frames, rows, cols, _ = own.shape
     for lane in range(blocks):
@@ -245,50 +245,34 @@
             near[1, side, frame] = value
             near[0, side, frame], near[2, side, frame] = column_shifts(value)
 
-    patches[...] = jnp.zeros_like(patches)
-    lat = w_in.shape[3]
-    for n in range(4 * 3 * 2 * 2 * 2 * 2):
-        p, q, kt, a, b, pp, qq = [
-            n // size % top
-            for size, top in ((96, 2), (48, 2), (16, 3), (8, 2), (4, 2), (2, 2), (1, 2))
-        ]
-        ky, kx = p - 1 + 2 * a + pp, q - 1 + 2 * b + qq
-        if 0 <= ky < 3 and 0 <= kx < 3:
-            at = (((kt * 2 + a) * 2 + b) * 4 + 2 * pp + qq) * lat
-            patches[2 * p + q, at : at + lat] = w_in[kt, ky, kx]
-
-    for kt, ky in taps:
+    for n, (kt, ky) in enumerate(taps):
         if ky == 1:
             continue
         side = 0 if ky == 2 else 1
         window = jnp.concatenate(
             [flat(near[kx, side, 2 - kt : frames + 2 - kt]) for kx in range(3)], axis=-1
         )
-        part = dot_turned(window, weight_matrix(held, kt, ky))
+        part = dot_turned(window, weight_matrix(held_first, held_rest, n))
         for lane in range(blocks):
             value = part[:, lane * lanes : (lane + 1) * lanes]
             total[lane, :, side] += value.reshape(frames, cols, lanes)
 
 
-def edge_part(places, own, near_rows, far_rows, held, w_in):
+def edge_part(places, own, near_rows, far_rows, held_first, held_rest):
     blocks, frames, _, cols, _ = own.shape
     channels = blocks * lanes
-    pair = 8 * w_in.shape[3]
     return pl.pallas_call(
         edge_kernel,
-        out_shape=[
-            jax.ShapeDtypeStruct((blocks, frames, 2, cols, lanes), f32),
-            jax.ShapeDtypeStruct((4, 6 * pair, channels), bf16),
-        ],
+        out_shape=jax.ShapeDtypeStruct((blocks, frames, 2, cols, lanes), f32),
         in_specs=[scalars] + [whole] * 5,
-        out_specs=[whole] * 2,
+        out_specs=whole,
         scratch_shapes=[pltpu.VMEM((3, 2, frames + 2, cols, channels), bf16)],
         compiler_params=params(10),
         cost_estimate=pl.CostEstimate(
             flops=2 * 4 * own.size * channels, bytes_accessed=0, transcendentals=0
         ),
         name="edge_part",
-    )(places, own, near_rows, far_rows, held, w_in)
+    )(places, own, near_rows, far_rows, held_first, held_rest)
 
 
 def latent_phase(total, slot_of, row_of, spread_row, windows, patches, spread):
@@ -440,48 +424,75 @@
     )(own, windows, patches, spread)
 
 
-def weight_kernel(shares, modulated, token_grad, send, field):
-    groups, depth, _, pair = shares.shape
+def share_kernel(places, centre, near_share, far_share, *pieces):
+    groups = len(pieces)
+    for step, piece in enumerate(pieces):
+        dst = lax.rem(places[2] + step, groups)
+        value = centre[dst] + near_share[dst].astype(f32) + far_share[dst].astype(f32)
+        piece[...] = value.astype(bf16)
+
+
+def share_pieces(places, centre, near_share, far_share):
+    groups = centre.shape[0]
+    return pl.pallas_call(
+        share_kernel,
+        out_shape=[jax.ShapeDtypeStruct(centre.shape[1:], bf16)] * groups,
+        in_specs=[scalars] + [whole] * 3,
+        out_specs=[whole] * groups,
+        compiler_params=params(4),
+        name="share_pieces",
+    )(places, centre, near_share, far_share)
+
+
+def weight_kernel(places, modulated, *rest):
+    shares, token_grad, pieces, (field, weight) = rest[:4], rest[4], rest[5:9], rest[9:]
+    groups = len(shares)
+    depth, _, pair = shares[0].shape
     width = pair // 2
-    frames, token_rows = modulated.shape[:2]
+    frames = modulated.shape[0]
     model = modulated.shape[-1]
     field[...] = jnp.zeros_like(field)
-    for src in range(groups):
-        at = src * (frames // groups)
-        field[at : at + depth] += shares[src].astype(f32)
+    for step, share in enumerate(shares):
+        src = lax.rem(places[2] + groups - step, groups)
+        field[pl.ds(src * (frames // groups), depth)] += share[...].astype(f32)
     values = field[2 : 2 + frames]
     token_grad[:, 0] = values[:, :, :width].astype(bf16)
     token_grad[:, 1] = values[:, :, width:].astype(bf16)
     turned = jnp.transpose(token_grad[...].reshape(-1, width).astype(f32)).astype(bf16)
-    weight = dot(turned, modulated[...].reshape(-1, model))
+    total = dot(turned, modulated[...].reshape(-1, model))
     half = model // (2 * groups)
     for dst in range(groups):
         at = 2 * half * dst
-        stacked = jnp.concatenate(
-            [weight[:, at : at + half], weight[:, at + half : at + 2 * half]], axis=0
-        )
-        send[dst] = jnp.transpose(stacked).astype(bf16)
-
-
-def weight_terms(shares, modulated):
-    groups, depth, _, pair = shares.shape
+        weight[dst, :width] = total[:, at : at + half]
+        weight[dst, width:] = total[:, at + half : at + 2 * half]
+    for step, piece in enumerate(pieces):
+        dst = lax.rem(places[2] + step, groups)
+        piece[...] = jnp.transpose(weight[dst]).astype(bf16)
+
+
+def weight_terms(places, modulated, shares):
+    groups = len(shares)
+    depth, _, pair = shares[0].shape
     frames, token_rows, _, model = modulated.shape
+    half = model // (2 * groups)
     return pl.pallas_call(
         weight_kernel,
-        out_shape=[
-            jax.ShapeDtypeStruct((frames, token_rows, slots, pair // 2), bf16),
-            jax.ShapeDtypeStruct((groups, model // (2 * groups), pair), bf16),
+        out_shape=[jax.ShapeDtypeStruct((frames, token_rows, slots, pair // 2), bf16)]
+        + [jax.ShapeDtypeStruct((half, pair), bf16)] * groups,
+        in_specs=[scalars] + [whole] * (1 + groups),
+        out_specs=[whole] * (1 + groups),
+        scratch_shapes=[
+            pltpu.VMEM((frames + 2, slots, pair), f32),
+            pltpu.VMEM((groups, pair, half), f32),
         ],
-        in_specs=[whole] * 2,
-        out_specs=[whole] * 2,
-        scratch_shapes=[pltpu.VMEM((frames + 2, slots, pair), f32)],
         compiler_params=params(12),
         name="weight_terms",
-    )(shares, modulated)
-
-
-def middle_kernel(got, send):
-    total = jnp.sum(got[...].astype(f32), axis=0)
+    )(places, modulated, *shares)
+
+
+def middle_kernel(*refs):
+    send = refs[-1]
+    total = sum(ref[...].astype(f32) for ref in refs[:-1])
     count, rows, width = send.shape
     total = total.reshape(count // 2, rows, 2 * width).astype(bf16)
     send[0 : count // 2] = total[:, :, :width]
@@ -489,15 +500,15 @@
 
 
 def middle_sum(got, count):
-    groups, depth, pair = got.shape
+    depth, pair = got[0].shape
     return pl.pallas_call(
         middle_kernel,
         out_shape=jax.ShapeDtypeStruct((count, 2 * depth // count, pair // 2), bf16),
-        in_specs=[whole],
+        in_specs=[whole] * len(got),
         out_specs=whole,
         compiler_params=params(4),
         name="middle_sum",
-    )(got)
+    )(*got)
 
 
 def hidden_kernel(hidden, token_grad, scale, w_out, grad_hidden):
@@ -546,28 +557,35 @@
     near = sum([swap(i, i + 1) for i in range(0, strips - 1, 2)], [])
     far = sum([swap(i, i + 1) for i in range(1, strips - 1, 2)], [])
     odd = lax.rem(lax.axis_index("height"), 2)
-    places = jnp.stack([(1 - odd) * (rows - 1), odd * (rows - 1)]).astype(jnp.int32)
+    places = jnp.stack([(1 - odd) * (rows - 1), odd * (rows - 1), lax.axis_index("tm")])
+    places = places.astype(jnp.int32)
     w_out = jnp.transpose(w_out)
+    w_section = pltpu.with_memory_space_constraint(w_section, pltpu.HBM)
+
+    def round_tm(pieces):
+        hops = lambda k: [(g, (g + k) % groups) for g in range(groups)]
+        return [pieces[0]] + [
+            lax.ppermute(pieces[k], "tm", hops(k)) for k in range(1, groups)
+        ]
 
     grad_ahead = lax.ppermute(section_grad, "tm", [(g + 1, g) for g in range(groups - 1)])
-    modulated, latent_send = modulate(hidden, mod_scale, mod_shift, w_out, groups)
-    latent = lax.all_to_all(latent_send, "tm", 0, 0, tiled=True)
-    near_send, far_send = pack_rows(places, section_grad, grad_ahead, latent)
+    modulated, *pieces = modulate(places, hidden, mod_scale, mod_shift, w_out, groups)
+    near_send, far_send, latent, shifts, patches, held_first = pack_rows(
+        places, section_grad, grad_ahead, w_section, w_in, round_tm(pieces)
+    )
     far_rows = lax.ppermute(far_send, "height", far)
     near_rows = lax.ppermute(near_send, "height", near)
-    own, held = own_part(section_grad, grad_ahead, w_section)
-    edge, patches = edge_part(places, own, near_rows, far_rows, held, w_in)
+    own, held_rest = own_part(section_grad, grad_ahead, shifts, w_section, held_first)
+    edge = edge_part(places, own, near_rows, far_rows, held_first, held_rest)
     near_share, far_share, windows, spread = edge_latent(
         places, edge, latent, near_rows, far_rows, patches
     )
     far_share = lax.ppermute(far_share, "height", far)
     near_share = lax.ppermute(near_share, "height", near)
     centre = inner_part(own, windows, patches, spread, groups)
-    centre = centre + near_share.astype(f32) + far_share.astype(f32)
-    shares = lax.all_to_all(centre.astype(bf16), "tm", 0, 0, tiled=True)
-
-    token_grad, send = weight_terms(shares, modulated)
-    got = lax.all_to_all(send, "tm", 0, 0, tiled=True)
+    shares = round_tm(share_pieces(places, centre, near_share, far_share))
+    token_grad, *pieces = weight_terms(places, modulated, shares)
+    got = round_tm(pieces)
     grad_hidden = hidden_grad(hidden, token_grad, mod_scale, w_out)
     pieces = lax.all_to_all(middle_sum(got, strips), "height", 0, 0, tiled=True)
     total_tokens = math.prod(hidden.shape[:3]) * groups * strips

time: 100 us -> 97.2 us (0.972); the launches traced: 98.5 us -> 96.9 us
  blocking collectives: 17.2 us -> 0 us
  waiting for transfers between devices: 5.82 us -> 18 us
  starting transfers between devices: 29 us -> 32.6 us
  local copies, waits for them, and re-layouts: 7.41 us -> 5.98 us
  Pallas kernels: 37.5 us -> 38.7 us
    all_to_all x2 -> x0, blocking collectives: 17.2 us -> none  [the longest x1 9.7 us: shards(): got = lax.all_to_all(send, 'tm', 0, 0, tiled=True)]
    ppermute x0 -> x9, waiting for transfers between devices: none -> 15.5 us  [round_tm(): lax.ppermute(pieces[k], 'tm', hops(k))]
    ppermute x0 -> x9, starting transfers between devices: none -> 6.72 us  [round_tm(): lax.ppermute(pieces[k], 'tm', hops(k))]
    all_to_all x1 -> x0, waiting for transfers between devices: 3.7 us -> none  [shards(): latent = lax.all_to_all(latent_send, 'tm', 0, 0, tiled=True)]
    all_to_all x1 -> x0, starting transfers between devices: 3.3 us -> none  [shards(): latent = lax.all_to_all(latent_send, 'tm', 0, 0, tiled=True)]
    unnamed x18 -> x14, local copies, waits for them, and re-layouts: 7.41 us -> 5.98 us
    pallas_call x3 -> x4, Pallas kernels: 10.7 us -> 10.5 us  [the longest x1 3.71 us: modulate(): pl.pallas_call(modulate_kernel, out_shape=[jax.ShapeDtypeStruct((frames,...]
  transfers between devices with their start and end apart: 7 -> 15, of which waited for: 2 -> 8; matrix products, arithmetic and copies ran while one was open for 7% -> 5% of each run, Pallas kernels for 29% -> 28%
where the time goes in v6:
time: 97.2 us; the launch traced here: 96.9 us
  Pallas kernels  38.7 us (40%)
  starting transfers between devices  32.6 us (34%)
  waiting for transfers between devices  18 us (19%)
  local copies, waits for them, and re-layouts  5.98 us (6%)
    pallas_call x1, Pallas kernels, own_part(): pl.pallas_call(own_kernel, out_shape=[jax.ShapeDtypeStruct((channels // l...  17.7 us
    ppermute x9, waiting for transfers between devices, round_tm(): lax.ppermute(pieces[k], 'tm', hops(k))  15.5 us
    all_to_all x1, starting transfers between devices, shards(): pieces = lax.all_to_all(middle_sum(got, strips), 'height', 0, 0, tiled=True)  15 us
    ppermute x9, starting transfers between devices, round_tm(): lax.ppermute(pieces[k], 'tm', hops(k))  6.72 us
    unnamed x14, local copies, waits for them, and re-layouts  5.98 us
    ppermute x1, starting transfers between devices, shards(): near_share = lax.ppermute(near_share, 'height', near)  4.27 us
    pallas_call x1, Pallas kernels, modulate(): pl.pallas_call(modulate_kernel, out_shape=[jax.ShapeDtypeStruct((frames,...  3.71 us
    pallas_call x1, Pallas kernels, hidden_grad(): pl.pallas_call(hidden_kernel, out_shape=jax.ShapeDtypeStruct(hidden.shape...  3.61 us
  transfers between devices with their start and end apart: 15, of which 8 were waited for; matrix products, arithmetic and copies ran while one was open for 5% of the time, Pallas kernels for 28%

profile of v6, /device:TPU:1, one launch (start us, length us, event | category | flops | bytes accessed | tf_op | source)
XLA Modules:
  0.0 96.9 jit_solution(2600676854200040293)
XLA Ops:
  0.7 3.5 %collective-permute-start = (bf16[3,4,96,512]{3,2,1,0:T(8,128)(2,1)}, bf16[3,4,96,512]{3,2,1,0:T(8,128)(2,1)}, u32[]{:S(2)}, u32[]{:S(2)}) collective-permute-start(bf16[3,4,96,512]{3,2,1,0:T(8,128)(2,1)} %grad.3), channel_id=1, source_target_pairs={{32,0},{64,32},{96,64},{33,1},{65,33},{97,65},{34,2},{66,34},{98,6... | collective-permute-start | bytes 3538952 | tf_op jit(solution)/shard_map/ppermute | solution.py:571
  4.1 1.9 %copy.10.hidden = bf16[12,2,12,3072]{3,2,1,0:T(8,128)(2,1)S(1)} copy(bf16[12,2,12,3072]{3,1,2,0:T(2,128)(2,1)} %param.7) | data formatting | bytes 3538944 | tf_op args[0]
  6.2 3.7 %modulate.1 = (bf16[12,2,16,3072]{3,2,1,0:T(8,128)(2,1)S(1)}, bf16[5,16,128]{2,1,0:T(8,128)(2,1)S(1)}, bf16[5,16,128]{2,1,0:T(8,128)(2,1)S(1)}, bf16[5,16,128]{2,1,0:T(8,128)(2,1)S(1)}, bf16[5,16,128]{2,1,0:T(8,128)(2,1)S(1)}) custom-call(s32[3]{0:T(128)S(1)} %pad_add_fusion.places, bf16[12,2,12,3072]{3,2,1,0:T(8,128)(2,1)S(1)} %copy.10.hidden, ...), custom_call_target="tpu_custom_call" | custom-call | flops 150994944 | bytes 4718592 | tf_op jit(solution)/shard_map/modulate/pallas_call | solution.py:74
  9.9 1.3 %collective-permute-start.1 = (bf16[5,16,128]{2,1,0:T(8,128)(2,1)S(1)}, bf16[5,16,128]{2,1,0:T(8,128)(2,1)S(1)}, u32[]{:S(2)}, u32[]{:S(2)}) collective-permute-start(bf16[5,16,128]{2,1,0:T(8,128)(2,1)S(1)} %get-tuple-element.30), channel_id=1, source_target_pairs={{0,32},{32,64},{64,96},{96,0},{1,33},{33,65},{65,97},{97,1},{2,34}... | collective-permute-start | bytes 61448 | tf_op jit(solution)/shard_map/ppermute | solution.py:568
  11.2 1.2 %collective-permute-start.2 = (bf16[5,16,128]{2,1,0:T(8,128)(2,1)S(1)}, bf16[5,16,128]{2,1,0:T(8,128)(2,1)S(1)}, u32[]{:S(2)}, u32[]{:S(2)}) collective-permute-start(bf16[5,16,128]{2,1,0:T(8,128)(2,1)S(1)} %get-tuple-element.31), channel_id=1, source_target_pairs={{0,64},{32,96},{64,0},{96,32},{1,65},{33,97},{65,1},{97,33},{2,66}... | collective-permute-start | bytes 61448 | tf_op jit(solution)/shard_map/ppermute | solution.py:568
  13.1 1.1 %collective-permute-done.2.rest_2_ = bf16[5,16,128]{2,1,0:T(8,128)(2,1)S(1)} collective-permute-done((bf16[5,16,128]{2,1,0:T(8,128)(2,1)S(1)}, bf16[5,16,128]{2,1,0:T(8,128)(2,1)S(1)}, u32[]{:S(2)}, u32[]{:S(2)}) %collective-permute-start.2) | collective-permute-done | bytes 20512 | tf_op jit(solution)/shard_map/ppermute | solution.py:568
  14.2 6.2 %collective-permute-done.3.rest_3_ = bf16[5,16,128]{2,1,0:T(8,128)(2,1)S(1)} collective-permute-done((bf16[5,16,128]{2,1,0:T(8,128)(2,1)S(1)}, bf16[5,16,128]{2,1,0:T(8,128)(2,1)S(1)}, u32[]{:S(2)}, u32[]{:S(2)}) %collective-permute-start.3) | collective-permute-done | bytes 20512 | tf_op jit(solution)/shard_map/ppermute | solution.py:568
  20.4 2.7 %pack_rows.1 = (bf16[560,512]{1,0:T(8,128)(2,1)S(1)}, bf16[560,512]{1,0:T(8,128)(2,1)S(1)}, bf16[4,5,16,128]{3,2,1,0:T(8,128)(2,1)S(1)}, bf16[2,5,4,96,512]{4,3,...) custom-call(s32[3]{0:T(128)S(1)} %pad_add_fusion.places, ...), custom_call_target="tpu_custom_call" | custom-call | tf_op jit(solution)/shard_map/pack_rows/pallas_call | solution.py:165
  23.1 1.7 %collective-permute-start.4 = (bf16[560,512]{1,0:T(8,128)(2,1)S(1)}, bf16[560,512]{1,0:T(8,128)(2,1)S(1)}, u32[]{:S(2)}, u32[]{:S(2)}) collective-permute-start(bf16[560,512]{1,0:T(8,128)(2,1)S(1)} %get-tuple-element.36), channel_id=1, source_target_pairs={{0,1},{1,0},{2,3},{3,2},{4,5},{5,4},{6,7},{7,6},{8,9},{9,8},{10,11... | collective-permute-start | bytes 1720328 | tf_op jit(solution)/shard_map/ppermute | solution.py:577
  25.7 17.7 %own_part.1 = (f32[4,3,4,96,128]{4,3,2,1,0:T(8,128)S(1)}, bf16[8,3,512,512]{3,2,1,0:T(8,128)(2,1)S(1)}) custom-call(bf16[3,4,96,512]{3,2,1,0:T(8,128)(2,1)S(1)} %copy-done.1, bf16[3,4,96,512]{3,2,1,0:T(8,128)(2,1)} %collective-permute-done.grad_ahead, bf16[2,5,4,96,512]{4,3,2,1,0:T(8,128)(2,1)S(1)} %get-tuple-element.33.shifts, ...), custom_call_target="tpu_custom_call" | custom-call | flops 14495514624 | bytes 14155776 | tf_op jit(solution)/shard_map/own_part/pallas_call | solution.py:215
  43.4 3.5 %edge_part.1.total = f32[4,3,2,96,128]{4,3,2,1,0:T(8,128)S(1)} custom-call(s32[3]{0:T(128)S(1)} %pad_add_fusion.places, f32[4,3,4,96,128]{4,3,2,1,0:T(8,128)S(1)} %get-tuple-element.35.own, bf16[560,512]{1,0:T(8,128)(2,1)S(1)} %collective-permute-done.4.near_rows, bf16[560,512]{1,0:T(8,128)(2,1)S(1)} %collective-permute-done.5.far_rows, ...), custom_call_target="tpu_custom_call" | custom-call | flops 2415919104 | tf_op jit(solution)/shard_map/edge_part/pallas_call | solution.py:264
  46.9 3.2 %edge_latent.1 = (bf16[4,5,16,128]{3,2,1,0:T(8,128)(2,1)S(1)}, bf16[4,5,16,128]{3,2,1,0:T(8,128)(2,1)S(1)}, bf16[2,5,4,48,128]{4,3,2,1,0:T(8,128)(2,1)S(1)}, f32[5,4,56,128]{3,2,1,0:T(8,128)S(1)}) custom-call(s32[3]{0:T(128)S(1)} %pad_add_fusion.places, f32[4,3,2,96,128]{4,3,2,1,0:T(8,128)S(1)} %edge_part.1.total, ...), custom_call_target="tpu_custom_call" | custom-call | tf_op jit(solution)/shard_map/edge_latent/pallas_call | solution.py:375
  50.0 4.3 %collective-permute-start.6 = (bf16[4,5,16,128]{3,2,1,0:T(8,128)(2,1)S(1)}, bf16[4,5,16,128]{3,2,1,0:T(8,128)(2,1)S(1)}, u32[]{:S(2)}, u32[]{:S(2)}) collective-permute-start(bf16[4,5,16,128]{3,2,1,0:T(8,128)(2,1)S(1)} %get-tuple-element.43), channel_id=1, source_target_pairs={{0,1},{1,0},{2,3},{3,2},{4,5},{5,4},{6,7},{7,6},{8,9},{9,8},{10,11... | collective-permute-start | bytes 245768 | tf_op jit(solution)/shard_map/ppermute | solution.py:584
  55.0 2.2 %inner_part.1.centre = f32[4,5,16,128]{3,2,1,0:T(8,128)S(1)} custom-call(f32[4,3,4,96,128]{4,3,2,1,0:T(8,128)S(1)} %get-tuple-element.35.own, bf16[2,5,4,48,128]{4,3,2,1,0:T(8,128)(2,1)S(1)} %get-tuple-element.41.windows, bf16[4,768,512]{2,1,0:T(8,128)(2,1)S(1)} %get-tuple-element.40.patches, f32[5,4,56,128]{3,2,1,0:T(8,128)S(1)} %get-tuple-element.42.spread_in), custom_call_target="tpu_custom_call" | custom-call | flops 3623878656 | tf_op jit(solution)/shard_map/inner_part/pallas_call | solution.py:410
  58.5 2.0 %collective-permute-start.9 = (bf16[5,16,128]{2,1,0:T(8,128)(2,1)S(1)}, bf16[5,16,128]{2,1,0:T(8,128)(2,1)S(1)}, u32[]{:S(2)}, u32[]{:S(2)}) collective-permute-start(bf16[5,16,128]{2,1,0:T(8,128)(2,1)S(1)} %get-tuple-element.47), channel_id=1, source_target_pairs={{0,64},{32,96},{64,0},{96,32},{1,65},{33,97},{65,1},{97,33},{2,66}... | collective-permute-start | bytes 61448 | tf_op jit(solution)/shard_map/ppermute | solution.py:568
  60.5 1.5 %collective-permute-done.9.rest_2_ = bf16[5,16,128]{2,1,0:T(8,128)(2,1)S(1)} collective-permute-done((bf16[5,16,128]{2,1,0:T(8,128)(2,1)S(1)}, bf16[5,16,128]{2,1,0:T(8,128)(2,1)S(1)}, u32[]{:S(2)}, u32[]{:S(2)}) %collective-permute-start.9) | collective-permute-done | bytes 20512 | tf_op jit(solution)/shard_map/ppermute | solution.py:568
  61.9 1.7 %collective-permute-done.10.rest_3_ = bf16[5,16,128]{2,1,0:T(8,128)(2,1)S(1)} collective-permute-done((bf16[5,16,128]{2,1,0:T(8,128)(2,1)S(1)}, bf16[5,16,128]{2,1,0:T(8,128)(2,1)S(1)}, u32[]{:S(2)}, u32[]{:S(2)}) %collective-permute-start.10) | collective-permute-done | bytes 20512 | tf_op jit(solution)/shard_map/ppermute | solution.py:568
  63.7 1.4 %weight_terms.1 = (bf16[12,2,16,64]{3,2,1,0:T(8,128)(2,1)S(1)}, bf16[384,128]{1,0:T(8,128)(2,1)S(1)}, bf16[384,128]{1,0:T(8,128)(2,1)S(1)}, bf16[384,128]{1,0:T(8,128)(2,1)S(1)}, bf16[384,128]{1,0:T(8,128)(2,1)S(1)}) custom-call(s32[3]{0:T(128)S(1)} %pad_add_fusion.places, bf16[12,2,16,3072]{3,2,1,0:T(8,128)(2,1)S(1)} %get-tuple-element.28.modulated, ...), custom_call_target="tpu_custom_call" | custom-call | tf_op jit(solution)/shard_map/weight_terms/pallas_call | solution.py:478
  66.8 2.6 %collective-permute-done.12.refs_2_ = bf16[384,128]{1,0:T(8,128)(2,1)S(1)} collective-permute-done((bf16[384,128]{1,0:T(8,128)(2,1)S(1)}, bf16[384,128]{1,0:T(8,128)(2,1)S(1)}, u32[]{:S(2)}, u32[]{:S(2)}) %collective-permute-start.12) | collective-permute-done | bytes 98336 | tf_op jit(solution)/shard_map/ppermute | solution.py:568
  69.5 1.5 %collective-permute-done.13.refs_3_ = bf16[384,128]{1,0:T(8,128)(2,1)S(1)} collective-permute-done((bf16[384,128]{1,0:T(8,128)(2,1)S(1)}, bf16[384,128]{1,0:T(8,128)(2,1)S(1)}, u32[]{:S(2)}, u32[]{:S(2)}) %collective-permute-start.13) | collective-permute-done | bytes 98336 | tf_op jit(solution)/shard_map/ppermute | solution.py:568
  71.9 15.0 %all-to-all-start = ((bf16[32,2,768]{2,1,0:T(2,128)(2,1)}), bf16[32,2,768]{2,1,0:T(2,128)(2,1)S(1)}, u32[]{:S(2)}, u32[]{:S(2)}) async-start(bf16[32,2,768]{2,1,0:T(2,128)(2,1)} %reshape.13), calls=%async_computation | async-start | bytes 196608 | tf_op jit(solution)/shard_map/all_to_all | solution.py:590
  86.9 3.6 %hidden_grad.1 = bf16[12,2,12,3072]{3,2,1,0:T(8,128)(2,1)S(1)} custom-call(bf16[12,2,12,3072]{3,2,1,0:T(8,128)(2,1)S(1)} %copy.10.hidden, bf16[12,2,16,64]{3,2,1,0:T(8,128)(2,1)S(1)} %get-tuple-element.49.token_grad, f32[1,3072]{1,0:T(1,128)S(1)} %bitcast.9, bf16[64,3072]{1,0:T(8,128)(2,1)S(1)} %bitcast.7), custom_call_target="tpu_custom_call" | custom-call | flops 150994944 | bytes 4718592 | tf_op jit(solution)/shard_map/hidden_grad/pallas_call | solution.py:538
  90.5 3.0 %copy.11 = bf16[12,2,12,3072]{3,1,2,0:T(2,128)(2,1)} copy(bf16[12,2,12,3072]{3,2,1,0:T(8,128)(2,1)S(1)} %hidden_grad.1) | data formatting | bytes 3538944
  93.6 2.5 %all-to-all-done = bf16[32,2,768]{2,1,0:T(2,128)(2,1)S(1)} async-done(((bf16[32,2,768]{2,1,0:T(2,128)(2,1)}), bf16[32,2,768]{2,1,0:T(2,128)(2,1)S(1)}, u32[]{:S(2)}, u32[]{:S(2)}) %all-to-all-start) | async-done | bytes 98336 | tf_op jit(solution)/shard_map/all_to_all | solution.py:590
  (33 shorter events, 7.1 us)
Async XLA Ops:
  0.6 5.6 %copy-start = (bf16[3072,64]{0,1:T(8,128)(2,1)S(1)}, bf16[3072,64]{0,1:T(8,128)(2,1)}, u32[]{:S(2)}) copy-start(bf16[3072,64]{0,1:T(8,128)(2,1)} %param.10) | copy-start | bytes 1179652
  0.6 5.6 %copy-start.4 = (f32[3072]{0:T(1024)S(1)}, f32[3072]{0:T(1024)}, u32[]{:S(2)}) copy-start(f32[3072]{0:T(1024)} %param.9) | copy-start | bytes 36868
  0.7 5.6 %copy-start.3 = (f32[3072]{0:T(1024)S(1)}, f32[3072]{0:T(1024)}, u32[]{:S(2)}) copy-start(f32[3072]{0:T(1024)} %param.8) | copy-start | bytes 36868
  0.7 19.7 %collective-permute-start = (bf16[3,4,96,512]{3,2,1,0:T(8,128)(2,1)}, bf16[3,4,96,512]{3,2,1,0:T(8,128)(2,1)}, u32[]{:S(2)}, u32[]{:S(2)}) collective-permute-start(bf16[3,4,96,512]{3,2,1,0:T(8,128)(2,1)} %grad.3), channel_id=1, source_target_pairs={{32,0},{64,32},{96,64},{33,1},{65,33},{97,65},{34,2},{66,34},{98,6... | collective-permute-start | bytes 3538952 | tf_op jit(solution)/shard_map/ppermute | solution.py:571
  6.1 14.3 %copy-start.1 = (bf16[3,4,96,512]{3,2,1,0:T(8,128)(2,1)S(1)}, bf16[3,4,96,512]{3,2,1,0:T(8,128)(2,1)}, u32[]{:S(2)}) copy-start(bf16[3,4,96,512]{3,2,1,0:T(8,128)(2,1)} %grad.3) | copy-start | bytes 3538948
  6.1 14.2 %copy-start.2 = (bf16[3,3,3,16,512]{4,3,2,1,0:T(8,128)(2,1)S(1)}, bf16[3,3,3,16,512]{4,3,2,1,0:T(8,128)(2,1)}, u32[]{:S(2)}) copy-start(bf16[3,3,3,16,512]{4,3,2,1,0:T(8,128)(2,1)} %w_in.1) | copy-start | bytes 1327108
  9.9 3.2 %collective-permute-start.1 = (bf16[5,16,128]{2,1,0:T(8,128)(2,1)S(1)}, bf16[5,16,128]{2,1,0:T(8,128)(2,1)S(1)}, u32[]{:S(2)}, u32[]{:S(2)}) collective-permute-start(bf16[5,16,128]{2,1,0:T(8,128)(2,1)S(1)} %get-tuple-element.30), channel_id=1, source_target_pairs={{0,32},{32,64},{64,96},{96,0},{1,33},{33,65},{65,97},{97,1},{2,34}... | collective-permute-start | bytes 61448 | tf_op jit(solution)/shard_map/ppermute | solution.py:568
  11.2 3.0 %collective-permute-start.2 = (bf16[5,16,128]{2,1,0:T(8,128)(2,1)S(1)}, bf16[5,16,128]{2,1,0:T(8,128)(2,1)S(1)}, u32[]{:S(2)}, u32[]{:S(2)}) collective-permute-start(bf16[5,16,128]{2,1,0:T(8,128)(2,1)S(1)} %get-tuple-element.31), channel_id=1, source_target_pairs={{0,64},{32,96},{64,0},{96,32},{1,65},{33,97},{65,1},{97,33},{2,66}... | collective-permute-start | bytes 61448 | tf_op jit(solution)/shard_map/ppermute | solution.py:568
  12.4 8.0 %collective-permute-start.3 = (bf16[5,16,128]{2,1,0:T(8,128)(2,1)S(1)}, bf16[5,16,128]{2,1,0:T(8,128)(2,1)S(1)}, u32[]{:S(2)}, u32[]{:S(2)}) collective-permute-start(bf16[5,16,128]{2,1,0:T(8,128)(2,1)S(1)} %get-tuple-element.32), channel_id=1, source_target_pairs={{0,96},{32,0},{64,32},{96,64},{1,97},{33,1},{65,33},{97,65},{2,98}... | collective-permute-start | bytes 61448 | tf_op jit(solution)/shard_map/ppermute | solution.py:568
  23.1 20.3 %collective-permute-start.4 = (bf16[560,512]{1,0:T(8,128)(2,1)S(1)}, bf16[560,512]{1,0:T(8,128)(2,1)S(1)}, u32[]{:S(2)}, u32[]{:S(2)}) collective-permute-start(bf16[560,512]{1,0:T(8,128)(2,1)S(1)} %get-tuple-element.36), channel_id=1, source_target_pairs={{0,1},{1,0},{2,3},{3,2},{4,5},{5,4},{6,7},{7,6},{8,9},{9,8},{10,11... | collective-permute-start | bytes 1720328 | tf_op jit(solution)/shard_map/ppermute | solution.py:577
  24.8 18.6 %collective-permute-start.5 = (bf16[560,512]{1,0:T(8,128)(2,1)S(1)}, bf16[560,512]{1,0:T(8,128)(2,1)S(1)}, u32[]{:S(2)}, u32[]{:S(2)}) collective-permute-start(bf16[560,512]{1,0:T(8,128)(2,1)S(1)} %get-tuple-element.37), channel_id=1, source_target_pairs={{1,2},{2,1},{3,4},{4,3},{5,6},{6,5},{7,8},{8,7},{9,10},{10,9},{11,... | collective-permute-start | bytes 1720328 | tf_op jit(solution)/shard_map/ppermute | solution.py:576
  50.0 7.2 %collective-permute-start.6 = (bf16[4,5,16,128]{3,2,1,0:T(8,128)(2,1)S(1)}, bf16[4,5,16,128]{3,2,1,0:T(8,128)(2,1)S(1)}, u32[]{:S(2)}, u32[]{:S(2)}) collective-permute-start(bf16[4,5,16,128]{3,2,1,0:T(8,128)(2,1)S(1)} %get-tuple-element.43), channel_id=1, source_target_pairs={{0,1},{1,0},{2,3},{3,2},{4,5},{5,4},{6,7},{7,6},{8,9},{9,8},{10,11... | collective-permute-start | bytes 245768 | tf_op jit(solution)/shard_map/ppermute | solution.py:584
  54.3 2.9 %collective-permute-start.7 = (bf16[4,5,16,128]{3,2,1,0:T(8,128)(2,1)S(1)}, bf16[4,5,16,128]{3,2,1,0:T(8,128)(2,1)S(1)}, u32[]{:S(2)}, u32[]{:S(2)}) collective-permute-start(bf16[4,5,16,128]{3,2,1,0:T(8,128)(2,1)S(1)} %get-tuple-element.44), channel_id=1, source_target_pairs={{1,2},{2,1},{3,4},{4,3},{5,6},{6,5},{7,8},{8,7},{9,10},{10,9},{11,... | collective-permute-start | bytes 245768 | tf_op jit(solution)/shard_map/ppermute | solution.py:583
  57.8 2.7 %collective-permute-start.8 = (bf16[5,16,128]{2,1,0:T(8,128)(2,1)S(1)}, bf16[5,16,128]{2,1,0:T(8,128)(2,1)S(1)}, u32[]{:S(2)}, u32[]{:S(2)}) collective-permute-start(bf16[5,16,128]{2,1,0:T(8,128)(2,1)S(1)} %get-tuple-element.46), channel_id=1, source_target_pairs={{0,32},{32,64},{64,96},{96,0},{1,33},{33,65},{65,97},{97,1},{2,34}... | collective-permute-start | bytes 61448 | tf_op jit(solution)/shard_map/ppermute | solution.py:568
  58.5 3.5 %collective-permute-start.9 = (bf16[5,16,128]{2,1,0:T(8,128)(2,1)S(1)}, bf16[5,16,128]{2,1,0:T(8,128)(2,1)S(1)}, u32[]{:S(2)}, u32[]{:S(2)}) collective-permute-start(bf16[5,16,128]{2,1,0:T(8,128)(2,1)S(1)} %get-tuple-element.47), channel_id=1, source_target_pairs={{0,64},{32,96},{64,0},{96,32},{1,65},{33,97},{65,1},{97,33},{2,66}... | collective-permute-start | bytes 61448 | tf_op jit(solution)/shard_map/ppermute | solution.py:568
  60.5 3.2 %collective-permute-start.10 = (bf16[5,16,128]{2,1,0:T(8,128)(2,1)S(1)}, bf16[5,16,128]{2,1,0:T(8,128)(2,1)S(1)}, u32[]{:S(2)}, u32[]{:S(2)}) collective-permute-start(bf16[5,16,128]{2,1,0:T(8,128)(2,1)S(1)} %get-tuple-element.48), channel_id=1, source_target_pairs={{0,96},{32,0},{64,32},{96,64},{1,97},{33,1},{65,33},{97,65},{2,98}... | collective-permute-start | bytes 61448 | tf_op jit(solution)/shard_map/ppermute | solution.py:568
  65.1 1.7 %collective-permute-start.11 = (bf16[384,128]{1,0:T(8,128)(2,1)S(1)}, bf16[384,128]{1,0:T(8,128)(2,1)S(1)}, u32[]{:S(2)}, u32[]{:S(2)}) collective-permute-start(bf16[384,128]{1,0:T(8,128)(2,1)S(1)} %get-tuple-element.51), channel_id=1, source_target_pairs={{0,32},{32,64},{64,96},{96,0},{1,33},{33,65},{65,97},{97,1},{2,34}... | collective-permute-start | bytes 294920 | tf_op jit(solution)/shard_map/ppermute | solution.py:568
  65.2 4.3 %collective-permute-start.12 = (bf16[384,128]{1,0:T(8,128)(2,1)S(1)}, bf16[384,128]{1,0:T(8,128)(2,1)S(1)}, u32[]{:S(2)}, u32[]{:S(2)}) collective-permute-start(bf16[384,128]{1,0:T(8,128)(2,1)S(1)} %get-tuple-element.52), channel_id=1, source_target_pairs={{0,64},{32,96},{64,0},{96,32},{1,65},{33,97},{65,1},{97,33},{2,66}... | collective-permute-start | bytes 294920 | tf_op jit(solution)/shard_map/ppermute | solution.py:568
  65.9 5.2 %collective-permute-start.13 = (bf16[384,128]{1,0:T(8,128)(2,1)S(1)}, bf16[384,128]{1,0:T(8,128)(2,1)S(1)}, u32[]{:S(2)}, u32[]{:S(2)}) collective-permute-start(bf16[384,128]{1,0:T(8,128)(2,1)S(1)} %get-tuple-element.53), channel_id=1, source_target_pairs={{0,96},{32,0},{64,32},{96,64},{1,97},{33,1},{65,33},{97,65},{2,98}... | collective-permute-start | bytes 294920 | tf_op jit(solution)/shard_map/ppermute | solution.py:568
  71.9 24.1 %all-to-all-start = ((bf16[32,2,768]{2,1,0:T(2,128)(2,1)}), bf16[32,2,768]{2,1,0:T(2,128)(2,1)S(1)}, u32[]{:S(2)}, u32[]{:S(2)}) async-start(bf16[32,2,768]{2,1,0:T(2,128)(2,1)} %reshape.13), calls=%async_computation | async-start | bytes 196608 | tf_op jit(solution)/shard_map/all_to_all | solution.py:590

commit v7 on v6

--- a/solution.py
+++ b/solution.py
@@ -16,7 +16,8 @@
 whole = pl.BlockSpec(memory_space=pltpu.VMEM)
 scalars = pl.BlockSpec(memory_space=pltpu.SMEM)
 far_off = pl.BlockSpec(memory_space=pltpu.HBM)
-early = 1
+early = 2
+taps = [(2 - n // 3, (1, 0, 2)[n % 3]) for n in range(9)]
 
 
 def params(mib):
@@ -39,8 +40,48 @@
     return shifted * inverse, inverse
 
 
-def modulate_kernel(places, hidden, scale, shift, w_out, modulated, *rest):
-    pieces, latent = rest[:-1], rest[-1]
+def fetch_kernel(grad, ahead, sem):
+    copy = pltpu.make_async_copy(grad.at[0:2], ahead, sem)
+    copy.start()
+    copy.wait()
+
+
+def fetch(grad):
+    return pl.pallas_call(
+        fetch_kernel,
+        out_shape=jax.ShapeDtypeStruct((2,) + grad.shape[1:], bf16),
+        in_specs=[far_off],
+        out_specs=whole,
+        scratch_shapes=[pltpu.SemaphoreType.DMA],
+        compiler_params=params(4),
+        name="fetch",
+    )(grad)
+
+
+def wide_weight(w_section):
+    return w_section.shape[-2], 3 * w_section.shape[-1]
+
+
+def weight_copies(w_section, held, some, sems):
+    channels = w_section.shape[-1]
+    return [
+        [
+            pltpu.make_async_copy(
+                w_section.at[kt, ky, kx],
+                held.at[n, :, kx * channels : (kx + 1) * channels],
+                sems.at[3 * n + kx],
+            )
+            for kx in range(3)
+        ]
+        for n, (kt, ky) in enumerate(some)
+    ]
+
+
+def modulate_kernel(places, hidden, scale, shift, w_out, w_section, modulated, held, *rest):
+    pieces, latent, sems = rest[:-2], rest[-2], rest[-1]
+    copies = sum(weight_copies(w_section, held, taps[:early], sems), [])
+    for copy in copies:
+        copy.start()
     frames, token_rows, tokens, width = hidden.shape
     groups = len(pieces)
     block = frames // groups
@@ -65,19 +106,27 @@
     for step, piece in enumerate(pieces):
         dst = lax.rem(places[2] + step, groups)
         piece[...] = latent[pl.ds(dst * block, block + 2)]
-
-
-def modulate(places, hidden, mod_scale, mod_shift, w_out, groups):
+    for copy in copies:
+        copy.wait()
+
+
+def modulate(places, hidden, mod_scale, mod_shift, w_out, w_section, groups):
     frames, token_rows, tokens, width = hidden.shape
     pair = 2 * w_out.shape[0]
     piece = jax.ShapeDtypeStruct((frames // groups + 2, slots, pair), bf16)
     return pl.pallas_call(
         modulate_kernel,
-        out_shape=[jax.ShapeDtypeStruct((frames, token_rows, slots, width), bf16)]
+        out_shape=[
+            jax.ShapeDtypeStruct((frames, token_rows, slots, width), bf16),
+            jax.ShapeDtypeStruct((early,) + wide_weight(w_section), bf16),
+        ]
         + [piece] * groups,
-        in_specs=[scalars] + [whole] * 4,
-        out_specs=[whole] * (1 + groups),
-        scratch_shapes=[pltpu.VMEM((frames + 2, slots, pair), bf16)],
+        in_specs=[scalars] + [whole] * 4 + [far_off],
+        out_specs=[whole] * (2 + groups),
+        scratch_shapes=[
+            pltpu.VMEM((frames + 2, slots, pair), bf16),
+            pltpu.SemaphoreType.DMA((3 * early,)),
+        ],
         compiler_params=params(8),
         cost_estimate=pl.CostEstimate(
             flops=2 * frames * slots * width * pair,
@@ -85,19 +134,16 @@
             transcendentals=0,
         ),
         name="modulate",
-    )(places, hidden, mod_scale.reshape(1, -1), mod_shift.reshape(1, -1), w_out)
-
-
-def column_shifts(value):
+    )(places, hidden, mod_scale.reshape(1, -1), mod_shift.reshape(1, -1), w_out, w_section)
+
+
+def widened(value):
     cols, channels = value.shape
     wide = value.astype(f32)
     place = lax.broadcasted_iota(jnp.int32, (cols, channels), 0)
-    nxt = jnp.where(place == cols - 1, 0.0, pltpu.roll(wide, cols - 1, 0))
-    prv = jnp.where(place == 0, 0.0, pltpu.roll(wide, 1, 0))
-    return nxt.astype(bf16), prv.astype(bf16)
-
-
-taps = [(2 - n // 3, (1, 0, 2)[n % 3]) for n in range(9)]
+    right = jnp.where(place == cols - 1, 0.0, pltpu.roll(wide, cols - 1, 0)).astype(bf16)
+    left = jnp.where(place == 0, 0.0, pltpu.roll(wide, 1, 0)).astype(bf16)
+    return jnp.concatenate([right, value, left], axis=-1)
 
 
 def flat(value):
@@ -105,23 +151,14 @@
 
 
 def weight_matrix(held_first, held_rest, n):
-    block = held_first[n] if n < early else held_rest[n - early]
-    return jnp.concatenate([block[kx] for kx in range(3)], axis=-1)
-
-
-def pack_kernel(
-    places, grad, grad_ahead, w_section, w_in, *rest
-):
+    return held_first[n] if n < early else held_rest[n - early]
+
+
+def pack_kernel(places, grad, grad_ahead, w_in, *rest):
     pieces = rest[:4]
-    near, far, latent, shifts, patches, held, sems = rest[4:]
+    near, far, latent, wide, patches = rest[4:]
     frames, rows, cols, channels = grad.shape
     groups = len(pieces)
-    copies = [
-        pltpu.make_async_copy(w_section.at[kt, ky], held.at[n], sems.at[n])
-        for n, (kt, ky) in enumerate(taps[:early])
-    ]
-    for copy in copies:
-        copy.start()
     for step, piece in enumerate(pieces):
         latent[lax.rem(places[2] + groups - step, groups)] = piece[...]
     for side, out in ((0, near), (1, far)):
@@ -140,7 +177,7 @@
     for frame in range(frames + 2):
         for row in range(rows):
             value = grad[frame, row] if frame < frames else grad_ahead[frame - frames, row]
-            shifts[0, frame, row], shifts[1, frame, row] = column_shifts(value)
+            wide[frame, row] = widened(value)
 
     patches[...] = jnp.zeros_like(patches)
     lat = w_in.shape[3]
@@ -153,55 +190,43 @@
         if 0 <= ky < 3 and 0 <= kx < 3:
             at = (((kt * 2 + a) * 2 + b) * 4 + 2 * pp + qq) * lat
             patches[2 * p + q, at : at + lat] = w_in[kt, ky, kx]
-    for copy in copies:
-        copy.wait()
-
-
-def pack_rows(places, grad, grad_ahead, w_section, w_in, pieces):
+
+
+def pack_rows(places, grad, grad_ahead, w_in, pieces):
     frames, rows, cols, channels = grad.shape
     groups = len(pieces)
     latent = jax.ShapeDtypeStruct((groups,) + pieces[0].shape, bf16)
     total = (frames + 2) * cols + latent.size // channels
     return pl.pallas_call(
         pack_kernel,
-        in_specs=[scalars, whole, whole, far_off, whole] + [whole] * groups,
-        out_specs=[whole] * 6,
+        in_specs=[scalars] + [whole] * (3 + groups),
+        out_specs=[whole] * 5,
         out_shape=[
             jax.ShapeDtypeStruct((total, channels), bf16),
             jax.ShapeDtypeStruct((total, channels), bf16),
             latent,
-            jax.ShapeDtypeStruct((2, frames + 2, rows, cols, channels), bf16),
+            jax.ShapeDtypeStruct((frames + 2, rows, cols, 3 * channels), bf16),
             jax.ShapeDtypeStruct((4, 48 * w_in.shape[3], channels), bf16),
-            jax.ShapeDtypeStruct((early,) + w_section.shape[2:], bf16),
         ],
-        scratch_shapes=[pltpu.SemaphoreType.DMA((early,))],
         compiler_params=params(8),
         name="pack_rows",
-    )(places, grad, grad_ahead, w_section, w_in, *pieces)
-
-
-def own_kernel(grad, grad_ahead, shifts, w_section, held_first, total, held_rest, sems):
-    frames, rows, cols, channels = grad.shape
-    copies = [
-        pltpu.make_async_copy(w_section.at[kt, ky], held_rest.at[n], sems.at[n])
-        for n, (kt, ky) in enumerate(taps[early:])
-    ]
-    for copy in copies:
+    )(places, grad, grad_ahead, w_in, *pieces)
+
+
+def own_kernel(wide, w_section, held_first, total, held_rest, sems):
+    depth, rows, cols, _ = wide.shape
+    frames = depth - 2
+    copies = weight_copies(w_section, held_rest, taps[early:], sems)
+    for copy in sum(copies, []):
         copy.start()
     for n, (kt, ky) in enumerate(taps):
         lo, hi = max(0, ky - 1), rows + min(0, ky - 1)
-        at = slice(lo + 1 - ky, hi + 1 - ky)
-        src = slice(2 - kt, frames + 2 - kt), at
-        centre = flat(grad[2 - kt :, at])
-        if kt < 2:
-            centre = jnp.concatenate([centre, flat(grad_ahead[: 2 - kt, at])], axis=0)
-        window = jnp.concatenate(
-            [flat(shifts[(0,) + src]), centre, flat(shifts[(1,) + src])], axis=-1
-        )
+        window = flat(wide[2 - kt : depth - kt, lo + 1 - ky : hi + 1 - ky])
         if n >= early:
-            copies[n - early].wait()
+            for copy in copies[n - early]:
+                copy.wait()
         part = dot_turned(window, weight_matrix(held_first, held_rest, n))
-        for lane in range(channels // lanes):
+        for lane in range(total.shape[0]):
             value = part[:, lane * lanes : (lane + 1) * lanes]
             value = value.reshape(frames, hi - lo, cols, lanes)
             if n == 0:
@@ -210,29 +235,29 @@
                 total[lane, :, lo:hi] += value
 
 
-def own_part(grad, grad_ahead, shifts, w_section, held_first):
-    frames, rows, cols, channels = grad.shape
+def own_part(wide, w_section, held_first):
+    depth, rows, cols, _ = wide.shape
+    channels = w_section.shape[-1]
     return pl.pallas_call(
         own_kernel,
         out_shape=[
-            jax.ShapeDtypeStruct((channels // lanes, frames, rows, cols, lanes), f32),
-            jax.ShapeDtypeStruct((len(taps) - early,) + w_section.shape[2:], bf16),
+            jax.ShapeDtypeStruct((channels // lanes, depth - 2, rows, cols, lanes), f32),
+            jax.ShapeDtypeStruct((len(taps) - early,) + wide_weight(w_section), bf16),
         ],
-        in_specs=[whole, whole, whole, far_off, whole],
+        in_specs=[whole, far_off, whole],
         out_specs=[whole] * 2,
-        scratch_shapes=[pltpu.SemaphoreType.DMA((len(taps) - early,))],
+        scratch_shapes=[pltpu.SemaphoreType.DMA((3 * (len(taps) - early),))],
         compiler_params=params(12),
         cost_estimate=pl.CostEstimate(
-            flops=2 * 24 * grad.size * channels,
+            flops=2 * 14 * wide.size * channels,
             bytes_accessed=2 * w_section.size,
             transcendentals=0,
         ),
         name="own_part",
-    )(grad, grad_ahead, shifts, w_section, held_first)
-
-
-def edge_kernel(places, own, near_rows, far_rows, held_first, held_rest, total, near):
-    even = places[0] != 0
+    )(wide, w_section, held_first)
+
+
+def edge_conv(even, own, near_rows, far_rows, held_first, held_rest, total, wide):
     blocks, frames, rows, cols, _ = own.shape
     for lane in range(blocks):
         total[lane, :, 0] = own[lane, :, 0]
@@ -241,38 +266,16 @@
         at = slice(frame * cols, (frame + 1) * cols)
         ends = near_rows[at], far_rows[at]
         for side in range(2):
-            value = jnp.where(even == (side == 1), ends[0], ends[1])
-            near[1, side, frame] = value
-            near[0, side, frame], near[2, side, frame] = column_shifts(value)
-
+            wide[side, frame] = widened(jnp.where(even == (side == 1), ends[0], ends[1]))
     for n, (kt, ky) in enumerate(taps):
         if ky == 1:
             continue
         side = 0 if ky == 2 else 1
-        window = jnp.concatenate(
-            [flat(near[kx, side, 2 - kt : frames + 2 - kt]) for kx in range(3)], axis=-1
-        )
+        window = flat(wide[side, 2 - kt : frames + 2 - kt])
         part = dot_turned(window, weight_matrix(held_first, held_rest, n))
         for lane in range(blocks):
             value = part[:, lane * lanes : (lane + 1) * lanes]
             total[lane, :, side] += value.reshape(frames, cols, lanes)
-
-
-def edge_part(places, own, near_rows, far_rows, held_first, held_rest):
-    blocks, frames, _, cols, _ = own.shape
-    channels = blocks * lanes
-    return pl.pallas_call(
-        edge_kernel,
-        out_shape=jax.ShapeDtypeStruct((blocks, frames, 2, cols, lanes), f32),
-        in_specs=[scalars] + [whole] * 5,
-        out_specs=whole,
-        scratch_shapes=[pltpu.VMEM((3, 2, frames + 2, cols, channels), bf16)],
-        compiler_params=params(10),
-        cost_estimate=pl.CostEstimate(
-            flops=2 * 4 * own.size * channels, bytes_accessed=0, transcendentals=0
-        ),
-        name="edge_part",
-    )(places, own, near_rows, far_rows, held_first, held_rest)
 
 
 def latent_phase(total, slot_of, row_of, spread_row, windows, patches, spread):
@@ -321,11 +324,12 @@
     return spread[:, row, 1 : half + 1, :width] + spread[:, row, 0:half, width:]
 
 
-def edge_latent_kernel(
-    places, total, latent, near_rows, far_rows, patches,
-    near_out, far_out, windows, spread, tokens,
+def edge_kernel(
+    places, own, latent, near_rows, far_rows, held_first, held_rest, patches,
+    near_out, far_out, windows, spread, tokens, total, wide,
 ):
     even = places[0] != 0
+    edge_conv(even, own, near_rows, far_rows, held_first, held_rest, total, wide)
     groups, depth, _, pair = latent.shape
     width = pair // 2
     count = groups * depth * slots * lanes // near_rows.shape[1]
@@ -368,24 +372,31 @@
             far_out[dst, frame] = padded(jnp.where(even, up, down))
 
 
-def edge_latent(places, total, latent, near_rows, far_rows, patches):
+def edge_part(places, own, latent, near_rows, far_rows, held_first, held_rest, patches):
     groups, depth, _, pair = latent.shape
-    cols = total.shape[3]
+    blocks, frames, _, cols, _ = own.shape
     out = jax.ShapeDtypeStruct(latent.shape, bf16)
     return pl.pallas_call(
-        edge_latent_kernel,
+        edge_kernel,
         out_shape=[
             out,
             out,
             jax.ShapeDtypeStruct((2, depth, 4, cols // 2, pair), bf16),
             jax.ShapeDtypeStruct((depth, 4, cols // 2 + 8, pair), f32),
         ],
-        in_specs=[scalars] + [whole] * 5,
+        in_specs=[scalars] + [whole] * 7,
         out_specs=[whole] * 4,
-        scratch_shapes=[pltpu.VMEM((depth, 4, 72, pair // 2), f32)],
-        compiler_params=params(10),
-        name="edge_latent",
-    )(places, total, latent, near_rows, far_rows, patches)
+        scratch_shapes=[
+            pltpu.VMEM((depth, 4, 72, pair // 2), f32),
+            pltpu.VMEM((blocks, frames, 2, cols, lanes), f32),
+            pltpu.VMEM((2, depth, cols, 3 * blocks * lanes), bf16),
+        ],
+        compiler_params=params(14),
+        cost_estimate=pl.CostEstimate(
+            flops=2 * 6 * own.size * blocks * lanes, bytes_accessed=0, transcendentals=own.size
+        ),
+        name="edge_part",
+    )(places, own, latent, near_rows, far_rows, held_first, held_rest, patches)
 
 
 def inner_kernel(own, windows, patches, spread_in, out, spread, tokens):
@@ -568,17 +579,19 @@
             lax.ppermute(pieces[k], "tm", hops(k)) for k in range(1, groups)
         ]
 
-    grad_ahead = lax.ppermute(section_grad, "tm", [(g + 1, g) for g in range(groups - 1)])
-    modulated, *pieces = modulate(places, hidden, mod_scale, mod_shift, w_out, groups)
-    near_send, far_send, latent, shifts, patches, held_first = pack_rows(
-        places, section_grad, grad_ahead, w_section, w_in, round_tm(pieces)
+    ahead = fetch(pltpu.with_memory_space_constraint(section_grad, pltpu.HBM))
+    grad_ahead = lax.ppermute(ahead, "tm", [(g + 1, g) for g in range(groups - 1)])
+    modulated, held_first, *pieces = modulate(
+        places, hidden, mod_scale, mod_shift, w_out, w_section, groups
+    )
+    near_send, far_send, latent, wide, patches = pack_rows(
+        places, section_grad, grad_ahead, w_in, round_tm(pieces)
     )
     far_rows = lax.ppermute(far_send, "height", far)
     near_rows = lax.ppermute(near_send, "height", near)
-    own, held_rest = own_part(section_grad, grad_ahead, shifts, w_section, held_first)
-    edge = edge_part(places, own, near_rows, far_rows, held_first, held_rest)
-    near_share, far_share, windows, spread = edge_latent(
-        places, edge, latent, near_rows, far_rows, patches
+    own, held_rest = own_part(wide, w_section, held_first)
+    near_share, far_share, windows, spread = edge_part(
+        places, own, latent, near_rows, far_rows, held_first, held_rest, patches
     )
     far_share = lax.ppermute(far_share, "height", far)
     near_share = lax.ppermute(near_share, "height", near)

time: 97.2 us -> 92.6 us (0.953)
  waiting for transfers between devices: 18 us -> 14 us
  Pallas kernels: 38.7 us -> 37.5 us
    ppermute x9, waiting for transfers between devices: 15.5 us -> 11.5 us  [round_tm(): lax.ppermute(pieces[k], 'tm', hops(k))]
    pallas_call x1, Pallas kernels: 17.7 us -> 16.3 us  [own_part(): pl.pallas_call(own_kernel, out_shape=[jax.ShapeDtypeStruct((channels // l...]
where the time goes in v7:
time: 92.6 us; the launch traced here: 92.3 us
  Pallas kernels  37.5 us (40%)
  starting transfers between devices  32.6 us (35%)
  waiting for transfers between devices  14 us (15%)
  local copies, waits for them, and re-layouts  6.68 us (7%)
    pallas_call x1, Pallas kernels, own_part(): pl.pallas_call(own_kernel, out_shape=[jax.ShapeDtypeStruct((channels // l...  16.3 us
    all_to_all x1, starting transfers between devices, shards(): pieces = lax.all_to_all(middle_sum(got, strips), 'height', 0, 0, tiled=True)  15.9 us
    ppermute x9, waiting for transfers between devices, round_tm(): lax.ppermute(pieces[k], 'tm', hops(k))  11.5 us
    unnamed x14, local copies, waits for them, and re-layouts  6.68 us
    ppermute x9, starting transfers between devices, round_tm(): lax.ppermute(pieces[k], 'tm', hops(k))  5.76 us
    pallas_call x1, Pallas kernels, edge_part(): pl.pallas_call(edge_kernel, out_shape=[out, out, jax.ShapeDtypeStruct((2,...  5.53 us
    ppermute x1, starting transfers between devices, shards(): near_share = lax.ppermute(near_share, 'height', near)  4.27 us
    pallas_call x1, Pallas kernels, modulate(): pl.pallas_call(modulate_kernel, out_shape=[jax.ShapeDtypeStruct((frames,...  3.78 us
  transfers between devices with their start and end apart: 15, of which 8 were waited for; matrix products, arithmetic and copies ran while one was open for 5% of the time, Pallas kernels for 28%

profile of v7, /device:TPU:1, one launch (start us, length us, event | category | flops | bytes accessed | tf_op | source)
XLA Modules:
  0.0 92.3 jit_solution(4487671892075023825)
XLA Ops:
  0.6 2.0 %fetch.1 = bf16[2,4,96,512]{3,2,1,0:T(8,128)(2,1)} custom-call(bf16[3,4,96,512]{3,2,1,0:T(8,128)(2,1)} %grad.3), custom_call_target="tpu_custom_call" | custom-call | tf_op jit(solution)/shard_map/fetch/pallas_call | solution.py:50
  2.7 3.5 %collective-permute-start = (bf16[2,4,96,512]{3,2,1,0:T(8,128)(2,1)}, bf16[2,4,96,512]{3,2,1,0:T(8,128)(2,1)S(1)}, u32[]{:S(2)}, u32[]{:S(2)}) collective-permute-start(bf16[2,4,96,512]{3,2,1,0:T(8,128)(2,1)} %fetch.1), channel_id=1, source_target_pairs={{32,0},{64,32},{96,64},{33,1},{65,33},{97,65},{34,2},{66,34},{98,6... | collective-permute-start | bytes 2359304 | tf_op jit(solution)/shard_map/ppermute | solution.py:583
  6.2 1.9 %copy.10.hidden = bf16[12,2,12,3072]{3,2,1,0:T(8,128)(2,1)S(1)} copy(bf16[12,2,12,3072]{3,1,2,0:T(2,128)(2,1)} %param.7) | data formatting | bytes 3538944 | tf_op args[0]
  8.9 3.8 %modulate.1 = (bf16[12,2,16,3072]{3,2,1,0:T(8,128)(2,1)S(1)}, bf16[2,512,1536]{2,1,0:T(8,128)(2,1)S(1)}, bf16[5,16,128]{2,1,0:T(8,128)(2,1)S(1)}, bf16[5,16,128]...) custom-call(s32[3]{0:T(128)S(1)} %pad_add_fusion.places, ...), custom_call_target="tpu_custom_call" | custom-call | flops 150994944 | bytes 4718592 | tf_op jit(solution)/shard_map/modulate/pallas_call | solution.py:117
  12.7 1.3 %collective-permute-start.1 = (bf16[5,16,128]{2,1,0:T(8,128)(2,1)S(1)}, bf16[5,16,128]{2,1,0:T(8,128)(2,1)S(1)}, u32[]{:S(2)}, u32[]{:S(2)}) collective-permute-start(bf16[5,16,128]{2,1,0:T(8,128)(2,1)S(1)} %get-tuple-element.30), channel_id=1, source_target_pairs={{0,32},{32,64},{64,96},{96,0},{1,33},{33,65},{65,97},{97,1},{2,34}... | collective-permute-start | bytes 61448 | tf_op jit(solution)/shard_map/ppermute | solution.py:579
  14.9 2.0 %collective-permute-done.2.rest_2_ = bf16[5,16,128]{2,1,0:T(8,128)(2,1)S(1)} collective-permute-done((bf16[5,16,128]{2,1,0:T(8,128)(2,1)S(1)}, bf16[5,16,128]{2,1,0:T(8,128)(2,1)S(1)}, u32[]{:S(2)}, u32[]{:S(2)}) %collective-permute-start.2) | collective-permute-done | bytes 20512 | tf_op jit(solution)/shard_map/ppermute | solution.py:579
  16.9 1.3 %collective-permute-done.3.rest_3_ = bf16[5,16,128]{2,1,0:T(8,128)(2,1)S(1)} collective-permute-done((bf16[5,16,128]{2,1,0:T(8,128)(2,1)S(1)}, bf16[5,16,128]{2,1,0:T(8,128)(2,1)S(1)}, u32[]{:S(2)}, u32[]{:S(2)}) %collective-permute-start.3) | collective-permute-done | bytes 20512 | tf_op jit(solution)/shard_map/ppermute | solution.py:579
  18.2 1.8 %pack_rows.1 = (bf16[560,512]{1,0:T(8,128)(2,1)S(1)}, bf16[560,512]{1,0:T(8,128)(2,1)S(1)}, bf16[4,5,16,128]{3,2,1,0:T(8,128)(2,1)S(1)}, bf16[5,4,96,1536]{3,2,1,0:T(8,128)(2,1)S(1)}, bf16[4,768,512]{2,1,0:T(8,128)(2,1)S(1)}) custom-call(s32[3]{0:T(128)S(1)} %pad_add_fusion.places, bf16[3,4,96,512]{3,2,1,0:T(8,128)(2,1)S(1)} %copy-done, ...), custom_call_target="tpu_custom_call" | custom-call | tf_op jit(solution)/shard_map/pack_rows/pallas_call | solution.py:200
  20.0 1.7 %collective-permute-start.4 = (bf16[560,512]{1,0:T(8,128)(2,1)S(1)}, bf16[560,512]{1,0:T(8,128)(2,1)S(1)}, u32[]{:S(2)}, u32[]{:S(2)}) collective-permute-start(bf16[560,512]{1,0:T(8,128)(2,1)S(1)} %get-tuple-element.37), channel_id=1, source_target_pairs={{0,1},{1,0},{2,3},{3,2},{4,5},{5,4},{6,7},{7,6},{8,9},{9,8},{10,11... | collective-permute-start | bytes 1720328 | tf_op jit(solution)/shard_map/ppermute | solution.py:591
  22.6 16.3 %own_part.1 = (f32[4,3,4,96,128]{4,3,2,1,0:T(8,128)S(1)}, bf16[7,512,1536]{2,1,0:T(8,128)(2,1)S(1)}) custom-call(bf16[5,4,96,1536]{3,2,1,0:T(8,128)(2,1)S(1)} %get-tuple-element.33.wide, bf16[3,3,3,512,512]{4,3,2,1,0:T(8,128)(2,1)} %w_section.3, bf16[2,512,1536]{2,1,0:T(8,128)(2,1)S(1)} %get-tuple-element.34.held_first), custom_call_target="tpu_custom_call" | custom-call | flops 42278584320 | bytes 14155776 | tf_op jit(solution)/shard_map/own_part/pallas_call | solution.py:241
  39.0 5.5 %edge_part.1 = (bf16[4,5,16,128]{3,2,1,0:T(8,128)(2,1)S(1)}, bf16[4,5,16,128]{3,2,1,0:T(8,128)(2,1)S(1)}, bf16[2,5,4,48,128]{4,3,2,1,0:T(8,128)(2,1)S(1)}, f32[5,4,56,128]{3,2,1,0:T(8,128)S(1)}) custom-call(s32[3]{0:T(128)S(1)} %pad_add_fusion.places, f32[4,3,4,96,128]{4,3,2,1,0:T(8,128)S(1)} %get-tuple-element.35.own, ...), custom_call_target="tpu_custom_call" | custom-call | flops 3623878656 | tf_op jit(solution)/shard_map/edge_part/pallas_call | solution.py:379
  44.5 4.3 %collective-permute-start.6 = (bf16[4,5,16,128]{3,2,1,0:T(8,128)(2,1)S(1)}, bf16[4,5,16,128]{3,2,1,0:T(8,128)(2,1)S(1)}, u32[]{:S(2)}, u32[]{:S(2)}) collective-permute-start(bf16[4,5,16,128]{3,2,1,0:T(8,128)(2,1)S(1)} %get-tuple-element.43), channel_id=1, source_target_pairs={{0,1},{1,0},{2,3},{3,2},{4,5},{5,4},{6,7},{7,6},{8,9},{9,8},{10,11... | collective-permute-start | bytes 245768 | tf_op jit(solution)/shard_map/ppermute | solution.py:597
  49.4 2.2 %inner_part.1.centre = f32[4,5,16,128]{3,2,1,0:T(8,128)S(1)} custom-call(f32[4,3,4,96,128]{4,3,2,1,0:T(8,128)S(1)} %get-tuple-element.35.own, bf16[2,5,4,48,128]{4,3,2,1,0:T(8,128)(2,1)S(1)} %get-tuple-element.41.windows, bf16[4,768,512]{2,1,0:T(8,128)(2,1)S(1)} %get-tuple-element.40.patches, f32[5,4,56,128]{3,2,1,0:T(8,128)S(1)} %get-tuple-element.42.spread_in), custom_call_target="tpu_custom_call" | custom-call | flops 3623878656 | tf_op jit(solution)/shard_map/inner_part/pallas_call | solution.py:421
  52.3 1.1 %collective-permute-start.8 = (bf16[5,16,128]{2,1,0:T(8,128)(2,1)S(1)}, bf16[5,16,128]{2,1,0:T(8,128)(2,1)S(1)}, u32[]{:S(2)}, u32[]{:S(2)}) collective-permute-start(bf16[5,16,128]{2,1,0:T(8,128)(2,1)S(1)} %get-tuple-element.46), channel_id=1, source_target_pairs={{0,32},{32,64},{64,96},{96,0},{1,33},{33,65},{65,97},{97,1},{2,34}... | collective-permute-start | bytes 61448 | tf_op jit(solution)/shard_map/ppermute | solution.py:579
  53.3 1.6 %collective-permute-start.9 = (bf16[5,16,128]{2,1,0:T(8,128)(2,1)S(1)}, bf16[5,16,128]{2,1,0:T(8,128)(2,1)S(1)}, u32[]{:S(2)}, u32[]{:S(2)}) collective-permute-start(bf16[5,16,128]{2,1,0:T(8,128)(2,1)S(1)} %get-tuple-element.47), channel_id=1, source_target_pairs={{0,64},{32,96},{64,0},{96,32},{1,65},{33,97},{65,1},{97,33},{2,66}... | collective-permute-start | bytes 61448 | tf_op jit(solution)/shard_map/ppermute | solution.py:579
  54.9 1.5 %collective-permute-done.9.rest_2_ = bf16[5,16,128]{2,1,0:T(8,128)(2,1)S(1)} collective-permute-done((bf16[5,16,128]{2,1,0:T(8,128)(2,1)S(1)}, bf16[5,16,128]{2,1,0:T(8,128)(2,1)S(1)}, u32[]{:S(2)}, u32[]{:S(2)}) %collective-permute-start.9) | collective-permute-done | bytes 20512 | tf_op jit(solution)/shard_map/ppermute | solution.py:579
  56.4 1.7 %collective-permute-done.10.rest_3_ = bf16[5,16,128]{2,1,0:T(8,128)(2,1)S(1)} collective-permute-done((bf16[5,16,128]{2,1,0:T(8,128)(2,1)S(1)}, bf16[5,16,128]{2,1,0:T(8,128)(2,1)S(1)}, u32[]{:S(2)}, u32[]{:S(2)}) %collective-permute-start.10) | collective-permute-done | bytes 20512 | tf_op jit(solution)/shard_map/ppermute | solution.py:579
  58.1 1.4 %weight_terms.1 = (bf16[12,2,16,64]{3,2,1,0:T(8,128)(2,1)S(1)}, bf16[384,128]{1,0:T(8,128)(2,1)S(1)}, bf16[384,128]{1,0:T(8,128)(2,1)S(1)}, bf16[384,128]{1,0:T(8,128)(2,1)S(1)}, bf16[384,128]{1,0:T(8,128)(2,1)S(1)}) custom-call(s32[3]{0:T(128)S(1)} %pad_add_fusion.places, bf16[12,2,16,3072]{3,2,1,0:T(8,128)(2,1)S(1)} %get-tuple-element.28.modulated, ...), custom_call_target="tpu_custom_call" | custom-call | tf_op jit(solution)/shard_map/weight_terms/pallas_call | solution.py:489
  61.3 2.6 %collective-permute-done.12.refs_2_ = bf16[384,128]{1,0:T(8,128)(2,1)S(1)} collective-permute-done((bf16[384,128]{1,0:T(8,128)(2,1)S(1)}, bf16[384,128]{1,0:T(8,128)(2,1)S(1)}, u32[]{:S(2)}, u32[]{:S(2)}) %collective-permute-start.12) | collective-permute-done | bytes 98336 | tf_op jit(solution)/shard_map/ppermute | solution.py:579
  63.9 1.5 %collective-permute-done.13.refs_3_ = bf16[384,128]{1,0:T(8,128)(2,1)S(1)} collective-permute-done((bf16[384,128]{1,0:T(8,128)(2,1)S(1)}, bf16[384,128]{1,0:T(8,128)(2,1)S(1)}, u32[]{:S(2)}, u32[]{:S(2)}) %collective-permute-start.13) | collective-permute-done | bytes 98336 | tf_op jit(solution)/shard_map/ppermute | solution.py:579
  66.4 15.9 %all-to-all-start = ((bf16[32,2,768]{2,1,0:T(2,128)(2,1)}), bf16[32,2,768]{2,1,0:T(2,128)(2,1)S(1)}, u32[]{:S(2)}, u32[]{:S(2)}) async-start(bf16[32,2,768]{2,1,0:T(2,128)(2,1)} %reshape.13), calls=%async_computation | async-start | bytes 196608 | tf_op jit(solution)/shard_map/all_to_all | solution.py:603
  82.3 3.6 %hidden_grad.1 = bf16[12,2,12,3072]{3,2,1,0:T(8,128)(2,1)S(1)} custom-call(bf16[12,2,12,3072]{3,2,1,0:T(8,128)(2,1)S(1)} %copy.10.hidden, bf16[12,2,16,64]{3,2,1,0:T(8,128)(2,1)S(1)} %get-tuple-element.49.token_grad, f32[1,3072]{1,0:T(1,128)S(1)} %bitcast.9, bf16[64,3072]{1,0:T(8,128)(2,1)S(1)} %bitcast.7), custom_call_target="tpu_custom_call" | custom-call | flops 150994944 | bytes 4718592 | tf_op jit(solution)/shard_map/hidden_grad/pallas_call | solution.py:549
  85.9 3.0 %copy.11 = bf16[12,2,12,3072]{3,1,2,0:T(2,128)(2,1)} copy(bf16[12,2,12,3072]{3,2,1,0:T(8,128)(2,1)S(1)} %hidden_grad.1) | data formatting | bytes 3538944
  88.9 2.5 %all-to-all-done = bf16[32,2,768]{2,1,0:T(2,128)(2,1)S(1)} async-done(((bf16[32,2,768]{2,1,0:T(2,128)(2,1)}), bf16[32,2,768]{2,1,0:T(2,128)(2,1)S(1)}, u32[]{:S(2)}, u32[]{:S(2)}) %all-to-all-start) | async-done | bytes 98336 | tf_op jit(solution)/shard_map/all_to_all | solution.py:603
  (33 shorter events, 7.4 us)
Async XLA Ops:
  2.7 5.5 %copy-start.1 = (bf16[3072,64]{0,1:T(8,128)(2,1)S(1)}, bf16[3072,64]{0,1:T(8,128)(2,1)}, u32[]{:S(2)}) copy-start(bf16[3072,64]{0,1:T(8,128)(2,1)} %param.10) | copy-start | bytes 1179652
  2.7 5.5 %copy-start.3 = (f32[3072]{0:T(1024)S(1)}, f32[3072]{0:T(1024)}, u32[]{:S(2)}) copy-start(f32[3072]{0:T(1024)} %param.8) | copy-start | bytes 36868
  2.7 15.5 %collective-permute-start = (bf16[2,4,96,512]{3,2,1,0:T(8,128)(2,1)}, bf16[2,4,96,512]{3,2,1,0:T(8,128)(2,1)S(1)}, u32[]{:S(2)}, u32[]{:S(2)}) collective-permute-start(bf16[2,4,96,512]{3,2,1,0:T(8,128)(2,1)} %fetch.1), channel_id=1, source_target_pairs={{32,0},{64,32},{96,64},{33,1},{65,33},{97,65},{34,2},{66,34},{98,6... | collective-permute-start | bytes 2359304 | tf_op jit(solution)/shard_map/ppermute | solution.py:583
  8.2 0.7 copy-start.4
  8.9 9.2 %copy-start = (bf16[3,4,96,512]{3,2,1,0:T(8,128)(2,1)S(1)}, bf16[3,4,96,512]{3,2,1,0:T(8,128)(2,1)}, u32[]{:S(2)}) copy-start(bf16[3,4,96,512]{3,2,1,0:T(8,128)(2,1)} %grad.3) | copy-start | bytes 3538948
  8.9 9.2 %copy-start.2 = (bf16[3,3,3,16,512]{4,3,2,1,0:T(8,128)(2,1)S(1)}, bf16[3,3,3,16,512]{4,3,2,1,0:T(8,128)(2,1)}, u32[]{:S(2)}) copy-start(bf16[3,3,3,16,512]{4,3,2,1,0:T(8,128)(2,1)} %w_in.1) | copy-start | bytes 1327108
  12.7 2.2 %collective-permute-start.1 = (bf16[5,16,128]{2,1,0:T(8,128)(2,1)S(1)}, bf16[5,16,128]{2,1,0:T(8,128)(2,1)S(1)}, u32[]{:S(2)}, u32[]{:S(2)}) collective-permute-start(bf16[5,16,128]{2,1,0:T(8,128)(2,1)S(1)} %get-tuple-element.30), channel_id=1, source_target_pairs={{0,32},{32,64},{64,96},{96,0},{1,33},{33,65},{65,97},{97,1},{2,34}... | collective-permute-start | bytes 61448 | tf_op jit(solution)/shard_map/ppermute | solution.py:579
  14.0 2.9 %collective-permute-start.2 = (bf16[5,16,128]{2,1,0:T(8,128)(2,1)S(1)}, bf16[5,16,128]{2,1,0:T(8,128)(2,1)S(1)}, u32[]{:S(2)}, u32[]{:S(2)}) collective-permute-start(bf16[5,16,128]{2,1,0:T(8,128)(2,1)S(1)} %get-tuple-element.31), channel_id=1, source_target_pairs={{0,64},{32,96},{64,0},{96,32},{1,65},{33,97},{65,1},{97,33},{2,66}... | collective-permute-start | bytes 61448 | tf_op jit(solution)/shard_map/ppermute | solution.py:579
  14.2 3.9 %collective-permute-start.3 = (bf16[5,16,128]{2,1,0:T(8,128)(2,1)S(1)}, bf16[5,16,128]{2,1,0:T(8,128)(2,1)S(1)}, u32[]{:S(2)}, u32[]{:S(2)}) collective-permute-start(bf16[5,16,128]{2,1,0:T(8,128)(2,1)S(1)} %get-tuple-element.32), channel_id=1, source_target_pairs={{0,96},{32,0},{64,32},{96,64},{1,97},{33,1},{65,33},{97,65},{2,98}... | collective-permute-start | bytes 61448 | tf_op jit(solution)/shard_map/ppermute | solution.py:579
  20.0 18.9 %collective-permute-start.4 = (bf16[560,512]{1,0:T(8,128)(2,1)S(1)}, bf16[560,512]{1,0:T(8,128)(2,1)S(1)}, u32[]{:S(2)}, u32[]{:S(2)}) collective-permute-start(bf16[560,512]{1,0:T(8,128)(2,1)S(1)} %get-tuple-element.37), channel_id=1, source_target_pairs={{0,1},{1,0},{2,3},{3,2},{4,5},{5,4},{6,7},{7,6},{8,9},{9,8},{10,11... | collective-permute-start | bytes 1720328 | tf_op jit(solution)/shard_map/ppermute | solution.py:591
  21.7 17.2 %collective-permute-start.5 = (bf16[560,512]{1,0:T(8,128)(2,1)S(1)}, bf16[560,512]{1,0:T(8,128)(2,1)S(1)}, u32[]{:S(2)}, u32[]{:S(2)}) collective-permute-start(bf16[560,512]{1,0:T(8,128)(2,1)S(1)} %get-tuple-element.38), channel_id=1, source_target_pairs={{1,2},{2,1},{3,4},{4,3},{5,6},{6,5},{7,8},{8,7},{9,10},{10,9},{11,... | collective-permute-start | bytes 1720328 | tf_op jit(solution)/shard_map/ppermute | solution.py:590
  44.5 7.2 %collective-permute-start.6 = (bf16[4,5,16,128]{3,2,1,0:T(8,128)(2,1)S(1)}, bf16[4,5,16,128]{3,2,1,0:T(8,128)(2,1)S(1)}, u32[]{:S(2)}, u32[]{:S(2)}) collective-permute-start(bf16[4,5,16,128]{3,2,1,0:T(8,128)(2,1)S(1)} %get-tuple-element.43), channel_id=1, source_target_pairs={{0,1},{1,0},{2,3},{3,2},{4,5},{5,4},{6,7},{7,6},{8,9},{9,8},{10,11... | collective-permute-start | bytes 245768 | tf_op jit(solution)/shard_map/ppermute | solution.py:597
  48.8 2.9 %collective-permute-start.7 = (bf16[4,5,16,128]{3,2,1,0:T(8,128)(2,1)S(1)}, bf16[4,5,16,128]{3,2,1,0:T(8,128)(2,1)S(1)}, u32[]{:S(2)}, u32[]{:S(2)}) collective-permute-start(bf16[4,5,16,128]{3,2,1,0:T(8,128)(2,1)S(1)} %get-tuple-element.44), channel_id=1, source_target_pairs={{1,2},{2,1},{3,4},{4,3},{5,6},{6,5},{7,8},{8,7},{9,10},{10,9},{11,... | collective-permute-start | bytes 245768 | tf_op jit(solution)/shard_map/ppermute | solution.py:596
  52.3 2.7 %collective-permute-start.8 = (bf16[5,16,128]{2,1,0:T(8,128)(2,1)S(1)}, bf16[5,16,128]{2,1,0:T(8,128)(2,1)S(1)}, u32[]{:S(2)}, u32[]{:S(2)}) collective-permute-start(bf16[5,16,128]{2,1,0:T(8,128)(2,1)S(1)} %get-tuple-element.46), channel_id=1, source_target_pairs={{0,32},{32,64},{64,96},{96,0},{1,33},{33,65},{65,97},{97,1},{2,34}... | collective-permute-start | bytes 61448 | tf_op jit(solution)/shard_map/ppermute | solution.py:579
  53.3 3.1 %collective-permute-start.9 = (bf16[5,16,128]{2,1,0:T(8,128)(2,1)S(1)}, bf16[5,16,128]{2,1,0:T(8,128)(2,1)S(1)}, u32[]{:S(2)}, u32[]{:S(2)}) collective-permute-start(bf16[5,16,128]{2,1,0:T(8,128)(2,1)S(1)} %get-tuple-element.47), channel_id=1, source_target_pairs={{0,64},{32,96},{64,0},{96,32},{1,65},{33,97},{65,1},{97,33},{2,66}... | collective-permute-start | bytes 61448 | tf_op jit(solution)/shard_map/ppermute | solution.py:579
  54.9 3.2 %collective-permute-start.10 = (bf16[5,16,128]{2,1,0:T(8,128)(2,1)S(1)}, bf16[5,16,128]{2,1,0:T(8,128)(2,1)S(1)}, u32[]{:S(2)}, u32[]{:S(2)}) collective-permute-start(bf16[5,16,128]{2,1,0:T(8,128)(2,1)S(1)} %get-tuple-element.48), channel_id=1, source_target_pairs={{0,96},{32,0},{64,32},{96,64},{1,97},{33,1},{65,33},{97,65},{2,98}... | collective-permute-start | bytes 61448 | tf_op jit(solution)/shard_map/ppermute | solution.py:579
  59.6 1.7 %collective-permute-start.11 = (bf16[384,128]{1,0:T(8,128)(2,1)S(1)}, bf16[384,128]{1,0:T(8,128)(2,1)S(1)}, u32[]{:S(2)}, u32[]{:S(2)}) collective-permute-start(bf16[384,128]{1,0:T(8,128)(2,1)S(1)} %get-tuple-element.51), channel_id=1, source_target_pairs={{0,32},{32,64},{64,96},{96,0},{1,33},{33,65},{65,97},{97,1},{2,34}... | collective-permute-start | bytes 294920 | tf_op jit(solution)/shard_map/ppermute | solution.py:579
  59.6 4.3 %collective-permute-start.12 = (bf16[384,128]{1,0:T(8,128)(2,1)S(1)}, bf16[384,128]{1,0:T(8,128)(2,1)S(1)}, u32[]{:S(2)}, u32[]{:S(2)}) collective-permute-start(bf16[384,128]{1,0:T(8,128)(2,1)S(1)} %get-tuple-element.52), channel_id=1, source_target_pairs={{0,64},{32,96},{64,0},{96,32},{1,65},{33,97},{65,1},{97,33},{2,66}... | collective-permute-start | bytes 294920 | tf_op jit(solution)/shard_map/ppermute | solution.py:579
  60.3 5.2 %collective-permute-start.13 = (bf16[384,128]{1,0:T(8,128)(2,1)S(1)}, bf16[384,128]{1,0:T(8,128)(2,1)S(1)}, u32[]{:S(2)}, u32[]{:S(2)}) collective-permute-start(bf16[384,128]{1,0:T(8,128)(2,1)S(1)} %get-tuple-element.53), channel_id=1, source_target_pairs={{0,96},{32,0},{64,32},{96,64},{1,97},{33,1},{65,33},{97,65},{2,98}... | collective-permute-start | bytes 294920 | tf_op jit(solution)/shard_map/ppermute | solution.py:579
  66.4 25.0 %all-to-all-start = ((bf16[32,2,768]{2,1,0:T(2,128)(2,1)}), bf16[32,2,768]{2,1,0:T(2,128)(2,1)S(1)}, u32[]{:S(2)}, u32[]{:S(2)}) async-start(bf16[32,2,768]{2,1,0:T(2,128)(2,1)} %reshape.13), calls=%async_computation | async-start | bytes 196608 | tf_op jit(solution)/shard_map/all_to_all | solution.py:603

commit v8 on v7

--- a/solution.py
+++ b/solution.py
@@ -16,7 +16,7 @@
 whole = pl.BlockSpec(memory_space=pltpu.VMEM)
 scalars = pl.BlockSpec(memory_space=pltpu.SMEM)
 far_off = pl.BlockSpec(memory_space=pltpu.HBM)
-early = 2
+early = 3
 taps = [(2 - n // 3, (1, 0, 2)[n % 3]) for n in range(9)]
 
 
@@ -95,14 +95,22 @@
                 normed, _ = normalise(hidden[step * block + frame, row].astype(f32))
                 value = jnp.concatenate([normed * gain + shift[...], blank], axis=0)
                 modulated[step * block + frame, row] = value.astype(bf16)
+        return carry
+
+    def project(step):
         value = modulated[pl.ds(step * block, block)].reshape(-1, width)
         value = dot_turned(value, w_out[...]).astype(bf16)
         value = value.reshape(block, token_rows, slots, value.shape[-1])
         paired = jnp.concatenate([value[:, 0], value[:, 1]], axis=-1)
         latent[pl.ds(step * block + 2, block)] = paired
-        return carry
-
-    lax.fori_loop(0, groups, share, 0)
+
+    def share_after(step, carry):
+        project(step - 1)
+        return share(step, carry)
+
+    share(0, 0)
+    lax.fori_loop(1, groups, share_after, 0)
+    project(groups - 1)
     for step, piece in enumerate(pieces):
         dst = lax.rem(places[2] + step, groups)
         piece[...] = latent[pl.ds(dst * block, block + 2)]
@@ -154,6 +162,15 @@
     return held_first[n] if n < early else held_rest[n - early]
 
 
+def tail_rows(depth, channels):
+    return -(-depth // (channels // lanes)) * slots
+
+
+def tail_place(frame, start, channels):
+    blocks = channels // lanes
+    return start + frame // blocks * slots, frame % blocks * lanes
+
+
 def pack_kernel(places, grad, grad_ahead, w_in, *rest):
     pieces = rest[:4]
     near, far, latent, wide, patches = rest[4:]
@@ -167,13 +184,13 @@
             at = frame * cols
             value = grad[frame, row] if frame < frames else grad_ahead[frame - frames, row]
             out[at : at + cols] = value
-        at = (frames + 2) * cols
-        tail = flat(latent[...])
-        count = tail.shape[0] * lanes // channels
-        for lane in range(channels // lanes):
-            out[at : at + count, lane * lanes : (lane + 1) * lanes] = tail[
-                lane * count : (lane + 1) * count
-            ]
+        half = lanes // groups
+        for frame in range(frames + 2):
+            tops = [latent[src, frame][:, :half] for src in range(groups)]
+            ends = [latent[src, frame][:, -half:] for src in range(groups)]
+            tops, ends = jnp.concatenate(tops, axis=-1), jnp.concatenate(ends, axis=-1)
+            at, lane = tail_place(frame, (frames + 2) * cols, channels)
+            out[at : at + slots, lane : lane + lanes] = jnp.where(row == 0, tops, ends)
     for frame in range(frames + 2):
         for row in range(rows):
             value = grad[frame, row] if frame < frames else grad_ahead[frame - frames, row]
@@ -196,7 +213,7 @@
     frames, rows, cols, channels = grad.shape
     groups = len(pieces)
     latent = jax.ShapeDtypeStruct((groups,) + pieces[0].shape, bf16)
-    total = (frames + 2) * cols + latent.size // channels
+    total = (frames + 2) * cols + tail_rows(frames + 2, channels)
     return pl.pallas_call(
         pack_kernel,
         in_specs=[scalars] + [whole] * (3 + groups),
@@ -222,8 +239,8 @@
     for n, (kt, ky) in enumerate(taps):
         lo, hi = max(0, ky - 1), rows + min(0, ky - 1)
         window = flat(wide[2 - kt : depth - kt, lo + 1 - ky : hi + 1 - ky])
-        if n >= early:
-            for copy in copies[n - early]:
+        if n >= early and n % 3 == 0:
+            for copy in sum(copies[n - early : n - early + 3], []):
                 copy.wait()
         part = dot_turned(window, weight_matrix(held_first, held_rest, n))
         for lane in range(total.shape[0]):
@@ -332,8 +349,9 @@
     edge_conv(even, own, near_rows, far_rows, held_first, held_rest, total, wide)
     groups, depth, _, pair = latent.shape
     width = pair // 2
-    count = groups * depth * slots * lanes // near_rows.shape[1]
-    start = near_rows.shape[0] - count
+    channels = near_rows.shape[1]
+    start = depth * own.shape[3]
+    part = width // 2
     half = windows.shape[3]
     block = half // groups
     tokens[...] = jnp.zeros_like(tokens)
@@ -343,15 +361,17 @@
             value = latent[src, frame].astype(f32)[:block]
             tokens[frame, 1, at] = value[:, :width]
             tokens[frame, 2, at] = value[:, width:]
-            row = (src * depth + frame) * slots
-            lane = row // count * lanes
-            row = start + row % count
+            row, lane = tail_place(frame, start, channels)
             ends = [
                 ref[row : row + slots, lane : lane + lanes].astype(f32)[:block]
                 for ref in (near_rows, far_rows)
             ]
-            tokens[frame, 0, at] = jnp.where(even, ends[1], ends[0])[:, width:]
-            tokens[frame, 3, at] = jnp.where(even, ends[0], ends[1])[:, :width]
+            pick = slice(src * part, (src + 1) * part)
+            none = jnp.zeros((block, part), f32)
+            above = jnp.where(even, ends[1], ends[0])[:, pick]
+            below = jnp.where(even, ends[0], ends[1])[:, pick]
+            tokens[frame, 0, at] = jnp.concatenate([none, above], axis=-1)
+            tokens[frame, 3, at] = jnp.concatenate([below, none], axis=-1)
     for q in range(2):
         left = tokens[:, :, 7 + q : 7 + q + half]
         right = tokens[:, :, 8 + q : 8 + q + half]
@@ -360,22 +380,27 @@
     latent_phase(total, (0, 1), (0, 1), 0, windows, patches, spread)
     for n, row in enumerate((0, 3)):
         tokens[:, n, 0:half] = shares_of(spread, row, half)
-    none = jnp.zeros((block, width), f32)
-    fill = jnp.zeros((slots - block, 2 * width), f32)
-    for dst in range(groups):
-        at = slice(dst * block, (dst + 1) * block)
-        for frame in range(depth):
-            up = jnp.concatenate([none, tokens[frame, 0, at]], axis=-1)
-            down = jnp.concatenate([tokens[frame, 1, at], none], axis=-1)
-            padded = lambda v: jnp.concatenate([v, fill], axis=0).astype(bf16)
-            near_out[dst, frame] = padded(jnp.where(even, down, up))
-            far_out[dst, frame] = padded(jnp.where(even, up, down))
+    fill = jnp.zeros((slots - block, groups * part), f32)
+    for frame in range(depth):
+        up, down = [
+            jnp.concatenate(
+                [
+                    tokens[frame, n, dst * block : (dst + 1) * block][:, lo : lo + part]
+                    for dst in range(groups)
+                ],
+                axis=-1,
+            )
+            for n, lo in ((0, part), (1, 0))
+        ]
+        padded = lambda v: jnp.concatenate([v, fill], axis=0).astype(bf16)
+        near_out[frame] = padded(jnp.where(even, down, up))
+        far_out[frame] = padded(jnp.where(even, up, down))
 
 
 def edge_part(places, own, latent, near_rows, far_rows, held_first, held_rest, patches):
     groups, depth, _, pair = latent.shape
     blocks, frames, _, cols, _ = own.shape
-    out = jax.ShapeDtypeStruct(latent.shape, bf16)
+    out = jax.ShapeDtypeStruct((depth, slots, groups * pair // 4), bf16)
     return pl.pallas_call(
         edge_kernel,
         out_shape=[
@@ -435,12 +460,21 @@
     )(own, windows, patches, spread)
 
 
-def share_kernel(places, centre, near_share, far_share, *pieces):
+def share_kernel(places, centre, near_share, far_share, *rest):
+    pieces, total = rest[:-1], rest[-1]
+    even = places[0] != 0
     groups = len(pieces)
+    near, far = near_share[...].astype(f32), far_share[...].astype(f32)
+    first = jnp.where(even, far, near)
+    last = jnp.where(even, near, far)
+    part = centre.shape[-1] // 4
+    none = jnp.zeros(first.shape[:2] + (2 * part,), f32)
+    for dst in range(groups):
+        pick = slice(dst * part, (dst + 1) * part)
+        terms = jnp.concatenate([first[:, :, pick], none, last[:, :, pick]], axis=-1)
+        total[dst] = centre[dst] + terms
     for step, piece in enumerate(pieces):
-        dst = lax.rem(places[2] + step, groups)
-        value = centre[dst] + near_share[dst].astype(f32) + far_share[dst].astype(f32)
-        piece[...] = value.astype(bf16)
+        piece[...] = total[lax.rem(places[2] + step, groups)].astype(bf16)
 
 
 def share_pieces(places, centre, near_share, far_share):
@@ -450,6 +484,7 @@
         out_shape=[jax.ShapeDtypeStruct(centre.shape[1:], bf16)] * groups,
         in_specs=[scalars] + [whole] * 3,
         out_specs=[whole] * groups,
+        scratch_shapes=[pltpu.VMEM(centre.shape, f32)],
         compiler_params=params(4),
         name="share_pieces",
     )(places, centre, near_share, far_share)
@@ -502,24 +537,51 @@
 
 
 def middle_kernel(*refs):
-    send = refs[-1]
-    total = sum(ref[...].astype(f32) for ref in refs[:-1])
-    count, rows, width = send.shape
-    total = total.reshape(count // 2, rows, 2 * width).astype(bf16)
-    send[0 : count // 2] = total[:, :, :width]
-    send[count // 2 :] = total[:, :, width:]
+    refs, send, total = refs[:-2], refs[-2], refs[-1]
+    count = send.shape[0]
+    total[...] = sum(ref[...].astype(f32) for ref in refs)
+    depth, pair = total.shape
+    width = pair // 2
+    rows = 2 * depth // count
+    half = rows // 2
+    fill = jnp.zeros((send.shape[1] - half, pair), f32)
+    for n in range(count):
+        at, lane = n % (count // 2) * rows, n // (count // 2) * width
+        value = total[at : at + rows, lane : lane + width]
+        value = jnp.concatenate([value[:half], value[half:]], axis=-1)
+        send[n] = jnp.concatenate([value, fill], axis=0).astype(bf16)
 
 
 def middle_sum(got, count):
     depth, pair = got[0].shape
+    rows = -(-depth // count // 16) * 16
     return pl.pallas_call(
         middle_kernel,
-        out_shape=jax.ShapeDtypeStruct((count, 2 * depth // count, pair // 2), bf16),
+        out_shape=jax.ShapeDtypeStruct((count, rows, pair), bf16),
         in_specs=[whole] * len(got),
         out_specs=whole,
+        scratch_shapes=[pltpu.VMEM((depth, pair), f32)],
         compiler_params=params(4),
         name="middle_sum",
     )(*got)
+
+
+def final_kernel(factor, pieces, out):
+    half, width = out.shape[0] // 2, out.shape[1]
+    total = jnp.sum(pieces[...].astype(f32), axis=0) * factor
+    out[:half] = total[:half, :width]
+    out[half:] = total[:half, width:]
+
+
+def final_sum(pieces, rows, factor):
+    return pl.pallas_call(
+        functools.partial(final_kernel, factor),
+        out_shape=jax.ShapeDtypeStruct((rows, pieces.shape[2] // 2), f32),
+        in_specs=[whole],
+        out_specs=whole,
+        compiler_params=params(4),
+        name="final_sum",
+    )(pieces)
 
 
 def hidden_kernel(hidden, token_grad, scale, w_out, grad_hidden):
@@ -602,7 +664,8 @@
     grad_hidden = hidden_grad(hidden, token_grad, mod_scale, w_out)
     pieces = lax.all_to_all(middle_sum(got, strips), "height", 0, 0, tiled=True)
     total_tokens = math.prod(hidden.shape[:3]) * groups * strips
-    grad_out_weight = jnp.sum(pieces.astype(f32), axis=0) / math.sqrt(total_tokens)
+    model_rows = w_out.shape[1] // (groups * strips)
+    grad_out_weight = final_sum(pieces, model_rows, 1.0 / math.sqrt(total_tokens))
     return (grad_hidden, grad_out_weight)
 
 

time: 92.6 us -> 91.1 us (0.984)
  starting transfers between devices: 32.6 us -> 31.5 us
  local copies, waits for them, and re-layouts: 6.68 us -> 5.7 us
    pallas_call x1 -> x2, Pallas kernels: 0.12 us -> 1.49 us  [the longest x1 0.78 us: middle_sum(): pl.pallas_call(middle_kernel, out_shape=jax.ShapeDtypeStruct((count, rows...]
    all_to_all x1, starting transfers between devices: 15.9 us -> 14.6 us  [shards(): pieces = lax.all_to_all(middle_sum(got, strips), 'height', 0, 0, tiled=True)]
    unnamed x14 -> x12, local copies, waits for them, and re-layouts: 6.68 us -> 5.7 us
  transfers between devices with their start and end apart: 15 -> 15, of which waited for: 8 -> 8; matrix products, arithmetic and copies ran while one was open for 5% -> 6% of each run, Pallas kernels for 28% -> 28%
where the time goes in v8:
time: 91.1 us; the launch traced here: 90.7 us
  Pallas kernels  38 us (42%)
  starting transfers between devices  31.5 us (35%)
  waiting for transfers between devices  14.6 us (16%)
  local copies, waits for them, and re-layouts  5.7 us (6%)
    pallas_call x1, Pallas kernels, own_part(): pl.pallas_call(own_kernel, out_shape=[jax.ShapeDtypeStruct((channels // l...  15.9 us
    all_to_all x1, starting transfers between devices, shards(): pieces = lax.all_to_all(middle_sum(got, strips), 'height', 0, 0, tiled=True)  14.6 us
    ppermute x9, waiting for transfers between devices, round_tm(): lax.ppermute(pieces[k], 'tm', hops(k))  11.9 us
    ppermute x9, starting transfers between devices, round_tm(): lax.ppermute(pieces[k], 'tm', hops(k))  5.78 us
    unnamed x12, local copies, waits for them, and re-layouts  5.7 us
    pallas_call x1, Pallas kernels, edge_part(): pl.pallas_call(edge_kernel, out_shape=[out, out, jax.ShapeDtypeStruct((2,...  5.35 us
    ppermute x1, starting transfers between devices, shards(): near_share = lax.ppermute(near_share, 'height', near)  4.49 us
    pallas_call x1, Pallas kernels, hidden_grad(): pl.pallas_call(hidden_kernel, out_shape=jax.ShapeDtypeStruct(hidden.shape...  3.61 us
  transfers between devices with their start and end apart: 15, of which 8 were waited for; matrix products, arithmetic and copies ran while one was open for 6% of the time, Pallas kernels for 28%

profile of v8, /device:TPU:1, one launch (start us, length us, event | category | flops | bytes accessed | tf_op | source)
XLA Modules:
  0.0 90.7 jit_solution(1049797322326029132)
XLA Ops:
  0.6 2.0 %fetch.1 = bf16[2,4,96,512]{3,2,1,0:T(8,128)(2,1)} custom-call(bf16[3,4,96,512]{3,2,1,0:T(8,128)(2,1)} %grad.3), custom_call_target="tpu_custom_call" | custom-call | tf_op jit(solution)/shard_map/fetch/pallas_call | solution.py:50
  2.7 3.5 %collective-permute-start = (bf16[2,4,96,512]{3,2,1,0:T(8,128)(2,1)}, bf16[2,4,96,512]{3,2,1,0:T(8,128)(2,1)S(1)}, u32[]{:S(2)}, u32[]{:S(2)}) collective-permute-start(bf16[2,4,96,512]{3,2,1,0:T(8,128)(2,1)} %fetch.1), channel_id=1, source_target_pairs={{32,0},{64,32},{96,64},{33,1},{65,33},{97,65},{34,2},{66,34},{98,6... | collective-permute-start | bytes 2359304 | tf_op jit(solution)/shard_map/ppermute | solution.py:645
  6.2 1.9 %copy.10.hidden = bf16[12,2,12,3072]{3,2,1,0:T(8,128)(2,1)S(1)} copy(bf16[12,2,12,3072]{3,1,2,0:T(2,128)(2,1)} %param.7) | data formatting | bytes 3538944 | tf_op args[0]
  8.9 3.4 %modulate.1 = (bf16[12,2,16,3072]{3,2,1,0:T(8,128)(2,1)S(1)}, bf16[3,512,1536]{2,1,0:T(8,128)(2,1)S(1)}, bf16[5,16,128]{2,1,0:T(8,128)(2,1)S(1)}, bf16[5,16,128]...) custom-call(s32[3]{0:T(128)S(1)} %pad_add_fusion.places, ...), custom_call_target="tpu_custom_call" | custom-call | flops 150994944 | bytes 4718592 | tf_op jit(solution)/shard_map/modulate/pallas_call | solution.py:125
  12.3 1.3 %collective-permute-start.1 = (bf16[5,16,128]{2,1,0:T(8,128)(2,1)S(1)}, bf16[5,16,128]{2,1,0:T(8,128)(2,1)S(1)}, u32[]{:S(2)}, u32[]{:S(2)}) collective-permute-start(bf16[5,16,128]{2,1,0:T(8,128)(2,1)S(1)} %get-tuple-element.30), channel_id=1, source_target_pairs={{0,32},{32,64},{64,96},{96,0},{1,33},{33,65},{65,97},{97,1},{2,34}... | collective-permute-start | bytes 61448 | tf_op jit(solution)/shard_map/ppermute | solution.py:641
  14.5 2.0 %collective-permute-done.2.rest_2_ = bf16[5,16,128]{2,1,0:T(8,128)(2,1)S(1)} collective-permute-done((bf16[5,16,128]{2,1,0:T(8,128)(2,1)S(1)}, bf16[5,16,128]{2,1,0:T(8,128)(2,1)S(1)}, u32[]{:S(2)}, u32[]{:S(2)}) %collective-permute-start.2) | collective-permute-done | bytes 20512 | tf_op jit(solution)/shard_map/ppermute | solution.py:641
  16.5 1.7 %collective-permute-done.3.rest_3_ = bf16[5,16,128]{2,1,0:T(8,128)(2,1)S(1)} collective-permute-done((bf16[5,16,128]{2,1,0:T(8,128)(2,1)S(1)}, bf16[5,16,128]{2,1,0:T(8,128)(2,1)S(1)}, u32[]{:S(2)}, u32[]{:S(2)}) %collective-permute-start.3) | collective-permute-done | bytes 20512 | tf_op jit(solution)/shard_map/ppermute | solution.py:641
  18.2 1.9 %pack_rows.1 = (bf16[512,512]{1,0:T(8,128)(2,1)S(1)}, bf16[512,512]{1,0:T(8,128)(2,1)S(1)}, bf16[4,5,16,128]{3,2,1,0:T(8,128)(2,1)S(1)}, bf16[5,4,96,1536]{3,2,1,0:T(8,128)(2,1)S(1)}, bf16[4,768,512]{2,1,0:T(8,128)(2,1)S(1)}) custom-call(s32[3]{0:T(128)S(1)} %pad_add_fusion.places, bf16[3,4,96,512]{3,2,1,0:T(8,128)(2,1)S(1)} %copy-done, ...), custom_call_target="tpu_custom_call" | custom-call | tf_op jit(solution)/shard_map/pack_rows/pallas_call | solution.py:217
  20.1 1.7 %collective-permute-start.4 = (bf16[512,512]{1,0:T(8,128)(2,1)S(1)}, bf16[512,512]{1,0:T(8,128)(2,1)S(1)}, u32[]{:S(2)}, u32[]{:S(2)}) collective-permute-start(bf16[512,512]{1,0:T(8,128)(2,1)S(1)} %get-tuple-element.37), channel_id=1, source_target_pairs={{0,1},{1,0},{2,3},{3,2},{4,5},{5,4},{6,7},{7,6},{8,9},{9,8},{10,11... | collective-permute-start | bytes 1572872 | tf_op jit(solution)/shard_map/ppermute | solution.py:653
  21.8 0.9 collective-permute-start.5
  22.7 15.9 %own_part.1 = (f32[4,3,4,96,128]{4,3,2,1,0:T(8,128)S(1)}, bf16[6,512,1536]{2,1,0:T(8,128)(2,1)S(1)}) custom-call(bf16[5,4,96,1536]{3,2,1,0:T(8,128)(2,1)S(1)} %get-tuple-element.33.wide, bf16[3,3,3,512,512]{4,3,2,1,0:T(8,128)(2,1)} %w_section.3, bf16[3,512,1536]{2,1,0:T(8,128)(2,1)S(1)} %get-tuple-element.34.held_first), custom_call_target="tpu_custom_call" | custom-call | flops 42278584320 | bytes 14155776 | tf_op jit(solution)/shard_map/own_part/pallas_call | solution.py:258
  38.6 5.4 %edge_part.1 = (bf16[5,16,128]{2,1,0:T(8,128)(2,1)S(1)}, bf16[5,16,128]{2,1,0:T(8,128)(2,1)S(1)}, bf16[2,5,4,48,128]{4,3,2,1,0:T(8,128)(2,1)S(1)}, f32[5,4,56,128]{3,2,1,0:T(8,128)S(1)}) custom-call(s32[3]{0:T(128)S(1)} %pad_add_fusion.places, f32[4,3,4,96,128]{4,3,2,1,0:T(8,128)S(1)} %get-tuple-element.35.own, ...), custom_call_target="tpu_custom_call" | custom-call | flops 3623878656 | tf_op jit(solution)/shard_map/edge_part/pallas_call | solution.py:404
  44.0 4.5 %collective-permute-start.6 = (bf16[5,16,128]{2,1,0:T(8,128)(2,1)S(1)}, bf16[5,16,128]{2,1,0:T(8,128)(2,1)S(1)}, u32[]{:S(2)}, u32[]{:S(2)}) collective-permute-start(bf16[5,16,128]{2,1,0:T(8,128)(2,1)S(1)} %get-tuple-element.43), channel_id=1, source_target_pairs={{0,1},{1,0},{2,3},{3,2},{4,5},{5,4},{6,7},{7,6},{8,9},{9,8},{10,11... | collective-permute-start | bytes 61448 | tf_op jit(solution)/shard_map/ppermute | solution.py:659
  49.1 2.2 %inner_part.1.centre = f32[4,5,16,128]{3,2,1,0:T(8,128)S(1)} custom-call(f32[4,3,4,96,128]{4,3,2,1,0:T(8,128)S(1)} %get-tuple-element.35.own, bf16[2,5,4,48,128]{4,3,2,1,0:T(8,128)(2,1)S(1)} %get-tuple-element.41.windows, bf16[4,768,512]{2,1,0:T(8,128)(2,1)S(1)} %get-tuple-element.40.patches, f32[5,4,56,128]{3,2,1,0:T(8,128)S(1)} %get-tuple-element.42.spread_in), custom_call_target="tpu_custom_call" | custom-call | flops 3623878656 | tf_op jit(solution)/shard_map/inner_part/pallas_call | solution.py:446
  52.7 2.0 %collective-permute-start.9 = (bf16[5,16,128]{2,1,0:T(8,128)(2,1)S(1)}, bf16[5,16,128]{2,1,0:T(8,128)(2,1)S(1)}, u32[]{:S(2)}, u32[]{:S(2)}) collective-permute-start(bf16[5,16,128]{2,1,0:T(8,128)(2,1)S(1)} %get-tuple-element.47), channel_id=1, source_target_pairs={{0,64},{32,96},{64,0},{96,32},{1,65},{33,97},{65,1},{97,33},{2,66}... | collective-permute-start | bytes 61448 | tf_op jit(solution)/shard_map/ppermute | solution.py:641
  54.7 1.5 %collective-permute-done.9.rest_2_ = bf16[5,16,128]{2,1,0:T(8,128)(2,1)S(1)} collective-permute-done((bf16[5,16,128]{2,1,0:T(8,128)(2,1)S(1)}, bf16[5,16,128]{2,1,0:T(8,128)(2,1)S(1)}, u32[]{:S(2)}, u32[]{:S(2)}) %collective-permute-start.9) | collective-permute-done | bytes 20512 | tf_op jit(solution)/shard_map/ppermute | solution.py:641
  56.2 1.7 %collective-permute-done.10.rest_3_ = bf16[5,16,128]{2,1,0:T(8,128)(2,1)S(1)} collective-permute-done((bf16[5,16,128]{2,1,0:T(8,128)(2,1)S(1)}, bf16[5,16,128]{2,1,0:T(8,128)(2,1)S(1)}, u32[]{:S(2)}, u32[]{:S(2)}) %collective-permute-start.10) | collective-permute-done | bytes 20512 | tf_op jit(solution)/shard_map/ppermute | solution.py:641
  57.9 1.4 %weight_terms.1 = (bf16[12,2,16,64]{3,2,1,0:T(8,128)(2,1)S(1)}, bf16[384,128]{1,0:T(8,128)(2,1)S(1)}, bf16[384,128]{1,0:T(8,128)(2,1)S(1)}, bf16[384,128]{1,0:T(8,128)(2,1)S(1)}, bf16[384,128]{1,0:T(8,128)(2,1)S(1)}) custom-call(s32[3]{0:T(128)S(1)} %pad_add_fusion.places, bf16[12,2,16,3072]{3,2,1,0:T(8,128)(2,1)S(1)} %get-tuple-element.28.modulated, ...), custom_call_target="tpu_custom_call" | custom-call | tf_op jit(solution)/shard_map/weight_terms/pallas_call | solution.py:524
  61.1 2.6 %collective-permute-done.12.refs_2_ = bf16[384,128]{1,0:T(8,128)(2,1)S(1)} collective-permute-done((bf16[384,128]{1,0:T(8,128)(2,1)S(1)}, bf16[384,128]{1,0:T(8,128)(2,1)S(1)}, u32[]{:S(2)}, u32[]{:S(2)}) %collective-permute-start.12) | collective-permute-done | bytes 98336 | tf_op jit(solution)/shard_map/ppermute | solution.py:641
  63.7 1.5 %collective-permute-done.13.refs_3_ = bf16[384,128]{1,0:T(8,128)(2,1)S(1)} collective-permute-done((bf16[384,128]{1,0:T(8,128)(2,1)S(1)}, bf16[384,128]{1,0:T(8,128)(2,1)S(1)}, u32[]{:S(2)}, u32[]{:S(2)}) %collective-permute-start.13) | collective-permute-done | bytes 98336 | tf_op jit(solution)/shard_map/ppermute | solution.py:641
  66.0 14.6 %all-to-all-start = ((bf16[32,16,128]{2,1,0:T(8,128)(2,1)}), bf16[32,16,128]{2,1,0:T(8,128)(2,1)S(1)}, u32[]{:S(2)}, u32[]{:S(2)}) async-start(bf16[32,16,128]{2,1,0:T(8,128)(2,1)} %middle_sum.1), calls=%async_computation | async-start | bytes 262144 | tf_op jit(solution)/shard_map/all_to_all | solution.py:665
  80.6 3.6 %hidden_grad.1 = bf16[12,2,12,3072]{3,2,1,0:T(8,128)(2,1)S(1)} custom-call(bf16[12,2,12,3072]{3,2,1,0:T(8,128)(2,1)S(1)} %copy.10.hidden, bf16[12,2,16,64]{3,2,1,0:T(8,128)(2,1)S(1)} %get-tuple-element.49.token_grad, f32[1,3072]{1,0:T(1,128)S(1)} %bitcast.9, bf16[64,3072]{1,0:T(8,128)(2,1)S(1)} %bitcast.7), custom_call_target="tpu_custom_call" | custom-call | flops 150994944 | bytes 4718592 | tf_op jit(solution)/shard_map/hidden_grad/pallas_call | solution.py:611
  84.2 3.0 %copy.11 = bf16[12,2,12,3072]{3,1,2,0:T(2,128)(2,1)} copy(bf16[12,2,12,3072]{3,2,1,0:T(8,128)(2,1)S(1)} %hidden_grad.1) | data formatting | bytes 3538944
  87.3 2.8 %all-to-all-done.pieces = bf16[32,16,128]{2,1,0:T(8,128)(2,1)S(1)} async-done(((bf16[32,16,128]{2,1,0:T(8,128)(2,1)}), bf16[32,16,128]{2,1,0:T(8,128)(2,1)S(1)}, u32[]{:S(2)}, u32[]{:S(2)}) %all-to-all-start) | async-done | bytes 131104 | tf_op jit(solution)/shard_map/all_to_all | solution.py:665
  (30 shorter events, 7.0 us)
Async XLA Ops:
  2.7 5.5 %copy-start.1 = (bf16[3072,64]{0,1:T(8,128)(2,1)S(1)}, bf16[3072,64]{0,1:T(8,128)(2,1)}, u32[]{:S(2)}) copy-start(bf16[3072,64]{0,1:T(8,128)(2,1)} %param.10) | copy-start | bytes 1179652
  2.7 5.5 %copy-start.3 = (f32[3072]{0:T(1024)S(1)}, f32[3072]{0:T(1024)}, u32[]{:S(2)}) copy-start(f32[3072]{0:T(1024)} %param.8) | copy-start | bytes 36868
  2.7 15.5 %collective-permute-start = (bf16[2,4,96,512]{3,2,1,0:T(8,128)(2,1)}, bf16[2,4,96,512]{3,2,1,0:T(8,128)(2,1)S(1)}, u32[]{:S(2)}, u32[]{:S(2)}) collective-permute-start(bf16[2,4,96,512]{3,2,1,0:T(8,128)(2,1)} %fetch.1), channel_id=1, source_target_pairs={{32,0},{64,32},{96,64},{33,1},{65,33},{97,65},{34,2},{66,34},{98,6... | collective-permute-start | bytes 2359304 | tf_op jit(solution)/shard_map/ppermute | solution.py:645
  8.2 0.7 copy-start.4
  8.9 9.2 %copy-start = (bf16[3,4,96,512]{3,2,1,0:T(8,128)(2,1)S(1)}, bf16[3,4,96,512]{3,2,1,0:T(8,128)(2,1)}, u32[]{:S(2)}) copy-start(bf16[3,4,96,512]{3,2,1,0:T(8,128)(2,1)} %grad.3) | copy-start | bytes 3538948
  8.9 9.2 %copy-start.2 = (bf16[3,3,3,16,512]{4,3,2,1,0:T(8,128)(2,1)S(1)}, bf16[3,3,3,16,512]{4,3,2,1,0:T(8,128)(2,1)}, u32[]{:S(2)}) copy-start(bf16[3,3,3,16,512]{4,3,2,1,0:T(8,128)(2,1)} %w_in.1) | copy-start | bytes 1327108
  12.3 2.2 %collective-permute-start.1 = (bf16[5,16,128]{2,1,0:T(8,128)(2,1)S(1)}, bf16[5,16,128]{2,1,0:T(8,128)(2,1)S(1)}, u32[]{:S(2)}, u32[]{:S(2)}) collective-permute-start(bf16[5,16,128]{2,1,0:T(8,128)(2,1)S(1)} %get-tuple-element.30), channel_id=1, source_target_pairs={{0,32},{32,64},{64,96},{96,0},{1,33},{33,65},{65,97},{97,1},{2,34}... | collective-permute-start | bytes 61448 | tf_op jit(solution)/shard_map/ppermute | solution.py:641
  13.5 2.9 %collective-permute-start.2 = (bf16[5,16,128]{2,1,0:T(8,128)(2,1)S(1)}, bf16[5,16,128]{2,1,0:T(8,128)(2,1)S(1)}, u32[]{:S(2)}, u32[]{:S(2)}) collective-permute-start(bf16[5,16,128]{2,1,0:T(8,128)(2,1)S(1)} %get-tuple-element.31), channel_id=1, source_target_pairs={{0,64},{32,96},{64,0},{96,32},{1,65},{33,97},{65,1},{97,33},{2,66}... | collective-permute-start | bytes 61448 | tf_op jit(solution)/shard_map/ppermute | solution.py:641
  13.8 4.4 %collective-permute-start.3 = (bf16[5,16,128]{2,1,0:T(8,128)(2,1)S(1)}, bf16[5,16,128]{2,1,0:T(8,128)(2,1)S(1)}, u32[]{:S(2)}, u32[]{:S(2)}) collective-permute-start(bf16[5,16,128]{2,1,0:T(8,128)(2,1)S(1)} %get-tuple-element.32), channel_id=1, source_target_pairs={{0,96},{32,0},{64,32},{96,64},{1,97},{33,1},{65,33},{97,65},{2,98}... | collective-permute-start | bytes 61448 | tf_op jit(solution)/shard_map/ppermute | solution.py:641
  20.1 18.5 %collective-permute-start.4 = (bf16[512,512]{1,0:T(8,128)(2,1)S(1)}, bf16[512,512]{1,0:T(8,128)(2,1)S(1)}, u32[]{:S(2)}, u32[]{:S(2)}) collective-permute-start(bf16[512,512]{1,0:T(8,128)(2,1)S(1)} %get-tuple-element.37), channel_id=1, source_target_pairs={{0,1},{1,0},{2,3},{3,2},{4,5},{5,4},{6,7},{7,6},{8,9},{9,8},{10,11... | collective-permute-start | bytes 1572872 | tf_op jit(solution)/shard_map/ppermute | solution.py:653
  21.8 16.8 %collective-permute-start.5 = (bf16[512,512]{1,0:T(8,128)(2,1)S(1)}, bf16[512,512]{1,0:T(8,128)(2,1)S(1)}, u32[]{:S(2)}, u32[]{:S(2)}) collective-permute-start(bf16[512,512]{1,0:T(8,128)(2,1)S(1)} %get-tuple-element.38), channel_id=1, source_target_pairs={{1,2},{2,1},{3,4},{4,3},{5,6},{6,5},{7,8},{8,7},{9,10},{10,9},{11,... | collective-permute-start | bytes 1572872 | tf_op jit(solution)/shard_map/ppermute | solution.py:652
  44.0 7.4 %collective-permute-start.6 = (bf16[5,16,128]{2,1,0:T(8,128)(2,1)S(1)}, bf16[5,16,128]{2,1,0:T(8,128)(2,1)S(1)}, u32[]{:S(2)}, u32[]{:S(2)}) collective-permute-start(bf16[5,16,128]{2,1,0:T(8,128)(2,1)S(1)} %get-tuple-element.43), channel_id=1, source_target_pairs={{0,1},{1,0},{2,3},{3,2},{4,5},{5,4},{6,7},{7,6},{8,9},{9,8},{10,11... | collective-permute-start | bytes 61448 | tf_op jit(solution)/shard_map/ppermute | solution.py:659
  48.5 2.9 %collective-permute-start.7 = (bf16[5,16,128]{2,1,0:T(8,128)(2,1)S(1)}, bf16[5,16,128]{2,1,0:T(8,128)(2,1)S(1)}, u32[]{:S(2)}, u32[]{:S(2)}) collective-permute-start(bf16[5,16,128]{2,1,0:T(8,128)(2,1)S(1)} %get-tuple-element.44), channel_id=1, source_target_pairs={{1,2},{2,1},{3,4},{4,3},{5,6},{6,5},{7,8},{8,7},{9,10},{10,9},{11,... | collective-permute-start | bytes 61448 | tf_op jit(solution)/shard_map/ppermute | solution.py:658
  52.0 2.7 %collective-permute-start.8 = (bf16[5,16,128]{2,1,0:T(8,128)(2,1)S(1)}, bf16[5,16,128]{2,1,0:T(8,128)(2,1)S(1)}, u32[]{:S(2)}, u32[]{:S(2)}) collective-permute-start(bf16[5,16,128]{2,1,0:T(8,128)(2,1)S(1)} %get-tuple-element.46), channel_id=1, source_target_pairs={{0,32},{32,64},{64,96},{96,0},{1,33},{33,65},{65,97},{97,1},{2,34}... | collective-permute-start | bytes 61448 | tf_op jit(solution)/shard_map/ppermute | solution.py:641
  52.7 3.5 %collective-permute-start.9 = (bf16[5,16,128]{2,1,0:T(8,128)(2,1)S(1)}, bf16[5,16,128]{2,1,0:T(8,128)(2,1)S(1)}, u32[]{:S(2)}, u32[]{:S(2)}) collective-permute-start(bf16[5,16,128]{2,1,0:T(8,128)(2,1)S(1)} %get-tuple-element.47), channel_id=1, source_target_pairs={{0,64},{32,96},{64,0},{96,32},{1,65},{33,97},{65,1},{97,33},{2,66}... | collective-permute-start | bytes 61448 | tf_op jit(solution)/shard_map/ppermute | solution.py:641
  54.7 3.2 %collective-permute-start.10 = (bf16[5,16,128]{2,1,0:T(8,128)(2,1)S(1)}, bf16[5,16,128]{2,1,0:T(8,128)(2,1)S(1)}, u32[]{:S(2)}, u32[]{:S(2)}) collective-permute-start(bf16[5,16,128]{2,1,0:T(8,128)(2,1)S(1)} %get-tuple-element.48), channel_id=1, source_target_pairs={{0,96},{32,0},{64,32},{96,64},{1,97},{33,1},{65,33},{97,65},{2,98}... | collective-permute-start | bytes 61448 | tf_op jit(solution)/shard_map/ppermute | solution.py:641
  59.3 1.7 %collective-permute-start.11 = (bf16[384,128]{1,0:T(8,128)(2,1)S(1)}, bf16[384,128]{1,0:T(8,128)(2,1)S(1)}, u32[]{:S(2)}, u32[]{:S(2)}) collective-permute-start(bf16[384,128]{1,0:T(8,128)(2,1)S(1)} %get-tuple-element.51), channel_id=1, source_target_pairs={{0,32},{32,64},{64,96},{96,0},{1,33},{33,65},{65,97},{97,1},{2,34}... | collective-permute-start | bytes 294920 | tf_op jit(solution)/shard_map/ppermute | solution.py:641
  59.4 4.3 %collective-permute-start.12 = (bf16[384,128]{1,0:T(8,128)(2,1)S(1)}, bf16[384,128]{1,0:T(8,128)(2,1)S(1)}, u32[]{:S(2)}, u32[]{:S(2)}) collective-permute-start(bf16[384,128]{1,0:T(8,128)(2,1)S(1)} %get-tuple-element.52), channel_id=1, source_target_pairs={{0,64},{32,96},{64,0},{96,32},{1,65},{33,97},{65,1},{97,33},{2,66}... | collective-permute-start | bytes 294920 | tf_op jit(solution)/shard_map/ppermute | solution.py:641
  60.1 5.2 %collective-permute-start.13 = (bf16[384,128]{1,0:T(8,128)(2,1)S(1)}, bf16[384,128]{1,0:T(8,128)(2,1)S(1)}, u32[]{:S(2)}, u32[]{:S(2)}) collective-permute-start(bf16[384,128]{1,0:T(8,128)(2,1)S(1)} %get-tuple-element.53), channel_id=1, source_target_pairs={{0,96},{32,0},{64,32},{96,64},{1,97},{33,1},{65,33},{97,65},{2,98}... | collective-permute-start | bytes 294920 | tf_op jit(solution)/shard_map/ppermute | solution.py:641
  66.0 24.0 %all-to-all-start = ((bf16[32,16,128]{2,1,0:T(8,128)(2,1)}), bf16[32,16,128]{2,1,0:T(8,128)(2,1)S(1)}, u32[]{:S(2)}, u32[]{:S(2)}) async-start(bf16[32,16,128]{2,1,0:T(8,128)(2,1)} %middle_sum.1), calls=%async_computation | async-start | bytes 262144 | tf_op jit(solution)/shard_map/all_to_all | solution.py:665

commit v9 on v8

--- a/solution.py
+++ b/solution.py
@@ -77,8 +77,12 @@
     ]
 
 
-def modulate_kernel(places, hidden, scale, shift, w_out, w_section, modulated, held, *rest):
-    pieces, latent, sems = rest[:-2], rest[-2], rest[-1]
+def modulate_kernel(
+    places, hidden, scale, shift, w_out_far, w_section, modulated, held, *rest
+):
+    pieces, (latent, w_out, sems, out_sem) = rest[:-4], rest[-4:]
+    out_copy = pltpu.make_async_copy(w_out_far, w_out, out_sem)
+    out_copy.start()
     copies = sum(weight_copies(w_section, held, taps[:early], sems), [])
     for copy in copies:
         copy.start()
@@ -109,6 +113,7 @@
         return share(step, carry)
 
     share(0, 0)
+    out_copy.wait()
     lax.fori_loop(1, groups, share_after, 0)
     project(groups - 1)
     for step, piece in enumerate(pieces):
@@ -129,11 +134,13 @@
             jax.ShapeDtypeStruct((early,) + wide_weight(w_section), bf16),
         ]
         + [piece] * groups,
-        in_specs=[scalars] + [whole] * 4 + [far_off],
+        in_specs=[scalars] + [whole] * 3 + [far_off] * 2,
         out_specs=[whole] * (2 + groups),
         scratch_shapes=[
             pltpu.VMEM((frames + 2, slots, pair), bf16),
+            pltpu.VMEM(w_out.shape, bf16),
             pltpu.SemaphoreType.DMA((3 * early,)),
+            pltpu.SemaphoreType.DMA,
         ],
         compiler_params=params(8),
         cost_estimate=pl.CostEstimate(
@@ -171,9 +178,45 @@
     return start + frame // blocks * slots, frame % blocks * lanes
 
 
-def pack_kernel(places, grad, grad_ahead, w_in, *rest):
+def widen_kernel(grad, w_in, wide, patches):
+    frames, rows, _, _ = grad.shape
+    for frame in range(frames):
+        for row in range(rows):
+            wide[frame, row] = widened(grad[frame, row])
+    patches[...] = jnp.zeros_like(patches)
+    lat = w_in.shape[3]
+    for n in range(4 * 3 * 2 * 2 * 2 * 2):
+        p, q, kt, a, b, pp, qq = [
+            n // size % top
+            for size, top in ((96, 2), (48, 2), (16, 3), (8, 2), (4, 2), (2, 2), (1, 2))
+        ]
+        ky, kx = p - 1 + 2 * a + pp, q - 1 + 2 * b + qq
+        if 0 <= ky < 3 and 0 <= kx < 3:
+            at = (((kt * 2 + a) * 2 + b) * 4 + 2 * pp + qq) * lat
+            patches[2 * p + q, at : at + lat] = w_in[kt, ky, kx]
+
+
+def widen_rows(grad, w_in):
+    frames, rows, cols, channels = grad.shape
+    return pl.pallas_call(
+        widen_kernel,
+        in_specs=[whole] * 2,
+        out_specs=[whole] * 2,
+        out_shape=[
+            jax.ShapeDtypeStruct((frames, rows, cols, 3 * channels), bf16),
+            jax.ShapeDtypeStruct((4, 48 * w_in.shape[3], channels), bf16),
+        ],
+        compiler_params=params(4),
+        cost_estimate=pl.CostEstimate(
+            flops=20 * grad.size, bytes_accessed=12 * grad.size, transcendentals=0
+        ),
+        name="widen_rows",
+    )(grad, w_in)
+
+
+def pack_kernel(places, grad, grad_ahead, *rest):
     pieces = rest[:4]
-    near, far, latent, wide, patches = rest[4:]
+    near, far, latent = rest[4:]
     frames, rows, cols, channels = grad.shape
     groups = len(pieces)
     for step, piece in enumerate(pieces):
@@ -191,87 +234,80 @@
             tops, ends = jnp.concatenate(tops, axis=-1), jnp.concatenate(ends, axis=-1)
             at, lane = tail_place(frame, (frames + 2) * cols, channels)
             out[at : at + slots, lane : lane + lanes] = jnp.where(row == 0, tops, ends)
-    for frame in range(frames + 2):
-        for row in range(rows):
-            value = grad[frame, row] if frame < frames else grad_ahead[frame - frames, row]
-            wide[frame, row] = widened(value)
-
-    patches[...] = jnp.zeros_like(patches)
-    lat = w_in.shape[3]
-    for n in range(4 * 3 * 2 * 2 * 2 * 2):
-        p, q, kt, a, b, pp, qq = [
-            n // size % top
-            for size, top in ((96, 2), (48, 2), (16, 3), (8, 2), (4, 2), (2, 2), (1, 2))
-        ]
-        ky, kx = p - 1 + 2 * a + pp, q - 1 + 2 * b + qq
-        if 0 <= ky < 3 and 0 <= kx < 3:
-            at = (((kt * 2 + a) * 2 + b) * 4 + 2 * pp + qq) * lat
-            patches[2 * p + q, at : at + lat] = w_in[kt, ky, kx]
-
-
-def pack_rows(places, grad, grad_ahead, w_in, pieces):
-    frames, rows, cols, channels = grad.shape
+
+
+def pack_rows(places, grad, grad_ahead, pieces):
+    frames, _, cols, channels = grad.shape
     groups = len(pieces)
-    latent = jax.ShapeDtypeStruct((groups,) + pieces[0].shape, bf16)
     total = (frames + 2) * cols + tail_rows(frames + 2, channels)
     return pl.pallas_call(
         pack_kernel,
-        in_specs=[scalars] + [whole] * (3 + groups),
-        out_specs=[whole] * 5,
+        in_specs=[scalars] + [whole] * (2 + groups),
+        out_specs=[whole] * 3,
         out_shape=[
             jax.ShapeDtypeStruct((total, channels), bf16),
             jax.ShapeDtypeStruct((total, channels), bf16),
-            latent,
-            jax.ShapeDtypeStruct((frames + 2, rows, cols, 3 * channels), bf16),
-            jax.ShapeDtypeStruct((4, 48 * w_in.shape[3], channels), bf16),
-        ],
-        compiler_params=params(8),
+            jax.ShapeDtypeStruct((groups,) + pieces[0].shape, bf16),
+        ],
+        compiler_params=params(4),
         name="pack_rows",
-    )(places, grad, grad_ahead, w_in, *pieces)
-
-
-def own_kernel(wide, w_section, held_first, total, held_rest, sems):
-    depth, rows, cols, _ = wide.shape
-    frames = depth - 2
+    )(places, grad, grad_ahead, *pieces)
+
+
+def own_kernel(wide, grad_ahead, w_section, held_first, total, held_rest, beyond, sems):
+    frames, rows, cols, _ = wide.shape
     copies = weight_copies(w_section, held_rest, taps[early:], sems)
     for copy in sum(copies, []):
         copy.start()
+    for frame in range(2):
+        for row in range(rows):
+            beyond[frame, row] = widened(grad_ahead[frame, row])
     for n, (kt, ky) in enumerate(taps):
         lo, hi = max(0, ky - 1), rows + min(0, ky - 1)
-        window = flat(wide[2 - kt : depth - kt, lo + 1 - ky : hi + 1 - ky])
+        at = slice(lo + 1 - ky, hi + 1 - ky)
         if n >= early and n % 3 == 0:
             for copy in sum(copies[n - early : n - early + 3], []):
                 copy.wait()
-        part = dot_turned(window, weight_matrix(held_first, held_rest, n))
-        for lane in range(total.shape[0]):
-            value = part[:, lane * lanes : (lane + 1) * lanes]
-            value = value.reshape(frames, hi - lo, cols, lanes)
-            if n == 0:
-                total[lane] = value
-            else:
-                total[lane, :, lo:hi] += value
-
-
-def own_part(wide, w_section, held_first):
-    depth, rows, cols, _ = wide.shape
+        weight = weight_matrix(held_first, held_rest, n)
+        for source, first, last in (
+            (wide[2 - kt :, at], 0, kt + 1),
+            (beyond[: 2 - kt, at], kt + 1, frames),
+        ):
+            if first == last:
+                continue
+            part = dot_turned(flat(source), weight)
+            for lane in range(total.shape[0]):
+                value = part[:, lane * lanes : (lane + 1) * lanes]
+                value = value.reshape(last - first, hi - lo, cols, lanes)
+                if n == 0:
+                    total[lane] = value
+                else:
+                    total[lane, first:last, lo:hi] += value
+
+
+def own_part(wide, grad_ahead, w_section, held_first):
+    frames, rows, cols, _ = wide.shape
     channels = w_section.shape[-1]
     return pl.pallas_call(
         own_kernel,
         out_shape=[
-            jax.ShapeDtypeStruct((channels // lanes, depth - 2, rows, cols, lanes), f32),
+            jax.ShapeDtypeStruct((channels // lanes, frames, rows, cols, lanes), f32),
             jax.ShapeDtypeStruct((len(taps) - early,) + wide_weight(w_section), bf16),
         ],
-        in_specs=[whole, far_off, whole],
+        in_specs=[whole, whole, far_off, whole],
         out_specs=[whole] * 2,
-        scratch_shapes=[pltpu.SemaphoreType.DMA((3 * (len(taps) - early),))],
-        compiler_params=params(12),
+        scratch_shapes=[
+            pltpu.VMEM((2, rows, cols, 3 * channels), bf16),
+            pltpu.SemaphoreType.DMA((3 * (len(taps) - early),)),
+        ],
+        compiler_params=params(14),
         cost_estimate=pl.CostEstimate(
-            flops=2 * 14 * wide.size * channels,
+            flops=2 * 24 * wide.size * channels,
             bytes_accessed=2 * w_section.size,
             transcendentals=0,
         ),
         name="own_part",
-    )(wide, w_section, held_first)
+    )(wide, grad_ahead, w_section, held_first)
 
 
 def edge_conv(even, own, near_rows, far_rows, held_first, held_rest, total, wide):
@@ -642,16 +678,23 @@
         ]
 
     ahead = fetch(pltpu.with_memory_space_constraint(section_grad, pltpu.HBM))
+    ahead, hidden = lax.optimization_barrier((ahead, hidden))
     grad_ahead = lax.ppermute(ahead, "tm", [(g + 1, g) for g in range(groups - 1)])
     modulated, held_first, *pieces = modulate(
-        places, hidden, mod_scale, mod_shift, w_out, w_section, groups
+        places,
+        hidden,
+        mod_scale,
+        mod_shift,
+        pltpu.with_memory_space_constraint(w_out, pltpu.HBM),
+        w_section,
+        groups,
     )
-    near_send, far_send, latent, wide, patches = pack_rows(
-        places, section_grad, grad_ahead, w_in, round_tm(pieces)
-    )
+    section_grad, pieces = lax.optimization_barrier((section_grad, pieces))
+    wide, patches = widen_rows(section_grad, w_in)
+    near_send, far_send, latent = pack_rows(places, section_grad, grad_ahead, round_tm(pieces))
     far_rows = lax.ppermute(far_send, "height", far)
     near_rows = lax.ppermute(near_send, "height", near)
-    own, held_rest = own_part(wide, w_section, held_first)
+    own, held_rest = own_part(wide, grad_ahead, w_section, held_first)
     near_share, far_share, windows, spread = edge_part(
         places, own, latent, near_rows, far_rows, held_first, held_rest, patches
     )

time: 91.1 us -> 89.9 us (0.987)
  local copies, waits for them, and re-layouts: 5.7 us -> 3.54 us
  Pallas kernels: 38 us -> 39.1 us
    unnamed x12 -> x13, local copies, waits for them, and re-layouts: 5.7 us -> 3.06 us
    pallas_call x1, Pallas kernels: 3.35 us -> 4.97 us  [modulate(): pl.pallas_call(modulate_kernel, out_shape=[jax.ShapeDtypeStruct((frames,...]
    pallas_call x1 -> x2, Pallas kernels: 1.92 us -> 1.34 us  [the longest x1 0.69 us: pack_rows(): pl.pallas_call(pack_kernel, in_specs=[scalars] + [whole] * (2 + groups),...]
  transfers between devices with their start and end apart: 15 -> 15, of which waited for: 8 -> 8; matrix products, arithmetic and copies ran while one was open for 6% -> 4% of each run, Pallas kernels for 28% -> 30%
where the time goes in v9:
time: 89.9 us; the launch traced here: 89.6 us
  Pallas kernels  39.1 us (43%)
  starting transfers between devices  31.5 us (35%)
  waiting for transfers between devices  14.5 us (16%)
  local copies, waits for them, and re-layouts  3.54 us (4%)
    pallas_call x1, Pallas kernels, own_part(): pl.pallas_call(own_kernel, out_shape=[jax.ShapeDtypeStruct((channels // l...  15.5 us
    all_to_all x1, starting transfers between devices, shards(): pieces = lax.all_to_all(middle_sum(got, strips), 'height', 0, 0, tiled=True)  14.9 us
    ppermute x9, waiting for transfers between devices, round_tm(): lax.ppermute(pieces[k], 'tm', hops(k))  11.8 us
    ppermute x9, starting transfers between devices, round_tm(): lax.ppermute(pieces[k], 'tm', hops(k))  5.77 us
    pallas_call x1, Pallas kernels, edge_part(): pl.pallas_call(edge_kernel, out_shape=[out, out, jax.ShapeDtypeStruct((2,...  5.71 us
    pallas_call x1, Pallas kernels, modulate(): pl.pallas_call(modulate_kernel, out_shape=[jax.ShapeDtypeStruct((frames,...  4.97 us
    ppermute x1, starting transfers between devices, shards(): near_share = lax.ppermute(near_share, 'height', near)  4.27 us
    pallas_call x1, Pallas kernels, hidden_grad(): pl.pallas_call(hidden_kernel, out_shape=jax.ShapeDtypeStruct(hidden.shape...  3.61 us
  transfers between devices with their start and end apart: 15, of which 8 were waited for; matrix products, arithmetic and copies ran while one was open for 4% of the time, Pallas kernels for 30%

profile of v9, /device:TPU:1, one launch (start us, length us, event | category | flops | bytes accessed | tf_op | source)
XLA Modules:
  0.0 89.6 jit_solution(11697785306782367503)
XLA Ops:
  0.6 2.2 %fetch.1 = bf16[2,4,96,512]{3,2,1,0:T(8,128)(2,1)} custom-call(bf16[3,4,96,512]{3,2,1,0:T(8,128)(2,1)} %grad.3), custom_call_target="tpu_custom_call" | custom-call | tf_op jit(solution)/shard_map/fetch/pallas_call | solution.py:50
  2.8 3.3 %collective-permute-start = (bf16[2,4,96,512]{3,2,1,0:T(8,128)(2,1)}, bf16[2,4,96,512]{3,2,1,0:T(8,128)(2,1)S(1)}, u32[]{:S(2)}, u32[]{:S(2)}) collective-permute-start(bf16[2,4,96,512]{3,2,1,0:T(8,128)(2,1)} %fetch.1), channel_id=1, source_target_pairs={{32,0},{64,32},{96,64},{33,1},{65,33},{97,65},{34,2},{66,34},{98,6... | collective-permute-start | bytes 2359304 | tf_op jit(solution)/shard_map/ppermute | solution.py:682
  6.8 5.0 %modulate.1 = (bf16[12,2,16,3072]{3,2,1,0:T(8,128)(2,1)S(1)}, bf16[3,512,1536]{2,1,0:T(8,128)(2,1)S(1)}, bf16[5,16,128]{2,1,0:T(8,128)(2,1)S(1)}, bf16[5,16,128]...) custom-call(s32[3]{0:T(128)S(1)} %pad_add_fusion.places, ...), custom_call_target="tpu_custom_call" | custom-call | flops 150994944 | bytes 4718592 | tf_op jit(solution)/shard_map/modulate/pallas_call | solution.py:130
  11.7 1.3 %collective-permute-start.1 = (bf16[5,16,128]{2,1,0:T(8,128)(2,1)S(1)}, bf16[5,16,128]{2,1,0:T(8,128)(2,1)S(1)}, u32[]{:S(2)}, u32[]{:S(2)}) collective-permute-start(bf16[5,16,128]{2,1,0:T(8,128)(2,1)S(1)} %get-tuple-element.47), channel_id=1, source_target_pairs={{0,32},{32,64},{64,96},{96,0},{1,33},{33,65},{65,97},{97,1},{2,34}... | collective-permute-start | bytes 61448 | tf_op jit(solution)/shard_map/ppermute | solution.py:677
  14.6 1.3 %collective-permute-done.2.rest_2_ = bf16[5,16,128]{2,1,0:T(8,128)(2,1)S(1)} collective-permute-done((bf16[5,16,128]{2,1,0:T(8,128)(2,1)S(1)}, bf16[5,16,128]{2,1,0:T(8,128)(2,1)S(1)}, u32[]{:S(2)}, u32[]{:S(2)}) %collective-permute-start.2) | collective-permute-done | bytes 20512 | tf_op jit(solution)/shard_map/ppermute | solution.py:677
  15.9 2.2 %collective-permute-done.3.rest_3_ = bf16[5,16,128]{2,1,0:T(8,128)(2,1)S(1)} collective-permute-done((bf16[5,16,128]{2,1,0:T(8,128)(2,1)S(1)}, bf16[5,16,128]{2,1,0:T(8,128)(2,1)S(1)}, u32[]{:S(2)}, u32[]{:S(2)}) %collective-permute-start.3) | collective-permute-done | bytes 20512 | tf_op jit(solution)/shard_map/ppermute | solution.py:677
  18.9 1.7 %collective-permute-start.4 = (bf16[512,512]{1,0:T(8,128)(2,1)S(1)}, bf16[512,512]{1,0:T(8,128)(2,1)S(1)}, u32[]{:S(2)}, u32[]{:S(2)}) collective-permute-start(bf16[512,512]{1,0:T(8,128)(2,1)S(1)} %get-tuple-element.51), channel_id=1, source_target_pairs={{0,1},{1,0},{2,3},{3,2},{4,5},{5,4},{6,7},{7,6},{8,9},{9,8},{10,11... | collective-permute-start | bytes 1572872 | tf_op jit(solution)/shard_map/ppermute | solution.py:696
  20.6 0.9 collective-permute-start.5
  21.4 15.5 %own_part.1 = (f32[4,3,4,96,128]{4,3,2,1,0:T(8,128)S(1)}, bf16[6,512,1536]{2,1,0:T(8,128)(2,1)S(1)}) custom-call(bf16[3,4,96,1536]{3,2,1,0:T(8,128)(2,1)S(1)} %get-tuple-element.42.wide, bf16[2,4,96,512]{3,2,1,0:T(8,128)(2,1)S(1)} %collective-permute-done.grad_ahead, bf16[3,3,3,512,512]{4,3,2,1,0:T(8,128)(2,1)} %w_section.3, ...), custom_call_target="tpu_custom_call" | custom-call | flops 43486543872 | bytes 14155776 | tf_op jit(solution)/shard_map/own_part/pallas_call | solution.py:291
  37.0 5.7 %edge_part.1 = (bf16[5,16,128]{2,1,0:T(8,128)(2,1)S(1)}, bf16[5,16,128]{2,1,0:T(8,128)(2,1)S(1)}, bf16[2,5,4,48,128]{4,3,2,1,0:T(8,128)(2,1)S(1)}, f32[5,4,56,128]{3,2,1,0:T(8,128)S(1)}) custom-call(s32[3]{0:T(128)S(1)} %pad_add_fusion.places, f32[4,3,4,96,128]{4,3,2,1,0:T(8,128)S(1)} %get-tuple-element.45.own, ...), custom_call_target="tpu_custom_call" | custom-call | flops 3623878656 | tf_op jit(solution)/shard_map/edge_part/pallas_call | solution.py:440
  42.7 4.3 %collective-permute-start.6 = (bf16[5,16,128]{2,1,0:T(8,128)(2,1)S(1)}, bf16[5,16,128]{2,1,0:T(8,128)(2,1)S(1)}, u32[]{:S(2)}, u32[]{:S(2)}) collective-permute-start(bf16[5,16,128]{2,1,0:T(8,128)(2,1)S(1)} %get-tuple-element.57), channel_id=1, source_target_pairs={{0,1},{1,0},{2,3},{3,2},{4,5},{5,4},{6,7},{7,6},{8,9},{9,8},{10,11... | collective-permute-start | bytes 61448 | tf_op jit(solution)/shard_map/ppermute | solution.py:702
  47.6 2.3 %inner_part.1.centre = f32[4,5,16,128]{3,2,1,0:T(8,128)S(1)} custom-call(f32[4,3,4,96,128]{4,3,2,1,0:T(8,128)S(1)} %get-tuple-element.45.own, bf16[2,5,4,48,128]{4,3,2,1,0:T(8,128)(2,1)S(1)} %get-tuple-element.55.windows, bf16[4,768,512]{2,1,0:T(8,128)(2,1)S(1)} %get-tuple-element.54.patches, f32[5,4,56,128]{3,2,1,0:T(8,128)S(1)} %get-tuple-element.56.spread_in), custom_call_target="tpu_custom_call" | custom-call | flops 3623878656 | tf_op jit(solution)/shard_map/inner_part/pallas_call | solution.py:482
  51.2 2.0 %collective-permute-start.9 = (bf16[5,16,128]{2,1,0:T(8,128)(2,1)S(1)}, bf16[5,16,128]{2,1,0:T(8,128)(2,1)S(1)}, u32[]{:S(2)}, u32[]{:S(2)}) collective-permute-start(bf16[5,16,128]{2,1,0:T(8,128)(2,1)S(1)} %get-tuple-element.61), channel_id=1, source_target_pairs={{0,64},{32,96},{64,0},{96,32},{1,65},{33,97},{65,1},{97,33},{2,66}... | collective-permute-start | bytes 61448 | tf_op jit(solution)/shard_map/ppermute | solution.py:677
  53.3 1.5 %collective-permute-done.9.rest_2_ = bf16[5,16,128]{2,1,0:T(8,128)(2,1)S(1)} collective-permute-done((bf16[5,16,128]{2,1,0:T(8,128)(2,1)S(1)}, bf16[5,16,128]{2,1,0:T(8,128)(2,1)S(1)}, u32[]{:S(2)}, u32[]{:S(2)}) %collective-permute-start.9) | collective-permute-done | bytes 20512 | tf_op jit(solution)/shard_map/ppermute | solution.py:677
  54.7 1.7 %collective-permute-done.10.rest_3_ = bf16[5,16,128]{2,1,0:T(8,128)(2,1)S(1)} collective-permute-done((bf16[5,16,128]{2,1,0:T(8,128)(2,1)S(1)}, bf16[5,16,128]{2,1,0:T(8,128)(2,1)S(1)}, u32[]{:S(2)}, u32[]{:S(2)}) %collective-permute-start.10) | collective-permute-done | bytes 20512 | tf_op jit(solution)/shard_map/ppermute | solution.py:677
  56.5 1.4 %weight_terms.1 = (bf16[12,2,16,64]{3,2,1,0:T(8,128)(2,1)S(1)}, bf16[384,128]{1,0:T(8,128)(2,1)S(1)}, bf16[384,128]{1,0:T(8,128)(2,1)S(1)}, bf16[384,128]{1,0:T(8,128)(2,1)S(1)}, bf16[384,128]{1,0:T(8,128)(2,1)S(1)}) custom-call(s32[3]{0:T(128)S(1)} %pad_add_fusion.places, bf16[12,2,16,3072]{3,2,1,0:T(8,128)(2,1)S(1)} %get-tuple-element.36.modulated, ...), custom_call_target="tpu_custom_call" | custom-call | tf_op jit(solution)/shard_map/weight_terms/pallas_call | solution.py:560
  58.8 0.8 collective-permute-done.11.refs_1_
  59.6 2.6 %collective-permute-done.12.refs_2_ = bf16[384,128]{1,0:T(8,128)(2,1)S(1)} collective-permute-done((bf16[384,128]{1,0:T(8,128)(2,1)S(1)}, bf16[384,128]{1,0:T(8,128)(2,1)S(1)}, u32[]{:S(2)}, u32[]{:S(2)}) %collective-permute-start.12) | collective-permute-done | bytes 98336 | tf_op jit(solution)/shard_map/ppermute | solution.py:677
  62.2 1.5 %collective-permute-done.13.refs_3_ = bf16[384,128]{1,0:T(8,128)(2,1)S(1)} collective-permute-done((bf16[384,128]{1,0:T(8,128)(2,1)S(1)}, bf16[384,128]{1,0:T(8,128)(2,1)S(1)}, u32[]{:S(2)}, u32[]{:S(2)}) %collective-permute-start.13) | collective-permute-done | bytes 98336 | tf_op jit(solution)/shard_map/ppermute | solution.py:677
  63.8 0.8 middle_sum.1
  64.6 14.9 %all-to-all-start = ((bf16[32,16,128]{2,1,0:T(8,128)(2,1)}), bf16[32,16,128]{2,1,0:T(8,128)(2,1)S(1)}, u32[]{:S(2)}, u32[]{:S(2)}) async-start(bf16[32,16,128]{2,1,0:T(8,128)(2,1)} %middle_sum.1), calls=%async_computation | async-start | bytes 262144 | tf_op jit(solution)/shard_map/all_to_all | solution.py:708
  79.5 3.6 %hidden_grad.1 = bf16[12,2,12,3072]{3,2,1,0:T(8,128)(2,1)S(1)} custom-call(bf16[12,2,12,3072]{3,2,1,0:T(8,128)(2,1)S(1)} %copy.10.hidden, bf16[12,2,16,64]{3,2,1,0:T(8,128)(2,1)S(1)} %get-tuple-element.63.token_grad, f32[1,3072]{1,0:T(1,128)S(1)} %bitcast.9, bf16[64,3072]{1,0:T(8,128)(2,1)S(1)} %bitcast.7), custom_call_target="tpu_custom_call" | custom-call | flops 150994944 | bytes 4718592 | tf_op jit(solution)/shard_map/hidden_grad/pallas_call | solution.py:647
  83.1 3.0 %copy.11 = bf16[12,2,12,3072]{3,1,2,0:T(2,128)(2,1)} copy(bf16[12,2,12,3072]{3,2,1,0:T(8,128)(2,1)S(1)} %hidden_grad.1) | data formatting | bytes 3538944
  86.2 2.8 %all-to-all-done.pieces = bf16[32,16,128]{2,1,0:T(8,128)(2,1)S(1)} async-done(((bf16[32,16,128]{2,1,0:T(8,128)(2,1)}), bf16[32,16,128]{2,1,0:T(8,128)(2,1)S(1)}, u32[]{:S(2)}, u32[]{:S(2)}) %all-to-all-start) | async-done | bytes 131104 | tf_op jit(solution)/shard_map/all_to_all | solution.py:708
  (33 shorter events, 6.5 us)
Async XLA Ops:
  0.6 5.5 %copy-start.5 = (bf16[12,2,12,3072]{3,1,2,0:T(2,128)(2,1)S(1)}, bf16[12,2,12,3072]{3,1,2,0:T(2,128)(2,1)}, u32[]{:S(2)}) copy-start(bf16[12,2,12,3072]{3,1,2,0:T(2,128)(2,1)} %param.7) | copy-start | bytes 5308420
  2.8 3.9 %copy-start.3 = (f32[3072]{0:T(1024)S(1)}, f32[3072]{0:T(1024)}, u32[]{:S(2)}) copy-start(f32[3072]{0:T(1024)} %param.8) | copy-start | bytes 36868
  2.8 3.9 %copy-start.4 = (f32[3072]{0:T(1024)S(1)}, f32[3072]{0:T(1024)}, u32[]{:S(2)}) copy-start(f32[3072]{0:T(1024)} %param.9) | copy-start | bytes 36868
  2.8 15.3 %collective-permute-start = (bf16[2,4,96,512]{3,2,1,0:T(8,128)(2,1)}, bf16[2,4,96,512]{3,2,1,0:T(8,128)(2,1)S(1)}, u32[]{:S(2)}, u32[]{:S(2)}) collective-permute-start(bf16[2,4,96,512]{3,2,1,0:T(8,128)(2,1)} %fetch.1), channel_id=1, source_target_pairs={{32,0},{64,32},{96,64},{33,1},{65,33},{97,65},{34,2},{66,34},{98,6... | collective-permute-start | bytes 2359304 | tf_op jit(solution)/shard_map/ppermute | solution.py:682
  6.7 7.2 %copy-start = (bf16[3,4,96,512]{3,2,1,0:T(8,128)(2,1)S(1)}, bf16[3,4,96,512]{3,2,1,0:T(8,128)(2,1)}, u32[]{:S(2)}) copy-start(bf16[3,4,96,512]{3,2,1,0:T(8,128)(2,1)} %grad.3) | copy-start | bytes 3538948
  6.7 7.2 %copy-start.2 = (bf16[3,3,3,16,512]{4,3,2,1,0:T(8,128)(2,1)S(1)}, bf16[3,3,3,16,512]{4,3,2,1,0:T(8,128)(2,1)}, u32[]{:S(2)}) copy-start(bf16[3,3,3,16,512]{4,3,2,1,0:T(8,128)(2,1)} %w_in.1) | copy-start | bytes 1327108
  11.7 2.9 %collective-permute-start.1 = (bf16[5,16,128]{2,1,0:T(8,128)(2,1)S(1)}, bf16[5,16,128]{2,1,0:T(8,128)(2,1)S(1)}, u32[]{:S(2)}, u32[]{:S(2)}) collective-permute-start(bf16[5,16,128]{2,1,0:T(8,128)(2,1)S(1)} %get-tuple-element.47), channel_id=1, source_target_pairs={{0,32},{32,64},{64,96},{96,0},{1,33},{33,65},{65,97},{97,1},{2,34}... | collective-permute-start | bytes 61448 | tf_op jit(solution)/shard_map/ppermute | solution.py:677
  13.0 2.9 %collective-permute-start.2 = (bf16[5,16,128]{2,1,0:T(8,128)(2,1)S(1)}, bf16[5,16,128]{2,1,0:T(8,128)(2,1)S(1)}, u32[]{:S(2)}, u32[]{:S(2)}) collective-permute-start(bf16[5,16,128]{2,1,0:T(8,128)(2,1)S(1)} %get-tuple-element.48), channel_id=1, source_target_pairs={{0,64},{32,96},{64,0},{96,32},{1,65},{33,97},{65,1},{97,33},{2,66}... | collective-permute-start | bytes 61448 | tf_op jit(solution)/shard_map/ppermute | solution.py:677
  13.2 4.9 %collective-permute-start.3 = (bf16[5,16,128]{2,1,0:T(8,128)(2,1)S(1)}, bf16[5,16,128]{2,1,0:T(8,128)(2,1)S(1)}, u32[]{:S(2)}, u32[]{:S(2)}) collective-permute-start(bf16[5,16,128]{2,1,0:T(8,128)(2,1)S(1)} %get-tuple-element.49), channel_id=1, source_target_pairs={{0,96},{32,0},{64,32},{96,64},{1,97},{33,1},{65,33},{97,65},{2,98}... | collective-permute-start | bytes 61448 | tf_op jit(solution)/shard_map/ppermute | solution.py:677
  18.9 18.1 %collective-permute-start.4 = (bf16[512,512]{1,0:T(8,128)(2,1)S(1)}, bf16[512,512]{1,0:T(8,128)(2,1)S(1)}, u32[]{:S(2)}, u32[]{:S(2)}) collective-permute-start(bf16[512,512]{1,0:T(8,128)(2,1)S(1)} %get-tuple-element.51), channel_id=1, source_target_pairs={{0,1},{1,0},{2,3},{3,2},{4,5},{5,4},{6,7},{7,6},{8,9},{9,8},{10,11... | collective-permute-start | bytes 1572872 | tf_op jit(solution)/shard_map/ppermute | solution.py:696
  20.6 16.4 %collective-permute-start.5 = (bf16[512,512]{1,0:T(8,128)(2,1)S(1)}, bf16[512,512]{1,0:T(8,128)(2,1)S(1)}, u32[]{:S(2)}, u32[]{:S(2)}) collective-permute-start(bf16[512,512]{1,0:T(8,128)(2,1)S(1)} %get-tuple-element.52), channel_id=1, source_target_pairs={{1,2},{2,1},{3,4},{4,3},{5,6},{6,5},{7,8},{8,7},{9,10},{10,9},{11,... | collective-permute-start | bytes 1572872 | tf_op jit(solution)/shard_map/ppermute | solution.py:695
  42.7 7.2 %collective-permute-start.6 = (bf16[5,16,128]{2,1,0:T(8,128)(2,1)S(1)}, bf16[5,16,128]{2,1,0:T(8,128)(2,1)S(1)}, u32[]{:S(2)}, u32[]{:S(2)}) collective-permute-start(bf16[5,16,128]{2,1,0:T(8,128)(2,1)S(1)} %get-tuple-element.57), channel_id=1, source_target_pairs={{0,1},{1,0},{2,3},{3,2},{4,5},{5,4},{6,7},{7,6},{8,9},{9,8},{10,11... | collective-permute-start | bytes 61448 | tf_op jit(solution)/shard_map/ppermute | solution.py:702
  46.9 3.0 %collective-permute-start.7 = (bf16[5,16,128]{2,1,0:T(8,128)(2,1)S(1)}, bf16[5,16,128]{2,1,0:T(8,128)(2,1)S(1)}, u32[]{:S(2)}, u32[]{:S(2)}) collective-permute-start(bf16[5,16,128]{2,1,0:T(8,128)(2,1)S(1)} %get-tuple-element.58), channel_id=1, source_target_pairs={{1,2},{2,1},{3,4},{4,3},{5,6},{6,5},{7,8},{8,7},{9,10},{10,9},{11,... | collective-permute-start | bytes 61448 | tf_op jit(solution)/shard_map/ppermute | solution.py:701
  49.9 29.6 %copy-start.1 = (bf16[3072,64]{0,1:T(8,128)(2,1)S(1)}, bf16[3072,64]{0,1:T(8,128)(2,1)}, u32[]{:S(2)}) copy-start(bf16[3072,64]{0,1:T(8,128)(2,1)} %param.10) | copy-start | bytes 1179652
  50.6 2.7 %collective-permute-start.8 = (bf16[5,16,128]{2,1,0:T(8,128)(2,1)S(1)}, bf16[5,16,128]{2,1,0:T(8,128)(2,1)S(1)}, u32[]{:S(2)}, u32[]{:S(2)}) collective-permute-start(bf16[5,16,128]{2,1,0:T(8,128)(2,1)S(1)} %get-tuple-element.60), channel_id=1, source_target_pairs={{0,32},{32,64},{64,96},{96,0},{1,33},{33,65},{65,97},{97,1},{2,34}... | collective-permute-start | bytes 61448 | tf_op jit(solution)/shard_map/ppermute | solution.py:677
  51.2 3.5 %collective-permute-start.9 = (bf16[5,16,128]{2,1,0:T(8,128)(2,1)S(1)}, bf16[5,16,128]{2,1,0:T(8,128)(2,1)S(1)}, u32[]{:S(2)}, u32[]{:S(2)}) collective-permute-start(bf16[5,16,128]{2,1,0:T(8,128)(2,1)S(1)} %get-tuple-element.61), channel_id=1, source_target_pairs={{0,64},{32,96},{64,0},{96,32},{1,65},{33,97},{65,1},{97,33},{2,66}... | collective-permute-start | bytes 61448 | tf_op jit(solution)/shard_map/ppermute | solution.py:677
  53.2 3.2 %collective-permute-start.10 = (bf16[5,16,128]{2,1,0:T(8,128)(2,1)S(1)}, bf16[5,16,128]{2,1,0:T(8,128)(2,1)S(1)}, u32[]{:S(2)}, u32[]{:S(2)}) collective-permute-start(bf16[5,16,128]{2,1,0:T(8,128)(2,1)S(1)} %get-tuple-element.62), channel_id=1, source_target_pairs={{0,96},{32,0},{64,32},{96,64},{1,97},{33,1},{65,33},{97,65},{2,98}... | collective-permute-start | bytes 61448 | tf_op jit(solution)/shard_map/ppermute | solution.py:677
  57.9 1.7 %collective-permute-start.11 = (bf16[384,128]{1,0:T(8,128)(2,1)S(1)}, bf16[384,128]{1,0:T(8,128)(2,1)S(1)}, u32[]{:S(2)}, u32[]{:S(2)}) collective-permute-start(bf16[384,128]{1,0:T(8,128)(2,1)S(1)} %get-tuple-element.65), channel_id=1, source_target_pairs={{0,32},{32,64},{64,96},{96,0},{1,33},{33,65},{65,97},{97,1},{2,34}... | collective-permute-start | bytes 294920 | tf_op jit(solution)/shard_map/ppermute | solution.py:677
  58.0 4.3 %collective-permute-start.12 = (bf16[384,128]{1,0:T(8,128)(2,1)S(1)}, bf16[384,128]{1,0:T(8,128)(2,1)S(1)}, u32[]{:S(2)}, u32[]{:S(2)}) collective-permute-start(bf16[384,128]{1,0:T(8,128)(2,1)S(1)} %get-tuple-element.66), channel_id=1, source_target_pairs={{0,64},{32,96},{64,0},{96,32},{1,65},{33,97},{65,1},{97,33},{2,66}... | collective-permute-start | bytes 294920 | tf_op jit(solution)/shard_map/ppermute | solution.py:677
  58.6 5.2 %collective-permute-start.13 = (bf16[384,128]{1,0:T(8,128)(2,1)S(1)}, bf16[384,128]{1,0:T(8,128)(2,1)S(1)}, u32[]{:S(2)}, u32[]{:S(2)}) collective-permute-start(bf16[384,128]{1,0:T(8,128)(2,1)S(1)} %get-tuple-element.67), channel_id=1, source_target_pairs={{0,96},{32,0},{64,32},{96,64},{1,97},{33,1},{65,33},{97,65},{2,98}... | collective-permute-start | bytes 294920 | tf_op jit(solution)/shard_map/ppermute | solution.py:677
  64.6 24.3 %all-to-all-start = ((bf16[32,16,128]{2,1,0:T(8,128)(2,1)}), bf16[32,16,128]{2,1,0:T(8,128)(2,1)S(1)}, u32[]{:S(2)}, u32[]{:S(2)}) async-start(bf16[32,16,128]{2,1,0:T(8,128)(2,1)} %middle_sum.1), calls=%async_computation | async-start | bytes 262144 | tf_op jit(solution)/shard_map/all_to_all | solution.py:708

commit v10 on v9

--- a/solution.py
+++ b/solution.py
@@ -40,19 +40,30 @@
     return shifted * inverse, inverse
 
 
-def fetch_kernel(grad, ahead, sem):
-    copy = pltpu.make_async_copy(grad.at[0:2], ahead, sem)
-    copy.start()
-    copy.wait()
+def fetch_kernel(grad, ends, between, sems):
+    rows = grad.shape[1]
+    copies = [
+        pltpu.make_async_copy(grad.at[0:2, 0:1], ends.at[:, 0:1], sems.at[0]),
+        pltpu.make_async_copy(grad.at[0:2, rows - 1 : rows], ends.at[:, 1:2], sems.at[1]),
+        pltpu.make_async_copy(grad.at[0:2, 1 : rows - 1], between, sems.at[2]),
+    ]
+    for copy in copies:
+        copy.start()
+    for copy in copies:
+        copy.wait()
 
 
 def fetch(grad):
+    _, rows, cols, channels = grad.shape
     return pl.pallas_call(
         fetch_kernel,
-        out_shape=jax.ShapeDtypeStruct((2,) + grad.shape[1:], bf16),
+        out_shape=[
+            jax.ShapeDtypeStruct((2, 2, cols, channels), bf16),
+            jax.ShapeDtypeStruct((2, rows - 2, cols, channels), bf16),
+        ],
         in_specs=[far_off],
-        out_specs=whole,
-        scratch_shapes=[pltpu.SemaphoreType.DMA],
+        out_specs=[whole] * 2,
+        scratch_shapes=[pltpu.SemaphoreType.DMA((3,))],
         compiler_params=params(4),
         name="fetch",
     )(grad)
@@ -214,7 +225,7 @@
     )(grad, w_in)
 
 
-def pack_kernel(places, grad, grad_ahead, *rest):
+def pack_kernel(places, grad, ends_ahead, *rest):
     pieces = rest[:4]
     near, far, latent = rest[4:]
     frames, rows, cols, channels = grad.shape
@@ -223,10 +234,11 @@
         latent[lax.rem(places[2] + groups - step, groups)] = piece[...]
     for side, out in ((0, near), (1, far)):
         row = places[side]
-        for frame in range(frames + 2):
-            at = frame * cols
-            value = grad[frame, row] if frame < frames else grad_ahead[frame - frames, row]
-            out[at : at + cols] = value
+        for frame in range(frames):
+            out[frame * cols : (frame + 1) * cols] = grad[frame, row]
+        for frame in range(2):
+            at = (frames + frame) * cols
+            out[at : at + cols] = ends_ahead[frame, jnp.minimum(row, 1)]
         half = lanes // groups
         for frame in range(frames + 2):
             tops = [latent[src, frame][:, :half] for src in range(groups)]
@@ -236,7 +248,7 @@
             out[at : at + slots, lane : lane + lanes] = jnp.where(row == 0, tops, ends)
 
 
-def pack_rows(places, grad, grad_ahead, pieces):
+def pack_rows(places, grad, ends_ahead, pieces):
     frames, _, cols, channels = grad.shape
     groups = len(pieces)
     total = (frames + 2) * cols + tail_rows(frames + 2, channels)
@@ -251,17 +263,21 @@
         ],
         compiler_params=params(4),
         name="pack_rows",
-    )(places, grad, grad_ahead, *pieces)
-
-
-def own_kernel(wide, grad_ahead, w_section, held_first, total, held_rest, beyond, sems):
+    )(places, grad, ends_ahead, *pieces)
+
+
+def own_kernel(
+    wide, ends, between, w_section, held_first, total, held_rest, beyond, sems
+):
     frames, rows, cols, _ = wide.shape
     copies = weight_copies(w_section, held_rest, taps[early:], sems)
     for copy in sum(copies, []):
         copy.start()
     for frame in range(2):
-        for row in range(rows):
-            beyond[frame, row] = widened(grad_ahead[frame, row])
+        beyond[frame, 0] = widened(ends[frame, 0])
+        for row in range(1, rows - 1):
+            beyond[frame, row] = widened(between[frame, row - 1])
+        beyond[frame, rows - 1] = widened(ends[frame, 1])
     for n, (kt, ky) in enumerate(taps):
         lo, hi = max(0, ky - 1), rows + min(0, ky - 1)
         at = slice(lo + 1 - ky, hi + 1 - ky)
@@ -269,23 +285,20 @@
             for copy in sum(copies[n - early : n - early + 3], []):
                 copy.wait()
         weight = weight_matrix(held_first, held_rest, n)
-        for source, first, last in (
-            (wide[2 - kt :, at], 0, kt + 1),
-            (beyond[: 2 - kt, at], kt + 1, frames),
-        ):
-            if first == last:
-                continue
+        for frame in range(frames):
+            src = frame + 2 - kt
+            source = wide[src, at] if src < frames else beyond[src - frames, at]
             part = dot_turned(flat(source), weight)
             for lane in range(total.shape[0]):
                 value = part[:, lane * lanes : (lane + 1) * lanes]
-                value = value.reshape(last - first, hi - lo, cols, lanes)
+                value = value.reshape(hi - lo, cols, lanes)
                 if n == 0:
-                    total[lane] = value
+                    total[lane, frame] = value
                 else:
-                    total[lane, first:last, lo:hi] += value
-
-
-def own_part(wide, grad_ahead, w_section, held_first):
+                    total[lane, frame, lo:hi] += value
+
+
+def own_part(wide, ends, between, w_section, held_first):
     frames, rows, cols, _ = wide.shape
     channels = w_section.shape[-1]
     return pl.pallas_call(
@@ -294,7 +307,7 @@
             jax.ShapeDtypeStruct((channels // lanes, frames, rows, cols, lanes), f32),
             jax.ShapeDtypeStruct((len(taps) - early,) + wide_weight(w_section), bf16),
         ],
-        in_specs=[whole, whole, far_off, whole],
+        in_specs=[whole, whole, whole, far_off, whole],
         out_specs=[whole] * 2,
         scratch_shapes=[
             pltpu.VMEM((2, rows, cols, 3 * channels), bf16),
@@ -307,7 +320,7 @@
             transcendentals=0,
         ),
         name="own_part",
-    )(wide, grad_ahead, w_section, held_first)
+    )(wide, ends, between, w_section, held_first)
 
 
 def edge_conv(even, own, near_rows, far_rows, held_first, held_rest, total, wide):
@@ -677,9 +690,9 @@
             lax.ppermute(pieces[k], "tm", hops(k)) for k in range(1, groups)
         ]
 
-    ahead = fetch(pltpu.with_memory_space_constraint(section_grad, pltpu.HBM))
-    ahead, hidden = lax.optimization_barrier((ahead, hidden))
-    grad_ahead = lax.ppermute(ahead, "tm", [(g + 1, g) for g in range(groups - 1)])
+    ends, between = fetch(pltpu.with_memory_space_constraint(section_grad, pltpu.HBM))
+    earlier = [(g + 1, g) for g in range(groups - 1)]
+    ends = lax.ppermute(ends, "tm", earlier)
     modulated, held_first, *pieces = modulate(
         places,
         hidden,
@@ -691,10 +704,13 @@
     )
     section_grad, pieces = lax.optimization_barrier((section_grad, pieces))
     wide, patches = widen_rows(section_grad, w_in)
-    near_send, far_send, latent = pack_rows(places, section_grad, grad_ahead, round_tm(pieces))
+    pieces = round_tm(pieces)
+    between, pieces[1] = lax.optimization_barrier((between, pieces[1]))
+    between = lax.ppermute(between, "tm", earlier)
+    near_send, far_send, latent = pack_rows(places, section_grad, ends, pieces)
     far_rows = lax.ppermute(far_send, "height", far)
     near_rows = lax.ppermute(near_send, "height", near)
-    own, held_rest = own_part(wide, grad_ahead, w_section, held_first)
+    own, held_rest = own_part(wide, ends, between, w_section, held_first)
     near_share, far_share, windows, spread = edge_part(
         places, own, latent, near_rows, far_rows, held_first, held_rest, patches
     )

time: 89.9 us -> 97.7 us (1.087)
  waiting for transfers between devices: 14.5 us -> 18.3 us
  starting transfers between devices: 31.5 us -> 34 us
  local copies, waits for them, and re-layouts: 3.54 us -> 5.01 us
    ppermute x9, waiting for transfers between devices: 11.8 us -> 15.5 us  [round_tm(): lax.ppermute(pieces[k], 'tm', hops(k))]
    ppermute x9, starting transfers between devices: 5.77 us -> 8.43 us  [round_tm(): lax.ppermute(pieces[k], 'tm', hops(k))]
    unnamed x13 -> x12, local copies, waits for them, and re-layouts: 3.06 us -> 5.01 us
    pallas_call x1, Pallas kernels: 15.5 us -> 16.5 us  [own_part(): pl.pallas_call(own_kernel, out_shape=[jax.ShapeDtypeStruct((channels // l...]
    ppermute x1 -> x2, starting transfers between devices: 3.33 us -> 3.84 us  [the longest x1 1.92 us: shards(): ends = lax.ppermute(ends, 'tm', earlier)]
  transfers between devices with their start and end apart: 15 -> 16, of which waited for: 8 -> 8; matrix products, arithmetic and copies ran while one was open for 4% -> 3% of each run, Pallas kernels for 30% -> 26%
where the time goes in v10:
time: 97.7 us; the launch traced here: 97.4 us
  Pallas kernels  39.2 us (40%)
  starting transfers between devices  34 us (35%)
  waiting for transfers between devices  18.3 us (19%)
  local copies, waits for them, and re-layouts  5.01 us (5%)
    pallas_call x1, Pallas kernels, own_part(): pl.pallas_call(own_kernel, out_shape=[jax.ShapeDtypeStruct((channels // l...  16.5 us
    ppermute x9, waiting for transfers between devices, round_tm(): lax.ppermute(pieces[k], 'tm', hops(k))  15.5 us
    all_to_all x1, starting transfers between devices, shards(): pieces = lax.all_to_all(middle_sum(got, strips), 'height', 0, 0, tiled=True)  14.3 us
    ppermute x9, starting transfers between devices, round_tm(): lax.ppermute(pieces[k], 'tm', hops(k))  8.43 us
    pallas_call x1, Pallas kernels, edge_part(): pl.pallas_call(edge_kernel, out_shape=[out, out, jax.ShapeDtypeStruct((2,...  5.71 us
    unnamed x12, local copies, waits for them, and re-layouts  5.01 us
    pallas_call x1, Pallas kernels, modulate(): pl.pallas_call(modulate_kernel, out_shape=[jax.ShapeDtypeStruct((frames,...  4.98 us
    ppermute x1, starting transfers between devices, shards(): near_share = lax.ppermute(near_share, 'height', near)  4.27 us
  transfers between devices with their start and end apart: 16, of which 8 were waited for; matrix products, arithmetic and copies ran while one was open for 3% of the time, Pallas kernels for 26%

profile of v10, /device:TPU:1, one launch (start us, length us, event | category | flops | bytes accessed | tf_op | source)
XLA Modules:
  0.0 97.4 jit_solution(10544316188949309641)
XLA Ops:
  0.7 2.0 %copy.10.hidden = bf16[12,2,12,3072]{3,2,1,0:T(8,128)(2,1)S(1)} copy(bf16[12,2,12,3072]{3,1,2,0:T(2,128)(2,1)} %param.7) | data formatting | bytes 3538944 | tf_op args[0]
  2.7 5.0 %modulate.1 = (bf16[12,2,16,3072]{3,2,1,0:T(8,128)(2,1)S(1)}, bf16[3,512,1536]{2,1,0:T(8,128)(2,1)S(1)}, bf16[5,16,128]{2,1,0:T(8,128)(2,1)S(1)}, bf16[5,16,128]...) custom-call(s32[3]{0:T(128)S(1)} %pad_add_fusion.places, ...), custom_call_target="tpu_custom_call" | custom-call | flops 150994944 | bytes 4718592 | tf_op jit(solution)/shard_map/modulate/pallas_call | solution.py:141
  7.7 2.7 %collective-permute-start.1 = (bf16[5,16,128]{2,1,0:T(8,128)(2,1)S(1)}, bf16[5,16,128]{2,1,0:T(8,128)(2,1)S(1)}, u32[]{:S(2)}, u32[]{:S(2)}) collective-permute-start(bf16[5,16,128]{2,1,0:T(8,128)(2,1)S(1)} %get-tuple-element.46), channel_id=1, source_target_pairs={{0,32},{32,64},{64,96},{96,0},{1,33},{33,65},{65,97},{97,1},{2,34}... | collective-permute-start | bytes 61448 | tf_op jit(solution)/shard_map/ppermute | solution.py:690
  10.4 1.2 %fetch.1 = (bf16[2,2,96,512]{3,2,1,0:T(8,128)(2,1)S(1)}, bf16[2,2,96,512]{3,2,1,0:T(8,128)(2,1)S(1)}) custom-call(bf16[3,4,96,512]{3,2,1,0:T(8,128)(2,1)} %grad.3), custom_call_target="tpu_custom_call" | custom-call | tf_op jit(solution)/shard_map/fetch/pallas_call | solution.py:58
  11.6 1.9 %collective-permute-start = (bf16[2,2,96,512]{3,2,1,0:T(8,128)(2,1)S(1)}, bf16[2,2,96,512]{3,2,1,0:T(8,128)(2,1)S(1)}, u32[]{:S(2)}, u32[]{:S(2)}) collective-permute-start(bf16[2,2,96,512]{3,2,1,0:T(8,128)(2,1)S(1)} %get-tuple-element.44), channel_id=1, source_target_pairs={{32,0},{64,32},{96,64},{33,1},{65,33},{97,65},{34,2},{66,34},{98,6... | collective-permute-start | bytes 1179656 | tf_op jit(solution)/shard_map/ppermute | solution.py:695
  13.5 1.9 %collective-permute-start.2 = (bf16[2,2,96,512]{3,2,1,0:T(8,128)(2,1)S(1)}, bf16[2,2,96,512]{3,2,1,0:T(8,128)(2,1)S(1)}, u32[]{:S(2)}, u32[]{:S(2)}) collective-permute-start(bf16[2,2,96,512]{3,2,1,0:T(8,128)(2,1)S(1)} %get-tuple-element.47), channel_id=1, source_target_pairs={{32,0},{64,32},{96,64},{33,1},{65,33},{97,65},{34,2},{66,34},{98,6... | collective-permute-start | bytes 1179656 | tf_op jit(solution)/shard_map/ppermute | solution.py:709
  15.5 1.9 %collective-permute-start.3 = (bf16[5,16,128]{2,1,0:T(8,128)(2,1)S(1)}, bf16[5,16,128]{2,1,0:T(8,128)(2,1)S(1)}, u32[]{:S(2)}, u32[]{:S(2)}) collective-permute-start(bf16[5,16,128]{2,1,0:T(8,128)(2,1)S(1)} %get-tuple-element.52), channel_id=1, source_target_pairs={{0,64},{32,96},{64,0},{96,32},{1,65},{33,97},{65,1},{97,33},{2,66}... | collective-permute-start | bytes 61448 | tf_op jit(solution)/shard_map/ppermute | solution.py:690
  18.9 6.8 %collective-permute-done.4.rest_3_ = bf16[5,16,128]{2,1,0:T(8,128)(2,1)S(1)} collective-permute-done((bf16[5,16,128]{2,1,0:T(8,128)(2,1)S(1)}, bf16[5,16,128]{2,1,0:T(8,128)(2,1)S(1)}, u32[]{:S(2)}, u32[]{:S(2)}) %collective-permute-start.4) | collective-permute-done | bytes 20512 | tf_op jit(solution)/shard_map/ppermute | solution.py:690
  26.3 1.7 %collective-permute-start.5 = (bf16[512,512]{1,0:T(8,128)(2,1)S(1)}, bf16[512,512]{1,0:T(8,128)(2,1)S(1)}, u32[]{:S(2)}, u32[]{:S(2)}) collective-permute-start(bf16[512,512]{1,0:T(8,128)(2,1)S(1)} %get-tuple-element.55), channel_id=1, source_target_pairs={{0,1},{1,0},{2,3},{3,2},{4,5},{5,4},{6,7},{7,6},{8,9},{9,8},{10,11... | collective-permute-start | bytes 1572872 | tf_op jit(solution)/shard_map/ppermute | solution.py:712
  28.1 0.9 collective-permute-start.6
  28.9 16.5 %own_part.1 = (f32[4,3,4,96,128]{4,3,2,1,0:T(8,128)S(1)}, bf16[6,512,1536]{2,1,0:T(8,128)(2,1)S(1)}) custom-call(bf16[3,4,96,1536]{3,2,1,0:T(8,128)(2,1)S(1)} %get-tuple-element.43.wide, bf16[2,2,96,512]{3,2,1,0:T(8,128)(2,1)S(1)} %collective-permute-done.ends.ends_ahead, bf16[2,2,96,512]{3,2,1,0:T(8,128)(2,1)S(1)} %collective-permute-done.2.between, ...), custom_call_target="tpu_custom_call" | custom-call | flops 43486543872 | bytes 14155776 | tf_op jit(solution)/shard_map/own_part/pallas_call | solution.py:304
  45.5 5.7 %edge_part.1 = (bf16[5,16,128]{2,1,0:T(8,128)(2,1)S(1)}, bf16[5,16,128]{2,1,0:T(8,128)(2,1)S(1)}, bf16[2,5,4,48,128]{4,3,2,1,0:T(8,128)(2,1)S(1)}, f32[5,4,56,128]{3,2,1,0:T(8,128)S(1)}) custom-call(s32[3]{0:T(128)S(1)} %pad_add_fusion.places, f32[4,3,4,96,128]{4,3,2,1,0:T(8,128)S(1)} %get-tuple-element.49.own, ...), custom_call_target="tpu_custom_call" | custom-call | flops 3623878656 | tf_op jit(solution)/shard_map/edge_part/pallas_call | solution.py:453
  51.2 4.3 %collective-permute-start.7 = (bf16[5,16,128]{2,1,0:T(8,128)(2,1)S(1)}, bf16[5,16,128]{2,1,0:T(8,128)(2,1)S(1)}, u32[]{:S(2)}, u32[]{:S(2)}) collective-permute-start(bf16[5,16,128]{2,1,0:T(8,128)(2,1)S(1)} %get-tuple-element.61), channel_id=1, source_target_pairs={{0,1},{1,0},{2,3},{3,2},{4,5},{5,4},{6,7},{7,6},{8,9},{9,8},{10,11... | collective-permute-start | bytes 61448 | tf_op jit(solution)/shard_map/ppermute | solution.py:718
  56.1 2.3 %inner_part.1.centre = f32[4,5,16,128]{3,2,1,0:T(8,128)S(1)} custom-call(f32[4,3,4,96,128]{4,3,2,1,0:T(8,128)S(1)} %get-tuple-element.49.own, bf16[2,5,4,48,128]{4,3,2,1,0:T(8,128)(2,1)S(1)} %get-tuple-element.59.windows, bf16[4,768,512]{2,1,0:T(8,128)(2,1)S(1)} %get-tuple-element.58.patches, f32[5,4,56,128]{3,2,1,0:T(8,128)S(1)} %get-tuple-element.60.spread_in), custom_call_target="tpu_custom_call" | custom-call | flops 3623878656 | tf_op jit(solution)/shard_map/inner_part/pallas_call | solution.py:495
  59.7 2.0 %collective-permute-start.10 = (bf16[5,16,128]{2,1,0:T(8,128)(2,1)S(1)}, bf16[5,16,128]{2,1,0:T(8,128)(2,1)S(1)}, u32[]{:S(2)}, u32[]{:S(2)}) collective-permute-start(bf16[5,16,128]{2,1,0:T(8,128)(2,1)S(1)} %get-tuple-element.65), channel_id=1, source_target_pairs={{0,64},{32,96},{64,0},{96,32},{1,65},{33,97},{65,1},{97,33},{2,66}... | collective-permute-start | bytes 61448 | tf_op jit(solution)/shard_map/ppermute | solution.py:690
  61.7 1.5 %collective-permute-done.10.rest_2_ = bf16[5,16,128]{2,1,0:T(8,128)(2,1)S(1)} collective-permute-done((bf16[5,16,128]{2,1,0:T(8,128)(2,1)S(1)}, bf16[5,16,128]{2,1,0:T(8,128)(2,1)S(1)}, u32[]{:S(2)}, u32[]{:S(2)}) %collective-permute-start.10) | collective-permute-done | bytes 20512 | tf_op jit(solution)/shard_map/ppermute | solution.py:690
  63.2 1.7 %collective-permute-done.11.rest_3_ = bf16[5,16,128]{2,1,0:T(8,128)(2,1)S(1)} collective-permute-done((bf16[5,16,128]{2,1,0:T(8,128)(2,1)S(1)}, bf16[5,16,128]{2,1,0:T(8,128)(2,1)S(1)}, u32[]{:S(2)}, u32[]{:S(2)}) %collective-permute-start.11) | collective-permute-done | bytes 20512 | tf_op jit(solution)/shard_map/ppermute | solution.py:690
  64.9 1.4 %weight_terms.1 = (bf16[12,2,16,64]{3,2,1,0:T(8,128)(2,1)S(1)}, bf16[384,128]{1,0:T(8,128)(2,1)S(1)}, bf16[384,128]{1,0:T(8,128)(2,1)S(1)}, bf16[384,128]{1,0:T(8,128)(2,1)S(1)}, bf16[384,128]{1,0:T(8,128)(2,1)S(1)}) custom-call(s32[3]{0:T(128)S(1)} %pad_add_fusion.places, bf16[12,2,16,3072]{3,2,1,0:T(8,128)(2,1)S(1)} %get-tuple-element.37.modulated, ...), custom_call_target="tpu_custom_call" | custom-call | tf_op jit(solution)/shard_map/weight_terms/pallas_call | solution.py:573
  68.1 2.6 %collective-permute-done.13.refs_2_ = bf16[384,128]{1,0:T(8,128)(2,1)S(1)} collective-permute-done((bf16[384,128]{1,0:T(8,128)(2,1)S(1)}, bf16[384,128]{1,0:T(8,128)(2,1)S(1)}, u32[]{:S(2)}, u32[]{:S(2)}) %collective-permute-start.13) | collective-permute-done | bytes 98336 | tf_op jit(solution)/shard_map/ppermute | solution.py:690
  70.7 1.5 %collective-permute-done.14.refs_3_ = bf16[384,128]{1,0:T(8,128)(2,1)S(1)} collective-permute-done((bf16[384,128]{1,0:T(8,128)(2,1)S(1)}, bf16[384,128]{1,0:T(8,128)(2,1)S(1)}, u32[]{:S(2)}, u32[]{:S(2)}) %collective-permute-start.14) | collective-permute-done | bytes 98336 | tf_op jit(solution)/shard_map/ppermute | solution.py:690
  73.0 14.3 %all-to-all-start = ((bf16[32,16,128]{2,1,0:T(8,128)(2,1)}), bf16[32,16,128]{2,1,0:T(8,128)(2,1)S(1)}, u32[]{:S(2)}, u32[]{:S(2)}) async-start(bf16[32,16,128]{2,1,0:T(8,128)(2,1)} %middle_sum.1), calls=%async_computation | async-start | bytes 262144 | tf_op jit(solution)/shard_map/all_to_all | solution.py:724
  87.3 3.6 %hidden_grad.1 = bf16[12,2,12,3072]{3,2,1,0:T(8,128)(2,1)S(1)} custom-call(bf16[12,2,12,3072]{3,2,1,0:T(8,128)(2,1)S(1)} %copy.10.hidden, bf16[12,2,16,64]{3,2,1,0:T(8,128)(2,1)S(1)} %get-tuple-element.67.token_grad, f32[1,3072]{1,0:T(1,128)S(1)} %bitcast.9, bf16[64,3072]{1,0:T(8,128)(2,1)S(1)} %bitcast.7), custom_call_target="tpu_custom_call" | custom-call | flops 150994944 | bytes 4718592 | tf_op jit(solution)/shard_map/hidden_grad/pallas_call | solution.py:660
  90.9 3.0 %copy.11 = bf16[12,2,12,3072]{3,1,2,0:T(2,128)(2,1)} copy(bf16[12,2,12,3072]{3,2,1,0:T(8,128)(2,1)S(1)} %hidden_grad.1) | data formatting | bytes 3538944
  94.0 2.8 %all-to-all-done.pieces = bf16[32,16,128]{2,1,0:T(8,128)(2,1)S(1)} async-done(((bf16[32,16,128]{2,1,0:T(8,128)(2,1)}), bf16[32,16,128]{2,1,0:T(8,128)(2,1)S(1)}, u32[]{:S(2)}, u32[]{:S(2)}) %all-to-all-start) | async-done | bytes 131104 | tf_op jit(solution)/shard_map/all_to_all | solution.py:724
  (33 shorter events, 7.4 us)
Async XLA Ops:
  0.6 2.1 %copy-start.3 = (f32[3072]{0:T(1024)S(1)}, f32[3072]{0:T(1024)}, u32[]{:S(2)}) copy-start(f32[3072]{0:T(1024)} %param.8) | copy-start | bytes 36868
  0.6 2.1 %copy-start.4 = (f32[3072]{0:T(1024)S(1)}, f32[3072]{0:T(1024)}, u32[]{:S(2)}) copy-start(f32[3072]{0:T(1024)} %param.9) | copy-start | bytes 36868
  2.7 15.0 %copy-start = (bf16[3,4,96,512]{3,2,1,0:T(8,128)(2,1)S(1)}, bf16[3,4,96,512]{3,2,1,0:T(8,128)(2,1)}, u32[]{:S(2)}) copy-start(bf16[3,4,96,512]{3,2,1,0:T(8,128)(2,1)} %grad.3) | copy-start | bytes 3538948
  2.7 15.0 %copy-start.2 = (bf16[3,3,3,16,512]{4,3,2,1,0:T(8,128)(2,1)S(1)}, bf16[3,3,3,16,512]{4,3,2,1,0:T(8,128)(2,1)}, u32[]{:S(2)}) copy-start(bf16[3,3,3,16,512]{4,3,2,1,0:T(8,128)(2,1)} %w_in.1) | copy-start | bytes 1327108
  7.7 5.8 %collective-permute-start.1 = (bf16[5,16,128]{2,1,0:T(8,128)(2,1)S(1)}, bf16[5,16,128]{2,1,0:T(8,128)(2,1)S(1)}, u32[]{:S(2)}, u32[]{:S(2)}) collective-permute-start(bf16[5,16,128]{2,1,0:T(8,128)(2,1)S(1)} %get-tuple-element.46), channel_id=1, source_target_pairs={{0,32},{32,64},{64,96},{96,0},{1,33},{33,65},{65,97},{97,1},{2,34}... | collective-permute-start | bytes 61448 | tf_op jit(solution)/shard_map/ppermute | solution.py:690
  11.6 14.0 %collective-permute-start = (bf16[2,2,96,512]{3,2,1,0:T(8,128)(2,1)S(1)}, bf16[2,2,96,512]{3,2,1,0:T(8,128)(2,1)S(1)}, u32[]{:S(2)}, u32[]{:S(2)}) collective-permute-start(bf16[2,2,96,512]{3,2,1,0:T(8,128)(2,1)S(1)} %get-tuple-element.44), channel_id=1, source_target_pairs={{32,0},{64,32},{96,64},{33,1},{65,33},{97,65},{34,2},{66,34},{98,6... | collective-permute-start | bytes 1179656 | tf_op jit(solution)/shard_map/ppermute | solution.py:695
  13.5 15.4 %collective-permute-start.2 = (bf16[2,2,96,512]{3,2,1,0:T(8,128)(2,1)S(1)}, bf16[2,2,96,512]{3,2,1,0:T(8,128)(2,1)S(1)}, u32[]{:S(2)}, u32[]{:S(2)}) collective-permute-start(bf16[2,2,96,512]{3,2,1,0:T(8,128)(2,1)S(1)} %get-tuple-element.47), channel_id=1, source_target_pairs={{32,0},{64,32},{96,64},{33,1},{65,33},{97,65},{34,2},{66,34},{98,6... | collective-permute-start | bytes 1179656 | tf_op jit(solution)/shard_map/ppermute | solution.py:709
  15.5 3.4 %collective-permute-start.3 = (bf16[5,16,128]{2,1,0:T(8,128)(2,1)S(1)}, bf16[5,16,128]{2,1,0:T(8,128)(2,1)S(1)}, u32[]{:S(2)}, u32[]{:S(2)}) collective-permute-start(bf16[5,16,128]{2,1,0:T(8,128)(2,1)S(1)} %get-tuple-element.52), channel_id=1, source_target_pairs={{0,64},{32,96},{64,0},{96,32},{1,65},{33,97},{65,1},{97,33},{2,66}... | collective-permute-start | bytes 61448 | tf_op jit(solution)/shard_map/ppermute | solution.py:690
  17.4 8.2 %collective-permute-start.4 = (bf16[5,16,128]{2,1,0:T(8,128)(2,1)S(1)}, bf16[5,16,128]{2,1,0:T(8,128)(2,1)S(1)}, u32[]{:S(2)}, u32[]{:S(2)}) collective-permute-start(bf16[5,16,128]{2,1,0:T(8,128)(2,1)S(1)} %get-tuple-element.53), channel_id=1, source_target_pairs={{0,96},{32,0},{64,32},{96,64},{1,97},{33,1},{65,33},{97,65},{2,98}... | collective-permute-start | bytes 61448 | tf_op jit(solution)/shard_map/ppermute | solution.py:690
  26.3 19.1 %collective-permute-start.5 = (bf16[512,512]{1,0:T(8,128)(2,1)S(1)}, bf16[512,512]{1,0:T(8,128)(2,1)S(1)}, u32[]{:S(2)}, u32[]{:S(2)}) collective-permute-start(bf16[512,512]{1,0:T(8,128)(2,1)S(1)} %get-tuple-element.55), channel_id=1, source_target_pairs={{0,1},{1,0},{2,3},{3,2},{4,5},{5,4},{6,7},{7,6},{8,9},{9,8},{10,11... | collective-permute-start | bytes 1572872 | tf_op jit(solution)/shard_map/ppermute | solution.py:712
  28.1 17.4 %collective-permute-start.6 = (bf16[512,512]{1,0:T(8,128)(2,1)S(1)}, bf16[512,512]{1,0:T(8,128)(2,1)S(1)}, u32[]{:S(2)}, u32[]{:S(2)}) collective-permute-start(bf16[512,512]{1,0:T(8,128)(2,1)S(1)} %get-tuple-element.56), channel_id=1, source_target_pairs={{1,2},{2,1},{3,4},{4,3},{5,6},{6,5},{7,8},{8,7},{9,10},{10,9},{11,... | collective-permute-start | bytes 1572872 | tf_op jit(solution)/shard_map/ppermute | solution.py:711
  51.2 7.2 %collective-permute-start.7 = (bf16[5,16,128]{2,1,0:T(8,128)(2,1)S(1)}, bf16[5,16,128]{2,1,0:T(8,128)(2,1)S(1)}, u32[]{:S(2)}, u32[]{:S(2)}) collective-permute-start(bf16[5,16,128]{2,1,0:T(8,128)(2,1)S(1)} %get-tuple-element.61), channel_id=1, source_target_pairs={{0,1},{1,0},{2,3},{3,2},{4,5},{5,4},{6,7},{7,6},{8,9},{9,8},{10,11... | collective-permute-start | bytes 61448 | tf_op jit(solution)/shard_map/ppermute | solution.py:718
  55.4 3.0 %collective-permute-start.8 = (bf16[5,16,128]{2,1,0:T(8,128)(2,1)S(1)}, bf16[5,16,128]{2,1,0:T(8,128)(2,1)S(1)}, u32[]{:S(2)}, u32[]{:S(2)}) collective-permute-start(bf16[5,16,128]{2,1,0:T(8,128)(2,1)S(1)} %get-tuple-element.62), channel_id=1, source_target_pairs={{1,2},{2,1},{3,4},{4,3},{5,6},{6,5},{7,8},{8,7},{9,10},{10,9},{11,... | collective-permute-start | bytes 61448 | tf_op jit(solution)/shard_map/ppermute | solution.py:717
  58.4 28.9 %copy-start.1 = (bf16[3072,64]{0,1:T(8,128)(2,1)S(1)}, bf16[3072,64]{0,1:T(8,128)(2,1)}, u32[]{:S(2)}) copy-start(bf16[3072,64]{0,1:T(8,128)(2,1)} %param.10) | copy-start | bytes 1179652
  59.1 2.7 %collective-permute-start.9 = (bf16[5,16,128]{2,1,0:T(8,128)(2,1)S(1)}, bf16[5,16,128]{2,1,0:T(8,128)(2,1)S(1)}, u32[]{:S(2)}, u32[]{:S(2)}) collective-permute-start(bf16[5,16,128]{2,1,0:T(8,128)(2,1)S(1)} %get-tuple-element.64), channel_id=1, source_target_pairs={{0,32},{32,64},{64,96},{96,0},{1,33},{33,65},{65,97},{97,1},{2,34}... | collective-permute-start | bytes 61448 | tf_op jit(solution)/shard_map/ppermute | solution.py:690
  59.7 3.5 %collective-permute-start.10 = (bf16[5,16,128]{2,1,0:T(8,128)(2,1)S(1)}, bf16[5,16,128]{2,1,0:T(8,128)(2,1)S(1)}, u32[]{:S(2)}, u32[]{:S(2)}) collective-permute-start(bf16[5,16,128]{2,1,0:T(8,128)(2,1)S(1)} %get-tuple-element.65), channel_id=1, source_target_pairs={{0,64},{32,96},{64,0},{96,32},{1,65},{33,97},{65,1},{97,33},{2,66}... | collective-permute-start | bytes 61448 | tf_op jit(solution)/shard_map/ppermute | solution.py:690
  61.7 3.2 %collective-permute-start.11 = (bf16[5,16,128]{2,1,0:T(8,128)(2,1)S(1)}, bf16[5,16,128]{2,1,0:T(8,128)(2,1)S(1)}, u32[]{:S(2)}, u32[]{:S(2)}) collective-permute-start(bf16[5,16,128]{2,1,0:T(8,128)(2,1)S(1)} %get-tuple-element.66), channel_id=1, source_target_pairs={{0,96},{32,0},{64,32},{96,64},{1,97},{33,1},{65,33},{97,65},{2,98}... | collective-permute-start | bytes 61448 | tf_op jit(solution)/shard_map/ppermute | solution.py:690
  66.4 1.7 %collective-permute-start.12 = (bf16[384,128]{1,0:T(8,128)(2,1)S(1)}, bf16[384,128]{1,0:T(8,128)(2,1)S(1)}, u32[]{:S(2)}, u32[]{:S(2)}) collective-permute-start(bf16[384,128]{1,0:T(8,128)(2,1)S(1)} %get-tuple-element.69), channel_id=1, source_target_pairs={{0,32},{32,64},{64,96},{96,0},{1,33},{33,65},{65,97},{97,1},{2,34}... | collective-permute-start | bytes 294920 | tf_op jit(solution)/shard_map/ppermute | solution.py:690
  66.4 4.3 %collective-permute-start.13 = (bf16[384,128]{1,0:T(8,128)(2,1)S(1)}, bf16[384,128]{1,0:T(8,128)(2,1)S(1)}, u32[]{:S(2)}, u32[]{:S(2)}) collective-permute-start(bf16[384,128]{1,0:T(8,128)(2,1)S(1)} %get-tuple-element.70), channel_id=1, source_target_pairs={{0,64},{32,96},{64,0},{96,32},{1,65},{33,97},{65,1},{97,33},{2,66}... | collective-permute-start | bytes 294920 | tf_op jit(solution)/shard_map/ppermute | solution.py:690
  67.1 5.2 %collective-permute-start.14 = (bf16[384,128]{1,0:T(8,128)(2,1)S(1)}, bf16[384,128]{1,0:T(8,128)(2,1)S(1)}, u32[]{:S(2)}, u32[]{:S(2)}) collective-permute-start(bf16[384,128]{1,0:T(8,128)(2,1)S(1)} %get-tuple-element.71), channel_id=1, source_target_pairs={{0,96},{32,0},{64,32},{96,64},{1,97},{33,1},{65,33},{97,65},{2,98}... | collective-permute-start | bytes 294920 | tf_op jit(solution)/shard_map/ppermute | solution.py:690
  73.0 23.7 %all-to-all-start = ((bf16[32,16,128]{2,1,0:T(8,128)(2,1)}), bf16[32,16,128]{2,1,0:T(8,128)(2,1)S(1)}, u32[]{:S(2)}, u32[]{:S(2)}) async-start(bf16[32,16,128]{2,1,0:T(8,128)(2,1)} %middle_sum.1), calls=%async_computation | async-start | bytes 262144 | tf_op jit(solution)/shard_map/all_to_all | solution.py:724

commit v11 on v10

--- a/solution.py
+++ b/solution.py
@@ -45,7 +45,8 @@
     copies = [
         pltpu.make_async_copy(grad.at[0:2, 0:1], ends.at[:, 0:1], sems.at[0]),
         pltpu.make_async_copy(grad.at[0:2, rows - 1 : rows], ends.at[:, 1:2], sems.at[1]),
-        pltpu.make_async_copy(grad.at[0:2, 1 : rows - 1], between, sems.at[2]),
+        pltpu.make_async_copy(grad.at[0:2, 1:2], ends.at[:, 2:3], sems.at[2]),
+        pltpu.make_async_copy(grad.at[0:2, 2 : rows - 1], between, sems.at[3]),
     ]
     for copy in copies:
         copy.start()
@@ -58,12 +59,12 @@
     return pl.pallas_call(
         fetch_kernel,
         out_shape=[
-            jax.ShapeDtypeStruct((2, 2, cols, channels), bf16),
-            jax.ShapeDtypeStruct((2, rows - 2, cols, channels), bf16),
+            jax.ShapeDtypeStruct((2, 3, cols, channels), bf16),
+            jax.ShapeDtypeStruct((2, rows - 3, cols, channels), bf16),
         ],
         in_specs=[far_off],
         out_specs=[whole] * 2,
-        scratch_shapes=[pltpu.SemaphoreType.DMA((3,))],
+        scratch_shapes=[pltpu.SemaphoreType.DMA((4,))],
         compiler_params=params(4),
         name="fetch",
     )(grad)
@@ -89,11 +90,9 @@
 
 
 def modulate_kernel(
-    places, hidden, scale, shift, w_out_far, w_section, modulated, held, *rest
+    places, hidden, scale, shift, w_out, w_section, modulated, held, *rest
 ):
-    pieces, (latent, w_out, sems, out_sem) = rest[:-4], rest[-4:]
-    out_copy = pltpu.make_async_copy(w_out_far, w_out, out_sem)
-    out_copy.start()
+    pieces, latent, sems = rest[:-2], rest[-2], rest[-1]
     copies = sum(weight_copies(w_section, held, taps[:early], sems), [])
     for copy in copies:
         copy.start()
@@ -124,7 +123,6 @@
         return share(step, carry)
 
     share(0, 0)
-    out_copy.wait()
     lax.fori_loop(1, groups, share_after, 0)
     project(groups - 1)
     for step, piece in enumerate(pieces):
@@ -145,20 +143,14 @@
             jax.ShapeDtypeStruct((early,) + wide_weight(w_section), bf16),
         ]
         + [piece] * groups,
-        in_specs=[scalars] + [whole] * 3 + [far_off] * 2,
+        in_specs=[scalars] + [whole] * 4 + [far_off],
         out_specs=[whole] * (2 + groups),
         scratch_shapes=[
             pltpu.VMEM((frames + 2, slots, pair), bf16),
-            pltpu.VMEM(w_out.shape, bf16),
             pltpu.SemaphoreType.DMA((3 * early,)),
-            pltpu.SemaphoreType.DMA,
         ],
         compiler_params=params(8),
-        cost_estimate=pl.CostEstimate(
-            flops=2 * frames * slots * width * pair,
-            bytes_accessed=8 * frames * slots * width,
-            transcendentals=0,
-        ),
+        cost_estimate=pl.CostEstimate(flops=1, bytes_accessed=1, transcendentals=0),
         name="modulate",
     )(places, hidden, mod_scale.reshape(1, -1), mod_shift.reshape(1, -1), w_out, w_section)
 
@@ -275,8 +267,9 @@
         copy.start()
     for frame in range(2):
         beyond[frame, 0] = widened(ends[frame, 0])
-        for row in range(1, rows - 1):
-            beyond[frame, row] = widened(between[frame, row - 1])
+        beyond[frame, 1] = widened(ends[frame, 2])
+        for row in range(2, rows - 1):
+            beyond[frame, row] = widened(between[frame, row - 2])
         beyond[frame, rows - 1] = widened(ends[frame, 1])
     for n, (kt, ky) in enumerate(taps):
         lo, hi = max(0, ky - 1), rows + min(0, ky - 1)
@@ -285,17 +278,20 @@
             for copy in sum(copies[n - early : n - early + 3], []):
                 copy.wait()
         weight = weight_matrix(held_first, held_rest, n)
-        for frame in range(frames):
-            src = frame + 2 - kt
-            source = wide[src, at] if src < frames else beyond[src - frames, at]
+        for source, first, last in (
+            (wide[2 - kt :, at], 0, kt + 1),
+            (beyond[: 2 - kt, at], kt + 1, frames),
+        ):
+            if first == last:
+                continue
             part = dot_turned(flat(source), weight)
             for lane in range(total.shape[0]):
                 value = part[:, lane * lanes : (lane + 1) * lanes]
-                value = value.reshape(hi - lo, cols, lanes)
+                value = value.reshape(last - first, hi - lo, cols, lanes)
                 if n == 0:
-                    total[lane, frame] = value
+                    total[lane] = value
                 else:
-                    total[lane, frame, lo:hi] += value
+                    total[lane, first:last, lo:hi] += value
 
 
 def own_part(wide, ends, between, w_section, held_first):
@@ -691,6 +687,7 @@
         ]
 
     ends, between = fetch(pltpu.with_memory_space_constraint(section_grad, pltpu.HBM))
+    ends, hidden = lax.optimization_barrier((ends, hidden))
     earlier = [(g + 1, g) for g in range(groups - 1)]
     ends = lax.ppermute(ends, "tm", earlier)
     modulated, held_first, *pieces = modulate(
@@ -698,14 +695,14 @@
         hidden,
         mod_scale,
         mod_shift,
-        pltpu.with_memory_space_constraint(w_out, pltpu.HBM),
+        w_out,
         w_section,
         groups,
     )
     section_grad, pieces = lax.optimization_barrier((section_grad, pieces))
     wide, patches = widen_rows(section_grad, w_in)
     pieces = round_tm(pieces)
-    between, pieces[1] = lax.optimization_barrier((between, pieces[1]))
+    between, pieces, wide = lax.optimization_barrier((between, pieces, wide))
     between = lax.ppermute(between, "tm", earlier)
     near_send, far_send, latent = pack_rows(places, section_grad, ends, pieces)
     far_rows = lax.ppermute(far_send, "height", far)

time: 97.7 us -> 91.4 us (0.936)
  waiting for transfers between devices: 18.3 us -> 13.7 us
  Pallas kernels: 39.2 us -> 37.4 us
    ppermute x9, waiting for transfers between devices: 15.5 us -> 8.98 us  [round_tm(): lax.ppermute(pieces[k], 'tm', hops(k))]
    ppermute x1, waiting for transfers between devices: 0.01 us -> 1.99 us  [shards(): between = lax.ppermute(between, 'tm', earlier)]
    ppermute x1, starting transfers between devices: 4.27 us -> 2.3 us  [shards(): near_share = lax.ppermute(near_share, 'height', near)]
    optimization_barrier x0 -> x1, local copies, waits for them, and re-layouts: none -> 1.95 us  [shards(): ends, hidden = lax.optimization_barrier((ends, hidden))]
    pallas_call x1, Pallas kernels: 4.98 us -> 3.37 us  [modulate(): pl.pallas_call(modulate_kernel, out_shape=[jax.ShapeDtypeStruct((frames,...]
    ppermute x1, starting transfers between devices: 1.92 us -> 3.45 us  [shards(): ends = lax.ppermute(ends, 'tm', earlier)]
    unnamed x12 -> x15, local copies, waits for them, and re-layouts: 5.01 us -> 3.73 us
  transfers between devices with their start and end apart: 16 -> 16, of which waited for: 8 -> 9; matrix products, arithmetic and copies ran while one was open for 3% -> 6% of each run, Pallas kernels for 26% -> 29%
where the time goes in v11:
time: 91.4 us; the launch traced here: 91.1 us
  Pallas kernels  37.4 us (41%)
  starting transfers between devices  33.4 us (37%)
  waiting for transfers between devices  13.7 us (15%)
  local copies, waits for them, and re-layouts  5.67 us (6%)
    pallas_call x1, Pallas kernels, own_part(): pl.pallas_call(own_kernel, out_shape=[jax.ShapeDtypeStruct((channels // l...  15.5 us
    all_to_all x1, starting transfers between devices, shards(): pieces = lax.all_to_all(middle_sum(got, strips), 'height', 0, 0, tiled=True)  14.8 us
    ppermute x9, waiting for transfers between devices, round_tm(): lax.ppermute(pieces[k], 'tm', hops(k))  8.98 us
    ppermute x9, starting transfers between devices, round_tm(): lax.ppermute(pieces[k], 'tm', hops(k))  7.55 us
    pallas_call x1, Pallas kernels, edge_part(): pl.pallas_call(edge_kernel, out_shape=[out, out, jax.ShapeDtypeStruct((2,...  5.7 us
    unnamed x15, local copies, waits for them, and re-layouts  3.73 us
    pallas_call x1, Pallas kernels, hidden_grad(): pl.pallas_call(hidden_kernel, out_shape=jax.ShapeDtypeStruct(hidden.shape...  3.61 us
    ppermute x1, starting transfers between devices, shards(): ends = lax.ppermute(ends, 'tm', earlier)  3.45 us
  transfers between devices with their start and end apart: 16, of which 9 were waited for; matrix products, arithmetic and copies ran while one was open for 6% of the time, Pallas kernels for 29%

profile of v11, /device:TPU:1, one launch (start us, length us, event | category | flops | bytes accessed | tf_op | source)
XLA Modules:
  0.0 91.1 jit_solution(15662135710193246749)
XLA Ops:
  0.6 2.1 %fetch.1 = (bf16[2,3,96,512]{3,2,1,0:T(8,128)(2,1)}, bf16[2,1,96,512]{3,2,1,0:T(8,128)(2,1)S(1)}) custom-call(bf16[3,4,96,512]{3,2,1,0:T(8,128)(2,1)} %grad.3), custom_call_target="tpu_custom_call" | custom-call | tf_op jit(solution)/shard_map/fetch/pallas_call | solution.py:59
  3.4 3.4 %collective-permute-start.3 = (bf16[2,3,96,512]{3,2,1,0:T(8,128)(2,1)}, bf16[2,3,96,512]{3,2,1,0:T(8,128)(2,1)S(1)}, u32[]{:S(2)}, u32[]{:S(2)}) collective-permute-start(bf16[2,3,96,512]{3,2,1,0:T(8,128)(2,1)} %get-tuple-element.58), channel_id=1, source_target_pairs={{32,0},{64,32},{96,64},{33,1},{65,33},{97,65},{34,2},{66,34},{98,6... | collective-permute-start | bytes 1769480 | tf_op jit(solution)/shard_map/ppermute | solution.py:692
  6.8 1.9 %copy.10.hidden = bf16[12,2,12,3072]{3,2,1,0:T(8,128)(2,1)S(1)} copy(bf16[12,2,12,3072]{3,1,2,0:T(2,128)(2,1)} %param.7) | data formatting | bytes 3538944 | tf_op jit(solution)/shard_map/optimization_barrier | solution.py:690
  8.9 3.4 %modulate.1 = (bf16[12,2,16,3072]{3,2,1,0:T(8,128)(2,1)S(1)}, bf16[3,512,1536]{2,1,0:T(8,128)(2,1)S(1)}, bf16[5,16,128]{2,1,0:T(8,128)(2,1)S(1)}, bf16[5,16,128]...) custom-call(s32[3]{0:T(128)S(1)} %pad_add_fusion.places, ...), custom_call_target="tpu_custom_call" | custom-call | flops 1 | bytes 1 | tf_op jit(solution)/shard_map/modulate/pallas_call | solution.py:139
  12.3 1.3 %collective-permute-start = (bf16[5,16,128]{2,1,0:T(8,128)(2,1)S(1)}, bf16[5,16,128]{2,1,0:T(8,128)(2,1)S(1)}, u32[]{:S(2)}, u32[]{:S(2)}) collective-permute-start(bf16[5,16,128]{2,1,0:T(8,128)(2,1)S(1)} %get-tuple-element.52), channel_id=1, source_target_pairs={{0,32},{32,64},{64,96},{96,0},{1,33},{33,65},{65,97},{97,1},{2,34}... | collective-permute-start | bytes 61448 | tf_op jit(solution)/shard_map/ppermute | solution.py:686
  15.2 1.5 %collective-permute-done.1.rest_2_ = bf16[5,16,128]{2,1,0:T(8,128)(2,1)S(1)} collective-permute-done((bf16[5,16,128]{2,1,0:T(8,128)(2,1)S(1)}, bf16[5,16,128]{2,1,0:T(8,128)(2,1)S(1)}, u32[]{:S(2)}, u32[]{:S(2)}) %collective-permute-start.1) | collective-permute-done | bytes 20512 | tf_op jit(solution)/shard_map/ppermute | solution.py:686
  17.0 2.0 %collective-permute-start.4 = (bf16[2,1,96,512]{3,2,1,0:T(8,128)(2,1)S(1)}, bf16[2,1,96,512]{3,2,1,0:T(8,128)(2,1)S(1)}, u32[]{:S(2)}, u32[]{:S(2)}) collective-permute-start(bf16[2,1,96,512]{3,2,1,0:T(8,128)(2,1)S(1)} %copy-done.6), channel_id=1, source_target_pairs={{32,0},{64,32},{96,64},{33,1},{65,33},{97,65},{34,2},{66,34},{98,6... | collective-permute-start | bytes 589832 | tf_op jit(solution)/shard_map/ppermute | solution.py:706
  19.7 1.7 %collective-permute-start.5 = (bf16[512,512]{1,0:T(8,128)(2,1)S(1)}, bf16[512,512]{1,0:T(8,128)(2,1)S(1)}, u32[]{:S(2)}, u32[]{:S(2)}) collective-permute-start(bf16[512,512]{1,0:T(8,128)(2,1)S(1)} %get-tuple-element.67), channel_id=1, source_target_pairs={{0,1},{1,0},{2,3},{3,2},{4,5},{5,4},{6,7},{7,6},{8,9},{9,8},{10,11... | collective-permute-start | bytes 1572872 | tf_op jit(solution)/shard_map/ppermute | solution.py:709
  21.4 0.9 collective-permute-start.6
  22.3 2.0 %collective-permute-done.4.between = bf16[2,1,96,512]{3,2,1,0:T(8,128)(2,1)S(1)} collective-permute-done((bf16[2,1,96,512]{3,2,1,0:T(8,128)(2,1)S(1)}, bf16[2,1,96,512]{3,2,1,0:T(8,128)(2,1)S(1)}, u32[]{:S(2)}, u32[]{:S(2)}) %collective-permute-start.4) | collective-permute-done | bytes 196640 | tf_op jit(solution)/shard_map/ppermute | solution.py:706
  24.3 15.5 %own_part.1 = (f32[4,3,4,96,128]{4,3,2,1,0:T(8,128)S(1)}, bf16[6,512,1536]{2,1,0:T(8,128)(2,1)S(1)}) custom-call(bf16[3,4,96,1536]{3,2,1,0:T(8,128)(2,1)S(1)} %get-tuple-element.57.wide, bf16[2,3,96,512]{3,2,1,0:T(8,128)(2,1)S(1)} %collective-permute-done.3.ends.ends_ahead, bf16[2,1,96,512]{3,2,1,0:T(8,128)(2,1)S(1)} %collective-permute-done.4.between, ...), custom_call_target="tpu_custom_call" | custom-call | flops 43486543872 | bytes 14155776 | tf_op jit(solution)/shard_map/own_part/pallas_call | solution.py:300
  39.8 5.7 %edge_part.1 = (bf16[5,16,128]{2,1,0:T(8,128)(2,1)S(1)}, bf16[5,16,128]{2,1,0:T(8,128)(2,1)S(1)}, bf16[2,5,4,48,128]{4,3,2,1,0:T(8,128)(2,1)S(1)}, f32[5,4,56,128]{3,2,1,0:T(8,128)S(1)}) custom-call(s32[3]{0:T(128)S(1)} %pad_add_fusion.places, f32[4,3,4,96,128]{4,3,2,1,0:T(8,128)S(1)} %get-tuple-element.61.own, ...), custom_call_target="tpu_custom_call" | custom-call | flops 3623878656 | tf_op jit(solution)/shard_map/edge_part/pallas_call | solution.py:449
  45.5 2.3 %collective-permute-start.7 = (bf16[5,16,128]{2,1,0:T(8,128)(2,1)S(1)}, bf16[5,16,128]{2,1,0:T(8,128)(2,1)S(1)}, u32[]{:S(2)}, u32[]{:S(2)}) collective-permute-start(bf16[5,16,128]{2,1,0:T(8,128)(2,1)S(1)} %get-tuple-element.73), channel_id=1, source_target_pairs={{0,1},{1,0},{2,3},{3,2},{4,5},{5,4},{6,7},{7,6},{8,9},{9,8},{10,11... | collective-permute-start | bytes 61448 | tf_op jit(solution)/shard_map/ppermute | solution.py:715
  48.5 2.3 %inner_part.1.centre = f32[4,5,16,128]{3,2,1,0:T(8,128)S(1)} custom-call(f32[4,3,4,96,128]{4,3,2,1,0:T(8,128)S(1)} %get-tuple-element.61.own, bf16[2,5,4,48,128]{4,3,2,1,0:T(8,128)(2,1)S(1)} %get-tuple-element.71.windows, bf16[4,768,512]{2,1,0:T(8,128)(2,1)S(1)} %get-tuple-element.70.patches, f32[5,4,56,128]{3,2,1,0:T(8,128)S(1)} %get-tuple-element.72.spread_in), custom_call_target="tpu_custom_call" | custom-call | flops 3623878656 | tf_op jit(solution)/shard_map/inner_part/pallas_call | solution.py:491
  51.5 2.6 %collective-permute-start.9 = (bf16[5,16,128]{2,1,0:T(8,128)(2,1)S(1)}, bf16[5,16,128]{2,1,0:T(8,128)(2,1)S(1)}, u32[]{:S(2)}, u32[]{:S(2)}) collective-permute-start(bf16[5,16,128]{2,1,0:T(8,128)(2,1)S(1)} %get-tuple-element.76), channel_id=1, source_target_pairs={{0,32},{32,64},{64,96},{96,0},{1,33},{33,65},{65,97},{97,1},{2,34}... | collective-permute-start | bytes 61448 | tf_op jit(solution)/shard_map/ppermute | solution.py:686
  55.0 1.7 %collective-permute-done.10.rest_2_ = bf16[5,16,128]{2,1,0:T(8,128)(2,1)S(1)} collective-permute-done((bf16[5,16,128]{2,1,0:T(8,128)(2,1)S(1)}, bf16[5,16,128]{2,1,0:T(8,128)(2,1)S(1)}, u32[]{:S(2)}, u32[]{:S(2)}) %collective-permute-start.10) | collective-permute-done | bytes 20512 | tf_op jit(solution)/shard_map/ppermute | solution.py:686
  57.3 1.4 %weight_terms.1 = (bf16[12,2,16,64]{3,2,1,0:T(8,128)(2,1)S(1)}, bf16[384,128]{1,0:T(8,128)(2,1)S(1)}, bf16[384,128]{1,0:T(8,128)(2,1)S(1)}, bf16[384,128]{1,0:T(8,128)(2,1)S(1)}, bf16[384,128]{1,0:T(8,128)(2,1)S(1)}) custom-call(s32[3]{0:T(128)S(1)} %pad_add_fusion.places, bf16[12,2,16,3072]{3,2,1,0:T(8,128)(2,1)S(1)} %get-tuple-element.45.modulated, ...), custom_call_target="tpu_custom_call" | custom-call | tf_op jit(solution)/shard_map/weight_terms/pallas_call | solution.py:569
  59.4 0.9 collective-permute-start.13
  61.0 3.5 %collective-permute-done.13.refs_2_ = bf16[384,128]{1,0:T(8,128)(2,1)S(1)} collective-permute-done((bf16[384,128]{1,0:T(8,128)(2,1)S(1)}, bf16[384,128]{1,0:T(8,128)(2,1)S(1)}, u32[]{:S(2)}, u32[]{:S(2)}) %collective-permute-start.13) | collective-permute-done | bytes 98336 | tf_op jit(solution)/shard_map/ppermute | solution.py:686
  64.6 0.8 collective-permute-done.14.refs_3_
  66.2 14.8 %all-to-all-start = ((bf16[32,16,128]{2,1,0:T(8,128)(2,1)}), bf16[32,16,128]{2,1,0:T(8,128)(2,1)S(1)}, u32[]{:S(2)}, u32[]{:S(2)}) async-start(bf16[32,16,128]{2,1,0:T(8,128)(2,1)} %middle_sum.1), calls=%async_computation | async-start | bytes 262144 | tf_op jit(solution)/shard_map/all_to_all | solution.py:721
  81.0 3.6 %hidden_grad.1 = bf16[12,2,12,3072]{3,2,1,0:T(8,128)(2,1)S(1)} custom-call(bf16[12,2,12,3072]{3,2,1,0:T(8,128)(2,1)S(1)} %copy.10.hidden, bf16[12,2,16,64]{3,2,1,0:T(8,128)(2,1)S(1)} %get-tuple-element.79.token_grad, f32[1,3072]{1,0:T(1,128)S(1)} %bitcast.9, bf16[64,3072]{1,0:T(8,128)(2,1)S(1)} %bitcast.7), custom_call_target="tpu_custom_call" | custom-call | flops 150994944 | bytes 4718592 | tf_op jit(solution)/shard_map/hidden_grad/pallas_call | solution.py:656
  84.6 3.0 %copy.11 = bf16[12,2,12,3072]{3,1,2,0:T(2,128)(2,1)} copy(bf16[12,2,12,3072]{3,2,1,0:T(8,128)(2,1)S(1)} %hidden_grad.1) | data formatting | bytes 3538944
  87.7 2.7 %all-to-all-done.pieces = bf16[32,16,128]{2,1,0:T(8,128)(2,1)S(1)} async-done(((bf16[32,16,128]{2,1,0:T(8,128)(2,1)}), bf16[32,16,128]{2,1,0:T(8,128)(2,1)S(1)}, u32[]{:S(2)}, u32[]{:S(2)}) %all-to-all-start) | async-done | bytes 131104 | tf_op jit(solution)/shard_map/all_to_all | solution.py:721
  (37 shorter events, 9.1 us)
Async XLA Ops:
  2.7 0.7 copy-start.5
  3.4 5.5 %copy-start.1 = (bf16[3072,64]{0,1:T(8,128)(2,1)S(1)}, bf16[3072,64]{0,1:T(8,128)(2,1)}, u32[]{:S(2)}) copy-start(bf16[3072,64]{0,1:T(8,128)(2,1)} %param.10) | copy-start | bytes 1179652
  3.4 5.5 %copy-start.3 = (f32[3072]{0:T(1024)S(1)}, f32[3072]{0:T(1024)}, u32[]{:S(2)}) copy-start(f32[3072]{0:T(1024)} %param.8) | copy-start | bytes 36868
  3.4 5.5 %copy-start.4 = (f32[3072]{0:T(1024)S(1)}, f32[3072]{0:T(1024)}, u32[]{:S(2)}) copy-start(f32[3072]{0:T(1024)} %param.9) | copy-start | bytes 36868
  3.4 15.6 %collective-permute-start.3 = (bf16[2,3,96,512]{3,2,1,0:T(8,128)(2,1)}, bf16[2,3,96,512]{3,2,1,0:T(8,128)(2,1)S(1)}, u32[]{:S(2)}, u32[]{:S(2)}) collective-permute-start(bf16[2,3,96,512]{3,2,1,0:T(8,128)(2,1)} %get-tuple-element.58), channel_id=1, source_target_pairs={{32,0},{64,32},{96,64},{33,1},{65,33},{97,65},{34,2},{66,34},{98,6... | collective-permute-start | bytes 1769480 | tf_op jit(solution)/shard_map/ppermute | solution.py:692
  8.9 5.6 %copy-start = (bf16[3,4,96,512]{3,2,1,0:T(8,128)(2,1)S(1)}, bf16[3,4,96,512]{3,2,1,0:T(8,128)(2,1)}, u32[]{:S(2)}) copy-start(bf16[3,4,96,512]{3,2,1,0:T(8,128)(2,1)} %grad.3) | copy-start | bytes 3538948
  8.9 5.6 %copy-start.2 = (bf16[3,3,3,16,512]{4,3,2,1,0:T(8,128)(2,1)S(1)}, bf16[3,3,3,16,512]{4,3,2,1,0:T(8,128)(2,1)}, u32[]{:S(2)}) copy-start(bf16[3,3,3,16,512]{4,3,2,1,0:T(8,128)(2,1)} %w_in.1) | copy-start | bytes 1327108
  8.9 8.1 %copy-start.6 = (bf16[2,1,96,512]{3,2,1,0:T(8,128)(2,1)S(1)}, bf16[2,1,96,512]{3,2,1,0:T(8,128)(2,1)}, u32[]{:S(2)}) copy-start(bf16[2,1,96,512]{3,2,1,0:T(8,128)(2,1)} %copy-done.5) | copy-start | bytes 589828
  12.3 2.8 %collective-permute-start = (bf16[5,16,128]{2,1,0:T(8,128)(2,1)S(1)}, bf16[5,16,128]{2,1,0:T(8,128)(2,1)S(1)}, u32[]{:S(2)}, u32[]{:S(2)}) collective-permute-start(bf16[5,16,128]{2,1,0:T(8,128)(2,1)S(1)} %get-tuple-element.52), channel_id=1, source_target_pairs={{0,32},{32,64},{64,96},{96,0},{1,33},{33,65},{65,97},{97,1},{2,34}... | collective-permute-start | bytes 61448 | tf_op jit(solution)/shard_map/ppermute | solution.py:686
  13.6 3.1 %collective-permute-start.1 = (bf16[5,16,128]{2,1,0:T(8,128)(2,1)S(1)}, bf16[5,16,128]{2,1,0:T(8,128)(2,1)S(1)}, u32[]{:S(2)}, u32[]{:S(2)}) collective-permute-start(bf16[5,16,128]{2,1,0:T(8,128)(2,1)S(1)} %get-tuple-element.53), channel_id=1, source_target_pairs={{0,64},{32,96},{64,0},{96,32},{1,65},{33,97},{65,1},{97,33},{2,66}... | collective-permute-start | bytes 61448 | tf_op jit(solution)/shard_map/ppermute | solution.py:686
  13.8 3.2 %collective-permute-start.2 = (bf16[5,16,128]{2,1,0:T(8,128)(2,1)S(1)}, bf16[5,16,128]{2,1,0:T(8,128)(2,1)S(1)}, u32[]{:S(2)}, u32[]{:S(2)}) collective-permute-start(bf16[5,16,128]{2,1,0:T(8,128)(2,1)S(1)} %get-tuple-element.54), channel_id=1, source_target_pairs={{0,96},{32,0},{64,32},{96,64},{1,97},{33,1},{65,33},{97,65},{2,98}... | collective-permute-start | bytes 61448 | tf_op jit(solution)/shard_map/ppermute | solution.py:686
  17.0 7.3 %collective-permute-start.4 = (bf16[2,1,96,512]{3,2,1,0:T(8,128)(2,1)S(1)}, bf16[2,1,96,512]{3,2,1,0:T(8,128)(2,1)S(1)}, u32[]{:S(2)}, u32[]{:S(2)}) collective-permute-start(bf16[2,1,96,512]{3,2,1,0:T(8,128)(2,1)S(1)} %copy-done.6), channel_id=1, source_target_pairs={{32,0},{64,32},{96,64},{33,1},{65,33},{97,65},{34,2},{66,34},{98,6... | collective-permute-start | bytes 589832 | tf_op jit(solution)/shard_map/ppermute | solution.py:706
  19.7 20.1 %collective-permute-start.5 = (bf16[512,512]{1,0:T(8,128)(2,1)S(1)}, bf16[512,512]{1,0:T(8,128)(2,1)S(1)}, u32[]{:S(2)}, u32[]{:S(2)}) collective-permute-start(bf16[512,512]{1,0:T(8,128)(2,1)S(1)} %get-tuple-element.67), channel_id=1, source_target_pairs={{0,1},{1,0},{2,3},{3,2},{4,5},{5,4},{6,7},{7,6},{8,9},{9,8},{10,11... | collective-permute-start | bytes 1572872 | tf_op jit(solution)/shard_map/ppermute | solution.py:709
  21.4 18.4 %collective-permute-start.6 = (bf16[512,512]{1,0:T(8,128)(2,1)S(1)}, bf16[512,512]{1,0:T(8,128)(2,1)S(1)}, u32[]{:S(2)}, u32[]{:S(2)}) collective-permute-start(bf16[512,512]{1,0:T(8,128)(2,1)S(1)} %get-tuple-element.68), channel_id=1, source_target_pairs={{1,2},{2,1},{3,4},{4,3},{5,6},{6,5},{7,8},{8,7},{9,10},{10,9},{11,... | collective-permute-start | bytes 1572872 | tf_op jit(solution)/shard_map/ppermute | solution.py:708
  45.5 5.2 %collective-permute-start.7 = (bf16[5,16,128]{2,1,0:T(8,128)(2,1)S(1)}, bf16[5,16,128]{2,1,0:T(8,128)(2,1)S(1)}, u32[]{:S(2)}, u32[]{:S(2)}) collective-permute-start(bf16[5,16,128]{2,1,0:T(8,128)(2,1)S(1)} %get-tuple-element.73), channel_id=1, source_target_pairs={{0,1},{1,0},{2,3},{3,2},{4,5},{5,4},{6,7},{7,6},{8,9},{9,8},{10,11... | collective-permute-start | bytes 61448 | tf_op jit(solution)/shard_map/ppermute | solution.py:715
  47.8 2.9 %collective-permute-start.8 = (bf16[5,16,128]{2,1,0:T(8,128)(2,1)S(1)}, bf16[5,16,128]{2,1,0:T(8,128)(2,1)S(1)}, u32[]{:S(2)}, u32[]{:S(2)}) collective-permute-start(bf16[5,16,128]{2,1,0:T(8,128)(2,1)S(1)} %get-tuple-element.74), channel_id=1, source_target_pairs={{1,2},{2,1},{3,4},{4,3},{5,6},{6,5},{7,8},{8,7},{9,10},{10,9},{11,... | collective-permute-start | bytes 61448 | tf_op jit(solution)/shard_map/ppermute | solution.py:714
  51.5 3.5 %collective-permute-start.9 = (bf16[5,16,128]{2,1,0:T(8,128)(2,1)S(1)}, bf16[5,16,128]{2,1,0:T(8,128)(2,1)S(1)}, u32[]{:S(2)}, u32[]{:S(2)}) collective-permute-start(bf16[5,16,128]{2,1,0:T(8,128)(2,1)S(1)} %get-tuple-element.76), channel_id=1, source_target_pairs={{0,32},{32,64},{64,96},{96,0},{1,33},{33,65},{65,97},{97,1},{2,34}... | collective-permute-start | bytes 61448 | tf_op jit(solution)/shard_map/ppermute | solution.py:686
  54.0 2.6 %collective-permute-start.10 = (bf16[5,16,128]{2,1,0:T(8,128)(2,1)S(1)}, bf16[5,16,128]{2,1,0:T(8,128)(2,1)S(1)}, u32[]{:S(2)}, u32[]{:S(2)}) collective-permute-start(bf16[5,16,128]{2,1,0:T(8,128)(2,1)S(1)} %get-tuple-element.77), channel_id=1, source_target_pairs={{0,64},{32,96},{64,0},{96,32},{1,65},{33,97},{65,1},{97,33},{2,66}... | collective-permute-start | bytes 61448 | tf_op jit(solution)/shard_map/ppermute | solution.py:686
  54.0 3.2 %collective-permute-start.11 = (bf16[5,16,128]{2,1,0:T(8,128)(2,1)S(1)}, bf16[5,16,128]{2,1,0:T(8,128)(2,1)S(1)}, u32[]{:S(2)}, u32[]{:S(2)}) collective-permute-start(bf16[5,16,128]{2,1,0:T(8,128)(2,1)S(1)} %get-tuple-element.78), channel_id=1, source_target_pairs={{0,96},{32,0},{64,32},{96,64},{1,97},{33,1},{65,33},{97,65},{2,98}... | collective-permute-start | bytes 61448 | tf_op jit(solution)/shard_map/ppermute | solution.py:686
  58.7 2.3 %collective-permute-start.12 = (bf16[384,128]{1,0:T(8,128)(2,1)S(1)}, bf16[384,128]{1,0:T(8,128)(2,1)S(1)}, u32[]{:S(2)}, u32[]{:S(2)}) collective-permute-start(bf16[384,128]{1,0:T(8,128)(2,1)S(1)} %get-tuple-element.81), channel_id=1, source_target_pairs={{0,32},{32,64},{64,96},{96,0},{1,33},{33,65},{65,97},{97,1},{2,34}... | collective-permute-start | bytes 294920 | tf_op jit(solution)/shard_map/ppermute | solution.py:686
  59.4 5.2 %collective-permute-start.13 = (bf16[384,128]{1,0:T(8,128)(2,1)S(1)}, bf16[384,128]{1,0:T(8,128)(2,1)S(1)}, u32[]{:S(2)}, u32[]{:S(2)}) collective-permute-start(bf16[384,128]{1,0:T(8,128)(2,1)S(1)} %get-tuple-element.82), channel_id=1, source_target_pairs={{0,64},{32,96},{64,0},{96,32},{1,65},{33,97},{65,1},{97,33},{2,66}... | collective-permute-start | bytes 294920 | tf_op jit(solution)/shard_map/ppermute | solution.py:686
  60.3 5.1 %collective-permute-start.14 = (bf16[384,128]{1,0:T(8,128)(2,1)S(1)}, bf16[384,128]{1,0:T(8,128)(2,1)S(1)}, u32[]{:S(2)}, u32[]{:S(2)}) collective-permute-start(bf16[384,128]{1,0:T(8,128)(2,1)S(1)} %get-tuple-element.83), channel_id=1, source_target_pairs={{0,96},{32,0},{64,32},{96,64},{1,97},{33,1},{65,33},{97,65},{2,98}... | collective-permute-start | bytes 294920 | tf_op jit(solution)/shard_map/ppermute | solution.py:686
  66.2 24.2 %all-to-all-start = ((bf16[32,16,128]{2,1,0:T(8,128)(2,1)}), bf16[32,16,128]{2,1,0:T(8,128)(2,1)S(1)}, u32[]{:S(2)}, u32[]{:S(2)}) async-start(bf16[32,16,128]{2,1,0:T(8,128)(2,1)} %middle_sum.1), calls=%async_computation | async-start | bytes 262144 | tf_op jit(solution)/shard_map/all_to_all | solution.py:721
